TPU v7x, 32 devices: a whole 2x2x4 slice. The times are simulated.
32 devices in a mesh: space: 8 (over z, y), rhs: 4 (over x, core).
Axes of the slice: x: 2, y: 2, z: 4, core: 2. Of those that a mesh axis runs over, the one named last changes fastest.
Arguments:
- rhs_vec: float32 [64, 8192], P('rhs', 'space'), may hold values from -40 to 40
- self_coef: float32 [8192], P('space'), may hold values from 2 to 4
- near_mats: bfloat16 [64, 8, 128, 128], P('space'), may hold values from -0.1875 to 0.1875
- near_ids: int32 [64, 8], P('space'), may hold values from 0 to 63, as said below
- near_count: int32 [64], P('space'), may hold values from 3 to 8, as said below
- interp: bfloat16 [64, 128, 32], P('space'), may hold values from -0.5 to 0.5
- skel_idx: int32 [64, 32], P('space'), may hold values from 0 to 127, as said below
- coupling: bfloat16 [2048, 4, 512], P('space', 'rhs'), may hold values from -0.0625 to 0.0625
- diag_prec: float32 [8192], P('space'), may hold values from 1.5 to 4
- low_rank: float32 [8192, 512], P('space'), may hold values from -0.029646353 to 0.029646353
Outputs:
- solution: float32 [64, 8192], P('rhs', 'space')
Inputs may be any that keep to these rules, and one draw needn't show every extreme that they name: `near_ids`: slot 0 of each block names the block itself, slot 1 a block of the region before it (of its own region for the first region), slot 2 a block of the region after it (of its own region for the last region); every entry names a block of the same 8-block region or of the region before or after it. `near_count`: some regions use all 8 slots in every block. `skel_idx`: each row holds 32 distinct panel numbers of its block, rising.
All inputs are finite; a program needn't handle non-finite values.
Results may differ from a plain program's by a relative error of at most 0.001.
Values may be sent and summed in bfloat16 or wider, within the bound.
No kernel may reach another device: no remote copies, remote signals or barrier semaphores. Data moves between devices by JAX's collectives and lax.ppermute only.
A program may use at most 64 MiB of HBM per device.

v0:
```python
import jax
import jax.numpy as jnp
from jax import lax
from jax.sharding import PartitionSpec as P

HIGH = lax.Precision.HIGHEST
EPS = 1e-06


def padded(cells, sides, width):
    for axis, dim in sides:
        count = lax.axis_size(axis)
        ends = count - 1
        head = lax.slice_in_dim(cells, 0, width, axis=dim)
        tail = lax.slice_in_dim(cells, cells.shape[dim] - width, cells.shape[dim], axis=dim)
        cells = jnp.concatenate(
            [
                lax.ppermute(tail, axis, [(i, (i + 1) % count) for i in range(ends)]),
                cells,
                lax.ppermute(head, axis, [((i + 1) % count, i) for i in range(ends)]),
            ],
            axis=dim,
        )
    return cells


def givens_pair(start_len, diag_one, below_one, upper_two, diag_two, below_two):
    radius_one = jnp.sqrt(diag_one * diag_one + below_one * below_one)
    cos_one = diag_one / radius_one
    sin_one = below_one / radius_one
    upper = cos_one * upper_two + sin_one * diag_two
    lower = cos_one * diag_two - sin_one * upper_two
    radius_two = jnp.sqrt(lower * lower + below_two * below_two)
    step_two = lower / radius_two * (-sin_one * start_len) / radius_two
    step_one = (cos_one * start_len - upper * step_two) / radius_one
    return (step_one, step_two)


def column_sum(values):
    return jnp.sum(values, axis=1)


def on_device(
    rhs_vec,
    self_coef,
    near_mats,
    near_ids,
    near_count,
    interp,
    skel_idx,
    coupling,
    diag_prec,
    low_rank,
):
    excitations, panels = rhs_vec.shape
    block_count, slot_count, block_width, _ = near_mats.shape
    skel_rank = interp.shape[2]
    quarters = lax.axis_size("rhs")
    quarter_len = skel_rank * block_count // quarters
    region = lax.axis_index("space")
    onehot = (
        skel_idx[:, :, None] == jnp.arange(block_width, dtype=jnp.int32)[None, None, :]
    ).astype(jnp.float32)
    restrict = onehot + jnp.swapaxes(interp.astype(jnp.float32), 1, 2)
    local_ids = near_ids - (region - 1) * block_count
    live_slots = jnp.arange(slot_count, dtype=jnp.int32)[None, :] < near_count[:, None]
    full_rows = lax.all_gather(coupling, "rhs", axis=1, tiled=True)

    def precond(vector):
        projected = lax.psum(jnp.dot(vector, low_rank, precision=HIGH), "space")
        return diag_prec[None, :] * vector - jnp.dot(projected, low_rank.T, precision=HIGH)

    def operate(field):
        field_low = field.astype(jnp.bfloat16)
        extended = padded(field_low, (("space", 1),), panels)
        blocks = extended.reshape(excitations, 3 * block_count, block_width)
        picked = blocks[:, local_ids] * live_slots[None, :, :, None].astype(jnp.bfloat16)
        near = jnp.einsum("bkij,ebkj->ebi", near_mats, picked, preferred_element_type=jnp.float32)
        own_blocks = field_low.reshape(excitations, block_count, block_width).astype(jnp.float32)
        charges = jnp.einsum("brj,ebj->ebr", restrict, own_blocks, precision=HIGH)
        packed = charges.astype(jnp.bfloat16).reshape(excitations, quarters, quarter_len)
        charges_in = lax.all_gather(packed, "space", axis=2, tiled=True)
        far_field = jnp.einsum(
            "sqc,eqc->es", full_rows, charges_in, preferred_element_type=jnp.float32
        )
        far_pot = jnp.einsum(
            "brj,ebr->ebj",
            restrict,
            far_field.reshape(excitations, block_count, skel_rank),
            precision=HIGH,
        )
        return (
            self_coef[None, :] * field
            + near.reshape(excitations, panels)
            + far_pot.reshape(excitations, panels)
        )

    def orthogonalize(residue, basis_vecs):
        coeffs = lax.psum(
            jnp.stack([column_sum(residue * basis_one) for basis_one in basis_vecs]), "space"
        )
        for index_one in range(len(basis_vecs)):
            residue = residue - coeffs[index_one][:, None] * basis_vecs[index_one]
        length = jnp.sqrt(lax.psum(column_sum(residue * residue), "space") + EPS)
        return (residue, coeffs, length)

    start_len = jnp.sqrt(lax.psum(column_sum(rhs_vec * rhs_vec), "space") + EPS)
    first_dir = rhs_vec / start_len[:, None]
    first_pre = precond(first_dir)
    residue, coeffs_one, below_one = orthogonalize(operate(first_pre), [first_dir])
    second_dir = residue / below_one[:, None]
    second_pre = precond(second_dir)
    residue, coeffs_two, below_two = orthogonalize(operate(second_pre), [first_dir, second_dir])
    step_one, step_two = givens_pair(
        start_len, coeffs_one[0], below_one, coeffs_two[0], coeffs_two[1], below_two
    )
    return step_one[:, None] * first_pre + step_two[:, None] * second_pre


def solution(mesh):
    placed = (
        P("rhs", "space"),
        P("space"),
        P("space", None, None, None),
        P("space", None),
        P("space"),
        P("space", None, None),
        P("space", None),
        P("space", "rhs", None),
        P("space"),
        P("space", None),
    )
    return jax.shard_map(
        on_device, mesh=mesh, in_specs=placed, out_specs=P("rhs", "space"), check_vma=False
    )
```

profile of v0, /device:TPU:0, one launch (start us, length us, event | category | flops | bytes accessed | tf_op | source)
XLA Modules:
  0.0 272.9 jit_solution(2316246552183812912)
XLA Ops:
  6.5 0.0 copy-start
  6.5 1.1 multiply_reduce_fusion.5
  7.7 0.0 all-gather.2.cloned.1.call-update
  7.7 23.2 %psum.49 = f32[16]{0:T(128)S(1)} all-reduce(f32[16]{0:T(128)S(1)} %multiply_reduce_fusion.5), channel_id=1, replica_groups=mesh['space'=8,'rhs'=4] {'space'}, use_global_device_ids=true, to_apply=%region_1.0 | all-reduce | flops 16 | bytes 128 | tf_op jit(solution)/shard_map/psum | solution.py:107
  30.9 0.0 copy-start.17
  30.9 0.0 copy-start.18
  30.9 0.0 copy-start.3
  30.9 0.0 copy-start.11
  30.9 2.0 fusion.22
  32.9 33.0 %psum.50 = f32[16,512]{1,0:T(8,128)S(1)} all-reduce(f32[16,512]{1,0:T(8,128)S(1)} %fusion.22), channel_id=1, replica_groups=mesh['space'=8,'rhs'=4] {'space'}, use_global_device_ids=true, to_apply=%region_2.0 | all-reduce | flops 8192 | bytes 65536 | tf_op jit(solution)/shard_map/psum | solution.py:70
  65.9 0.0 copy-done.10
  65.9 1.8 fusion.23
  67.7 0.0 copy-done.19
  67.8 1.3 collective-permute-start.1
  69.1 4.5 %collective-permute-start = (bf16[16,1024]{1,0:T(8,128)(2,1)S(1)}, bf16[16,1024]{1,0:T(8,128)(2,1)S(1)}, u32[]{:S(2)}, u32[]{:S(2)}) collective-permute-start(bf16[16,1024]{1,0:T(8,128)(2,1)S(1)} %get-tuple-element.14), channel_id=1, source_target_pairs={{0,4},{4,8},{8,12},{12,16},{16,20},{20,24},{24,28},{1,5},{5,9},{9,... | collective-permute-start | bytes 98312 | tf_op jit(solution)/shard_map/ppermute | solution.py:18
  73.6 0.1 reshape.84
  73.7 0.1 fusion.20
  73.8 0.3 fusion
  74.2 0.1 reshape.72
  74.2 0.1 copy.39
  74.4 31.6 %all_gather.9 = bf16[16,4,512]{0,1,2:T(4,128)(2,1)S(1)} all-gather(bf16[16,4,64]{0,1,2:T(4,128)(2,1)S(1)} %copy.39), channel_id=1, replica_groups=mesh['space'=8,'rhs'=4] {'space'}, dimensions={2}, use_global_device_ids=true | all-gather | bytes 73728 | tf_op jit(solution)/shard_map/all_gather | solution.py:82
  106.0 0.0 collective-permute-done.1
  106.0 0.0 collective-permute-done
  106.0 0.6 gather_fusion
  106.7 0.0 copy-start.13
  106.7 2.3 convolution_bitcast_fusion.3
  109.0 1.6 convolution_bitcast_fusion.5
  110.6 0.0 copy-done.4
  110.6 0.1 reshape.73
  110.7 0.3 convolution_bitcast_fusion.1
  111.0 0.0 copy-done.13
  111.0 0.2 multiply_reduce_fusion.4
  111.2 17.1 %psum.51 = f32[16]{0:T(128)S(1)} all-reduce(f32[16]{0:T(128)S(1)} %get-tuple-element.10), channel_id=1, replica_groups=mesh['space'=8,'rhs'=4] {'space'}, use_global_device_ids=true, to_apply=%region_4.0 | all-reduce | flops 16 | bytes 128 | tf_op jit(solution)/shard_map/psum | solution.py:99
  128.3 0.2 multiply_reduce_fusion.3
  128.5 19.1 %psum.52 = f32[16]{0:T(128)S(1)} all-reduce(f32[16]{0:T(128)S(1)} %multiply_reduce_fusion.3), channel_id=1, replica_groups=mesh['space'=8,'rhs'=4] {'space'}, use_global_device_ids=true, to_apply=%region_6.0 | all-reduce | flops 16 | bytes 128 | tf_op jit(solution)/shard_map/psum | solution.py:104
  147.7 0.1 broadcast_divide_fusion
  147.8 0.5 copy-done.21
  148.3 1.1 fusion.25
  149.4 33.1 %psum.53 = f32[16,512]{1,0:T(8,128)S(1)} all-reduce(f32[16,512]{1,0:T(8,128)S(1)} %fusion.25), channel_id=1, replica_groups=mesh['space'=8,'rhs'=4] {'space'}, use_global_device_ids=true, to_apply=%region_7.0 | all-reduce | flops 8192 | bytes 65536 | tf_op jit(solution)/shard_map/psum | solution.py:70
  182.5 2.4 fusion.24
  185.0 1.1 fusion.1
  186.0 1.3 collective-permute-start.3
  187.3 5.2 %collective-permute-start.2 = (bf16[16,1024]{1,0:T(8,128)(2,1)}, bf16[16,1024]{1,0:T(8,128)(2,1)}, u32[]{:S(2)}, u32[]{:S(2)}) collective-permute-start(bf16[16,1024]{1,0:T(8,128)(2,1)} %get-tuple-element.16), channel_id=1, source_target_pairs={{0,4},{4,8},{8,12},{12,16},{16,20},{20,24},{24,28},{1,5},{5,9},{9,... | collective-permute-start | bytes 98312 | tf_op jit(solution)/shard_map/ppermute | solution.py:18
  192.5 0.1 reshape.78
  192.6 0.1 copy.47
  192.7 0.0 copy-start.12
  192.7 31.2 %all_gather.11 = bf16[16,4,512]{0,1,2:T(4,128)(2,1)S(1)} all-gather(bf16[16,4,64]{0,1,2:T(4,128)(2,1)S(1)} %copy.47), channel_id=1, replica_groups=mesh['space'=8,'rhs'=4] {'space'}, dimensions={2}, use_global_device_ids=true | all-gather | bytes 73728 | tf_op jit(solution)/shard_map/all_gather | solution.py:82
  223.9 0.4 convolution_bitcast_fusion.4
  224.3 0.0 copy-start.14
  224.3 0.0 copy-start.16
  224.3 0.0 copy-start.20
  224.4 0.1 reshape.79
  224.4 0.3 convolution_bitcast_fusion
  224.8 0.0 collective-permute-done.3
  224.8 0.0 collective-permute-done.2
  224.8 0.8 copy_bitcast_fusion
  225.6 0.6 gather_fusion.1
  226.3 2.3 convolution_bitcast_fusion.2
  228.5 0.0 copy-done.14
  228.6 0.2 multiply_reduce_fusion.2
  228.8 17.2 %psum.54 = f32[2,16]{1,0:T(2,128)S(1)} all-reduce(f32[2,16]{1,0:T(2,128)S(1)} %pad_maximum_fusion), channel_id=1, replica_groups=mesh['space'=8,'rhs'=4] {'space'}, use_global_device_ids=true, to_apply=%region_10.0 | all-reduce | flops 32 | bytes 256 | tf_op jit(solution)/shard_map/psum | solution.py:99
  245.9 0.2 multiply_reduce_fusion
  246.1 19.1 %psum.55 = f32[16]{0:T(128)S(1)} all-reduce(f32[16]{0:T(128)S(1)} %multiply_reduce_fusion), channel_id=1, replica_groups=mesh['space'=8,'rhs'=4] {'space'}, use_global_device_ids=true, to_apply=%region_12.0 | all-reduce | flops 16 | bytes 128 | tf_op jit(solution)/shard_map/psum | solution.py:104
  265.3 0.7 multiply_add_fusion
  (42 shorter events, 0.2 us)
Async XLA Ops:
  6.5 24.3 %copy-start = (f32[1024,512]{1,0:T(8,128)S(1)}, f32[1024,512]{1,0:T(8,128)}, u32[]{:S(2)}) copy-start(f32[1024,512]{1,0:T(8,128)} %param.19) | copy-start | bytes 6291460
  6.5 59.4 %copy-start.1 = (f32[16,1024]{1,0:T(8,128)S(1)}, f32[16,1024]{1,0:T(8,128)}, u32[]{:S(2)}) copy-start(f32[16,1024]{1,0:T(8,128)} %param.10) | copy-start | bytes 196612
  6.5 59.4 %copy-start.10 = (f32[1024]{0:T(1024)S(1)}, f32[1024]{0:T(1024)}, u32[]{:S(2)}) copy-start(f32[1024]{0:T(1024)} %param.18) | copy-start | bytes 12292
  6.5 102.4 %all-gather.2.cloned.1.call-start = ((), (), s32[]{:S(2)}) async-start(), calls=%async_computation | async-start | bytes 1310720 | tf_op jit(solution)/shard_map/all_gather | solution.py:67
  30.8 36.9 %copy-start.19 = (f32[16]{0:T(128)}, f32[16]{0:T(128)S(1)}, u32[]{:S(2)}) copy-start(f32[16]{0:T(128)S(1)} %psum.49) | copy-start | bytes 196
  30.9 116.8 %copy-start.6 = (f32[16]{0:T(128)}, f32[16]{0:T(128)S(1)}, u32[]{:S(2)}) copy-start(f32[16]{0:T(128)S(1)} %add_sqrt_fusion.2) | copy-start | bytes 196
  30.9 42.8 %copy-start.17 = (s32[8,8]{1,0:T(8,128)S(1)}, s32[8,8]{1,0:T(8,128)}, u32[]{:S(2)}) copy-start(s32[8,8]{1,0:T(8,128)} %param.13) | copy-start | bytes 772
  30.9 42.8 %copy-start.18 = (s32[8]{0:T(128)S(1)}, s32[8]{0:T(128)}, u32[]{:S(2)}) copy-start(s32[8]{0:T(128)} %param.14) | copy-start | bytes 100
  30.9 42.9 %copy-start.3 = (bf16[8,128,32]{1,2,0:T(8,128)(2,1)S(1)}, bf16[8,128,32]{1,2,0:T(8,128)(2,1)}, u32[]{:S(2)}) copy-start(bf16[8,128,32]{1,2,0:T(8,128)(2,1)} %param.15) | copy-start | bytes 196612
  30.9 42.9 %copy-start.11 = (s32[8,32]{1,0:T(8,128)S(1)}, s32[8,32]{1,0:T(8,128)}, u32[]{:S(2)}) copy-start(s32[8,32]{1,0:T(8,128)} %param.16) | copy-start | bytes 3076
  67.8 38.2 %collective-permute-start.1 = (bf16[16,1024]{1,0:T(8,128)(2,1)S(1)}, bf16[16,1024]{1,0:T(8,128)(2,1)S(1)}, u32[]{:S(2)}, u32[]{:S(2)}) collective-permute-start(bf16[16,1024]{1,0:T(8,128)(2,1)S(1)} %get-tuple-element.14), channel_id=1, source_target_pairs={{4,0},{8,4},{12,8},{16,12},{20,16},{24,20},{28,24},{5,1},{9,5},{13... | collective-permute-start | bytes 98312 | tf_op jit(solution)/shard_map/ppermute | solution.py:20
  69.1 37.0 %collective-permute-start = (bf16[16,1024]{1,0:T(8,128)(2,1)S(1)}, bf16[16,1024]{1,0:T(8,128)(2,1)S(1)}, u32[]{:S(2)}, u32[]{:S(2)}) collective-permute-start(bf16[16,1024]{1,0:T(8,128)(2,1)S(1)} %get-tuple-element.14), channel_id=1, source_target_pairs={{0,4},{4,8},{8,12},{12,16},{16,20},{20,24},{24,28},{1,5},{5,9},{9,... | collective-permute-start | bytes 98312 | tf_op jit(solution)/shard_map/ppermute | solution.py:18
  73.8 36.8 %copy-start.8 = (bf16[8,8]{1,0:T(8,128)(2,1)}, bf16[8,8]{1,0:T(8,128)(2,1)S(1)}, u32[]{:S(2)}) copy-start(bf16[8,8]{1,0:T(8,128)(2,1)S(1)} %fusion.20) | copy-start | bytes 388
  74.1 36.5 %copy-start.4 = (s32[1024]{0:T(1024)}, s32[1024]{0:T(1024)S(1)}, u32[]{:S(2)}) copy-start(s32[1024]{0:T(1024)S(1)} %pad_clamp_fusion) | copy-start | bytes 12292
  106.7 4.3 %copy-start.13 = (f32[1024]{0:T(1024)S(1)}, f32[1024]{0:T(1024)}, u32[]{:S(2)}) copy-start(f32[1024]{0:T(1024)} %param.11) | copy-start | bytes 12292
  128.3 19.4 %copy-start.15 = (f32[16]{0:T(128)}, f32[16]{0:T(128)S(1)}, u32[]{:S(2)}) copy-start(f32[16]{0:T(128)S(1)} %psum.51) | copy-start | bytes 196
  147.7 0.6 copy-start.21
  149.4 74.6 %copy-start.2 = (bf16[256,4,512]{2,0,1:T(8,128)(2,1)S(1)}, bf16[256,4,512]{2,0,1:T(8,128)(2,1)}, u32[]{:S(2)}) copy-start(bf16[256,4,512]{2,0,1:T(8,128)(2,1)} %all-gather.2.cloned.1.call-done) | copy-start | bytes 3145732
  186.0 38.7 %collective-permute-start.3 = (bf16[16,1024]{1,0:T(8,128)(2,1)}, bf16[16,1024]{1,0:T(8,128)(2,1)}, u32[]{:S(2)}, u32[]{:S(2)}) collective-permute-start(bf16[16,1024]{1,0:T(8,128)(2,1)} %get-tuple-element.16), channel_id=1, source_target_pairs={{4,0},{8,4},{12,8},{16,12},{20,16},{24,20},{28,24},{5,1},{9,5},{13... | collective-permute-start | bytes 98312 | tf_op jit(solution)/shard_map/ppermute | solution.py:20
  187.3 37.5 %collective-permute-start.2 = (bf16[16,1024]{1,0:T(8,128)(2,1)}, bf16[16,1024]{1,0:T(8,128)(2,1)}, u32[]{:S(2)}, u32[]{:S(2)}) collective-permute-start(bf16[16,1024]{1,0:T(8,128)(2,1)} %get-tuple-element.16), channel_id=1, source_target_pairs={{0,4},{4,8},{8,12},{12,16},{16,20},{20,24},{24,28},{1,5},{5,9},{9,... | collective-permute-start | bytes 98312 | tf_op jit(solution)/shard_map/ppermute | solution.py:18
  192.7 31.7 %copy-start.12 = (s32[8,32]{1,0:T(8,128)S(1)}, s32[8,32]{1,0:T(8,128)}, u32[]{:S(2)}) copy-start(s32[8,32]{1,0:T(8,128)} %param.16) | copy-start | bytes 3076
  192.7 32.9 %copy-start.5 = (s32[1024]{0:T(1024)S(1)}, s32[1024]{0:T(1024)}, u32[]{:S(2)}) copy-start(s32[1024]{0:T(1024)} %copy-done.4) | copy-start | bytes 12292
  192.7 33.5 %copy-start.9 = (bf16[8,8]{1,0:T(8,128)(2,1)S(1)}, bf16[8,8]{1,0:T(8,128)(2,1)}, u32[]{:S(2)}) copy-start(bf16[8,8]{1,0:T(8,128)(2,1)} %copy-done.8) | copy-start | bytes 388
  224.3 4.2 %copy-start.7 = (f32[16]{0:T(128)S(1)}, f32[16]{0:T(128)}, u32[]{:S(2)}) copy-start(f32[16]{0:T(128)} %copy-done.6) | copy-start | bytes 196
  224.3 4.2 %copy-start.14 = (f32[1024]{0:T(1024)S(1)}, f32[1024]{0:T(1024)}, u32[]{:S(2)}) copy-start(f32[1024]{0:T(1024)} %param.11) | copy-start | bytes 12292
  224.3 40.9 %copy-start.16 = (f32[16]{0:T(128)S(1)}, f32[16]{0:T(128)}, u32[]{:S(2)}) copy-start(f32[16]{0:T(128)} %copy-done.15) | copy-start | bytes 196
  224.3 40.9 %copy-start.20 = (f32[16]{0:T(128)S(1)}, f32[16]{0:T(128)}, u32[]{:S(2)}) copy-start(f32[16]{0:T(128)} %copy-done.19) | copy-start | bytes 196
  224.3 40.9 %copy-start.22 = (f32[16]{0:T(128)S(1)}, f32[16]{0:T(128)}, u32[]{:S(2)}) copy-start(f32[16]{0:T(128)} %copy-done.21) | copy-start | bytes 196
Sparse Core Ops, SparseCore 0:
  8.9 19.4 all-gather.1
where the time goes:
time: 274 us; the launch traced here: 273 us
  blocking collectives  225 us (82%)
  matrix products  15.9 us (6%)
  between operations  13.7 us (5%)
  starting transfers between devices  12.3 us (4%)
  other arithmetic  3.68 us (1%)
    psum x2, blocking collectives, precond(): projected = lax.psum(jnp.dot(vector, low_rank, precision=HIGH), 'space')  66.1 us
    all_gather x2, blocking collectives, operate(): charges_in = lax.all_gather(packed, 'space', axis=2, tiled=True)  62.8 us
    psum x2, blocking collectives, orthogonalize(): length = jnp.sqrt(lax.psum(column_sum(residue * residue), 'space') + EPS)  38.2 us
    psum x2, blocking collectives, orthogonalize(): lax.psum(jnp.stack([column_sum(residue * basis_one) for basis_one in basi...  34.3 us
    psum x1, blocking collectives, on_device(): start_len = jnp.sqrt(lax.psum(column_sum(rhs_vec * rhs_vec), 'space') + EPS)  23.2 us
    ppermute x2, starting transfers between devices, padded(): lax.ppermute(tail, axis, [(i, (i + 1) % count) for i in range(ends)])  9.71 us
  transfers between devices with their start and end apart: 5, of which 0 were waited for; matrix products, arithmetic and copies ran while one was open for 3% of the time, Pallas kernels for 0%

commit v1 on v0

v1 whole, which is shorter than its diff:
```python
import jax
import jax.numpy as jnp
from jax import lax
from jax.sharding import PartitionSpec as P

HIGH = lax.Precision.HIGH
EPS = 1e-06
BF = jnp.bfloat16
AXIS = "space"


def swap(values, mask, count):
    return lax.ppermute(values, AXIS, [(i, i ^ mask) for i in range(count)])


def total(values, count):
    if count != 8:
        return lax.psum(values, AXIS)
    pair = values + swap(values, 1, count)
    return (pair + swap(pair, 2, count)) + (swap(pair, 4, count) + swap(pair, 6, count))


def total_small(values, count):
    if count != 8:
        return lax.psum(values, AXIS)
    spread = jnp.broadcast_to(values[None], (count,) + values.shape)
    return jnp.sum(lax.all_to_all(spread, AXIS, 0, 0), axis=0)


def exchange(field, charges, count, region):
    excitations, panels = field.shape
    rank = charges.shape[1]
    if count != 8:
        ends = count - 1
        lower = lax.ppermute(field, AXIS, [(i, i + 1) for i in range(ends)])
        upper = lax.ppermute(field, AXIS, [(i + 1, i) for i in range(ends)])
        return [lower, field, upper], lax.all_gather(charges, AXIS)
    own = jnp.concatenate([field, charges], axis=1)
    near = swap(own, 1, count)
    pair = jnp.concatenate([charges, near[:, panels:], near[:, :panels]], axis=1)
    two = swap(pair, 2, count)
    four = swap(pair[:, : 2 * rank], 4, count)
    six = swap(pair, 6, count)
    by_mask = []
    for part in (pair, two, four, six):
        by_mask += [part[:, :rank], part[:, rank : 2 * rank]]
    stacked = jnp.stack(by_mask)
    order = jnp.arange(count, dtype=jnp.int32) ^ region
    return [field, near[:, :panels], two[:, 2 * rank :], six[:, 2 * rank :]], stacked[order]


def block_places(near_ids, block_count, count, region):
    if count != 8:
        return near_ids - (region - 1) * block_count
    source = near_ids // block_count
    slot = jnp.where(
        source == region,
        0,
        jnp.where(source == region ^ 1, 1, jnp.where(source == region ^ 3, 2, 3)),
    )
    return slot * block_count + near_ids % block_count


def givens_pair(start_len, diag_one, below_one, upper_two, diag_two, below_two):
    radius_one = jnp.sqrt(diag_one * diag_one + below_one * below_one)
    cos_one = diag_one / radius_one
    sin_one = below_one / radius_one
    upper = cos_one * upper_two + sin_one * diag_two
    lower = cos_one * diag_two - sin_one * upper_two
    radius_two = jnp.sqrt(lower * lower + below_two * below_two)
    step_two = lower / radius_two * (-sin_one * start_len) / radius_two
    step_one = (cos_one * start_len - upper * step_two) / radius_one
    return (step_one, step_two)


def dots(vector, others):
    return jnp.stack([jnp.sum(vector * other, axis=1) for other in others], axis=1)


def on_device(
    rhs_vec,
    self_coef,
    near_mats,
    near_ids,
    near_count,
    interp,
    skel_idx,
    coupling,
    diag_prec,
    low_rank,
):
    excitations, panels = rhs_vec.shape
    block_count, slot_count, block_width, _ = near_mats.shape
    skel_rank = interp.shape[2]
    quarters = lax.axis_size("rhs")
    count = lax.axis_size(AXIS)
    quarter_len = skel_rank * block_count // quarters
    low_rank_width = low_rank.shape[1]
    region = lax.axis_index(AXIS)
    onehot = (
        skel_idx[:, :, None] == jnp.arange(block_width, dtype=jnp.int32)[None, None, :]
    ).astype(BF)
    weights = jnp.swapaxes(interp, 1, 2)
    restrict_in = jnp.concatenate([onehot, weights], axis=2)
    restrict_out = jnp.concatenate([onehot, weights, onehot, weights], axis=1)
    places = block_places(near_ids, block_count, count, region)
    live_slots = jnp.arange(slot_count, dtype=jnp.int32)[None, :] < near_count[:, None]
    full_rows = lax.all_gather(coupling, "rhs", axis=1, tiled=True)
    full_rows = full_rows.reshape(skel_rank * block_count, quarters, count, quarter_len)

    def project(vector):
        return jnp.dot(vector, low_rank, precision=HIGH)

    def precond(vector, projected):
        return diag_prec[None, :] * vector - jnp.dot(projected, low_rank.T, precision=HIGH)

    def operate(field):
        field_low = field.astype(BF)
        own_blocks = field_low.reshape(excitations, block_count, block_width)
        charges = jnp.einsum(
            "brj,ebj->ebr",
            restrict_in,
            jnp.concatenate([own_blocks, own_blocks], axis=2),
            preferred_element_type=jnp.float32,
        )
        packed = charges.astype(BF).reshape(excitations, skel_rank * block_count)
        sources, charges_in = exchange(field_low, packed, count, region)
        blocks = jnp.concatenate(
            [part.reshape(excitations, block_count, block_width) for part in sources], axis=1
        )
        picked = blocks[:, places] * live_slots[None, :, :, None].astype(BF)
        near = jnp.einsum("bkij,ebkj->ebi", near_mats, picked, preferred_element_type=jnp.float32)
        far_field = jnp.einsum(
            "gqsj,seqj->eg",
            full_rows,
            charges_in.reshape(count, excitations, quarters, quarter_len),
            preferred_element_type=jnp.float32,
        ).reshape(excitations, block_count, skel_rank)
        far_high = far_field.astype(BF)
        far_low = (far_field - far_high.astype(jnp.float32)).astype(BF)
        far_pot = jnp.einsum(
            "brj,ebr->ebj",
            restrict_out,
            jnp.concatenate([far_high, far_high, far_low, far_low], axis=2),
            preferred_element_type=jnp.float32,
        )
        return (
            self_coef[None, :] * field
            + near.reshape(excitations, panels)
            + far_pot.reshape(excitations, panels)
        )

    def project_and_dots(vector, others):
        tail = dots(vector, others)
        tail = jnp.pad(tail, ((0, 0), (0, 128 - len(others))))
        summed = total(jnp.concatenate([project(vector), tail], axis=1), count)
        return summed[:, :low_rank_width], [
            summed[:, low_rank_width + i][:, None] for i in range(len(others))
        ]

    rhs_proj, (rhs_sq,) = project_and_dots(rhs_vec, [rhs_vec])
    start_len = jnp.sqrt(rhs_sq + EPS)
    first_dir = rhs_vec / start_len
    first_proj = rhs_proj / start_len
    first_sq = rhs_sq / (start_len * start_len)
    first_pre = precond(first_dir, first_proj)
    residue = operate(first_pre)
    res_proj, (diag_one, res_sq) = project_and_dots(residue, [first_dir, residue])
    below_sq = res_sq - diag_one * diag_one * (2.0 - first_sq)
    below_one = jnp.sqrt(jnp.maximum(below_sq, 0.0) + EPS)
    second_dir = (residue - diag_one * first_dir) / below_one
    second_proj = (res_proj - diag_one * first_proj) / below_one
    second_pre = precond(second_dir, second_proj)
    residue = operate(second_pre)
    tail = total_small(
        dots(residue, [first_dir, second_dir, residue]).T, count
    )
    upper_two, diag_two, res_sq = [tail[i][:, None] for i in range(3)]
    cross = diag_one * (1.0 - first_sq) / below_one
    second_sq = jnp.maximum(below_sq, 0.0) / (below_one * below_one)
    left_sq = (
        res_sq
        - upper_two * upper_two * (2.0 - first_sq)
        - diag_two * diag_two * (2.0 - second_sq)
        + 2.0 * upper_two * diag_two * cross
    )
    below_two = jnp.sqrt(jnp.maximum(left_sq, 0.0) + EPS)
    step_one, step_two = givens_pair(
        start_len, diag_one, below_one, upper_two, diag_two, below_two
    )
    return step_one * first_pre + step_two * second_pre


def solution(mesh):
    placed = (
        P("rhs", "space"),
        P("space"),
        P("space", None, None, None),
        P("space", None),
        P("space"),
        P("space", None, None),
        P("space", None),
        P("space", "rhs", None),
        P("space"),
        P("space", None),
    )
    return jax.shard_map(
        on_device, mesh=mesh, in_specs=placed, out_specs=P("rhs", "space"), check_vma=False
    )
```

time: 274 us -> 156 us (0.57)
  blocking collectives: 225 us -> 10.7 us
  waiting for transfers between devices: 0.03 us -> 72.1 us
  starting transfers between devices: 12.3 us -> 25.7 us
  local copies, waits for them, and re-layouts: 2.56 us -> 9.33 us
  matrix products: 15.9 us -> 20.8 us
    psum x7 -> x0, blocking collectives: 162 us -> none  [the longest x2 66.1 us: precond(): projected = lax.psum(jnp.dot(vector, low_rank, precision=HIGH), 'space')]
    ppermute x4 -> x16, waiting for transfers between devices: 0.01 us -> 71.4 us  [swap(): return lax.ppermute(values, AXIS, [(i, i ^ mask) for i in range(count)])]
    all_gather x2 -> x0, blocking collectives: 62.8 us -> none  [operate(): charges_in = lax.all_gather(packed, 'space', axis=2, tiled=True)]
    ppermute x4 -> x16, starting transfers between devices: 12.3 us -> 25.7 us  [swap(): return lax.ppermute(values, AXIS, [(i, i ^ mask) for i in range(count)])]
    all_to_all x0 -> x1, blocking collectives: none -> 10.7 us  [total_small(): return jnp.sum(lax.all_to_all(spread, AXIS, 0, 0), axis=0)]
    dot_general x8, matrix products: 7.05 us -> 13 us  [the longest x2 6.88 us: operate(): jnp.einsum('gqsj,seqj->eg', full_rows, charges_in.reshape(count, excitati...]
    dot_general x0 -> x1, local copies, waits for them, and re-layouts: none -> 3.8 us  [operate(): jnp.einsum('gqsj,seqj->eg', full_rows, charges_in.reshape(count, excitati...]
  transfers between devices with their start and end apart: 5 -> 17, of which waited for: 0 -> 12; matrix products, arithmetic and copies ran while one was open for 3% -> 7% of each run, Pallas kernels for 0% -> 0%
where the time goes in v1:
time: 156 us; the launch traced here: 155 us
  waiting for transfers between devices  72.1 us (46%)
  starting transfers between devices  25.7 us (16%)
  matrix products  20.8 us (13%)
  between operations  13.8 us (9%)
  blocking collectives  10.7 us (7%)
  local copies, waits for them, and re-layouts  9.33 us (6%)
  other arithmetic  2.76 us (2%)
    ppermute x16, waiting for transfers between devices, swap(): return lax.ppermute(values, AXIS, [(i, i ^ mask) for i in range(count)])  71.4 us
    ppermute x16, starting transfers between devices, swap(): return lax.ppermute(values, AXIS, [(i, i ^ mask) for i in range(count)])  25.7 us
    all_to_all x1, blocking collectives, total_small(): return jnp.sum(lax.all_to_all(spread, AXIS, 0, 0), axis=0)  10.7 us
    dot_general x2, matrix products, operate(): jnp.einsum('gqsj,seqj->eg', full_rows, charges_in.reshape(count, excitati...  6.88 us
    dot_general x2, matrix products, operate(): jnp.einsum('bkij,ebkj->ebi', near_mats, picked, preferred_element_type=jn...  5.19 us
    dot_general x2, matrix products, project(): return jnp.dot(vector, low_rank, precision=HIGH)  4.45 us
    dot_general x1, local copies, waits for them, and re-layouts, operate(): jnp.einsum('gqsj,seqj->eg', full_rows, charges_in.reshape(count, excitati...  3.8 us
  transfers between devices with their start and end apart: 17, of which 12 were waited for; matrix products, arithmetic and copies ran while one was open for 7% of the time, Pallas kernels for 0%

profile of v1, /device:TPU:0, one launch (start us, length us, event | category | flops | bytes accessed | tf_op | source)
XLA Modules:
  0.0 155.1 jit_solution(1656063117584190026)
XLA Ops:
  6.5 0.0 all-gather.2.cloned.1.call-start
  6.6 0.7 all-gather.2.cloned.1.call-update
  7.3 1.0 multiply_reduce_fusion.5
  8.2 2.6 %fusion.76 = f32[16,512]{0,1:T(8,128)S(1)} fusion(f32[16,1024]{1,0:T(8,128)} %param.10, f32[1024,512]{1,0:T(8,128)S(1)} %copy-done), kind=kOutput, calls=%fused_computation.189 | convolution fusion | flops 50331648 | bytes 2195456 | tf_op jit(solution)/shard_map/dot_general | solution.py:112
  10.9 0.0 copy-start.1
  10.9 0.0 copy-start.6
  10.9 3.0 %collective-permute-start = (f32[16,640]{0,1:T(8,128)S(1)}, f32[16,640]{0,1:T(8,128)S(1)}, u32[]{:S(2)}, u32[]{:S(2)}) collective-permute-start(f32[16,640]{0,1:T(8,128)S(1)} %select_maximum_fusion), channel_id=1, source_target_pairs={{0,4},{4,0},{8,12},{12,8},{16,20},{20,16},{24,28},{28,24},{1,5},{5... | collective-permute-start | bytes 122888 | tf_op jit(solution)/shard_map/ppermute | solution.py:13
  14.0 0.1 fusion.50
  14.1 0.1 reshape.167
  14.2 0.1 fusion.27
  14.3 7.4 %collective-permute-done = f32[16,640]{0,1:T(8,128)S(1)} collective-permute-done((f32[16,640]{0,1:T(8,128)S(1)}, f32[16,640]{0,1:T(8,128)S(1)}, u32[]{:S(2)}, u32[]{:S(2)}) %collective-permute-start) | collective-permute-done | bytes 40992 | tf_op jit(solution)/shard_map/ppermute | solution.py:13
  21.7 3.9 %collective-permute-start.3 = (f32[16,640]{0,1:T(8,128)S(1)}, f32[16,640]{0,1:T(8,128)S(1)}, u32[]{:S(2)}, u32[]{:S(2)}) collective-permute-start(f32[16,640]{0,1:T(8,128)S(1)} %fusion.70), channel_id=1, source_target_pairs={{0,24},{4,28},{8,16},{12,20},{16,8},{20,12},{24,0},{28,4},{1,25},{... | collective-permute-start | bytes 122888 | tf_op jit(solution)/shard_map/ppermute | solution.py:13
  25.6 0.6 collective-permute-start.1
  26.3 8.1 %collective-permute-done.3 = f32[16,640]{0,1:T(8,128)S(1)} collective-permute-done((f32[16,640]{0,1:T(8,128)S(1)}, f32[16,640]{0,1:T(8,128)S(1)}, u32[]{:S(2)}, u32[]{:S(2)}) %collective-permute-start.3) | collective-permute-done | bytes 40992 | tf_op jit(solution)/shard_map/ppermute | solution.py:13
  34.3 18.3 %collective-permute-done.2 = f32[16,640]{0,1:T(8,128)S(1)} collective-permute-done((f32[16,640]{0,1:T(8,128)S(1)}, f32[16,640]{0,1:T(8,128)S(1)}, u32[]{:S(2)}, u32[]{:S(2)}) %collective-permute-start.2) | collective-permute-done | bytes 40992 | tf_op jit(solution)/shard_map/ppermute | solution.py:13
  52.7 0.1 add_add_fusion.1
  52.8 1.6 %fusion.74 = (bf16[16,1024]{1,0:T(8,128)(2,1)S(1)}, f32[16,1024]{1,0:T(8,128)}) fusion(f32[1024,512]{1,0:T(8,128)S(1)} %copy-done, f32[16,640]{0,1:T(8,128)S(1)} %add_add_fusion.1, f32[16]{0:T(128)S(1)} %fusion.68, f32[16,1024]{1,0:T(8,128)S(1)} %copy-done.1, f32[1024]{0:T(1024)S(1)} %copy-done.6), kind=kOutput, calls=%fused_computation.187 | convolution fusion | flops 50405376 | bytes 2528256 | tf_op jit(solution)/shard_map/dot_general | solution.py:115
  54.4 0.1 fusion.10
  54.6 0.1 reshape.149
  54.7 0.1 stack_reshape.6
  54.8 1.6 %collective-permute-start.4 = (bf16[16,1280]{1,0:T(8,128)(2,1)S(1)}, bf16[16,1280]{1,0:T(8,128)(2,1)S(1)}, u32[]{:S(2)}, u32[]{:S(2)}) collective-permute-start(bf16[16,1280]{1,0:T(8,128)(2,1)S(1)} %pad_maximum_fusion.11), channel_id=1, source_target_pairs={{0,4},{4,0},{8,12},{12,8},{16,20},{20,16},{24,28},{28,24},{1,5},{5... | collective-permute-start | bytes 122888 | tf_op jit(solution)/shard_map/ppermute | solution.py:13
  56.3 2.5 %collective-permute-done.4 = bf16[16,1280]{1,0:T(8,128)(2,1)S(1)} collective-permute-done((bf16[16,1280]{1,0:T(8,128)(2,1)S(1)}, bf16[16,1280]{1,0:T(8,128)(2,1)S(1)}, u32[]{:S(2)}, u32[]{:S(2)}) %collective-permute-start.4) | collective-permute-done | bytes 40992 | tf_op jit(solution)/shard_map/ppermute | solution.py:13
  58.9 2.5 %collective-permute-start.6 = (bf16[16,1536]{1,0:T(8,128)(2,1)S(1)}, bf16[16,1536]{1,0:T(8,128)(2,1)S(1)}, u32[]{:S(2)}, u32[]{:S(2)}) collective-permute-start(bf16[16,1536]{1,0:T(8,128)(2,1)S(1)} %pad_maximum_fusion.9), channel_id=1, source_target_pairs={{0,24},{4,28},{8,16},{12,20},{16,8},{20,12},{24,0},{28,4},{1,25},{... | collective-permute-start | bytes 147464 | tf_op jit(solution)/shard_map/ppermute | solution.py:13
  61.4 1.9 %collective-permute-start.7 = (bf16[16,512]{1,0:T(8,128)(2,1)S(1)}, bf16[16,512]{1,0:T(8,128)(2,1)S(1)}, u32[]{:S(2)}, u32[]{:S(2)}) collective-permute-start(bf16[16,512]{1,0:T(8,128)(2,1)S(1)} %pad_maximum_fusion.13), channel_id=1, source_target_pairs={{0,16},{4,20},{8,24},{12,28},{16,0},{20,4},{24,8},{28,12},{1,17},{... | collective-permute-start | bytes 49160 | tf_op jit(solution)/shard_map/ppermute | solution.py:13
  63.3 2.2 %collective-permute-done.5 = bf16[16,1536]{1,0:T(8,128)(2,1)S(1)} collective-permute-done((bf16[16,1536]{1,0:T(8,128)(2,1)S(1)}, bf16[16,1536]{1,0:T(8,128)(2,1)S(1)}, u32[]{:S(2)}, u32[]{:S(2)}) %collective-permute-start.5) | collective-permute-done | bytes 49184 | tf_op jit(solution)/shard_map/ppermute | solution.py:13
  65.5 0.5 collective-permute-done.7
  66.1 0.6 gather_fusion.1
  66.6 0.8 reshape.154
  67.5 0.6 gather_fusion
  68.1 2.9 %convolution_bitcast_fusion.3 = f32[8,2,8,128]{3,2,1,0:T(8,128)} fusion(bf16[8,8,128,128]{3,2,1,0:T(8,128)(2,1)} %param.12, bf16[8,8,16,128]{3,2,1,0:T(8,128)(2,1)S(1)} %bitcast.249, bf16[8,8]{1,0:T(8,128)(2,1)S(1)} %fusion.50), kind=kOutput, calls=%fused_computation.14 | convolution fusion | flops 33685504 | bytes 2424960 | tf_op jit(solution)/shard_map/bkij,ebkj->ebi/dot_general | solution.py:132
  71.0 1.5 copy.271
  72.5 3.8 %copy.272 = bf16[256,64,4,8]{1,3,2,0:T(8,128)(2,1)} copy(bf16[256,64,4,8]{0,1,3,2:T(8,128)(2,1)S(1)} %bitcast.245) | data formatting | bytes 2097152 | tf_op jit(solution)/shard_map/gqsj,seqj->eg/dot_general | solution.py:133
  76.3 0.0 copy-start.7
  76.3 3.2 %fusion.73 = (bf16[16,8,32]{2,0,1:T(8,128)(2,1)S(1)}, bf16[16,8,32]{2,0,1:T(8,128)(2,1)S(1)}) fusion(bf16[8,32,64,4,8]{2,4,3,1,0:T(8,128)(2,1)} %bitcast.246, bf16[8,16,4,64]{3,2,1,0:T(4,128)(2,1)} %reshape.154), kind=kOutput, calls=%fused_computation.186 | convolution fusion | flops 16793600 | bytes 1130496 | tf_op jit(solution)/shard_map/gqsj,seqj->eg/dot_general | solution.py:133
  79.5 0.2 convolution_bitcast_fusion.1
  79.8 0.2 multiply_reduce_fusion.4
  80.0 1.8 %fusion.77 = f32[16,512]{0,1:T(8,128)S(1)} fusion(f32[16,1024]{1,0:T(8,128)S(1)} %get-tuple-element.14, f32[1024,512]{1,0:T(8,128)S(1)} %copy-done), kind=kOutput, calls=%fused_computation.190 | convolution fusion | flops 50331648 | bytes 2195456 | tf_op jit(solution)/shard_map/dot_general | solution.py:112
  81.8 1.6 %collective-permute-start.8 = (f32[16,640]{0,1:T(8,128)S(1)}, f32[16,640]{0,1:T(8,128)S(1)}, u32[]{:S(2)}, u32[]{:S(2)}) collective-permute-start(f32[16,640]{0,1:T(8,128)S(1)} %pad_maximum_fusion), channel_id=1, source_target_pairs={{0,4},{4,0},{8,12},{12,8},{16,20},{20,16},{24,28},{28,24},{1,5},{5... | collective-permute-start | bytes 122888 | tf_op jit(solution)/shard_map/ppermute | solution.py:13
  83.4 5.6 %collective-permute-done.8 = f32[16,640]{0,1:T(8,128)S(1)} collective-permute-done((f32[16,640]{0,1:T(8,128)S(1)}, f32[16,640]{0,1:T(8,128)S(1)}, u32[]{:S(2)}, u32[]{:S(2)}) %collective-permute-start.8) | collective-permute-done | bytes 40992 | tf_op jit(solution)/shard_map/ppermute | solution.py:13
  89.0 1.6 %collective-permute-start.11 = (f32[16,640]{0,1:T(8,128)S(1)}, f32[16,640]{0,1:T(8,128)S(1)}, u32[]{:S(2)}, u32[]{:S(2)}) collective-permute-start(f32[16,640]{0,1:T(8,128)S(1)} %fusion.69), channel_id=1, source_target_pairs={{0,24},{4,28},{8,16},{12,20},{16,8},{20,12},{24,0},{28,4},{1,25},{... | collective-permute-start | bytes 122888 | tf_op jit(solution)/shard_map/ppermute | solution.py:13
  90.6 2.0 %collective-permute-start.10 = (f32[16,640]{0,1:T(8,128)S(1)}, f32[16,640]{0,1:T(8,128)S(1)}, u32[]{:S(2)}, u32[]{:S(2)}) collective-permute-start(f32[16,640]{0,1:T(8,128)S(1)} %fusion.69), channel_id=1, source_target_pairs={{0,16},{4,20},{8,24},{12,28},{16,0},{20,4},{24,8},{28,12},{1,17},{... | collective-permute-start | bytes 122888 | tf_op jit(solution)/shard_map/ppermute | solution.py:13
  92.6 0.9 collective-permute-start.9
  93.5 8.1 %collective-permute-done.11 = f32[16,640]{0,1:T(8,128)S(1)} collective-permute-done((f32[16,640]{0,1:T(8,128)S(1)}, f32[16,640]{0,1:T(8,128)S(1)}, u32[]{:S(2)}, u32[]{:S(2)}) %collective-permute-start.11) | collective-permute-done | bytes 40992 | tf_op jit(solution)/shard_map/ppermute | solution.py:13
  101.5 13.7 %collective-permute-done.10 = f32[16,640]{0,1:T(8,128)S(1)} collective-permute-done((f32[16,640]{0,1:T(8,128)S(1)}, f32[16,640]{0,1:T(8,128)S(1)}, u32[]{:S(2)}, u32[]{:S(2)}) %collective-permute-start.10) | collective-permute-done | bytes 40992 | tf_op jit(solution)/shard_map/ppermute | solution.py:13
  115.3 0.1 add_add_fusion
  115.4 1.0 fusion.75
  116.4 0.1 fusion.11
  116.6 0.1 reshape.158
  116.7 0.1 stack_reshape.7
  116.7 1.6 %collective-permute-start.12 = (bf16[16,1280]{1,0:T(8,128)(2,1)S(1)}, bf16[16,1280]{1,0:T(8,128)(2,1)S(1)}, u32[]{:S(2)}, u32[]{:S(2)}) collective-permute-start(bf16[16,1280]{1,0:T(8,128)(2,1)S(1)} %pad_maximum_fusion.12), channel_id=1, source_target_pairs={{0,4},{4,0},{8,12},{12,8},{16,20},{20,16},{24,28},{28,24},{1,5},{5... | collective-permute-start | bytes 122888 | tf_op jit(solution)/shard_map/ppermute | solution.py:13
  118.3 2.5 %collective-permute-done.12 = bf16[16,1280]{1,0:T(8,128)(2,1)S(1)} collective-permute-done((bf16[16,1280]{1,0:T(8,128)(2,1)S(1)}, bf16[16,1280]{1,0:T(8,128)(2,1)S(1)}, u32[]{:S(2)}, u32[]{:S(2)}) %collective-permute-start.12) | collective-permute-done | bytes 40992 | tf_op jit(solution)/shard_map/ppermute | solution.py:13
  120.8 2.4 %collective-permute-start.14 = (bf16[16,1536]{1,0:T(8,128)(2,1)S(1)}, bf16[16,1536]{1,0:T(8,128)(2,1)S(1)}, u32[]{:S(2)}, u32[]{:S(2)}) collective-permute-start(bf16[16,1536]{1,0:T(8,128)(2,1)S(1)} %pad_maximum_fusion.10), channel_id=1, source_target_pairs={{0,24},{4,28},{8,16},{12,20},{16,8},{20,12},{24,0},{28,4},{1,25},{... | collective-permute-start | bytes 147464 | tf_op jit(solution)/shard_map/ppermute | solution.py:13
  123.3 2.0 %collective-permute-start.15 = (bf16[16,512]{1,0:T(8,128)(2,1)S(1)}, bf16[16,512]{1,0:T(8,128)(2,1)S(1)}, u32[]{:S(2)}, u32[]{:S(2)}) collective-permute-start(bf16[16,512]{1,0:T(8,128)(2,1)S(1)} %pad_maximum_fusion.14), channel_id=1, source_target_pairs={{0,16},{4,20},{8,24},{12,28},{16,0},{20,4},{24,8},{28,12},{1,17},{... | collective-permute-start | bytes 49160 | tf_op jit(solution)/shard_map/ppermute | solution.py:13
  125.3 2.1 %collective-permute-done.13 = bf16[16,1536]{1,0:T(8,128)(2,1)S(1)} collective-permute-done((bf16[16,1536]{1,0:T(8,128)(2,1)S(1)}, bf16[16,1536]{1,0:T(8,128)(2,1)S(1)}, u32[]{:S(2)}, u32[]{:S(2)}) %collective-permute-start.13) | collective-permute-done | bytes 49184 | tf_op jit(solution)/shard_map/ppermute | solution.py:13
  127.4 0.5 collective-permute-done.15
  127.9 0.7 gather_fusion.3
  128.6 0.1 reshape.163
  128.7 3.7 %fusion.72 = (bf16[16,8,32]{2,0,1:T(8,128)(2,1)S(1)}, bf16[16,8,32]{2,0,1:T(8,128)(2,1)}) fusion(bf16[8,32,64,4,8]{2,4,3,1,0:T(8,128)(2,1)} %bitcast.247, bf16[8,16,4,64]{3,2,1,0:T(4,128)(2,1)S(1)} %reshape.163), kind=kOutput, calls=%fused_computation.185 | convolution fusion | flops 16793600 | bytes 1130496 | tf_op jit(solution)/shard_map/gqsj,seqj->eg/dot_general | solution.py:133
  132.5 0.6 gather_fusion.2
  133.1 2.3 %convolution_bitcast_fusion.2 = f32[8,2,8,128]{3,2,1,0:T(8,128)S(1)} fusion(bf16[8,8,128,128]{3,2,1,0:T(8,128)(2,1)} %param.12, bf16[8,8,16,128]{3,2,1,0:T(8,128)(2,1)S(1)} %bitcast.248, bf16[8,8]{1,0:T(8,128)(2,1)S(1)} %fusion.50), kind=kOutput, calls=%fused_computation.12 | convolution fusion | flops 33685504 | bytes 2424960 | tf_op jit(solution)/shard_map/bkij,ebkj->ebi/dot_general | solution.py:132
  135.4 1.2 convolution_bitcast_fusion
  136.6 0.2 multiply_reduce_fusion.2
  136.8 10.7 %all_to_all.5 = f32[8,3,16]{2,1,0:T(4,128)S(1)} all-to-all(f32[8,3,16]{2,1,0:T(4,128)S(1)} %broadcast_in_dim.15), channel_id=1, replica_groups=mesh['space'=8,'rhs'=4] {'space'}, dimensions={0} | all-to-all | bytes 3072 | tf_op jit(solution)/shard_map/all_to_all | solution.py:27
  147.6 0.7 multiply_add_fusion
  (88 shorter events, 0.6 us)
Async XLA Ops:
  6.5 1.7 %copy-start = (f32[1024,512]{1,0:T(8,128)S(1)}, f32[1024,512]{1,0:T(8,128)}, u32[]{:S(2)}) copy-start(f32[1024,512]{1,0:T(8,128)} %param.19) | copy-start | bytes 6291460
  6.5 7.4 %copy-start.11 = (s32[8]{0:T(128)S(1)}, s32[8]{0:T(128)}, u32[]{:S(2)}) copy-start(s32[8]{0:T(128)} %param.14) | copy-start | bytes 100
  6.5 7.5 %copy-start.10 = (s32[8,8]{1,0:T(8,128)S(1)}, s32[8,8]{1,0:T(8,128)}, u32[]{:S(2)}) copy-start(s32[8,8]{1,0:T(8,128)} %param.13) | copy-start | bytes 772
  6.5 7.6 %copy-start.9 = (s32[8,32]{1,0:T(8,128)S(1)}, s32[8,32]{1,0:T(8,128)}, u32[]{:S(2)}) copy-start(s32[8,32]{1,0:T(8,128)} %param.16) | copy-start | bytes 3076
  6.5 64.5 %all-gather.2.cloned.1.call-start = ((), (), s32[]{:S(2)}) async-start(), calls=%async_computation.1 | async-start | bytes 1310720 | tf_op jit(solution)/shard_map/all_gather | solution.py:108
  10.9 41.9 %copy-start.1 = (f32[16,1024]{1,0:T(8,128)S(1)}, f32[16,1024]{1,0:T(8,128)}, u32[]{:S(2)}) copy-start(f32[16,1024]{1,0:T(8,128)} %param.10) | copy-start | bytes 196612
  10.9 41.9 %copy-start.6 = (f32[1024]{0:T(1024)S(1)}, f32[1024]{0:T(1024)}, u32[]{:S(2)}) copy-start(f32[1024]{0:T(1024)} %param.18) | copy-start | bytes 12292
  10.9 10.7 %collective-permute-start = (f32[16,640]{0,1:T(8,128)S(1)}, f32[16,640]{0,1:T(8,128)S(1)}, u32[]{:S(2)}, u32[]{:S(2)}) collective-permute-start(f32[16,640]{0,1:T(8,128)S(1)} %select_maximum_fusion), channel_id=1, source_target_pairs={{0,4},{4,0},{8,12},{12,8},{16,20},{20,16},{24,28},{28,24},{1,5},{5... | collective-permute-start | bytes 122888 | tf_op jit(solution)/shard_map/ppermute | solution.py:13
  14.3 40.1 %copy-start.4 = (bf16[8,32,128]{2,1,0:T(8,128)(2,1)}, bf16[8,32,128]{2,1,0:T(8,128)(2,1)S(1)}, u32[]{:S(2)}) copy-start(bf16[8,32,128]{2,1,0:T(8,128)(2,1)S(1)} %fusion.27) | copy-start | bytes 196612
  21.7 12.6 %collective-permute-start.3 = (f32[16,640]{0,1:T(8,128)S(1)}, f32[16,640]{0,1:T(8,128)S(1)}, u32[]{:S(2)}, u32[]{:S(2)}) collective-permute-start(f32[16,640]{0,1:T(8,128)S(1)} %fusion.70), channel_id=1, source_target_pairs={{0,24},{4,28},{8,16},{12,20},{16,8},{20,12},{24,0},{28,4},{1,25},{... | collective-permute-start | bytes 122888 | tf_op jit(solution)/shard_map/ppermute | solution.py:13
  25.6 27.1 %collective-permute-start.2 = (f32[16,640]{0,1:T(8,128)S(1)}, f32[16,640]{0,1:T(8,128)S(1)}, u32[]{:S(2)}, u32[]{:S(2)}) collective-permute-start(f32[16,640]{0,1:T(8,128)S(1)} %fusion.70), channel_id=1, source_target_pairs={{0,16},{4,20},{8,24},{12,28},{16,0},{20,4},{24,8},{28,12},{1,17},{... | collective-permute-start | bytes 122888 | tf_op jit(solution)/shard_map/ppermute | solution.py:13
  25.6 27.1 %collective-permute-start.1 = (f32[16,640]{0,1:T(8,128)S(1)}, f32[16,640]{0,1:T(8,128)S(1)}, u32[]{:S(2)}, u32[]{:S(2)}) collective-permute-start(f32[16,640]{0,1:T(8,128)S(1)} %fusion.70), channel_id=1, source_target_pairs={{0,8},{4,12},{8,0},{12,4},{16,24},{20,28},{24,16},{28,20},{1,9},{5... | collective-permute-start | bytes 122888 | tf_op jit(solution)/shard_map/ppermute | solution.py:13
  26.3 39.8 %copy-start.8 = (s32[1024]{0:T(1024)}, s32[1024]{0:T(1024)S(1)}, u32[]{:S(2)}) copy-start(s32[1024]{0:T(1024)S(1)} %pad_clamp_fusion) | copy-start | bytes 12292
  26.3 28.1 %copy-start.12 = (bf16[8,128,32]{1,2,0:T(8,128)(2,1)S(1)}, bf16[8,128,32]{1,2,0:T(8,128)(2,1)}, u32[]{:S(2)}) copy-start(bf16[8,128,32]{1,2,0:T(8,128)(2,1)} %param.15) | copy-start | bytes 196612
  54.8 4.1 %collective-permute-start.4 = (bf16[16,1280]{1,0:T(8,128)(2,1)S(1)}, bf16[16,1280]{1,0:T(8,128)(2,1)S(1)}, u32[]{:S(2)}, u32[]{:S(2)}) collective-permute-start(bf16[16,1280]{1,0:T(8,128)(2,1)S(1)} %pad_maximum_fusion.11), channel_id=1, source_target_pairs={{0,4},{4,0},{8,12},{12,8},{16,20},{20,16},{24,28},{28,24},{1,5},{5... | collective-permute-start | bytes 122888 | tf_op jit(solution)/shard_map/ppermute | solution.py:13
  58.9 7.2 %collective-permute-start.6 = (bf16[16,1536]{1,0:T(8,128)(2,1)S(1)}, bf16[16,1536]{1,0:T(8,128)(2,1)S(1)}, u32[]{:S(2)}, u32[]{:S(2)}) collective-permute-start(bf16[16,1536]{1,0:T(8,128)(2,1)S(1)} %pad_maximum_fusion.9), channel_id=1, source_target_pairs={{0,24},{4,28},{8,16},{12,20},{16,8},{20,12},{24,0},{28,4},{1,25},{... | collective-permute-start | bytes 147464 | tf_op jit(solution)/shard_map/ppermute | solution.py:13
  61.4 4.1 %collective-permute-start.5 = (bf16[16,1536]{1,0:T(8,128)(2,1)S(1)}, bf16[16,1536]{1,0:T(8,128)(2,1)S(1)}, u32[]{:S(2)}, u32[]{:S(2)}) collective-permute-start(bf16[16,1536]{1,0:T(8,128)(2,1)S(1)} %pad_maximum_fusion.9), channel_id=1, source_target_pairs={{0,8},{4,12},{8,0},{12,4},{16,24},{20,28},{24,16},{28,20},{1,9},{5... | collective-permute-start | bytes 147464 | tf_op jit(solution)/shard_map/ppermute | solution.py:13
  61.4 4.6 %collective-permute-start.7 = (bf16[16,512]{1,0:T(8,128)(2,1)S(1)}, bf16[16,512]{1,0:T(8,128)(2,1)S(1)}, u32[]{:S(2)}, u32[]{:S(2)}) collective-permute-start(bf16[16,512]{1,0:T(8,128)(2,1)S(1)} %pad_maximum_fusion.13), channel_id=1, source_target_pairs={{0,16},{4,20},{8,24},{12,28},{16,0},{20,4},{24,8},{28,12},{1,17},{... | collective-permute-start | bytes 49160 | tf_op jit(solution)/shard_map/ppermute | solution.py:13
  76.3 3.2 %copy-start.5 = (bf16[8,32,128]{2,1,0:T(8,128)(2,1)S(1)}, bf16[8,32,128]{2,1,0:T(8,128)(2,1)}, u32[]{:S(2)}) copy-start(bf16[8,32,128]{2,1,0:T(8,128)(2,1)} %copy-done.4) | copy-start | bytes 196612
  76.3 3.2 %copy-start.13 = (bf16[8,128,32]{1,2,0:T(8,128)(2,1)S(1)}, bf16[8,128,32]{1,2,0:T(8,128)(2,1)}, u32[]{:S(2)}) copy-start(bf16[8,128,32]{1,2,0:T(8,128)(2,1)} %param.15) | copy-start | bytes 196612
  76.3 3.5 %copy-start.2 = (f32[16,1024]{1,0:T(8,128)S(1)}, f32[16,1024]{1,0:T(8,128)}, u32[]{:S(2)}) copy-start(f32[16,1024]{1,0:T(8,128)} %get-tuple-element.25) | copy-start | bytes 196612
  76.3 3.5 %copy-start.3 = (f32[8,2,8,128]{3,2,1,0:T(8,128)S(1)}, f32[8,2,8,128]{3,2,1,0:T(8,128)}, u32[]{:S(2)}) copy-start(f32[8,2,8,128]{3,2,1,0:T(8,128)} %convolution_bitcast_fusion.3) | copy-start | bytes 196612
  76.3 3.5 %copy-start.7 = (f32[1024]{0:T(1024)S(1)}, f32[1024]{0:T(1024)}, u32[]{:S(2)}) copy-start(f32[1024]{0:T(1024)} %param.11) | copy-start | bytes 12292
  81.8 7.1 %collective-permute-start.8 = (f32[16,640]{0,1:T(8,128)S(1)}, f32[16,640]{0,1:T(8,128)S(1)}, u32[]{:S(2)}, u32[]{:S(2)}) collective-permute-start(f32[16,640]{0,1:T(8,128)S(1)} %pad_maximum_fusion), channel_id=1, source_target_pairs={{0,4},{4,0},{8,12},{12,8},{16,20},{20,16},{24,28},{28,24},{1,5},{5... | collective-permute-start | bytes 122888 | tf_op jit(solution)/shard_map/ppermute | solution.py:13
  89.0 12.5 %collective-permute-start.11 = (f32[16,640]{0,1:T(8,128)S(1)}, f32[16,640]{0,1:T(8,128)S(1)}, u32[]{:S(2)}, u32[]{:S(2)}) collective-permute-start(f32[16,640]{0,1:T(8,128)S(1)} %fusion.69), channel_id=1, source_target_pairs={{0,24},{4,28},{8,16},{12,20},{16,8},{20,12},{24,0},{28,4},{1,25},{... | collective-permute-start | bytes 122888 | tf_op jit(solution)/shard_map/ppermute | solution.py:13
  90.6 24.7 %collective-permute-start.10 = (f32[16,640]{0,1:T(8,128)S(1)}, f32[16,640]{0,1:T(8,128)S(1)}, u32[]{:S(2)}, u32[]{:S(2)}) collective-permute-start(f32[16,640]{0,1:T(8,128)S(1)} %fusion.69), channel_id=1, source_target_pairs={{0,16},{4,20},{8,24},{12,28},{16,0},{20,4},{24,8},{28,12},{1,17},{... | collective-permute-start | bytes 122888 | tf_op jit(solution)/shard_map/ppermute | solution.py:13
  92.6 22.7 %collective-permute-start.9 = (f32[16,640]{0,1:T(8,128)S(1)}, f32[16,640]{0,1:T(8,128)S(1)}, u32[]{:S(2)}, u32[]{:S(2)}) collective-permute-start(f32[16,640]{0,1:T(8,128)S(1)} %fusion.69), channel_id=1, source_target_pairs={{0,8},{4,12},{8,0},{12,4},{16,24},{20,28},{24,16},{28,20},{1,9},{5... | collective-permute-start | bytes 122888 | tf_op jit(solution)/shard_map/ppermute | solution.py:13
  116.7 4.1 %collective-permute-start.12 = (bf16[16,1280]{1,0:T(8,128)(2,1)S(1)}, bf16[16,1280]{1,0:T(8,128)(2,1)S(1)}, u32[]{:S(2)}, u32[]{:S(2)}) collective-permute-start(bf16[16,1280]{1,0:T(8,128)(2,1)S(1)} %pad_maximum_fusion.12), channel_id=1, source_target_pairs={{0,4},{4,0},{8,12},{12,8},{16,20},{20,16},{24,28},{28,24},{1,5},{5... | collective-permute-start | bytes 122888 | tf_op jit(solution)/shard_map/ppermute | solution.py:13
  120.8 7.1 %collective-permute-start.14 = (bf16[16,1536]{1,0:T(8,128)(2,1)S(1)}, bf16[16,1536]{1,0:T(8,128)(2,1)S(1)}, u32[]{:S(2)}, u32[]{:S(2)}) collective-permute-start(bf16[16,1536]{1,0:T(8,128)(2,1)S(1)} %pad_maximum_fusion.10), channel_id=1, source_target_pairs={{0,24},{4,28},{8,16},{12,20},{16,8},{20,12},{24,0},{28,4},{1,25},{... | collective-permute-start | bytes 147464 | tf_op jit(solution)/shard_map/ppermute | solution.py:13
  123.3 4.1 %collective-permute-start.13 = (bf16[16,1536]{1,0:T(8,128)(2,1)S(1)}, bf16[16,1536]{1,0:T(8,128)(2,1)S(1)}, u32[]{:S(2)}, u32[]{:S(2)}) collective-permute-start(bf16[16,1536]{1,0:T(8,128)(2,1)S(1)} %pad_maximum_fusion.10), channel_id=1, source_target_pairs={{0,8},{4,12},{8,0},{12,4},{16,24},{20,28},{24,16},{28,20},{1,9},{5... | collective-permute-start | bytes 147464 | tf_op jit(solution)/shard_map/ppermute | solution.py:13
  123.3 4.6 %collective-permute-start.15 = (bf16[16,512]{1,0:T(8,128)(2,1)S(1)}, bf16[16,512]{1,0:T(8,128)(2,1)S(1)}, u32[]{:S(2)}, u32[]{:S(2)}) collective-permute-start(bf16[16,512]{1,0:T(8,128)(2,1)S(1)} %pad_maximum_fusion.14), channel_id=1, source_target_pairs={{0,16},{4,20},{8,24},{12,28},{16,0},{20,4},{24,8},{28,12},{1,17},{... | collective-permute-start | bytes 49160 | tf_op jit(solution)/shard_map/ppermute | solution.py:13
  133.1 2.3 %copy-start.14 = (bf16[16,8,32]{2,0,1:T(8,128)(2,1)S(1)}, bf16[16,8,32]{2,0,1:T(8,128)(2,1)}, u32[]{:S(2)}) copy-start(bf16[16,8,32]{2,0,1:T(8,128)(2,1)} %get-tuple-element.17) | copy-start | bytes 24580
Sparse Core Ops, SparseCore 0:
  8.9 19.4 all-gather.1

commit v2 on v0

v2 whole, which is shorter than its diff:
```python
import jax
import jax.numpy as jnp
from jax import lax
from jax.experimental import pallas as pl
from jax.experimental.pallas import tpu as pltpu
from jax.sharding import PartitionSpec as P

EPS = 1e-06
F32 = jnp.float32
BF = jnp.bfloat16
AXIS = "space"
LANES = 128
HALF = 64


def swap(values, mask, count):
    return lax.ppermute(values, AXIS, [(i, i ^ mask) for i in range(count)])


def split(values):
    high = values.astype(BF)
    return high, (values - high.astype(F32)).astype(BF)


def dot_nn(left, right):
    return lax.dot_general(left, right, (((1,), (0,)), ((), ())), preferred_element_type=F32)


def dot_nt(left, right):
    return lax.dot_general(left, right, (((1,), (1,)), ((), ())), preferred_element_type=F32)


def dot_wide(dot, vector, high, low):
    rows = vector.shape[0]
    vec_high, vec_low = split(vector)
    first = dot(jnp.concatenate([vec_high, vec_low], axis=0), high)
    return first[:rows] + first[rows:] + dot(vec_high, low)


def row_sum(values):
    return jnp.sum(values, axis=1, keepdims=True)


def put_scalars(columns, rows):
    lane = lax.broadcasted_iota(jnp.int32, (rows, LANES), 1)
    out = jnp.zeros((rows, LANES), F32)
    for index, column in enumerate(columns):
        out = jnp.where(lane == index, column, out)
    return out


def column(values, index):
    return values[:, index : index + 1]


def charge_rows(field_low, maps_ref, send_ref, panels, quarters):
    width = panels // quarters
    for quarter in range(quarters):
        rows = slice(quarter * width, (quarter + 1) * width)
        both = dot_nn(field_low[:, rows], maps_ref[rows, :])
        start = panels + quarter * LANES
        send_ref[:, start : start + LANES] = (both[:, :LANES] + both[:, LANES:]).astype(BF)


def open_kernel(rhs_ref, factor_ref, out_ref, high_ref, low_ref):
    step = pl.program_id(0)
    width = factor_ref.shape[1]
    rhs = rhs_ref[...]
    high, low = split(factor_ref[...])
    high_ref[...] = high
    low_ref[...] = low
    part = dot_wide(dot_nn, rhs, high, low)
    tail = put_scalars([row_sum(rhs * rhs)], rhs.shape[0])

    @pl.when(step == 0)
    def _():
        out_ref[:, :width] = part
        out_ref[:, width:] = tail

    @pl.when(step > 0)
    def _():
        out_ref[:, :width] += part
        out_ref[:, width:] += tail


def first_kernel(quarters, parts, *refs):
    sums = refs[:parts]
    rhs_ref, diag_ref, high_ref, low_ref, maps_ref = refs[parts : parts + 5]
    dir_ref, pre_ref, send_ref, keep_ref = refs[parts + 5 :]
    width = high_ref.shape[1]
    rows, panels = rhs_ref.shape
    summed = sums[0][...]
    for ref in sums[1:]:
        summed = summed + ref[...]
    rhs_sq = column(summed[:, width:], 0)
    start_len = jnp.sqrt(rhs_sq + EPS)
    first_dir = rhs_ref[...] / start_len
    proj = summed[:, :width] / start_len
    first_pre = diag_ref[...] * first_dir - dot_wide(dot_nt, proj, high_ref[...], low_ref[...])
    field_low = first_pre.astype(BF)
    dir_ref[...] = first_dir
    pre_ref[...] = first_pre
    send_ref[:, :panels] = field_low
    charge_rows(field_low, maps_ref, send_ref, panels, quarters)
    keep_ref[:, :width] = proj
    keep_ref[:, width:] = put_scalars([start_len, rhs_sq / (start_len * start_len)], rows)


def apply_matrix(
    quarters, sources, place_ref, region_ref, field_refs, charge_refs, field, self_ref, mats_ref,
    coupling_ref, maps_ref, blocks_ref, charges_ref
):
    rows, panels = field.shape
    block_count, slots, block, _ = mats_ref.shape
    for index, ref in enumerate(field_refs):
        for b in range(block_count):
            blocks_ref[index * block_count + b] = ref[:, b * block : (b + 1) * block]
    blocks_ref[sources * block_count] = jnp.zeros((rows, block), BF)
    pairs = charges_ref.shape[0]
    if len(charge_refs) == pairs:
        for index, (ref, start) in enumerate(charge_refs):
            charges_ref[(region_ref[0] // 2) ^ index] = ref[:, start : start + quarters * LANES]
    else:
        charges_ref[...] = charge_refs[0][0][...]
    far = jnp.zeros((rows, coupling_ref.shape[1]), F32)
    for quarter in range(quarters):
        lanes = slice(quarter * LANES, (quarter + 1) * LANES)
        charge = jnp.concatenate([charges_ref[t, :, lanes] for t in range(pairs)], axis=1)
        far = far + dot_nt(charge, coupling_ref[quarter])
    odd = (region_ref[0] % 2) == 1
    per = panels // quarters
    out = []
    for quarter in range(quarters):
        start = (quarter // 2) * LANES
        chunk = far[:, start : start + LANES]
        turned = pltpu.roll(chunk, HALF, 1)
        chunk = jnp.where(odd, turned, chunk) if quarter % 2 == 0 else jnp.where(odd, chunk, turned)
        high, low = split(chunk)
        both = jnp.concatenate([high, low], axis=0)
        pot = dot_nt(
            jnp.concatenate([both, both], axis=1), maps_ref[quarter * per : (quarter + 1) * per, :]
        )
        out.append(pot[:rows] + pot[rows:])
    for b in range(block_count):
        picked = jnp.concatenate([blocks_ref[place_ref[b, k]] for k in range(slots)], axis=1)
        mats = jnp.concatenate([mats_ref[b, k] for k in range(slots)], axis=1)
        near = dot_nt(picked, mats)
        quarter, rest = divmod(b * block, per)
        cols = slice(b * block, (b + 1) * block)
        out_b = near + out[quarter][:, rest : rest + block]
        yield cols, out_b + self_ref[:, cols] * field[:, cols]


def second_kernel(quarters, nfields, ncharges, charge_starts, place_ref, region_ref, *refs):
    field_refs = refs[:nfields]
    charge_refs = list(zip(refs[nfields : nfields + ncharges], charge_starts))
    refs = refs[nfields + ncharges :]
    dir_ref, pre_ref, self_ref, mats_ref, coupling_ref, maps_ref, high_ref, low_ref = refs[:8]
    res_ref, out_ref, blocks_ref, charges_ref = refs[8:]
    width = high_ref.shape[1]
    rows = pre_ref.shape[0]
    for cols, values in apply_matrix(
        quarters, nfields, place_ref, region_ref, field_refs, charge_refs, pre_ref, self_ref,
        mats_ref, coupling_ref, maps_ref, blocks_ref, charges_ref
    ):
        res_ref[:, cols] = values
    res = res_ref[...]
    out_ref[:, :width] = dot_wide(dot_nn, res, high_ref[...], low_ref[...])
    out_ref[:, width:] = put_scalars([row_sum(res * dir_ref[...]), row_sum(res * res)], rows)


def third_kernel(quarters, parts, *refs):
    sums = refs[:parts]
    res_ref, dir_ref, keep_ref, diag_ref, high_ref, low_ref, maps_ref = refs[parts : parts + 7]
    next_ref, pre_ref, send_ref, scalars_ref = refs[parts + 7 :]
    width = high_ref.shape[1]
    rows, panels = res_ref.shape
    summed = sums[0][...]
    for ref in sums[1:]:
        summed = summed + ref[...]
    keep = keep_ref[:, width:]
    start_len, first_sq = column(keep, 0), column(keep, 1)
    diag_one, res_sq = column(summed[:, width:], 0), column(summed[:, width:], 1)
    below_sq = jnp.maximum(res_sq - diag_one * diag_one * (2.0 - first_sq), 0.0)
    below_one = jnp.sqrt(below_sq + EPS)
    second_dir = (res_ref[...] - diag_one * dir_ref[...]) / below_one
    proj = (summed[:, :width] - diag_one * keep_ref[:, :width]) / below_one
    pre = diag_ref[...] * second_dir - dot_wide(dot_nt, proj, high_ref[...], low_ref[...])
    field_low = pre.astype(BF)
    next_ref[...] = second_dir
    pre_ref[...] = pre
    send_ref[:, :panels] = field_low
    charge_rows(field_low, maps_ref, send_ref, panels, quarters)
    cross = diag_one * (1.0 - first_sq) / below_one
    second_sq = below_sq / (below_one * below_one)
    scalars_ref[...] = put_scalars(
        [start_len, first_sq, diag_one, below_one, cross, second_sq], rows
    )


def fourth_kernel(quarters, nfields, ncharges, charge_starts, place_ref, region_ref, *refs):
    field_refs = refs[:nfields]
    charge_refs = list(zip(refs[nfields : nfields + ncharges], charge_starts))
    refs = refs[nfields + ncharges :]
    dir_ref, next_ref, pre_ref, self_ref, mats_ref, coupling_ref, maps_ref = refs[:7]
    out_ref, blocks_ref, charges_ref = refs[7:]
    rows = pre_ref.shape[0]
    block = mats_ref.shape[2]
    upper = jnp.zeros((rows, block), F32)
    diag = jnp.zeros((rows, block), F32)
    square = jnp.zeros((rows, block), F32)
    for cols, values in apply_matrix(
        quarters, nfields, place_ref, region_ref, field_refs, charge_refs, pre_ref, self_ref,
        mats_ref, coupling_ref, maps_ref, blocks_ref, charges_ref
    ):
        upper = upper + values * dir_ref[:, cols]
        diag = diag + values * next_ref[:, cols]
        square = square + values * values
    out_ref[...] = put_scalars([row_sum(upper), row_sum(diag), row_sum(square)], rows)


def givens_pair(start_len, diag_one, below_one, upper_two, diag_two, below_two):
    radius_one = jnp.sqrt(diag_one * diag_one + below_one * below_one)
    cos_one = diag_one / radius_one
    sin_one = below_one / radius_one
    upper = cos_one * upper_two + sin_one * diag_two
    lower = cos_one * diag_two - sin_one * upper_two
    radius_two = jnp.sqrt(lower * lower + below_two * below_two)
    step_two = lower / radius_two * (-sin_one * start_len) / radius_two
    step_one = (cos_one * start_len - upper * step_two) / radius_one
    return (step_one, step_two)


def last_kernel(sums_ref, scalars_ref, first_ref, second_ref, out_ref):
    summed = jnp.sum(sums_ref[...], axis=0)
    start_len, first_sq, diag_one, below_one, cross, second_sq = [
        column(scalars_ref[...], i) for i in range(6)
    ]
    upper_two, diag_two, res_sq = [column(summed, i) for i in range(3)]
    left_sq = (
        res_sq
        - upper_two * upper_two * (2.0 - first_sq)
        - diag_two * diag_two * (2.0 - second_sq)
        + 2.0 * upper_two * diag_two * cross
    )
    below_two = jnp.sqrt(jnp.maximum(left_sq, 0.0) + EPS)
    step_one, step_two = givens_pair(
        start_len, diag_one, below_one, upper_two, diag_two, below_two
    )
    out_ref[...] = step_one * first_ref[...] + step_two * second_ref[...]


def sum_parts(values, count):
    if count != 8:
        return [lax.psum(values, AXIS)]
    pair = values + swap(values, 1, count)
    return [pair, swap(pair, 2, count), swap(pair, 4, count), swap(pair, 6, count)]


def exchange(send, panels, count):
    field, charges = send[:, :panels], send[:, panels:]
    if count != 8:
        ends = count - 1
        lower = lax.ppermute(field, AXIS, [(i, i + 1) for i in range(ends)])
        upper = lax.ppermute(field, AXIS, [(i + 1, i) for i in range(ends)])
        every = lax.all_gather(charges, AXIS)
        every = every.reshape((count // 2, 2) + charges.shape)
        return [lower, send, upper], [every[:, 0] + every[:, 1]], [0]
    near = swap(send, 1, count)
    pair = charges + near[:, panels:]
    onward = jnp.concatenate([near[:, :panels], pair], axis=1)
    two = swap(onward, 2, count)
    four = swap(pair, 4, count)
    six = swap(onward, 6, count)
    return [send, near, two, six], [pair, two, four, six], [0, panels, 0, panels]


def block_places(near_ids, near_count, block_count, count, region):
    sources = 4 if count == 8 else 3
    if count == 8:
        source = near_ids // block_count
        slot = jnp.where(
            source == region,
            0,
            jnp.where(source == region ^ 1, 1, jnp.where(source == region ^ 3, 2, 3)),
        )
        places = slot * block_count + near_ids % block_count
    else:
        places = near_ids - (region - 1) * block_count
    live = jnp.arange(near_ids.shape[1], dtype=jnp.int32)[None, :] < near_count[:, None]
    return jnp.where(live, places, sources * block_count)


def skeleton_maps(interp, skel_idx, block, odd):
    panel = jnp.arange(block, dtype=jnp.int32)
    onehot = (skel_idx[:, None, :] == panel[None, :, None]).astype(BF)
    second = (jnp.arange(interp.shape[0]) % 2 == 1)[:, None, None]

    def place(part):
        zero = jnp.zeros_like(part)
        wide = jnp.concatenate(
            [jnp.where(second, zero, part), jnp.where(second, part, zero)], axis=2
        )
        none = jnp.zeros_like(wide)
        return jnp.concatenate([jnp.where(odd, none, wide), jnp.where(odd, wide, none)], axis=2)

    maps = jnp.concatenate([place(onehot), place(interp)], axis=2)
    return maps.reshape(-1, maps.shape[2])


def call(kernel, out_shapes, args, scratch=(), scalars=0):
    specs = [pl.BlockSpec(memory_space=pltpu.SMEM)] * scalars
    specs += [pl.BlockSpec(memory_space=pltpu.VMEM)] * (len(args) - scalars)
    outs = [pl.BlockSpec(memory_space=pltpu.VMEM)] * len(out_shapes)
    return pl.pallas_call(
        kernel,
        out_shape=[jax.ShapeDtypeStruct(shape, kind) for shape, kind in out_shapes],
        in_specs=specs,
        out_specs=outs,
        scratch_shapes=list(scratch),
        compiler_params=pltpu.CompilerParams(vmem_limit_bytes=40 * 2**20),
    )(*args)


def on_device(
    rhs_vec,
    self_coef,
    near_mats,
    near_ids,
    near_count,
    interp,
    skel_idx,
    coupling,
    diag_prec,
    low_rank,
):
    rows, panels = rhs_vec.shape
    block_count, slots, block, _ = near_mats.shape
    skeletons = coupling.shape[0]
    quarters = lax.axis_size("rhs")
    count = lax.axis_size(AXIS)
    width = low_rank.shape[1]
    region = lax.axis_index(AXIS)
    full_rows = lax.all_gather(coupling[:, 0, :], "rhs")
    places = block_places(near_ids, near_count, block_count, count, region)
    maps = skeleton_maps(interp, skel_idx, block, region % 2 == 1)
    where = jnp.full((1,), region, jnp.int32)
    self_row = self_coef[None, :]
    diag_row = diag_prec[None, :]
    wide = width + LANES
    long = panels + quarters * LANES

    steps = 4
    depth = panels // steps
    payload, high, low = pl.pallas_call(
        open_kernel,
        grid=(steps,),
        out_shape=[
            jax.ShapeDtypeStruct((rows, wide), F32),
            jax.ShapeDtypeStruct((panels, width), BF),
            jax.ShapeDtypeStruct((panels, width), BF),
        ],
        in_specs=[
            pl.BlockSpec((rows, depth), lambda i: (0, i)),
            pl.BlockSpec((depth, width), lambda i: (i, 0)),
        ],
        out_specs=[
            pl.BlockSpec((rows, wide), lambda i: (0, 0)),
            pl.BlockSpec((depth, width), lambda i: (i, 0)),
            pl.BlockSpec((depth, width), lambda i: (i, 0)),
        ],
    )(rhs_vec, low_rank)

    sums = sum_parts(payload, count)
    first_dir, first_pre, send, keep = call(
        lambda *refs: first_kernel(quarters, len(sums), *refs),
        [((rows, panels), F32), ((rows, panels), F32), ((rows, long), BF), ((rows, wide), F32)],
        [*sums, rhs_vec, diag_row, high, low, maps],
    )
    fields, charges, starts = exchange(send, panels, count)
    nf, nc = len(fields), len(charges)
    scratch = [
        pltpu.VMEM((nf * block_count + 1, rows, block), BF),
        pltpu.VMEM((count // 2, rows, quarters * LANES), BF),
    ]
    residue, payload = call(
        lambda *refs: second_kernel(quarters, nf, nc, starts, *refs),
        [((rows, panels), F32), ((rows, wide), F32)],
        [places, where, *fields, *charges, first_dir, first_pre, self_row, near_mats, full_rows,
         maps, high, low],
        scratch,
        2,
    )
    sums = sum_parts(payload, count)
    second_dir, second_pre, send, scalars = call(
        lambda *refs: third_kernel(quarters, len(sums), *refs),
        [((rows, panels), F32), ((rows, panels), F32), ((rows, long), BF), ((rows, LANES), F32)],
        [*sums, residue, first_dir, keep, diag_row, high, low, maps],
    )
    fields, charges, starts = exchange(send, panels, count)
    (tail,) = call(
        lambda *refs: fourth_kernel(quarters, nf, nc, starts, *refs),
        [((rows, LANES), F32)],
        [places, where, *fields, *charges, first_dir, second_dir, second_pre,
         self_row, near_mats, full_rows, maps],
        scratch,
        2,
    )
    if count == 8:
        spread = jnp.broadcast_to(tail[None], (count,) + tail.shape)
        tails = lax.all_to_all(spread, AXIS, 0, 0)
    else:
        tails = lax.psum(tail, AXIS)[None]
    (result,) = call(last_kernel, [((rows, panels), F32)], [tails, scalars, first_pre, second_pre])
    return result


def solution(mesh):
    placed = (
        P("rhs", "space"),
        P("space"),
        P("space", None, None, None),
        P("space", None),
        P("space"),
        P("space", None, None),
        P("space", None),
        P("space", "rhs", None),
        P("space"),
        P("space", None),
    )
    return jax.shard_map(
        on_device, mesh=mesh, in_specs=placed, out_specs=P("rhs", "space"), check_vma=False
    )
```

time: 274 us -> 89.1 us (0.33)
  blocking collectives: 225 us -> 10.9 us
  waiting for transfers between devices: 0.03 us -> 23.1 us
  matrix products: 15.9 us -> 0 us
  starting transfers between devices: 12.3 us -> 24.7 us
  Pallas kernels: 0 us -> 11.9 us
    psum x7 -> x0, blocking collectives: 162 us -> none  [the longest x2 66.1 us: precond(): projected = lax.psum(jnp.dot(vector, low_rank, precision=HIGH), 'space')]
    all_gather x2 -> x0, blocking collectives: 62.8 us -> none  [operate(): charges_in = lax.all_gather(packed, 'space', axis=2, tiled=True)]
    ppermute x4 -> x16, waiting for transfers between devices: 0.01 us -> 22.4 us  [swap(): return lax.ppermute(values, AXIS, [(i, i ^ mask) for i in range(count)])]
    dot_general x12 -> x0, matrix products: 15.9 us -> none  [the longest x2 4.55 us: operate(): jnp.einsum('bkij,ebkj->ebi', near_mats, picked, preferred_element_type=jn...]
    ppermute x4 -> x16, starting transfers between devices: 12.3 us -> 24.7 us  [swap(): return lax.ppermute(values, AXIS, [(i, i ^ mask) for i in range(count)])]
    pallas_call x0 -> x6, Pallas kernels: none -> 11.9 us  [the longest x5 7.72 us: call(): pl.pallas_call(kernel, out_shape=[jax.ShapeDtypeStruct(shape, kind) for s...]
    all_to_all x0 -> x1, blocking collectives: none -> 10.9 us  [on_device(): tails = lax.all_to_all(spread, AXIS, 0, 0)]
  transfers between devices with their start and end apart: 5 -> 17, of which waited for: 0 -> 11; matrix products, arithmetic and copies ran while one was open for 3% -> 2% of each run, Pallas kernels for 0% -> 6%
where the time goes in v2:
time: 89.1 us; the launch traced here: 88.8 us
  starting transfers between devices  24.7 us (28%)
  waiting for transfers between devices  23.1 us (26%)
  between operations  13.5 us (15%)
  Pallas kernels  11.9 us (13%)
  blocking collectives  10.9 us (12%)
  local copies, waits for them, and re-layouts  3.34 us (4%)
  other arithmetic  1.29 us (1%)
    ppermute x16, starting transfers between devices, swap(): return lax.ppermute(values, AXIS, [(i, i ^ mask) for i in range(count)])  24.7 us
    ppermute x16, waiting for transfers between devices, swap(): return lax.ppermute(values, AXIS, [(i, i ^ mask) for i in range(count)])  22.4 us
    all_to_all x1, blocking collectives, on_device(): tails = lax.all_to_all(spread, AXIS, 0, 0)  10.9 us
    pallas_call x5, Pallas kernels, call(): pl.pallas_call(kernel, out_shape=[jax.ShapeDtypeStruct(shape, kind) for s...  7.72 us
    pallas_call x1, Pallas kernels, on_device(): pl.pallas_call(open_kernel, grid=(steps,), out_shape=[jax.ShapeDtypeStruc...  4.17 us
    unnamed x28, local copies, waits for them, and re-layouts  2.86 us
  transfers between devices with their start and end apart: 17, of which 11 were waited for; matrix products, arithmetic and copies ran while one was open for 2% of the time, Pallas kernels for 6%

profile of v2, /device:TPU:0, one launch (start us, length us, event | category | flops | bytes accessed | tf_op | source)
XLA Modules:
  0.0 88.8 jit_solution(4539950755495088797)
XLA Ops:
  6.5 0.0 all-gather.3.cloned.1.call-start
  6.5 0.7 all-gather.3.cloned.1.call-update
  7.3 4.2 %shard_map.100 = (f32[16,640]{1,0:T(8,128)}, bf16[1024,512]{1,0:T(8,128)(2,1)}, bf16[1024,512]{1,0:T(8,128)(2,1)}) custom-call(f32[16,1024]{1,0:T(8,128)} %refs_4_.1, f32[1024,512]{1,0:T(8,128)} %factor_ref.1), custom_call_target="tpu_custom_call" | custom-call | tf_op jit(solution)/shard_map/pallas_call | solution.py:355
  11.4 3.0 %collective-permute-start = (f32[16,640]{1,0:T(8,128)}, f32[16,640]{1,0:T(8,128)S(1)}, u32[]{:S(2)}, u32[]{:S(2)}) collective-permute-start(f32[16,640]{1,0:T(8,128)} %get-tuple-element.18), channel_id=1, source_target_pairs={{0,4},{4,0},{8,12},{12,8},{16,20},{20,16},{24,28},{28,24},{1,5},{5... | collective-permute-start | bytes 122888 | tf_op jit(solution)/shard_map/ppermute | solution.py:17
  14.4 0.0 copy-done.9
  14.4 0.1 broadcast_select_fusion.5
  14.5 0.2 copy.11
  14.7 0.2 copy.12
  14.9 0.1 broadcast_bitcast_fusion
  14.9 0.0 copy-done.11
  15.0 0.0 copy-start.7
  15.0 0.3 fusion.2
  15.3 0.4 broadcast_select_fusion.1
  15.7 0.9 %collective-permute-done = f32[16,640]{1,0:T(8,128)S(1)} collective-permute-done((f32[16,640]{1,0:T(8,128)}, f32[16,640]{1,0:T(8,128)S(1)}, u32[]{:S(2)}, u32[]{:S(2)}) %collective-permute-start) | collective-permute-done | bytes 40992 | tf_op jit(solution)/shard_map/ppermute | solution.py:17
  16.7 0.0 copy-done.10
  16.7 4.1 %collective-permute-start.3 = (f32[16,640]{1,0:T(8,128)S(1)}, f32[16,640]{1,0:T(8,128)S(1)}, u32[]{:S(2)}, u32[]{:S(2)}) collective-permute-start(f32[16,640]{1,0:T(8,128)S(1)} %add.44.refs_0_), channel_id=1, source_target_pairs={{0,24},{4,28},{8,16},{12,20},{16,8},{20,12},{24,0},{28,4},{1,25},{... | collective-permute-start | bytes 122888 | tf_op jit(solution)/shard_map/ppermute | solution.py:17
  20.8 0.0 collective-permute-start.2
  20.8 0.6 collective-permute-start.1
  21.4 0.4 pad_maximum_fusion.refs_8_.refs_15_.refs_10_.refs_16_
  21.8 1.0 %collective-permute-done.3.refs_3_ = f32[16,640]{1,0:T(8,128)S(1)} collective-permute-done((f32[16,640]{1,0:T(8,128)S(1)}, f32[16,640]{1,0:T(8,128)S(1)}, u32[]{:S(2)}, u32[]{:S(2)}) %collective-permute-start.3) | collective-permute-done | bytes 40992 | tf_op jit(solution)/shard_map/ppermute | solution.py:17
  22.8 2.9 %collective-permute-done.2.refs_2_ = f32[16,640]{1,0:T(8,128)S(1)} collective-permute-done((f32[16,640]{1,0:T(8,128)S(1)}, f32[16,640]{1,0:T(8,128)S(1)}, u32[]{:S(2)}, u32[]{:S(2)}) %collective-permute-start.2) | collective-permute-done | bytes 40992 | tf_op jit(solution)/shard_map/ppermute | solution.py:17
  25.7 0.0 collective-permute-done.1.refs_1_
  25.7 0.0 copy-done
  25.7 0.0 copy-done.1
  25.7 0.0 copy-done.6
  25.7 0.0 copy-done.7
  25.7 0.8 shard_map.101
  26.5 1.5 %collective-permute-start.4 = (bf16[16,1536]{1,0:T(8,128)(2,1)S(1)}, bf16[16,1536]{1,0:T(8,128)(2,1)S(1)}, u32[]{:S(2)}, u32[]{:S(2)}) collective-permute-start(bf16[16,1536]{1,0:T(8,128)(2,1)S(1)} %get-tuple-element.21.refs_2_), channel_id=1, source_target_pairs={{0,4},{4,0},{8,12},{12,8},{16,20},{20,16},{24,28},{28,24},{1,5},{5... | collective-permute-start | bytes 147464 | tf_op jit(solution)/shard_map/ppermute | solution.py:17
  28.1 2.6 %collective-permute-done.4.refs_3_ = bf16[16,1536]{1,0:T(8,128)(2,1)S(1)} collective-permute-done((bf16[16,1536]{1,0:T(8,128)(2,1)S(1)}, bf16[16,1536]{1,0:T(8,128)(2,1)S(1)}, u32[]{:S(2)}, u32[]{:S(2)}) %collective-permute-start.4) | collective-permute-done | bytes 49184 | tf_op jit(solution)/shard_map/ppermute | solution.py:17
  30.6 2.0 %collective-permute-start.7 = (bf16[16,512]{1,0:T(8,128)(2,1)S(1)}, bf16[16,512]{1,0:T(8,128)(2,1)S(1)}, u32[]{:S(2)}, u32[]{:S(2)}) collective-permute-start(bf16[16,512]{1,0:T(8,128)(2,1)S(1)} %slice_add_fusion.1.refs_6_), channel_id=1, source_target_pairs={{0,16},{4,20},{8,24},{12,28},{16,0},{20,4},{24,8},{28,12},{1,17},{... | collective-permute-start | bytes 49160 | tf_op jit(solution)/shard_map/ppermute | solution.py:17
  32.7 0.4 collective-permute-start.6
  33.0 1.2 %collective-permute-start.5 = (bf16[16,1536]{1,0:T(8,128)(2,1)S(1)}, bf16[16,1536]{1,0:T(8,128)(2,1)S(1)}, u32[]{:S(2)}, u32[]{:S(2)}) collective-permute-start(bf16[16,1536]{1,0:T(8,128)(2,1)S(1)} %pad_maximum_fusion.3), channel_id=1, source_target_pairs={{0,8},{4,12},{8,0},{12,4},{16,24},{20,28},{24,16},{28,20},{1,9},{5... | collective-permute-start | bytes 147464 | tf_op jit(solution)/shard_map/ppermute | solution.py:17
  34.2 0.0 copy-done.12
  34.2 0.0 copy-done.13
  34.2 0.1 fusion.4.refs_0_
  34.3 1.0 %collective-permute-done.7.refs_8_ = bf16[16,512]{1,0:T(8,128)(2,1)S(1)} collective-permute-done((bf16[16,512]{1,0:T(8,128)(2,1)S(1)}, bf16[16,512]{1,0:T(8,128)(2,1)S(1)}, u32[]{:S(2)}, u32[]{:S(2)}) %collective-permute-start.7) | collective-permute-done | bytes 16416 | tf_op jit(solution)/shard_map/ppermute | solution.py:17
  35.3 3.3 %collective-permute-done.6.refs_5_.refs_9_ = bf16[16,1536]{1,0:T(8,128)(2,1)S(1)} collective-permute-done((bf16[16,1536]{1,0:T(8,128)(2,1)S(1)}, bf16[16,1536]{1,0:T(8,128)(2,1)S(1)}, u32[]{:S(2)}, u32[]{:S(2)}) %collective-permute-start.6) | collective-permute-done | bytes 49184 | tf_op jit(solution)/shard_map/ppermute | solution.py:17
  38.6 0.0 collective-permute-done.5.refs_4_.refs_7_
  38.6 0.0 copy-done.8
  38.6 0.0 copy-start.2
  38.6 1.6 %copy-done.2 = bf16[8,8,128,128]{3,2,1,0:T(8,128)(2,1)S(1)} copy-done((bf16[8,8,128,128]{3,2,1,0:T(8,128)(2,1)S(1)}, bf16[8,8,128,128]{3,2,1,0:T(8,128)(2,1)}, u32[]{:S(2)}) %copy-start.2) | copy-done | bytes 2097176
  40.2 1.2 %copy-done.4 = bf16[1024,1,512]{2,0,1:T(8,128)(2,1)S(1)} copy-done((bf16[1024,1,512]{2,0,1:T(8,128)(2,1)S(1)}, bf16[1024,1,512]{2,0,1:T(8,128)(2,1)}, u32[]{:S(2)}) %copy-start.4) | copy-done | bytes 1048600
  41.4 2.6 %shard_map.102 = (f32[16,1024]{1,0:T(8,128)S(1)}, f32[16,640]{1,0:T(8,128)S(1)}) custom-call(s32[8,8]{1,0:T(8,128)S(1)} %fusion.4.refs_0_, s32[1]{0:T(128)} %bitcast.refs_1_, bf16[16,1536]{1,0:T(8,128)(2,1)S(1)} %get-tuple-element.21.refs_2_, bf16[16,1536]{1,0:T(8,128)(2,1)S(1)} %collective-permute-done.4.refs_3_, ...), custom_call_target="tpu_custom_call" | custom-call | tf_op jit(solution)/shard_map/pallas_call | solution.py:315
  44.0 1.6 %collective-permute-start.8 = (f32[16,640]{1,0:T(8,128)S(1)}, f32[16,640]{1,0:T(8,128)S(1)}, u32[]{:S(2)}, u32[]{:S(2)}) collective-permute-start(f32[16,640]{1,0:T(8,128)S(1)} %get-tuple-element.24), channel_id=1, source_target_pairs={{0,4},{4,0},{8,12},{12,8},{16,20},{20,16},{24,28},{28,24},{1,5},{5... | collective-permute-start | bytes 122888 | tf_op jit(solution)/shard_map/ppermute | solution.py:17
  45.6 2.5 %collective-permute-done.8 = f32[16,640]{1,0:T(8,128)S(1)} collective-permute-done((f32[16,640]{1,0:T(8,128)S(1)}, f32[16,640]{1,0:T(8,128)S(1)}, u32[]{:S(2)}, u32[]{:S(2)}) %collective-permute-start.8) | collective-permute-done | bytes 40992 | tf_op jit(solution)/shard_map/ppermute | solution.py:17
  48.1 2.0 %collective-permute-start.11 = (f32[16,640]{1,0:T(8,128)S(1)}, f32[16,640]{1,0:T(8,128)S(1)}, u32[]{:S(2)}, u32[]{:S(2)}) collective-permute-start(f32[16,640]{1,0:T(8,128)S(1)} %add.48.refs_0_), channel_id=1, source_target_pairs={{0,24},{4,28},{8,16},{12,20},{16,8},{20,12},{24,0},{28,4},{1,25},{... | collective-permute-start | bytes 122888 | tf_op jit(solution)/shard_map/ppermute | solution.py:17
  50.1 0.0 collective-permute-start.10
  50.1 2.4 %collective-permute-start.9 = (f32[16,640]{1,0:T(8,128)S(1)}, f32[16,640]{1,0:T(8,128)S(1)}, u32[]{:S(2)}, u32[]{:S(2)}) collective-permute-start(f32[16,640]{1,0:T(8,128)S(1)} %add.48.refs_0_), channel_id=1, source_target_pairs={{0,8},{4,12},{8,0},{12,4},{16,24},{20,28},{24,16},{28,20},{1,9},{5... | collective-permute-start | bytes 122888 | tf_op jit(solution)/shard_map/ppermute | solution.py:17
  52.5 1.4 %collective-permute-done.11.refs_3_ = f32[16,640]{1,0:T(8,128)S(1)} collective-permute-done((f32[16,640]{1,0:T(8,128)S(1)}, f32[16,640]{1,0:T(8,128)S(1)}, u32[]{:S(2)}, u32[]{:S(2)}) %collective-permute-start.11) | collective-permute-done | bytes 40992 | tf_op jit(solution)/shard_map/ppermute | solution.py:17
  53.9 1.1 %collective-permute-done.10.refs_2_ = f32[16,640]{1,0:T(8,128)S(1)} collective-permute-done((f32[16,640]{1,0:T(8,128)S(1)}, f32[16,640]{1,0:T(8,128)S(1)}, u32[]{:S(2)}, u32[]{:S(2)}) %collective-permute-start.10) | collective-permute-done | bytes 40992 | tf_op jit(solution)/shard_map/ppermute | solution.py:17
  55.0 0.0 collective-permute-done.9.refs_1_
  55.0 1.0 %shard_map.103 = (f32[16,1024]{1,0:T(8,128)S(1)}, f32[16,1024]{1,0:T(8,128)S(1)}, bf16[16,1536]{1,0:T(8,128)(2,1)S(1)}, f32[16,128]{1,0:T(8,128)S(1)}) custom-call(f32[16,640]{1,0:T(8,128)S(1)} %add.48.refs_0_, f32[16,640]{1,0:T(8,128)S(1)} %collective-permute-done.9.refs_1_, f32[16,640]{1,0:T(8,128)S(1)} %collective-permute-done.10.refs_2_, ...), custom_call_target="tpu_custom_call" | custom-call | tf_op jit(solution)/shard_map/pallas_call | solution.py:315
  56.0 1.5 %collective-permute-start.12 = (bf16[16,1536]{1,0:T(8,128)(2,1)S(1)}, bf16[16,1536]{1,0:T(8,128)(2,1)S(1)}, u32[]{:S(2)}, u32[]{:S(2)}) collective-permute-start(bf16[16,1536]{1,0:T(8,128)(2,1)S(1)} %get-tuple-element.27.refs_2_), channel_id=1, source_target_pairs={{0,4},{4,0},{8,12},{12,8},{16,20},{20,16},{24,28},{28,24},{1,5},{5... | collective-permute-start | bytes 147464 | tf_op jit(solution)/shard_map/ppermute | solution.py:17
  57.5 2.6 %collective-permute-done.12.refs_3_ = bf16[16,1536]{1,0:T(8,128)(2,1)S(1)} collective-permute-done((bf16[16,1536]{1,0:T(8,128)(2,1)S(1)}, bf16[16,1536]{1,0:T(8,128)(2,1)S(1)}, u32[]{:S(2)}, u32[]{:S(2)}) %collective-permute-start.12) | collective-permute-done | bytes 49184 | tf_op jit(solution)/shard_map/ppermute | solution.py:17
  60.1 2.0 %collective-permute-start.14 = (bf16[16,1536]{1,0:T(8,128)(2,1)S(1)}, bf16[16,1536]{1,0:T(8,128)(2,1)S(1)}, u32[]{:S(2)}, u32[]{:S(2)}) collective-permute-start(bf16[16,1536]{1,0:T(8,128)(2,1)S(1)} %pad_maximum_fusion.4), channel_id=1, source_target_pairs={{0,24},{4,28},{8,16},{12,20},{16,8},{20,12},{24,0},{28,4},{1,25},{... | collective-permute-start | bytes 147464 | tf_op jit(solution)/shard_map/ppermute | solution.py:17
  62.1 0.9 %collective-permute-start.13 = (bf16[16,1536]{1,0:T(8,128)(2,1)S(1)}, bf16[16,1536]{1,0:T(8,128)(2,1)S(1)}, u32[]{:S(2)}, u32[]{:S(2)}) collective-permute-start(bf16[16,1536]{1,0:T(8,128)(2,1)S(1)} %pad_maximum_fusion.4), channel_id=1, source_target_pairs={{0,8},{4,12},{8,0},{12,4},{16,24},{20,28},{24,16},{28,20},{1,9},{5... | collective-permute-start | bytes 147464 | tf_op jit(solution)/shard_map/ppermute | solution.py:17
  63.0 1.6 %collective-permute-start.15 = (bf16[16,512]{1,0:T(8,128)(2,1)S(1)}, bf16[16,512]{1,0:T(8,128)(2,1)S(1)}, u32[]{:S(2)}, u32[]{:S(2)}) collective-permute-start(bf16[16,512]{1,0:T(8,128)(2,1)S(1)} %slice_add_fusion.refs_6_), channel_id=1, source_target_pairs={{0,16},{4,20},{8,24},{12,28},{16,0},{20,4},{24,8},{28,12},{1,17},{... | collective-permute-start | bytes 49160 | tf_op jit(solution)/shard_map/ppermute | solution.py:17
  64.6 3.1 %collective-permute-done.15.refs_8_ = bf16[16,512]{1,0:T(8,128)(2,1)S(1)} collective-permute-done((bf16[16,512]{1,0:T(8,128)(2,1)S(1)}, bf16[16,512]{1,0:T(8,128)(2,1)S(1)}, u32[]{:S(2)}, u32[]{:S(2)}) %collective-permute-start.15) | collective-permute-done | bytes 16416 | tf_op jit(solution)/shard_map/ppermute | solution.py:17
  67.7 0.0 collective-permute-done.14.refs_5_.refs_9_
  67.7 0.0 collective-permute-done.13.refs_4_.refs_7_
  67.7 0.0 copy-done.5
  67.7 2.4 %shard_map.104 = f32[16,128]{1,0:T(8,128)S(1)} custom-call(s32[8,8]{1,0:T(8,128)S(1)} %fusion.4.refs_0_, s32[1]{0:T(128)} %bitcast.refs_1_, bf16[16,1536]{1,0:T(8,128)(2,1)S(1)} %get-tuple-element.27.refs_2_, bf16[16,1536]{1,0:T(8,128)(2,1)S(1)} %collective-permute-done.12.refs_3_, bf16[16,1536]{1,0:T(8,128)(2,1)S(1)} %collective-permute-done.13.refs_4_.refs_7_, ...), custom_call_target="tpu_custom_call" | custom-call | tf_op jit(solution)/shard_map/pallas_call | solution.py:315
  70.1 10.9 %all_to_all.5.sums_ref = f32[8,16,128]{2,1,0:T(8,128)S(1)} all-to-all(f32[8,16,128]{2,1,0:T(8,128)S(1)} %broadcast_in_dim.73), channel_id=1, replica_groups=mesh['space'=8,'rhs'=4] {'space'}, dimensions={0} | all-to-all | bytes 131072 | tf_op jit(solution)/shard_map/all_to_all | solution.py:411
  81.0 0.9 %shard_map.105 = f32[16,1024]{1,0:T(8,128)} custom-call(f32[8,16,128]{2,1,0:T(8,128)S(1)} %all_to_all.5.sums_ref, f32[16,128]{1,0:T(8,128)S(1)} %get-tuple-element.30.scalars_ref, f32[16,1024]{1,0:T(8,128)S(1)} %get-tuple-element.23.refs_11_.first_ref, f32[16,1024]{1,0:T(8,128)S(1)} %get-tuple-element.29.refs_12_.second_ref), custom_call_target="tpu_custom_call" | custom-call | tf_op jit(solution)/shard_map/pallas_call | solution.py:315
  (25 shorter events, 0.1 us)
Async XLA Ops:
  6.5 7.9 %copy-start.9 = (bf16[8,128,32]{1,2,0:T(8,128)(2,1)S(1)}, bf16[8,128,32]{1,2,0:T(8,128)(2,1)}, u32[]{:S(2)}) copy-start(bf16[8,128,32]{1,2,0:T(8,128)(2,1)} %param.15) | copy-start | bytes 196612
  6.5 8.4 %copy-start.11 = (s32[8,32]{1,0:T(8,128)S(1)}, s32[8,32]{1,0:T(8,128)}, u32[]{:S(2)}) copy-start(s32[8,32]{1,0:T(8,128)} %param.16) | copy-start | bytes 3076
  6.5 32.1 %all-gather.3.cloned.1.call-start = ((), (), s32[]{:S(2)}) async-start(), calls=%async_computation.1 | async-start | bytes 1310720 | tf_op jit(solution)/shard_map/all_gather | solution.py:344
  11.4 5.2 %copy-start.10 = (f32[16,640]{1,0:T(8,128)S(1)}, f32[16,640]{1,0:T(8,128)}, u32[]{:S(2)}) copy-start(f32[16,640]{1,0:T(8,128)} %get-tuple-element.18) | copy-start | bytes 122884
  11.4 5.2 %collective-permute-start = (f32[16,640]{1,0:T(8,128)}, f32[16,640]{1,0:T(8,128)S(1)}, u32[]{:S(2)}, u32[]{:S(2)}) collective-permute-start(f32[16,640]{1,0:T(8,128)} %get-tuple-element.18), channel_id=1, source_target_pairs={{0,4},{4,0},{8,12},{12,8},{16,20},{20,16},{24,28},{28,24},{1,5},{5... | collective-permute-start | bytes 122888 | tf_op jit(solution)/shard_map/ppermute | solution.py:17
  15.0 10.7 %copy-start = (bf16[1024,512]{1,0:T(8,128)(2,1)S(1)}, bf16[1024,512]{1,0:T(8,128)(2,1)}, u32[]{:S(2)}) copy-start(bf16[1024,512]{1,0:T(8,128)(2,1)} %get-tuple-element.19.refs_6_.refs_16_.refs_8_) | copy-start | bytes 3145732
  15.0 10.7 %copy-start.1 = (bf16[1024,512]{1,0:T(8,128)(2,1)S(1)}, bf16[1024,512]{1,0:T(8,128)(2,1)}, u32[]{:S(2)}) copy-start(bf16[1024,512]{1,0:T(8,128)(2,1)} %get-tuple-element.20.refs_7_.refs_17_.refs_9_) | copy-start | bytes 3145732
  15.0 10.7 %copy-start.6 = (f32[16,1024]{1,0:T(8,128)S(1)}, f32[16,1024]{1,0:T(8,128)}, u32[]{:S(2)}) copy-start(f32[16,1024]{1,0:T(8,128)} %refs_4_.1) | copy-start | bytes 196612
  15.0 10.7 %copy-start.7 = (f32[1024]{0:T(1024)S(1)}, f32[1024]{0:T(1024)}, u32[]{:S(2)}) copy-start(f32[1024]{0:T(1024)} %param.18) | copy-start | bytes 12292
  16.7 6.1 %collective-permute-start.3 = (f32[16,640]{1,0:T(8,128)S(1)}, f32[16,640]{1,0:T(8,128)S(1)}, u32[]{:S(2)}, u32[]{:S(2)}) collective-permute-start(f32[16,640]{1,0:T(8,128)S(1)} %add.44.refs_0_), channel_id=1, source_target_pairs={{0,24},{4,28},{8,16},{12,20},{16,8},{20,12},{24,0},{28,4},{1,25},{... | collective-permute-start | bytes 122888 | tf_op jit(solution)/shard_map/ppermute | solution.py:17
  20.8 4.9 %collective-permute-start.2 = (f32[16,640]{1,0:T(8,128)S(1)}, f32[16,640]{1,0:T(8,128)S(1)}, u32[]{:S(2)}, u32[]{:S(2)}) collective-permute-start(f32[16,640]{1,0:T(8,128)S(1)} %add.44.refs_0_), channel_id=1, source_target_pairs={{0,16},{4,20},{8,24},{12,28},{16,0},{20,4},{24,8},{28,12},{1,17},{... | collective-permute-start | bytes 122888 | tf_op jit(solution)/shard_map/ppermute | solution.py:17
  20.8 4.9 %collective-permute-start.1 = (f32[16,640]{1,0:T(8,128)S(1)}, f32[16,640]{1,0:T(8,128)S(1)}, u32[]{:S(2)}, u32[]{:S(2)}) collective-permute-start(f32[16,640]{1,0:T(8,128)S(1)} %add.44.refs_0_), channel_id=1, source_target_pairs={{0,8},{4,12},{8,0},{12,4},{16,24},{20,28},{24,16},{28,20},{1,9},{5... | collective-permute-start | bytes 122888 | tf_op jit(solution)/shard_map/ppermute | solution.py:17
  21.4 12.8 %copy-start.12 = (s32[8,8]{1,0:T(8,128)S(1)}, s32[8,8]{1,0:T(8,128)}, u32[]{:S(2)}) copy-start(s32[8,8]{1,0:T(8,128)} %param.13) | copy-start | bytes 772
  21.4 12.8 %copy-start.13 = (s32[8]{0:T(128)S(1)}, s32[8]{0:T(128)}, u32[]{:S(2)}) copy-start(s32[8]{0:T(128)} %param.14) | copy-start | bytes 100
  21.4 17.2 %copy-start.8 = (f32[1024]{0:T(1024)S(1)}, f32[1024]{0:T(1024)}, u32[]{:S(2)}) copy-start(f32[1024]{0:T(1024)} %param.11) | copy-start | bytes 12292
  26.5 4.1 %collective-permute-start.4 = (bf16[16,1536]{1,0:T(8,128)(2,1)S(1)}, bf16[16,1536]{1,0:T(8,128)(2,1)S(1)}, u32[]{:S(2)}, u32[]{:S(2)}) collective-permute-start(bf16[16,1536]{1,0:T(8,128)(2,1)S(1)} %get-tuple-element.21.refs_2_), channel_id=1, source_target_pairs={{0,4},{4,0},{8,12},{12,8},{16,20},{20,16},{24,28},{28,24},{1,5},{5... | collective-permute-start | bytes 147464 | tf_op jit(solution)/shard_map/ppermute | solution.py:17
  30.6 4.6 %collective-permute-start.7 = (bf16[16,512]{1,0:T(8,128)(2,1)S(1)}, bf16[16,512]{1,0:T(8,128)(2,1)S(1)}, u32[]{:S(2)}, u32[]{:S(2)}) collective-permute-start(bf16[16,512]{1,0:T(8,128)(2,1)S(1)} %slice_add_fusion.1.refs_6_), channel_id=1, source_target_pairs={{0,16},{4,20},{8,24},{12,28},{16,0},{20,4},{24,8},{28,12},{1,17},{... | collective-permute-start | bytes 49160 | tf_op jit(solution)/shard_map/ppermute | solution.py:17
  32.7 6.0 %collective-permute-start.6 = (bf16[16,1536]{1,0:T(8,128)(2,1)S(1)}, bf16[16,1536]{1,0:T(8,128)(2,1)S(1)}, u32[]{:S(2)}, u32[]{:S(2)}) collective-permute-start(bf16[16,1536]{1,0:T(8,128)(2,1)S(1)} %pad_maximum_fusion.3), channel_id=1, source_target_pairs={{0,24},{4,28},{8,16},{12,20},{16,8},{20,12},{24,0},{28,4},{1,25},{... | collective-permute-start | bytes 147464 | tf_op jit(solution)/shard_map/ppermute | solution.py:17
  33.0 5.6 %collective-permute-start.5 = (bf16[16,1536]{1,0:T(8,128)(2,1)S(1)}, bf16[16,1536]{1,0:T(8,128)(2,1)S(1)}, u32[]{:S(2)}, u32[]{:S(2)}) collective-permute-start(bf16[16,1536]{1,0:T(8,128)(2,1)S(1)} %pad_maximum_fusion.3), channel_id=1, source_target_pairs={{0,8},{4,12},{8,0},{12,4},{16,24},{20,28},{24,16},{28,20},{1,9},{5... | collective-permute-start | bytes 147464 | tf_op jit(solution)/shard_map/ppermute | solution.py:17
  38.6 1.6 %copy-start.2 = (bf16[8,8,128,128]{3,2,1,0:T(8,128)(2,1)S(1)}, bf16[8,8,128,128]{3,2,1,0:T(8,128)(2,1)}, u32[]{:S(2)}) copy-start(bf16[8,8,128,128]{3,2,1,0:T(8,128)(2,1)} %refs_14_.1) | copy-start | bytes 6291460
  40.2 1.2 %copy-start.4 = (bf16[1024,1,512]{2,0,1:T(8,128)(2,1)S(1)}, bf16[1024,1,512]{2,0,1:T(8,128)(2,1)}, u32[]{:S(2)}) copy-start(bf16[1024,1,512]{2,0,1:T(8,128)(2,1)} %all-gather.3.cloned.1.call-done) | copy-start | bytes 3145732
  44.0 23.6 %copy-start.3 = (bf16[8,8,128,128]{3,2,1,0:T(8,128)(2,1)S(1)}, bf16[8,8,128,128]{3,2,1,0:T(8,128)(2,1)}, u32[]{:S(2)}) copy-start(bf16[8,8,128,128]{3,2,1,0:T(8,128)(2,1)} %refs_14_.1) | copy-start | bytes 6291460
  44.0 23.6 %copy-start.5 = (bf16[1024,1,512]{2,0,1:T(8,128)(2,1)S(1)}, bf16[1024,1,512]{2,0,1:T(8,128)(2,1)}, u32[]{:S(2)}) copy-start(bf16[1024,1,512]{2,0,1:T(8,128)(2,1)} %all-gather.3.cloned.1.call-done) | copy-start | bytes 3145732
  44.0 4.1 %collective-permute-start.8 = (f32[16,640]{1,0:T(8,128)S(1)}, f32[16,640]{1,0:T(8,128)S(1)}, u32[]{:S(2)}, u32[]{:S(2)}) collective-permute-start(f32[16,640]{1,0:T(8,128)S(1)} %get-tuple-element.24), channel_id=1, source_target_pairs={{0,4},{4,0},{8,12},{12,8},{16,20},{20,16},{24,28},{28,24},{1,5},{5... | collective-permute-start | bytes 122888 | tf_op jit(solution)/shard_map/ppermute | solution.py:17
  48.1 5.8 %collective-permute-start.11 = (f32[16,640]{1,0:T(8,128)S(1)}, f32[16,640]{1,0:T(8,128)S(1)}, u32[]{:S(2)}, u32[]{:S(2)}) collective-permute-start(f32[16,640]{1,0:T(8,128)S(1)} %add.48.refs_0_), channel_id=1, source_target_pairs={{0,24},{4,28},{8,16},{12,20},{16,8},{20,12},{24,0},{28,4},{1,25},{... | collective-permute-start | bytes 122888 | tf_op jit(solution)/shard_map/ppermute | solution.py:17
  50.1 4.9 %collective-permute-start.10 = (f32[16,640]{1,0:T(8,128)S(1)}, f32[16,640]{1,0:T(8,128)S(1)}, u32[]{:S(2)}, u32[]{:S(2)}) collective-permute-start(f32[16,640]{1,0:T(8,128)S(1)} %add.48.refs_0_), channel_id=1, source_target_pairs={{0,16},{4,20},{8,24},{12,28},{16,0},{20,4},{24,8},{28,12},{1,17},{... | collective-permute-start | bytes 122888 | tf_op jit(solution)/shard_map/ppermute | solution.py:17
  50.1 4.9 %collective-permute-start.9 = (f32[16,640]{1,0:T(8,128)S(1)}, f32[16,640]{1,0:T(8,128)S(1)}, u32[]{:S(2)}, u32[]{:S(2)}) collective-permute-start(f32[16,640]{1,0:T(8,128)S(1)} %add.48.refs_0_), channel_id=1, source_target_pairs={{0,8},{4,12},{8,0},{12,4},{16,24},{20,28},{24,16},{28,20},{1,9},{5... | collective-permute-start | bytes 122888 | tf_op jit(solution)/shard_map/ppermute | solution.py:17
  56.0 4.1 %collective-permute-start.12 = (bf16[16,1536]{1,0:T(8,128)(2,1)S(1)}, bf16[16,1536]{1,0:T(8,128)(2,1)S(1)}, u32[]{:S(2)}, u32[]{:S(2)}) collective-permute-start(bf16[16,1536]{1,0:T(8,128)(2,1)S(1)} %get-tuple-element.27.refs_2_), channel_id=1, source_target_pairs={{0,4},{4,0},{8,12},{12,8},{16,20},{20,16},{24,28},{28,24},{1,5},{5... | collective-permute-start | bytes 147464 | tf_op jit(solution)/shard_map/ppermute | solution.py:17
  60.1 7.5 %collective-permute-start.14 = (bf16[16,1536]{1,0:T(8,128)(2,1)S(1)}, bf16[16,1536]{1,0:T(8,128)(2,1)S(1)}, u32[]{:S(2)}, u32[]{:S(2)}) collective-permute-start(bf16[16,1536]{1,0:T(8,128)(2,1)S(1)} %pad_maximum_fusion.4), channel_id=1, source_target_pairs={{0,24},{4,28},{8,16},{12,20},{16,8},{20,12},{24,0},{28,4},{1,25},{... | collective-permute-start | bytes 147464 | tf_op jit(solution)/shard_map/ppermute | solution.py:17
  62.1 5.6 %collective-permute-start.13 = (bf16[16,1536]{1,0:T(8,128)(2,1)S(1)}, bf16[16,1536]{1,0:T(8,128)(2,1)S(1)}, u32[]{:S(2)}, u32[]{:S(2)}) collective-permute-start(bf16[16,1536]{1,0:T(8,128)(2,1)S(1)} %pad_maximum_fusion.4), channel_id=1, source_target_pairs={{0,8},{4,12},{8,0},{12,4},{16,24},{20,28},{24,16},{28,20},{1,9},{5... | collective-permute-start | bytes 147464 | tf_op jit(solution)/shard_map/ppermute | solution.py:17
  63.0 4.6 %collective-permute-start.15 = (bf16[16,512]{1,0:T(8,128)(2,1)S(1)}, bf16[16,512]{1,0:T(8,128)(2,1)S(1)}, u32[]{:S(2)}, u32[]{:S(2)}) collective-permute-start(bf16[16,512]{1,0:T(8,128)(2,1)S(1)} %slice_add_fusion.refs_6_), channel_id=1, source_target_pairs={{0,16},{4,20},{8,24},{12,28},{16,0},{20,4},{24,8},{28,12},{1,17},{... | collective-permute-start | bytes 49160 | tf_op jit(solution)/shard_map/ppermute | solution.py:17
Sparse Core Ops, SparseCore 0:
  8.9 19.4 all-gather.2

commit v3 on v2

v3 whole, which is shorter than its diff:
```python
import math

import jax
import jax.numpy as jnp
from jax import lax
from jax.experimental import pallas as pl
from jax.experimental.pallas import tpu as pltpu
from jax.sharding import PartitionSpec as P

EPS = 1e-06
F32 = jnp.float32
BF = jnp.bfloat16
AXIS = "space"
LANES = 128
HALF = 64


def swap(values, mask, count):
    return lax.ppermute(values, AXIS, [(i, i ^ mask) for i in range(count)])


def split(values):
    high = values.astype(BF)
    return high, (values - high.astype(F32)).astype(BF)


def dot_nn(left, right):
    return lax.dot_general(left, right, (((1,), (0,)), ((), ())), preferred_element_type=F32)


def dot_nt(left, right):
    return lax.dot_general(left, right, (((1,), (1,)), ((), ())), preferred_element_type=F32)


def dot_wide(dot, vector, high, low):
    rows = vector.shape[0]
    vec_high, vec_low = split(vector)
    first = dot(jnp.concatenate([vec_high, vec_low], axis=0), high)
    return first[:rows] + first[rows:] + dot(vec_high, low)


def row_sum(values):
    return jnp.sum(values, axis=1, keepdims=True)


def put_scalars(columns, rows):
    lane = lax.broadcasted_iota(jnp.int32, (rows, LANES), 1)
    out = jnp.zeros((rows, LANES), F32)
    for index, column in enumerate(columns):
        out = jnp.where(lane == index, column, out)
    return out


def column(values, index):
    return values[:, index : index + 1]


def charge_rows(field_low, maps_ref, send_ref):
    rows, panels = field_low.shape
    quarters, _, width = maps_ref.shape
    for quarter in range(quarters):
        both = dot_nt(field_low[:, quarter * width : (quarter + 1) * width], maps_ref[quarter])
        start = panels + quarter * LANES
        send_ref[:, start : start + LANES] = (both[:, :LANES] + both[:, LANES:]).astype(BF)


def maps_kernel(weights_ref, skel_ref, maps_ref):
    block_count, rank, block = weights_ref.shape
    quarters = maps_ref.shape[0]
    per = block_count // quarters
    odd_start = pl.multiple_of((lax.axis_index(AXIS) % 2) * HALF, HALF)
    maps_ref[...] = jnp.zeros(maps_ref.shape, BF)
    skel = jnp.concatenate(
        [skel_ref[...].astype(F32), jnp.zeros((block_count, LANES - rank), F32)], axis=1
    ).T
    panel = lax.broadcasted_iota(jnp.int32, (rank, block), 1).astype(F32)
    for b in range(block_count):
        quarter, index = divmod(b, per)
        start = odd_start + index * rank
        cols = slice(index * block, (index + 1) * block)
        hot = jnp.where(skel[:rank, b : b + 1] == panel, 1.0, 0.0).astype(BF)
        maps_ref[quarter, pl.ds(start, rank), cols] = hot
        maps_ref[quarter, pl.ds(start + LANES, rank), cols] = weights_ref[b]


def onward_kernel(send_ref, near_ref, onward_ref, pair_ref):
    panels = near_ref.shape[1] - pair_ref.shape[1]
    pair = send_ref[:, panels:] + near_ref[:, panels:]
    onward_ref[:, :panels] = near_ref[:, :panels]
    onward_ref[:, panels:] = pair
    pair_ref[...] = pair


def open_kernel(parts, rhs_hbm, factor_hbm, diag_hbm, self_hbm, out_ref, rhs_ref, diag_ref,
                self_ref, held_ref, sems):
    panels, width = factor_hbm.shape
    rows = rhs_ref.shape[0]
    depth = panels // parts
    loads = [
        pltpu.make_async_copy(source, target, sems.at[parts + index])
        for index, (source, target) in enumerate(
            [(rhs_hbm, rhs_ref), (diag_hbm, diag_ref), (self_hbm, self_ref)]
        )
    ]
    for load in loads:
        load.start()
    copies = []
    for part in range(parts):
        span = pl.ds(part * depth, depth)
        copies.append(
            pltpu.make_async_copy(factor_hbm.at[span], held_ref.at[span], sems.at[part])
        )
        copies[-1].start()
    loads[0].wait()
    rhs = rhs_ref[...]
    out_ref[:, width:] = put_scalars([row_sum(rhs * rhs)], rows)
    total = jnp.zeros((rows, width), F32)
    for part in range(parts):
        span = slice(part * depth, (part + 1) * depth)
        copies[part].wait()
        high, low = split(held_ref[span, :])
        total = total + dot_wide(dot_nn, rhs[:, span], high, low)
    out_ref[:, :width] = total
    for load in loads[1:]:
        load.wait()


def first_kernel(parts, *refs):
    sums = refs[:parts]
    rhs_ref, diag_ref, factor_ref, maps_ref = refs[parts : parts + 4]
    dir_ref, pre_ref, send_ref, keep_ref, high_ref, low_ref = refs[parts + 4 :]
    width = factor_ref.shape[1]
    high_ref[...], low_ref[...] = split(factor_ref[...])
    rows, panels = rhs_ref.shape
    summed = sums[0][...]
    for ref in sums[1:]:
        summed = summed + ref[...]
    rhs_sq = column(summed[:, width:], 0)
    start_len = jnp.sqrt(rhs_sq + EPS)
    first_dir = rhs_ref[...] / start_len
    proj = summed[:, :width] / start_len
    first_pre = diag_ref[...] * first_dir - dot_wide(dot_nt, proj, high_ref[...], low_ref[...])
    field_low = first_pre.astype(BF)
    dir_ref[...] = first_dir
    pre_ref[...] = first_pre
    send_ref[:, :panels] = field_low
    charge_rows(field_low, maps_ref, send_ref)
    keep_ref[:, :width] = proj
    keep_ref[:, width:] = put_scalars([start_len, rhs_sq / (start_len * start_len)], rows)


def block_place(wanted, live, block_count, sources, region):
    source = wanted // block_count
    if sources == 4:
        slot = jnp.where(
            source == region,
            0,
            jnp.where(source == region ^ 1, 1, jnp.where(source == region ^ 3, 2, 3)),
        )
    else:
        slot = source - region + 1
    return jnp.where(live, slot * block_count + wanted % block_count, sources * block_count)


def apply_matrix(
    ids_ref, live_ref, field_refs, charge_refs, field, self_ref, mats_ref, coupling_refs, maps_ref,
    blocks_ref, charges_ref
):
    rows, panels = field.shape
    block_count, slots, block, _ = mats_ref.shape
    quarters, pairs = charges_ref.shape[:2]
    sources = len(field_refs)
    gathered = len(coupling_refs) == 1
    region = lax.axis_index(AXIS)
    first_quarter = 0 if gathered else lax.axis_index("rhs")
    for index, ref in enumerate(field_refs):
        for b in range(block_count):
            blocks_ref[index * block_count + b] = ref[:, b * block : (b + 1) * block]
    blocks_ref[sources * block_count] = jnp.zeros((rows, block), BF)
    for quarter in range(quarters):
        for index in range(pairs):
            if len(charge_refs) == pairs:
                ref, start = charge_refs[index]
                start += quarter * LANES
                charge = ref[:, start : start + LANES]
                charges_ref[quarter, (region // 2) ^ index] = charge
            else:
                lanes = slice(quarter * LANES, (quarter + 1) * LANES)
                charges_ref[quarter, index] = charge_refs[0][0][index, :, lanes]
    far = jnp.zeros((rows, coupling_refs[0].shape[-2]), F32)
    for index in range(quarters):
        quarter = first_quarter ^ index
        charge = jnp.concatenate([charges_ref[quarter, t] for t in range(pairs)], axis=1)
        rows_in = coupling_refs[0][index] if gathered else coupling_refs[index][...]
        far = far + dot_nt(charge, rows_in)
    odd = (region % 2) == 1
    per = panels // quarters
    out = []
    for quarter in range(quarters):
        start = (quarter // 2) * LANES
        chunk = far[:, start : start + LANES]
        turned = pltpu.roll(chunk, HALF, 1)
        chunk = jnp.where(odd, turned, chunk) if quarter % 2 == 0 else jnp.where(odd, chunk, turned)
        high, low = split(chunk)
        both = jnp.concatenate([high, low], axis=0)
        pot = dot_nn(jnp.concatenate([both, both], axis=1), maps_ref[quarter])
        out.append(pot[:rows] + pot[rows:])
    for b in range(block_count):
        places = [
            block_place(ids_ref[b, k], k < live_ref[b], block_count, sources, region)
            for k in range(slots)
        ]
        picked = jnp.concatenate([blocks_ref[place] for place in places], axis=1)
        mats = jnp.concatenate([mats_ref[b, k] for k in range(slots)], axis=1)
        near = dot_nt(picked, mats)
        quarter, rest = divmod(b * block, per)
        cols = slice(b * block, (b + 1) * block)
        out_b = near + out[quarter][:, rest : rest + block]
        yield cols, out_b + self_ref[:, cols] * field[:, cols]


def second_kernel(nfields, ncharges, charge_starts, ids_ref, live_ref, *refs):
    field_refs = refs[:nfields]
    charge_refs = list(zip(refs[nfields : nfields + ncharges], charge_starts))
    refs = refs[nfields + ncharges :]
    dir_ref, pre_ref, self_ref, mats_ref, maps_ref, high_ref, low_ref = refs[:7]
    *coupling_refs, res_ref, out_ref, blocks_ref, charges_ref = refs[7:]
    width = high_ref.shape[1]
    rows = pre_ref.shape[0]
    for cols, values in apply_matrix(
        ids_ref, live_ref, field_refs, charge_refs, pre_ref, self_ref, mats_ref, coupling_refs,
        maps_ref, blocks_ref, charges_ref
    ):
        res_ref[:, cols] = values
    res = res_ref[...]
    out_ref[:, :width] = dot_wide(dot_nn, res, high_ref[...], low_ref[...])
    out_ref[:, width:] = put_scalars([row_sum(res * dir_ref[...]), row_sum(res * res)], rows)


def third_kernel(parts, *refs):
    sums = refs[:parts]
    res_ref, dir_ref, keep_ref, diag_ref, high_ref, low_ref, maps_ref = refs[parts : parts + 7]
    next_ref, pre_ref, send_ref, scalars_ref = refs[parts + 7 :]
    width = high_ref.shape[1]
    rows, panels = res_ref.shape
    summed = sums[0][...]
    for ref in sums[1:]:
        summed = summed + ref[...]
    keep = keep_ref[:, width:]
    start_len, first_sq = column(keep, 0), column(keep, 1)
    diag_one, res_sq = column(summed[:, width:], 0), column(summed[:, width:], 1)
    below_sq = jnp.maximum(res_sq - diag_one * diag_one * (2.0 - first_sq), 0.0)
    below_one = jnp.sqrt(below_sq + EPS)
    second_dir = (res_ref[...] - diag_one * dir_ref[...]) / below_one
    proj = (summed[:, :width] - diag_one * keep_ref[:, :width]) / below_one
    pre = diag_ref[...] * second_dir - dot_wide(dot_nt, proj, high_ref[...], low_ref[...])
    field_low = pre.astype(BF)
    next_ref[...] = second_dir
    pre_ref[...] = pre
    send_ref[:, :panels] = field_low
    charge_rows(field_low, maps_ref, send_ref)
    cross = diag_one * (1.0 - first_sq) / below_one
    second_sq = below_sq / (below_one * below_one)
    scalars_ref[...] = put_scalars(
        [start_len, first_sq, diag_one, below_one, cross, second_sq], rows
    )


def fourth_kernel(nfields, ncharges, charge_starts, ids_ref, live_ref, *refs):
    field_refs = refs[:nfields]
    charge_refs = list(zip(refs[nfields : nfields + ncharges], charge_starts))
    refs = refs[nfields + ncharges :]
    dir_ref, next_ref, pre_ref, self_ref, mats_ref, maps_ref = refs[:6]
    *coupling_refs, out_ref, blocks_ref, charges_ref = refs[6:]
    rows = pre_ref.shape[0]
    block = mats_ref.shape[2]
    upper = jnp.zeros((rows, block), F32)
    diag = jnp.zeros((rows, block), F32)
    square = jnp.zeros((rows, block), F32)
    for cols, values in apply_matrix(
        ids_ref, live_ref, field_refs, charge_refs, pre_ref, self_ref, mats_ref, coupling_refs,
        maps_ref, blocks_ref, charges_ref
    ):
        upper = upper + values * dir_ref[:, cols]
        diag = diag + values * next_ref[:, cols]
        square = square + values * values
    scalars = put_scalars([row_sum(upper), row_sum(diag), row_sum(square)], rows)
    for index in range(out_ref.shape[0]):
        out_ref[index] = scalars


def givens_pair(start_len, diag_one, below_one, upper_two, diag_two, below_two):
    radius_one = jnp.sqrt(diag_one * diag_one + below_one * below_one)
    cos_one = diag_one / radius_one
    sin_one = below_one / radius_one
    upper = cos_one * upper_two + sin_one * diag_two
    lower = cos_one * diag_two - sin_one * upper_two
    radius_two = jnp.sqrt(lower * lower + below_two * below_two)
    step_two = lower / radius_two * (-sin_one * start_len) / radius_two
    step_one = (cos_one * start_len - upper * step_two) / radius_one
    return (step_one, step_two)


def last_kernel(sums_ref, scalars_ref, first_ref, second_ref, out_ref):
    summed = jnp.sum(sums_ref[...], axis=0)
    start_len, first_sq, diag_one, below_one, cross, second_sq = [
        column(scalars_ref[...], i) for i in range(6)
    ]
    upper_two, diag_two, res_sq = [column(summed, i) for i in range(3)]
    left_sq = (
        res_sq
        - upper_two * upper_two * (2.0 - first_sq)
        - diag_two * diag_two * (2.0 - second_sq)
        + 2.0 * upper_two * diag_two * cross
    )
    below_two = jnp.sqrt(jnp.maximum(left_sq, 0.0) + EPS)
    step_one, step_two = givens_pair(
        start_len, diag_one, below_one, upper_two, diag_two, below_two
    )
    out_ref[...] = step_one * first_ref[...] + step_two * second_ref[...]


def sum_parts(values, count):
    if count != 8:
        return [lax.psum(values, AXIS)]
    pair = values + swap(values, 1, count)
    return [pair, swap(pair, 2, count), swap(pair, 4, count), swap(pair, 6, count)]


def exchange(send, panels, count):
    if count != 8:
        field, charges = send[:, :panels], send[:, panels:]
        ends = count - 1
        lower = lax.ppermute(field, AXIS, [(i, i + 1) for i in range(ends)])
        upper = lax.ppermute(field, AXIS, [(i + 1, i) for i in range(ends)])
        every = lax.all_gather(charges, AXIS)
        every = every.reshape((count // 2, 2) + charges.shape)
        return [lower, send, upper], [every[:, 0] + every[:, 1]], [0]
    near = swap(send, 1, count)
    rows, long = send.shape
    onward, pair = call(
        "onward", onward_kernel, [((rows, long), BF), ((rows, long - panels), BF)], [send, near]
    )
    two = swap(onward, 2, count)
    four = swap(pair, 4, count)
    six = swap(onward, 6, count)
    return [send, near, two, six], [pair, two, four, six], [0, panels, 0, panels]


def gather_quarters(coupling, quarters, count, early):
    if count != 8 or quarters != 4:
        return [lax.all_gather(coupling, "rhs")], early

    def other(values, mask):
        return lax.ppermute(values, "rhs", [(i, i ^ mask) for i in range(quarters)])

    coupling, early = lax.optimization_barrier((coupling, early))
    far = other(coupling, 2)
    return [coupling, far], early


def finish_quarters(rows, quarters, late):
    if len(rows) == 1:
        return rows, late

    def other(values, mask):
        return lax.ppermute(values, "rhs", [(i, i ^ mask) for i in range(quarters)])

    own, far, late = lax.optimization_barrier((*rows, late))
    return [own, other(own, 1), far, other(far, 1)], late


def nbytes(shape, kind):
    return math.prod(shape) * jnp.dtype(kind).itemsize


def room(*arrays):
    return pltpu.CompilerParams(
        vmem_limit_bytes=sum(nbytes(a.shape, a.dtype) for a in arrays) * 5 // 4 + 4 * 2**20
    )


def call(name, kernel, out_shapes, args, scratch=(), scalars=0, far=()):
    out_shapes = [jax.ShapeDtypeStruct(shape, kind) for shape, kind in out_shapes]
    args = [pltpu.with_memory_space_constraint(x, pltpu.HBM) if i in far else x
            for i, x in enumerate(args)]
    specs = [
        pl.BlockSpec(
            memory_space=pltpu.SMEM if i < scalars else pltpu.HBM if i in far else pltpu.VMEM
        )
        for i in range(len(args))
    ]
    outs = [pl.BlockSpec(memory_space=pltpu.VMEM)] * len(out_shapes)
    held = [x for i, x in enumerate(args) if i not in far]
    held += [x for x in scratch if getattr(x, "memory_space", None) == pltpu.VMEM]
    return pl.pallas_call(
        kernel,
        name=name,
        out_shape=out_shapes,
        in_specs=specs,
        out_specs=outs,
        scratch_shapes=list(scratch),
        compiler_params=room(*held, *out_shapes),
    )(*args)


def on_device(
    rhs_vec,
    self_coef,
    near_mats,
    near_ids,
    near_count,
    interp,
    skel_idx,
    coupling,
    diag_prec,
    low_rank,
):
    rows, panels = rhs_vec.shape
    block_count, slots, block, _ = near_mats.shape
    skeletons = coupling.shape[0]
    quarters = lax.axis_size("rhs")
    count = lax.axis_size(AXIS)
    width = low_rank.shape[1]
    region = lax.axis_index(AXIS)
    (maps,) = call(
        "maps",
        maps_kernel,
        [((quarters, 2 * LANES, panels // quarters), BF)],
        [jnp.swapaxes(interp, 1, 2), skel_idx],
    )
    wide = width + LANES
    long = panels + quarters * LANES

    parts = 4
    payload, rhs_near, diag_row, self_row = call(
        "open",
        lambda *refs: open_kernel(parts, *refs),
        [((rows, wide), F32), ((rows, panels), F32), ((1, panels), F32), ((1, panels), F32)],
        [rhs_vec, low_rank, diag_prec[None, :], self_coef[None, :]],
        [pltpu.VMEM((panels, width), F32), pltpu.SemaphoreType.DMA((parts + 3,))],
        far=(0, 1, 2, 3),
    )

    some_rows, payload = gather_quarters(coupling[:, 0, :], quarters, count, payload)
    sums = sum_parts(payload, count)
    first_dir, first_pre, send, keep, high, low = call(
        "first",
        lambda *refs: first_kernel(len(sums), *refs),
        [((rows, panels), F32), ((rows, panels), F32), ((rows, long), BF), ((rows, wide), F32),
         (low_rank.shape, BF), (low_rank.shape, BF)],
        [*sums, rhs_near, diag_row, low_rank, maps],
    )
    full_rows, send = finish_quarters(some_rows, quarters, send)
    fields, charges, starts = exchange(send, panels, count)
    nf, nc = len(fields), len(charges)
    scratch = [
        pltpu.VMEM((nf * block_count + 1, rows, block), BF),
        pltpu.VMEM((quarters, count // 2, rows, LANES), BF),
    ]
    residue, payload = call(
        "second",
        lambda *refs: second_kernel(nf, nc, starts, *refs),
        [((rows, panels), F32), ((rows, wide), F32)],
        [near_ids, near_count, *fields, *charges, first_dir, first_pre, self_row, near_mats, maps,
         high, low, *full_rows],
        scratch,
        2,
    )
    sums = sum_parts(payload, count)
    second_dir, second_pre, send, scalars = call(
        "third",
        lambda *refs: third_kernel(len(sums), *refs),
        [((rows, panels), F32), ((rows, panels), F32), ((rows, long), BF), ((rows, LANES), F32)],
        [*sums, residue, first_dir, keep, diag_row, high, low, maps],
    )
    fields, charges, starts = exchange(send, panels, count)
    (tails,) = call(
        "fourth",
        lambda *refs: fourth_kernel(nf, nc, starts, *refs),
        [((count if count == 8 else 1, rows, LANES), F32)],
        [near_ids, near_count, *fields, *charges, first_dir, second_dir, second_pre,
         self_row, near_mats, maps, *full_rows],
        scratch,
        2,
    )
    tails = lax.all_to_all(tails, AXIS, 0, 0) if count == 8 else lax.psum(tails, AXIS)
    (result,) = call("last", last_kernel, [((rows, panels), F32)], [tails, scalars, first_pre, second_pre])
    return result


def solution(mesh):
    placed = (
        P("rhs", "space"),
        P("space"),
        P("space", None, None, None),
        P("space", None),
        P("space"),
        P("space", None, None),
        P("space", None),
        P("space", "rhs", None),
        P("space"),
        P("space", None),
    )
    return jax.shard_map(
        on_device, mesh=mesh, in_specs=placed, out_specs=P("rhs", "space"), check_vma=False
    )
```

time: 89.1 us -> 70.6 us (0.79)
  between operations: 13.5 us -> 0.13 us
  local copies, waits for them, and re-layouts: 3.34 us -> 0.05 us
  starting transfers between devices: 24.7 us -> 27.2 us
  Pallas kernels: 11.9 us -> 9.99 us
  other arithmetic: 1.29 us -> 0.01 us
  waiting for transfers between devices: 23.1 us -> 21.9 us
    ppermute x0 -> x3, starting transfers between devices: none -> 3.58 us  [other(): return lax.ppermute(values, 'rhs', [(i, i ^ mask) for i in range(quarters)])]
    unnamed x28 -> x14, local copies, waits for them, and re-layouts: 2.86 us -> 0.05 us
    pallas_call x6 -> x9, Pallas kernels: 11.9 us -> 9.99 us  [call(): pl.pallas_call(kernel, name=name, out_shape=out_shapes, in_specs=specs, o...]
    ppermute x16, starting transfers between devices: 24.7 us -> 23.7 us  [swap(): return lax.ppermute(values, AXIS, [(i, i ^ mask) for i in range(count)])]
  transfers between devices with their start and end apart: 17 -> 19, of which waited for: 11 -> 11; matrix products, arithmetic and copies ran while one was open for 2% -> 0% of each run, Pallas kernels for 6% -> 2%
where the time goes in v3:
time: 70.6 us; the launch traced here: 70.4 us
  starting transfers between devices  27.2 us (39%)
  waiting for transfers between devices  21.9 us (31%)
  blocking collectives  11.1 us (16%)
  Pallas kernels  9.99 us (14%)
    ppermute x16, starting transfers between devices, swap(): return lax.ppermute(values, AXIS, [(i, i ^ mask) for i in range(count)])  23.7 us
    ppermute x16, waiting for transfers between devices, swap(): return lax.ppermute(values, AXIS, [(i, i ^ mask) for i in range(count)])  21.9 us
    all_to_all x1, blocking collectives, on_device(): lax.all_to_all(tails, AXIS, 0, 0)  11.1 us
    pallas_call x9, Pallas kernels, call(): pl.pallas_call(kernel, name=name, out_shape=out_shapes, in_specs=specs, o...  9.99 us
    ppermute x3, starting transfers between devices, other(): return lax.ppermute(values, 'rhs', [(i, i ^ mask) for i in range(quarters)])  3.58 us
  transfers between devices with their start and end apart: 19, of which 11 were waited for; matrix products, arithmetic and copies ran while one was open for 0% of the time, Pallas kernels for 2%

profile of v3, /device:TPU:0, one launch (start us, length us, event | category | flops | bytes accessed | tf_op | source)
XLA Modules:
  0.0 70.4 jit_solution(15962068341936272451)
XLA Ops:
  0.0 0.0 copy-start
  0.0 0.0 copy-start.5
  0.0 0.0 copy-start.3
  0.0 2.0 %open.1 = (f32[16,640]{1,0:T(8,128)S(1)}, f32[16,1024]{1,0:T(8,128)S(1)}, f32[1,1024]{1,0:T(1,128)S(1)}, f32[1,1024]{1,0:T(1,128)S(1)}) custom-call(f32[16,1024]{1,0:T(8,128)} %refs_0_.3, f32[1024,512]{1,0:T(8,128)} %refs_6_.1, f32[1,1024]{1,0:T(1,128)} %bitcast.9, f32[1,1024]{1,0:T(1,128)} %bitcast.10), custom_call_target="tpu_custom_call" | custom-call | tf_op jit(solution)/shard_map/open/pallas_call | solution.py:396
  2.0 0.0 copy-start.2
  2.0 0.0 copy-start.1
  2.0 0.0 copy-start.4
  2.0 0.0 copy-start.6
  2.0 3.0 %collective-permute-start = (bf16[256,512]{1,0:T(8,128)(2,1)}, bf16[256,512]{1,0:T(8,128)(2,1)S(1)}, u32[]{:S(2)}, u32[]{:S(2)}) collective-permute-start(bf16[256,512]{1,0:T(8,128)(2,1)} %bitcast.4), channel_id=1, source_target_pairs={{0,2},{1,3},{2,0},{3,1},{4,6},{5,7},{6,4},{7,5},{8,10},{9,11},{10,... | collective-permute-start | bytes 786440 | tf_op jit(solution)/shard_map/ppermute | solution.py:355
  5.1 1.5 %collective-permute-start.1 = (f32[16,640]{1,0:T(8,128)S(1)}, f32[16,640]{1,0:T(8,128)S(1)}, u32[]{:S(2)}, u32[]{:S(2)}) collective-permute-start(f32[16,640]{1,0:T(8,128)S(1)} %get-tuple-element.32), channel_id=1, source_target_pairs={{0,4},{4,0},{8,12},{12,8},{16,20},{20,16},{24,28},{28,24},{1,5},{5... | collective-permute-start | bytes 122888 | tf_op jit(solution)/shard_map/ppermute | solution.py:19
  6.6 2.5 %collective-permute-done.1 = f32[16,640]{1,0:T(8,128)S(1)} collective-permute-done((f32[16,640]{1,0:T(8,128)S(1)}, f32[16,640]{1,0:T(8,128)S(1)}, u32[]{:S(2)}, u32[]{:S(2)}) %collective-permute-start.1) | collective-permute-done | bytes 40992 | tf_op jit(solution)/shard_map/ppermute | solution.py:19
  9.1 3.6 %collective-permute-start.4 = (f32[16,640]{1,0:T(8,128)S(1)}, f32[16,640]{1,0:T(8,128)S(1)}, u32[]{:S(2)}, u32[]{:S(2)}) collective-permute-start(f32[16,640]{1,0:T(8,128)S(1)} %add.6.refs_0_), channel_id=1, source_target_pairs={{0,24},{4,28},{8,16},{12,20},{16,8},{20,12},{24,0},{28,4},{1,25},{... | collective-permute-start | bytes 122888 | tf_op jit(solution)/shard_map/ppermute | solution.py:19
  12.7 0.0 collective-permute-start.3
  12.7 0.8 %collective-permute-start.2 = (f32[16,640]{1,0:T(8,128)S(1)}, f32[16,640]{1,0:T(8,128)S(1)}, u32[]{:S(2)}, u32[]{:S(2)}) collective-permute-start(f32[16,640]{1,0:T(8,128)S(1)} %add.6.refs_0_), channel_id=1, source_target_pairs={{0,8},{4,12},{8,0},{12,4},{16,24},{20,28},{24,16},{28,20},{1,9},{5... | collective-permute-start | bytes 122888 | tf_op jit(solution)/shard_map/ppermute | solution.py:19
  13.5 0.0 copy-done.5
  13.5 0.0 copy-done.3
  13.5 0.2 maps.1.refs_7_.refs_14_.refs_10_.refs_15_
  13.7 1.2 %collective-permute-done.4.refs_3_ = f32[16,640]{1,0:T(8,128)S(1)} collective-permute-done((f32[16,640]{1,0:T(8,128)S(1)}, f32[16,640]{1,0:T(8,128)S(1)}, u32[]{:S(2)}, u32[]{:S(2)}) %collective-permute-start.4) | collective-permute-done | bytes 40992 | tf_op jit(solution)/shard_map/ppermute | solution.py:19
  14.9 2.7 %collective-permute-done.3.refs_2_ = f32[16,640]{1,0:T(8,128)S(1)} collective-permute-done((f32[16,640]{1,0:T(8,128)S(1)}, f32[16,640]{1,0:T(8,128)S(1)}, u32[]{:S(2)}, u32[]{:S(2)}) %collective-permute-start.3) | collective-permute-done | bytes 40992 | tf_op jit(solution)/shard_map/ppermute | solution.py:19
  17.6 0.0 collective-permute-done.2.refs_1_
  17.6 0.0 copy-done
  17.6 0.9 %first.1 = (f32[16,1024]{1,0:T(8,128)S(1)}, f32[16,1024]{1,0:T(8,128)S(1)}, bf16[16,1536]{1,0:T(8,128)(2,1)S(1)}, f32[16,640]{1,0:T(8,128)S(1)}, bf16[1024,512]{...) custom-call(f32[16,640]{1,0:T(8,128)S(1)} %add.6.refs_0_, f32[16,640]{1,0:T(8,128)S(1)} %collective-permute-done.2.refs_1_, ...), custom_call_target="tpu_custom_call" | custom-call | tf_op jit(solution)/shard_map/first/pallas_call | solution.py:396
  18.5 0.0 collective-permute-done.refs_19_.refs_18_
  18.5 0.0 copy-done.2
  18.5 0.1 collective-permute-start.9
  18.6 0.5 collective-permute-start.10
  19.1 1.5 %collective-permute-start.5 = (bf16[16,1536]{1,0:T(8,128)(2,1)S(1)}, bf16[16,1536]{1,0:T(8,128)(2,1)S(1)}, u32[]{:S(2)}, u32[]{:S(2)}) collective-permute-start(bf16[16,1536]{1,0:T(8,128)(2,1)S(1)} %get-tuple-element.36.send_ref.refs_2_), channel_id=1, source_target_pairs={{0,4},{4,0},{8,12},{12,8},{16,20},{20,16},{24,28},{28,24},{1,5},{5... | collective-permute-start | bytes 147464 | tf_op jit(solution)/shard_map/ppermute | solution.py:19
  20.6 2.6 %collective-permute-done.5.near_ref.refs_3_ = bf16[16,1536]{1,0:T(8,128)(2,1)S(1)} collective-permute-done((bf16[16,1536]{1,0:T(8,128)(2,1)S(1)}, bf16[16,1536]{1,0:T(8,128)(2,1)S(1)}, u32[]{:S(2)}, u32[]{:S(2)}) %collective-permute-start.5) | collective-permute-done | bytes 49184 | tf_op jit(solution)/shard_map/ppermute | solution.py:19
  23.2 1.5 %collective-permute-start.7 = (bf16[16,1536]{1,0:T(8,128)(2,1)S(1)}, bf16[16,1536]{1,0:T(8,128)(2,1)S(1)}, u32[]{:S(2)}, u32[]{:S(2)}) collective-permute-start(bf16[16,1536]{1,0:T(8,128)(2,1)S(1)} %get-tuple-element.37), channel_id=1, source_target_pairs={{0,24},{4,28},{8,16},{12,20},{16,8},{20,12},{24,0},{28,4},{1,25},{... | collective-permute-start | bytes 147464 | tf_op jit(solution)/shard_map/ppermute | solution.py:19
  24.7 1.1 %collective-permute-start.6 = (bf16[16,1536]{1,0:T(8,128)(2,1)S(1)}, bf16[16,1536]{1,0:T(8,128)(2,1)S(1)}, u32[]{:S(2)}, u32[]{:S(2)}) collective-permute-start(bf16[16,1536]{1,0:T(8,128)(2,1)S(1)} %get-tuple-element.37), channel_id=1, source_target_pairs={{0,8},{4,12},{8,0},{12,4},{16,24},{20,28},{24,16},{28,20},{1,9},{5... | collective-permute-start | bytes 147464 | tf_op jit(solution)/shard_map/ppermute | solution.py:19
  25.8 1.8 %collective-permute-start.8 = (bf16[16,512]{1,0:T(8,128)(2,1)S(1)}, bf16[16,512]{1,0:T(8,128)(2,1)S(1)}, u32[]{:S(2)}, u32[]{:S(2)}) collective-permute-start(bf16[16,512]{1,0:T(8,128)(2,1)S(1)} %get-tuple-element.38.refs_6_), channel_id=1, source_target_pairs={{0,16},{4,20},{8,24},{12,28},{16,0},{20,4},{24,8},{28,12},{1,17},{... | collective-permute-start | bytes 49160 | tf_op jit(solution)/shard_map/ppermute | solution.py:19
  27.6 2.8 %collective-permute-done.8.refs_8_ = bf16[16,512]{1,0:T(8,128)(2,1)S(1)} collective-permute-done((bf16[16,512]{1,0:T(8,128)(2,1)S(1)}, bf16[16,512]{1,0:T(8,128)(2,1)S(1)}, u32[]{:S(2)}, u32[]{:S(2)}) %collective-permute-start.8) | collective-permute-done | bytes 16416 | tf_op jit(solution)/shard_map/ppermute | solution.py:19
  30.4 0.0 collective-permute-done.7.refs_5_.refs_9_
  30.4 0.0 collective-permute-done.6.refs_4_.refs_7_
  30.4 0.0 collective-permute-done.9.refs_18_.refs_17_
  30.4 0.0 collective-permute-done.10.refs_20_.refs_19_
  30.4 0.0 copy-done.1
  30.4 0.0 copy-done.4
  30.5 0.0 copy-done.6
  30.5 2.6 %second.1 = (f32[16,1024]{1,0:T(8,128)S(1)}, f32[16,640]{1,0:T(8,128)S(1)}) custom-call(s32[8,8]{1,0:T(8,128)S(1)} %copy-done.4, s32[8]{0:T(128)S(1)} %copy-done.6, bf16[16,1536]{1,0:T(8,128)(2,1)S(1)} %get-tuple-element.36.send_ref.refs_2_, bf16[16,1536]{1,0:T(8,128)(2,1)S(1)} %collective-permute-done.5.near_ref.refs_3_, ...), custom_call_target="tpu_custom_call" | custom-call | tf_op jit(solution)/shard_map/second/pallas_call | solution.py:396
  33.0 1.5 %collective-permute-start.11 = (f32[16,640]{1,0:T(8,128)S(1)}, f32[16,640]{1,0:T(8,128)S(1)}, u32[]{:S(2)}, u32[]{:S(2)}) collective-permute-start(f32[16,640]{1,0:T(8,128)S(1)} %get-tuple-element.46), channel_id=1, source_target_pairs={{0,4},{4,0},{8,12},{12,8},{16,20},{20,16},{24,28},{28,24},{1,5},{5... | collective-permute-start | bytes 122888 | tf_op jit(solution)/shard_map/ppermute | solution.py:19
  34.6 2.5 %collective-permute-done.11 = f32[16,640]{1,0:T(8,128)S(1)} collective-permute-done((f32[16,640]{1,0:T(8,128)S(1)}, f32[16,640]{1,0:T(8,128)S(1)}, u32[]{:S(2)}, u32[]{:S(2)}) %collective-permute-start.11) | collective-permute-done | bytes 40992 | tf_op jit(solution)/shard_map/ppermute | solution.py:19
  37.1 1.2 %collective-permute-start.14 = (f32[16,640]{1,0:T(8,128)S(1)}, f32[16,640]{1,0:T(8,128)S(1)}, u32[]{:S(2)}, u32[]{:S(2)}) collective-permute-start(f32[16,640]{1,0:T(8,128)S(1)} %add.7.refs_0_), channel_id=1, source_target_pairs={{0,24},{4,28},{8,16},{12,20},{16,8},{20,12},{24,0},{28,4},{1,25},{... | collective-permute-start | bytes 122888 | tf_op jit(solution)/shard_map/ppermute | solution.py:19
  38.3 1.1 %collective-permute-start.13 = (f32[16,640]{1,0:T(8,128)S(1)}, f32[16,640]{1,0:T(8,128)S(1)}, u32[]{:S(2)}, u32[]{:S(2)}) collective-permute-start(f32[16,640]{1,0:T(8,128)S(1)} %add.7.refs_0_), channel_id=1, source_target_pairs={{0,16},{4,20},{8,24},{12,28},{16,0},{20,4},{24,8},{28,12},{1,17},{... | collective-permute-start | bytes 122888 | tf_op jit(solution)/shard_map/ppermute | solution.py:19
  39.4 2.0 %collective-permute-start.12 = (f32[16,640]{1,0:T(8,128)S(1)}, f32[16,640]{1,0:T(8,128)S(1)}, u32[]{:S(2)}, u32[]{:S(2)}) collective-permute-start(f32[16,640]{1,0:T(8,128)S(1)} %add.7.refs_0_), channel_id=1, source_target_pairs={{0,8},{4,12},{8,0},{12,4},{16,24},{20,28},{24,16},{28,20},{1,9},{5... | collective-permute-start | bytes 122888 | tf_op jit(solution)/shard_map/ppermute | solution.py:19
  41.5 1.4 %collective-permute-done.14.refs_3_ = f32[16,640]{1,0:T(8,128)S(1)} collective-permute-done((f32[16,640]{1,0:T(8,128)S(1)}, f32[16,640]{1,0:T(8,128)S(1)}, u32[]{:S(2)}, u32[]{:S(2)}) %collective-permute-start.14) | collective-permute-done | bytes 40992 | tf_op jit(solution)/shard_map/ppermute | solution.py:19
  42.9 0.5 collective-permute-done.13.refs_2_
  43.3 0.4 collective-permute-done.12.refs_1_
  43.8 1.0 %third.1 = (f32[16,1024]{1,0:T(8,128)S(1)}, f32[16,1024]{1,0:T(8,128)S(1)}, bf16[16,1536]{1,0:T(8,128)(2,1)S(1)}, f32[16,128]{1,0:T(8,128)S(1)}) custom-call(f32[16,640]{1,0:T(8,128)S(1)} %add.7.refs_0_, f32[16,640]{1,0:T(8,128)S(1)} %collective-permute-done.12.refs_1_, f32[16,640]{1,0:T(8,128)S(1)} %collective-permute-done.13.refs_2_, ...), custom_call_target="tpu_custom_call" | custom-call | tf_op jit(solution)/shard_map/third/pallas_call | solution.py:396
  44.7 1.5 %collective-permute-start.15 = (bf16[16,1536]{1,0:T(8,128)(2,1)S(1)}, bf16[16,1536]{1,0:T(8,128)(2,1)S(1)}, u32[]{:S(2)}, u32[]{:S(2)}) collective-permute-start(bf16[16,1536]{1,0:T(8,128)(2,1)S(1)} %get-tuple-element.49.send_ref.refs_2_), channel_id=1, source_target_pairs={{0,4},{4,0},{8,12},{12,8},{16,20},{20,16},{24,28},{28,24},{1,5},{5... | collective-permute-start | bytes 147464 | tf_op jit(solution)/shard_map/ppermute | solution.py:19
  46.3 2.6 %collective-permute-done.15.near_ref.refs_3_ = bf16[16,1536]{1,0:T(8,128)(2,1)S(1)} collective-permute-done((bf16[16,1536]{1,0:T(8,128)(2,1)S(1)}, bf16[16,1536]{1,0:T(8,128)(2,1)S(1)}, u32[]{:S(2)}, u32[]{:S(2)}) %collective-permute-start.15) | collective-permute-done | bytes 49184 | tf_op jit(solution)/shard_map/ppermute | solution.py:19
  48.8 2.5 %collective-permute-start.17 = (bf16[16,1536]{1,0:T(8,128)(2,1)S(1)}, bf16[16,1536]{1,0:T(8,128)(2,1)S(1)}, u32[]{:S(2)}, u32[]{:S(2)}) collective-permute-start(bf16[16,1536]{1,0:T(8,128)(2,1)S(1)} %get-tuple-element.50), channel_id=1, source_target_pairs={{0,24},{4,28},{8,16},{12,20},{16,8},{20,12},{24,0},{28,4},{1,25},{... | collective-permute-start | bytes 147464 | tf_op jit(solution)/shard_map/ppermute | solution.py:19
  51.3 0.0 collective-permute-start.16
  51.3 1.9 %collective-permute-start.18 = (bf16[16,512]{1,0:T(8,128)(2,1)S(1)}, bf16[16,512]{1,0:T(8,128)(2,1)S(1)}, u32[]{:S(2)}, u32[]{:S(2)}) collective-permute-start(bf16[16,512]{1,0:T(8,128)(2,1)S(1)} %get-tuple-element.51.refs_6_), channel_id=1, source_target_pairs={{0,16},{4,20},{8,24},{12,28},{16,0},{20,4},{24,8},{28,12},{1,17},{... | collective-permute-start | bytes 49160 | tf_op jit(solution)/shard_map/ppermute | solution.py:19
  53.2 2.7 %collective-permute-done.18.refs_8_ = bf16[16,512]{1,0:T(8,128)(2,1)S(1)} collective-permute-done((bf16[16,512]{1,0:T(8,128)(2,1)S(1)}, bf16[16,512]{1,0:T(8,128)(2,1)S(1)}, u32[]{:S(2)}, u32[]{:S(2)}) %collective-permute-start.18) | collective-permute-done | bytes 16416 | tf_op jit(solution)/shard_map/ppermute | solution.py:19
  56.0 0.0 collective-permute-done.17.refs_5_.refs_9_
  56.0 0.0 collective-permute-done.16.refs_4_.refs_7_
  56.0 2.4 %fourth.1 = f32[8,16,128]{2,1,0:T(8,128)S(1)} custom-call(s32[8,8]{1,0:T(8,128)S(1)} %copy-done.4, s32[8]{0:T(128)S(1)} %copy-done.6, bf16[16,1536]{1,0:T(8,128)(2,1)S(1)} %get-tuple-element.49.send_ref.refs_2_, bf16[16,1536]{1,0:T(8,128)(2,1)S(1)} %collective-permute-done.15.near_ref.refs_3_, bf16[16,1536]{1,0:T(8,128)(2,1)S(1)} %collective-permute-done.16.refs_4_.refs_7_, ...), custom_call_target="tpu_custom_call" | custom-call | tf_op jit(solution)/shard_map/fourth/pallas_call | solution.py:396
  58.4 11.1 %all_to_all.5.sums_ref = f32[8,16,128]{2,1,0:T(8,128)S(1)} all-to-all(f32[8,16,128]{2,1,0:T(8,128)S(1)} %fourth.1), channel_id=1, replica_groups=mesh['space'=8,'rhs'=4] {'space'}, dimensions={0} | all-to-all | bytes 131072 | tf_op jit(solution)/shard_map/all_to_all | solution.py:487
  69.5 1.0 %last.1 = f32[16,1024]{1,0:T(8,128)} custom-call(f32[8,16,128]{2,1,0:T(8,128)S(1)} %all_to_all.5.sums_ref, f32[16,128]{1,0:T(8,128)S(1)} %get-tuple-element.54.scalars_ref, f32[16,1024]{1,0:T(8,128)S(1)} %get-tuple-element.40.refs_11_.first_ref, f32[16,1024]{1,0:T(8,128)S(1)} %get-tuple-element.53.refs_12_.second_ref), custom_call_target="tpu_custom_call" | custom-call | tf_op jit(solution)/shard_map/last/pallas_call | solution.py:396
  (4 shorter events, 0.0 us)
Async XLA Ops:
  0.0 17.6 %copy-start = (f32[1024,512]{1,0:T(8,128)S(1)}, f32[1024,512]{1,0:T(8,128)}, u32[]{:S(2)}) copy-start(f32[1024,512]{1,0:T(8,128)} %refs_6_.1) | copy-start | bytes 6291460
  0.0 13.5 %copy-start.5 = (s32[8,32]{1,0:T(8,128)S(1)}, s32[8,32]{1,0:T(8,128)}, u32[]{:S(2)}) copy-start(s32[8,32]{1,0:T(8,128)} %skel_ref.1) | copy-start | bytes 3076
  0.0 13.5 %copy-start.3 = (bf16[8,128,32]{1,2,0:T(8,128)(2,1)S(1)}, bf16[8,128,32]{1,2,0:T(8,128)(2,1)}, u32[]{:S(2)}) copy-start(bf16[8,128,32]{1,2,0:T(8,128)(2,1)} %param.15) | copy-start | bytes 196612
  2.0 16.5 %copy-start.2 = (bf16[256,1,512]{2,0,1:T(8,128)(2,1)S(1)}, bf16[256,1,512]{2,0,1:T(8,128)(2,1)}, u32[]{:S(2)}) copy-start(bf16[256,1,512]{2,0,1:T(8,128)(2,1)} %param.17) | copy-start | bytes 786436
  2.0 28.4 %copy-start.1 = (bf16[8,8,128,128]{3,2,1,0:T(8,128)(2,1)S(1)}, bf16[8,8,128,128]{3,2,1,0:T(8,128)(2,1)}, u32[]{:S(2)}) copy-start(bf16[8,8,128,128]{3,2,1,0:T(8,128)(2,1)} %refs_14_.1) | copy-start | bytes 6291460
  2.0 28.4 %copy-start.4 = (s32[8,8]{1,0:T(8,128)S(1)}, s32[8,8]{1,0:T(8,128)}, u32[]{:S(2)}) copy-start(s32[8,8]{1,0:T(8,128)} %refs_0_.5) | copy-start | bytes 772
  2.0 28.4 %copy-start.6 = (s32[8]{0:T(128)S(1)}, s32[8]{0:T(128)}, u32[]{:S(2)}) copy-start(s32[8]{0:T(128)} %refs_1_.5) | copy-start | bytes 100
  2.0 16.4 %collective-permute-start = (bf16[256,512]{1,0:T(8,128)(2,1)}, bf16[256,512]{1,0:T(8,128)(2,1)S(1)}, u32[]{:S(2)}, u32[]{:S(2)}) collective-permute-start(bf16[256,512]{1,0:T(8,128)(2,1)} %bitcast.4), channel_id=1, source_target_pairs={{0,2},{1,3},{2,0},{3,1},{4,6},{5,7},{6,4},{7,5},{8,10},{9,11},{10,... | collective-permute-start | bytes 786440 | tf_op jit(solution)/shard_map/ppermute | solution.py:355
  5.1 4.0 %collective-permute-start.1 = (f32[16,640]{1,0:T(8,128)S(1)}, f32[16,640]{1,0:T(8,128)S(1)}, u32[]{:S(2)}, u32[]{:S(2)}) collective-permute-start(f32[16,640]{1,0:T(8,128)S(1)} %get-tuple-element.32), channel_id=1, source_target_pairs={{0,4},{4,0},{8,12},{12,8},{16,20},{20,16},{24,28},{28,24},{1,5},{5... | collective-permute-start | bytes 122888 | tf_op jit(solution)/shard_map/ppermute | solution.py:19
  9.1 5.8 %collective-permute-start.4 = (f32[16,640]{1,0:T(8,128)S(1)}, f32[16,640]{1,0:T(8,128)S(1)}, u32[]{:S(2)}, u32[]{:S(2)}) collective-permute-start(f32[16,640]{1,0:T(8,128)S(1)} %add.6.refs_0_), channel_id=1, source_target_pairs={{0,24},{4,28},{8,16},{12,20},{16,8},{20,12},{24,0},{28,4},{1,25},{... | collective-permute-start | bytes 122888 | tf_op jit(solution)/shard_map/ppermute | solution.py:19
  12.7 4.9 %collective-permute-start.3 = (f32[16,640]{1,0:T(8,128)S(1)}, f32[16,640]{1,0:T(8,128)S(1)}, u32[]{:S(2)}, u32[]{:S(2)}) collective-permute-start(f32[16,640]{1,0:T(8,128)S(1)} %add.6.refs_0_), channel_id=1, source_target_pairs={{0,16},{4,20},{8,24},{12,28},{16,0},{20,4},{24,8},{28,12},{1,17},{... | collective-permute-start | bytes 122888 | tf_op jit(solution)/shard_map/ppermute | solution.py:19
  12.7 4.9 %collective-permute-start.2 = (f32[16,640]{1,0:T(8,128)S(1)}, f32[16,640]{1,0:T(8,128)S(1)}, u32[]{:S(2)}, u32[]{:S(2)}) collective-permute-start(f32[16,640]{1,0:T(8,128)S(1)} %add.6.refs_0_), channel_id=1, source_target_pairs={{0,8},{4,12},{8,0},{12,4},{16,24},{20,28},{24,16},{28,20},{1,9},{5... | collective-permute-start | bytes 122888 | tf_op jit(solution)/shard_map/ppermute | solution.py:19
  18.5 11.9 %collective-permute-start.9 = (bf16[256,512]{1,0:T(8,128)(2,1)S(1)}, bf16[256,512]{1,0:T(8,128)(2,1)S(1)}, u32[]{:S(2)}, u32[]{:S(2)}) collective-permute-start(bf16[256,512]{1,0:T(8,128)(2,1)S(1)} %bitcast.5), channel_id=1, source_target_pairs={{0,1},{1,0},{2,3},{3,2},{4,5},{5,4},{6,7},{7,6},{8,9},{9,8},{10,11... | collective-permute-start | bytes 786440 | tf_op jit(solution)/shard_map/ppermute | solution.py:367
  18.6 11.8 %collective-permute-start.10 = (bf16[256,512]{1,0:T(8,128)(2,1)S(1)}, bf16[256,512]{1,0:T(8,128)(2,1)S(1)}, u32[]{:S(2)}, u32[]{:S(2)}) collective-permute-start(bf16[256,512]{1,0:T(8,128)(2,1)S(1)} %collective-permute-done.refs_19_.refs_18_), channel_id=1, source_target_pairs={{0,1},{1,0},{2,3},{3,2},{4,5},{5,4},{6,7},{7,6},{8,9},{9,8},{10,11... | collective-permute-start | bytes 786440 | tf_op jit(solution)/shard_map/ppermute | solution.py:367
  19.1 4.1 %collective-permute-start.5 = (bf16[16,1536]{1,0:T(8,128)(2,1)S(1)}, bf16[16,1536]{1,0:T(8,128)(2,1)S(1)}, u32[]{:S(2)}, u32[]{:S(2)}) collective-permute-start(bf16[16,1536]{1,0:T(8,128)(2,1)S(1)} %get-tuple-element.36.send_ref.refs_2_), channel_id=1, source_target_pairs={{0,4},{4,0},{8,12},{12,8},{16,20},{20,16},{24,28},{28,24},{1,5},{5... | collective-permute-start | bytes 147464 | tf_op jit(solution)/shard_map/ppermute | solution.py:19
  23.2 7.2 %collective-permute-start.7 = (bf16[16,1536]{1,0:T(8,128)(2,1)S(1)}, bf16[16,1536]{1,0:T(8,128)(2,1)S(1)}, u32[]{:S(2)}, u32[]{:S(2)}) collective-permute-start(bf16[16,1536]{1,0:T(8,128)(2,1)S(1)} %get-tuple-element.37), channel_id=1, source_target_pairs={{0,24},{4,28},{8,16},{12,20},{16,8},{20,12},{24,0},{28,4},{1,25},{... | collective-permute-start | bytes 147464 | tf_op jit(solution)/shard_map/ppermute | solution.py:19
  24.7 5.8 %collective-permute-start.6 = (bf16[16,1536]{1,0:T(8,128)(2,1)S(1)}, bf16[16,1536]{1,0:T(8,128)(2,1)S(1)}, u32[]{:S(2)}, u32[]{:S(2)}) collective-permute-start(bf16[16,1536]{1,0:T(8,128)(2,1)S(1)} %get-tuple-element.37), channel_id=1, source_target_pairs={{0,8},{4,12},{8,0},{12,4},{16,24},{20,28},{24,16},{28,20},{1,9},{5... | collective-permute-start | bytes 147464 | tf_op jit(solution)/shard_map/ppermute | solution.py:19
  25.8 4.6 %collective-permute-start.8 = (bf16[16,512]{1,0:T(8,128)(2,1)S(1)}, bf16[16,512]{1,0:T(8,128)(2,1)S(1)}, u32[]{:S(2)}, u32[]{:S(2)}) collective-permute-start(bf16[16,512]{1,0:T(8,128)(2,1)S(1)} %get-tuple-element.38.refs_6_), channel_id=1, source_target_pairs={{0,16},{4,20},{8,24},{12,28},{16,0},{20,4},{24,8},{28,12},{1,17},{... | collective-permute-start | bytes 49160 | tf_op jit(solution)/shard_map/ppermute | solution.py:19
  33.0 4.0 %collective-permute-start.11 = (f32[16,640]{1,0:T(8,128)S(1)}, f32[16,640]{1,0:T(8,128)S(1)}, u32[]{:S(2)}, u32[]{:S(2)}) collective-permute-start(f32[16,640]{1,0:T(8,128)S(1)} %get-tuple-element.46), channel_id=1, source_target_pairs={{0,4},{4,0},{8,12},{12,8},{16,20},{20,16},{24,28},{28,24},{1,5},{5... | collective-permute-start | bytes 122888 | tf_op jit(solution)/shard_map/ppermute | solution.py:19
  37.1 5.8 %collective-permute-start.14 = (f32[16,640]{1,0:T(8,128)S(1)}, f32[16,640]{1,0:T(8,128)S(1)}, u32[]{:S(2)}, u32[]{:S(2)}) collective-permute-start(f32[16,640]{1,0:T(8,128)S(1)} %add.7.refs_0_), channel_id=1, source_target_pairs={{0,24},{4,28},{8,16},{12,20},{16,8},{20,12},{24,0},{28,4},{1,25},{... | collective-permute-start | bytes 122888 | tf_op jit(solution)/shard_map/ppermute | solution.py:19
  38.3 5.0 %collective-permute-start.13 = (f32[16,640]{1,0:T(8,128)S(1)}, f32[16,640]{1,0:T(8,128)S(1)}, u32[]{:S(2)}, u32[]{:S(2)}) collective-permute-start(f32[16,640]{1,0:T(8,128)S(1)} %add.7.refs_0_), channel_id=1, source_target_pairs={{0,16},{4,20},{8,24},{12,28},{16,0},{20,4},{24,8},{28,12},{1,17},{... | collective-permute-start | bytes 122888 | tf_op jit(solution)/shard_map/ppermute | solution.py:19
  39.4 4.3 %collective-permute-start.12 = (f32[16,640]{1,0:T(8,128)S(1)}, f32[16,640]{1,0:T(8,128)S(1)}, u32[]{:S(2)}, u32[]{:S(2)}) collective-permute-start(f32[16,640]{1,0:T(8,128)S(1)} %add.7.refs_0_), channel_id=1, source_target_pairs={{0,8},{4,12},{8,0},{12,4},{16,24},{20,28},{24,16},{28,20},{1,9},{5... | collective-permute-start | bytes 122888 | tf_op jit(solution)/shard_map/ppermute | solution.py:19
  44.7 4.1 %collective-permute-start.15 = (bf16[16,1536]{1,0:T(8,128)(2,1)S(1)}, bf16[16,1536]{1,0:T(8,128)(2,1)S(1)}, u32[]{:S(2)}, u32[]{:S(2)}) collective-permute-start(bf16[16,1536]{1,0:T(8,128)(2,1)S(1)} %get-tuple-element.49.send_ref.refs_2_), channel_id=1, source_target_pairs={{0,4},{4,0},{8,12},{12,8},{16,20},{20,16},{24,28},{28,24},{1,5},{5... | collective-permute-start | bytes 147464 | tf_op jit(solution)/shard_map/ppermute | solution.py:19
  48.8 7.1 %collective-permute-start.17 = (bf16[16,1536]{1,0:T(8,128)(2,1)S(1)}, bf16[16,1536]{1,0:T(8,128)(2,1)S(1)}, u32[]{:S(2)}, u32[]{:S(2)}) collective-permute-start(bf16[16,1536]{1,0:T(8,128)(2,1)S(1)} %get-tuple-element.50), channel_id=1, source_target_pairs={{0,24},{4,28},{8,16},{12,20},{16,8},{20,12},{24,0},{28,4},{1,25},{... | collective-permute-start | bytes 147464 | tf_op jit(solution)/shard_map/ppermute | solution.py:19
  51.3 4.6 %collective-permute-start.16 = (bf16[16,1536]{1,0:T(8,128)(2,1)S(1)}, bf16[16,1536]{1,0:T(8,128)(2,1)S(1)}, u32[]{:S(2)}, u32[]{:S(2)}) collective-permute-start(bf16[16,1536]{1,0:T(8,128)(2,1)S(1)} %get-tuple-element.50), channel_id=1, source_target_pairs={{0,8},{4,12},{8,0},{12,4},{16,24},{20,28},{24,16},{28,20},{1,9},{5... | collective-permute-start | bytes 147464 | tf_op jit(solution)/shard_map/ppermute | solution.py:19
  51.3 4.6 %collective-permute-start.18 = (bf16[16,512]{1,0:T(8,128)(2,1)S(1)}, bf16[16,512]{1,0:T(8,128)(2,1)S(1)}, u32[]{:S(2)}, u32[]{:S(2)}) collective-permute-start(bf16[16,512]{1,0:T(8,128)(2,1)S(1)} %get-tuple-element.51.refs_6_), channel_id=1, source_target_pairs={{0,16},{4,20},{8,24},{12,28},{16,0},{20,4},{24,8},{28,12},{1,17},{... | collective-permute-start | bytes 49160 | tf_op jit(solution)/shard_map/ppermute | solution.py:19

commit v4 on v3

--- a/solution.py
+++ b/solution.py
@@ -162,21 +162,32 @@
     return jnp.where(live, slot * block_count + wanted % block_count, sources * block_count)
 
 
-def apply_matrix(
-    ids_ref, live_ref, field_refs, charge_refs, field, self_ref, mats_ref, coupling_refs, maps_ref,
-    blocks_ref, charges_ref
-):
-    rows, panels = field.shape
+def near_kernel(sources, ids_ref, live_ref, *refs):
+    field_refs = refs[:sources]
+    mats_ref, near_ref, blocks_ref = refs[sources:]
+    rows, panels = near_ref.shape
     block_count, slots, block, _ = mats_ref.shape
-    quarters, pairs = charges_ref.shape[:2]
-    sources = len(field_refs)
-    gathered = len(coupling_refs) == 1
     region = lax.axis_index(AXIS)
-    first_quarter = 0 if gathered else lax.axis_index("rhs")
     for index, ref in enumerate(field_refs):
         for b in range(block_count):
             blocks_ref[index * block_count + b] = ref[:, b * block : (b + 1) * block]
     blocks_ref[sources * block_count] = jnp.zeros((rows, block), BF)
+    for b in range(block_count):
+        places = [
+            block_place(ids_ref[b, k], k < live_ref[b], block_count, sources, region)
+            for k in range(slots)
+        ]
+        picked = jnp.concatenate([blocks_ref[place] for place in places], axis=1)
+        mats = jnp.concatenate([mats_ref[b, k] for k in range(slots)], axis=1)
+        near_ref[:, b * block : (b + 1) * block] = dot_nt(picked, mats)
+
+
+def apply_matrix(field_ref, self_ref, near_ref, charge_refs, coupling_refs, maps_ref, charges_ref):
+    rows, panels = field_ref.shape
+    quarters, pairs = charges_ref.shape[:2]
+    gathered = len(coupling_refs) == 1
+    region = lax.axis_index(AXIS)
+    first_quarter = 0 if gathered else lax.axis_index("rhs")
     for quarter in range(quarters):
         for index in range(pairs):
             if len(charge_refs) == pairs:
@@ -195,7 +206,6 @@
         far = far + dot_nt(charge, rows_in)
     odd = (region % 2) == 1
     per = panels // quarters
-    out = []
     for quarter in range(quarters):
         start = (quarter // 2) * LANES
         chunk = far[:, start : start + LANES]
@@ -204,32 +214,20 @@
         high, low = split(chunk)
         both = jnp.concatenate([high, low], axis=0)
         pot = dot_nn(jnp.concatenate([both, both], axis=1), maps_ref[quarter])
-        out.append(pot[:rows] + pot[rows:])
-    for b in range(block_count):
-        places = [
-            block_place(ids_ref[b, k], k < live_ref[b], block_count, sources, region)
-            for k in range(slots)
-        ]
-        picked = jnp.concatenate([blocks_ref[place] for place in places], axis=1)
-        mats = jnp.concatenate([mats_ref[b, k] for k in range(slots)], axis=1)
-        near = dot_nt(picked, mats)
-        quarter, rest = divmod(b * block, per)
-        cols = slice(b * block, (b + 1) * block)
-        out_b = near + out[quarter][:, rest : rest + block]
-        yield cols, out_b + self_ref[:, cols] * field[:, cols]
-
-
-def second_kernel(nfields, ncharges, charge_starts, ids_ref, live_ref, *refs):
-    field_refs = refs[:nfields]
-    charge_refs = list(zip(refs[nfields : nfields + ncharges], charge_starts))
-    refs = refs[nfields + ncharges :]
-    dir_ref, pre_ref, self_ref, mats_ref, maps_ref, high_ref, low_ref = refs[:7]
-    *coupling_refs, res_ref, out_ref, blocks_ref, charges_ref = refs[7:]
+        cols = slice(quarter * per, (quarter + 1) * per)
+        near = near_ref[:, cols] + (pot[:rows] + pot[rows:])
+        yield cols, near + self_ref[:, cols] * field_ref[:, cols]
+
+
+def second_kernel(charge_starts, *refs):
+    parts = len(charge_starts)
+    charge_refs = list(zip(refs[:parts], charge_starts))
+    dir_ref, pre_ref, self_ref, near_ref, maps_ref, high_ref, low_ref = refs[parts : parts + 7]
+    *coupling_refs, res_ref, out_ref, charges_ref = refs[parts + 7 :]
     width = high_ref.shape[1]
     rows = pre_ref.shape[0]
     for cols, values in apply_matrix(
-        ids_ref, live_ref, field_refs, charge_refs, pre_ref, self_ref, mats_ref, coupling_refs,
-        maps_ref, blocks_ref, charges_ref
+        pre_ref, self_ref, near_ref, charge_refs, coupling_refs, maps_ref, charges_ref
     ):
         res_ref[:, cols] = values
     res = res_ref[...]
@@ -266,27 +264,20 @@
     )
 
 
-def fourth_kernel(nfields, ncharges, charge_starts, ids_ref, live_ref, *refs):
-    field_refs = refs[:nfields]
-    charge_refs = list(zip(refs[nfields : nfields + ncharges], charge_starts))
-    refs = refs[nfields + ncharges :]
-    dir_ref, next_ref, pre_ref, self_ref, mats_ref, maps_ref = refs[:6]
-    *coupling_refs, out_ref, blocks_ref, charges_ref = refs[6:]
+def fourth_kernel(charge_starts, *refs):
+    parts = len(charge_starts)
+    charge_refs = list(zip(refs[:parts], charge_starts))
+    dir_ref, next_ref, pre_ref, self_ref, near_ref, maps_ref = refs[parts : parts + 6]
+    *coupling_refs, out_ref, charges_ref = refs[parts + 6 :]
     rows = pre_ref.shape[0]
-    block = mats_ref.shape[2]
-    upper = jnp.zeros((rows, block), F32)
-    diag = jnp.zeros((rows, block), F32)
-    square = jnp.zeros((rows, block), F32)
+    upper = diag = square = 0.0
     for cols, values in apply_matrix(
-        ids_ref, live_ref, field_refs, charge_refs, pre_ref, self_ref, mats_ref, coupling_refs,
-        maps_ref, blocks_ref, charges_ref
+        pre_ref, self_ref, near_ref, charge_refs, coupling_refs, maps_ref, charges_ref
     ):
-        upper = upper + values * dir_ref[:, cols]
-        diag = diag + values * next_ref[:, cols]
-        square = square + values * values
-    scalars = put_scalars([row_sum(upper), row_sum(diag), row_sum(square)], rows)
-    for index in range(out_ref.shape[0]):
-        out_ref[index] = scalars
+        upper = upper + row_sum(values * dir_ref[:, cols])
+        diag = diag + row_sum(values * next_ref[:, cols])
+        square = square + row_sum(values * values)
+    out_ref[...] = put_scalars([upper, diag, square], rows)
 
 
 def givens_pair(start_len, diag_one, below_one, upper_two, diag_two, below_two):
@@ -301,8 +292,11 @@
     return (step_one, step_two)
 
 
-def last_kernel(sums_ref, scalars_ref, first_ref, second_ref, out_ref):
-    summed = jnp.sum(sums_ref[...], axis=0)
+def last_kernel(parts, *refs):
+    scalars_ref, first_ref, second_ref, out_ref = refs[parts:]
+    summed = refs[0][...]
+    for ref in refs[1:parts]:
+        summed = summed + ref[...]
     start_len, first_sq, diag_one, below_one, cross, second_sq = [
         column(scalars_ref[...], i) for i in range(6)
     ]
@@ -350,24 +344,16 @@
 def gather_quarters(coupling, quarters, count, early):
     if count != 8 or quarters != 4:
         return [lax.all_gather(coupling, "rhs")], early
-
-    def other(values, mask):
-        return lax.ppermute(values, "rhs", [(i, i ^ mask) for i in range(quarters)])
-
     coupling, early = lax.optimization_barrier((coupling, early))
-    far = other(coupling, 2)
-    return [coupling, far], early
+    return [coupling, lax.ppermute(coupling, "rhs", [(i, i ^ 2) for i in range(quarters)])], early
 
 
 def finish_quarters(rows, quarters, late):
     if len(rows) == 1:
         return rows, late
-
-    def other(values, mask):
-        return lax.ppermute(values, "rhs", [(i, i ^ mask) for i in range(quarters)])
-
     own, far, late = lax.optimization_barrier((*rows, late))
-    return [own, other(own, 1), far, other(far, 1)], late
+    near, other = [lax.ppermute(x, "rhs", [(i, i ^ 1) for i in range(quarters)]) for x in (own, far)]
+    return [own, near, far, other], late
 
 
 def nbytes(shape, kind):
@@ -453,19 +439,26 @@
     )
     full_rows, send = finish_quarters(some_rows, quarters, send)
     fields, charges, starts = exchange(send, panels, count)
-    nf, nc = len(fields), len(charges)
-    scratch = [
-        pltpu.VMEM((nf * block_count + 1, rows, block), BF),
-        pltpu.VMEM((quarters, count // 2, rows, LANES), BF),
-    ]
+
+    def near_product(fields):
+        (near,) = call(
+            "near",
+            lambda *refs: near_kernel(len(fields), *refs),
+            [((rows, panels), F32)],
+            [near_ids, near_count, *fields, near_mats],
+            [pltpu.VMEM((len(fields) * block_count + 1, rows, block), BF)],
+            2,
+        )
+        return near
+
+    near = near_product(fields)
+    scratch = [pltpu.VMEM((quarters, count // 2, rows, LANES), BF)]
     residue, payload = call(
         "second",
-        lambda *refs: second_kernel(nf, nc, starts, *refs),
+        lambda *refs: second_kernel(starts, *refs),
         [((rows, panels), F32), ((rows, wide), F32)],
-        [near_ids, near_count, *fields, *charges, first_dir, first_pre, self_row, near_mats, maps,
-         high, low, *full_rows],
+        [*charges, first_dir, first_pre, self_row, near, maps, high, low, *full_rows],
         scratch,
-        2,
     )
     sums = sum_parts(payload, count)
     second_dir, second_pre, send, scalars = call(
@@ -475,17 +468,21 @@
         [*sums, residue, first_dir, keep, diag_row, high, low, maps],
     )
     fields, charges, starts = exchange(send, panels, count)
-    (tails,) = call(
+    near = near_product(fields)
+    (tail,) = call(
         "fourth",
-        lambda *refs: fourth_kernel(nf, nc, starts, *refs),
-        [((count if count == 8 else 1, rows, LANES), F32)],
-        [near_ids, near_count, *fields, *charges, first_dir, second_dir, second_pre,
-         self_row, near_mats, maps, *full_rows],
+        lambda *refs: fourth_kernel(starts, *refs),
+        [((rows, LANES), F32)],
+        [*charges, first_dir, second_dir, second_pre, self_row, near, maps, *full_rows],
         scratch,
-        2,
-    )
-    tails = lax.all_to_all(tails, AXIS, 0, 0) if count == 8 else lax.psum(tails, AXIS)
-    (result,) = call("last", last_kernel, [((rows, panels), F32)], [tails, scalars, first_pre, second_pre])
+    )
+    sums = sum_parts(tail, count)
+    (result,) = call(
+        "last",
+        lambda *refs: last_kernel(len(sums), *refs),
+        [((rows, panels), F32)],
+        [*sums, scalars, first_pre, second_pre],
+    )
     return result
 
 

time: 70.6 us -> 68.1 us (0.965)
  blocking collectives: 11.1 us -> 0 us
  starting transfers between devices: 27.2 us -> 33.2 us
  waiting for transfers between devices: 21.9 us -> 24.6 us
    all_to_all x1 -> x0, blocking collectives: 11.1 us -> none  [on_device(): lax.all_to_all(tails, AXIS, 0, 0)]
    ppermute x16 -> x20, starting transfers between devices: 23.7 us -> 29.6 us  [swap(): return lax.ppermute(values, AXIS, [(i, i ^ mask) for i in range(count)])]
    ppermute x16 -> x20, waiting for transfers between devices: 21.9 us -> 24.6 us  [swap(): return lax.ppermute(values, AXIS, [(i, i ^ mask) for i in range(count)])]
    pallas_call x9 -> x11, Pallas kernels: 9.99 us -> 9.93 us  [call(): pl.pallas_call(kernel, name=name, out_shape=out_shapes, in_specs=specs, o...]
  transfers between devices with their start and end apart: 19 -> 23, of which waited for: 11 -> 15; matrix products, arithmetic and copies ran while one was open for 0% -> 0% of each run, Pallas kernels for 2% -> 5%
where the time goes in v4:
time: 68.1 us; the launch traced here: 67.9 us
  starting transfers between devices  33.2 us (49%)
  waiting for transfers between devices  24.6 us (36%)
  Pallas kernels  9.93 us (15%)
    ppermute x20, starting transfers between devices, swap(): return lax.ppermute(values, AXIS, [(i, i ^ mask) for i in range(count)])  29.6 us
    ppermute x20, waiting for transfers between devices, swap(): return lax.ppermute(values, AXIS, [(i, i ^ mask) for i in range(count)])  24.6 us
    pallas_call x11, Pallas kernels, call(): pl.pallas_call(kernel, name=name, out_shape=out_shapes, in_specs=specs, o...  9.93 us
    ppermute x1, starting transfers between devices, gather_quarters(): lax.ppermute(coupling, 'rhs', [(i, i ^ 2) for i in range(quarters)])  3.01 us
  transfers between devices with their start and end apart: 23, of which 15 were waited for; matrix products, arithmetic and copies ran while one was open for 0% of the time, Pallas kernels for 5%

profile of v4, /device:TPU:0, one launch (start us, length us, event | category | flops | bytes accessed | tf_op | source)
XLA Modules:
  0.0 67.9 jit_solution(12149303905685406493)
XLA Ops:
  0.0 2.0 %open.1 = (f32[16,640]{1,0:T(8,128)S(1)}, f32[16,1024]{1,0:T(8,128)S(1)}, f32[1,1024]{1,0:T(1,128)S(1)}, f32[1,1024]{1,0:T(1,128)S(1)}) custom-call(f32[16,1024]{1,0:T(8,128)} %refs_0_.3, f32[1024,512]{1,0:T(8,128)} %refs_6_.3, f32[1,1024]{1,0:T(1,128)} %bitcast.9, f32[1,1024]{1,0:T(1,128)} %bitcast.10), custom_call_target="tpu_custom_call" | custom-call | tf_op jit(solution)/shard_map/open/pallas_call | solution.py:382
  2.0 0.0 copy-start.2
  2.0 0.0 copy-start.1
  2.0 0.0 copy-start.4
  2.0 0.0 copy-start.6
  2.0 3.0 %collective-permute-start = (bf16[256,512]{1,0:T(8,128)(2,1)}, bf16[256,512]{1,0:T(8,128)(2,1)S(1)}, u32[]{:S(2)}, u32[]{:S(2)}) collective-permute-start(bf16[256,512]{1,0:T(8,128)(2,1)} %bitcast.4), channel_id=1, source_target_pairs={{0,2},{1,3},{2,0},{3,1},{4,6},{5,7},{6,4},{7,5},{8,10},{9,11},{10,... | collective-permute-start | bytes 786440 | tf_op jit(solution)/shard_map/ppermute | solution.py:348
  5.1 1.5 %collective-permute-start.1 = (f32[16,640]{1,0:T(8,128)S(1)}, f32[16,640]{1,0:T(8,128)S(1)}, u32[]{:S(2)}, u32[]{:S(2)}) collective-permute-start(f32[16,640]{1,0:T(8,128)S(1)} %get-tuple-element.32), channel_id=1, source_target_pairs={{0,4},{4,0},{8,12},{12,8},{16,20},{20,16},{24,28},{28,24},{1,5},{5... | collective-permute-start | bytes 122888 | tf_op jit(solution)/shard_map/ppermute | solution.py:19
  6.6 2.5 %collective-permute-done.1 = f32[16,640]{1,0:T(8,128)S(1)} collective-permute-done((f32[16,640]{1,0:T(8,128)S(1)}, f32[16,640]{1,0:T(8,128)S(1)}, u32[]{:S(2)}, u32[]{:S(2)}) %collective-permute-start.1) | collective-permute-done | bytes 40992 | tf_op jit(solution)/shard_map/ppermute | solution.py:19
  9.1 3.6 %collective-permute-start.4 = (f32[16,640]{1,0:T(8,128)S(1)}, f32[16,640]{1,0:T(8,128)S(1)}, u32[]{:S(2)}, u32[]{:S(2)}) collective-permute-start(f32[16,640]{1,0:T(8,128)S(1)} %add.9.refs_0_), channel_id=1, source_target_pairs={{0,24},{4,28},{8,16},{12,20},{16,8},{20,12},{24,0},{28,4},{1,25},{... | collective-permute-start | bytes 122888 | tf_op jit(solution)/shard_map/ppermute | solution.py:19
  12.7 0.0 collective-permute-start.3
  12.7 0.8 %collective-permute-start.2 = (f32[16,640]{1,0:T(8,128)S(1)}, f32[16,640]{1,0:T(8,128)S(1)}, u32[]{:S(2)}, u32[]{:S(2)}) collective-permute-start(f32[16,640]{1,0:T(8,128)S(1)} %add.9.refs_0_), channel_id=1, source_target_pairs={{0,8},{4,12},{8,0},{12,4},{16,24},{20,28},{24,16},{28,20},{1,9},{5... | collective-permute-start | bytes 122888 | tf_op jit(solution)/shard_map/ppermute | solution.py:19
  13.5 0.0 copy-done.5
  13.5 0.0 copy-done.3
  13.5 0.2 maps.1.refs_7_.refs_8_.refs_10_.refs_9_
  13.7 1.2 %collective-permute-done.4.refs_3_ = f32[16,640]{1,0:T(8,128)S(1)} collective-permute-done((f32[16,640]{1,0:T(8,128)S(1)}, f32[16,640]{1,0:T(8,128)S(1)}, u32[]{:S(2)}, u32[]{:S(2)}) %collective-permute-start.4) | collective-permute-done | bytes 40992 | tf_op jit(solution)/shard_map/ppermute | solution.py:19
  14.9 2.7 %collective-permute-done.3.refs_2_ = f32[16,640]{1,0:T(8,128)S(1)} collective-permute-done((f32[16,640]{1,0:T(8,128)S(1)}, f32[16,640]{1,0:T(8,128)S(1)}, u32[]{:S(2)}, u32[]{:S(2)}) %collective-permute-start.3) | collective-permute-done | bytes 40992 | tf_op jit(solution)/shard_map/ppermute | solution.py:19
  17.6 0.0 collective-permute-done.2.refs_1_
  17.6 0.9 %first.1 = (f32[16,1024]{1,0:T(8,128)S(1)}, f32[16,1024]{1,0:T(8,128)S(1)}, bf16[16,1536]{1,0:T(8,128)(2,1)S(1)}, f32[16,640]{1,0:T(8,128)S(1)}, bf16[1024,512]{...) custom-call(f32[16,640]{1,0:T(8,128)S(1)} %add.9.refs_0_, f32[16,640]{1,0:T(8,128)S(1)} %collective-permute-done.2.refs_1_, ...), custom_call_target="tpu_custom_call" | custom-call | tf_op jit(solution)/shard_map/first/pallas_call | solution.py:382
  18.5 0.0 collective-permute-done.refs_13_.refs_12_
  18.5 0.0 copy-done.2
  18.5 0.1 collective-permute-start.9
  18.6 0.5 collective-permute-start.10
  19.1 1.5 %collective-permute-start.5 = (bf16[16,1536]{1,0:T(8,128)(2,1)S(1)}, bf16[16,1536]{1,0:T(8,128)(2,1)S(1)}, u32[]{:S(2)}, u32[]{:S(2)}) collective-permute-start(bf16[16,1536]{1,0:T(8,128)(2,1)S(1)} %get-tuple-element.36.send_ref.refs_2_), channel_id=1, source_target_pairs={{0,4},{4,0},{8,12},{12,8},{16,20},{20,16},{24,28},{28,24},{1,5},{5... | collective-permute-start | bytes 147464 | tf_op jit(solution)/shard_map/ppermute | solution.py:19
  20.6 2.6 %collective-permute-done.5.near_ref.refs_3_ = bf16[16,1536]{1,0:T(8,128)(2,1)S(1)} collective-permute-done((bf16[16,1536]{1,0:T(8,128)(2,1)S(1)}, bf16[16,1536]{1,0:T(8,128)(2,1)S(1)}, u32[]{:S(2)}, u32[]{:S(2)}) %collective-permute-start.5) | collective-permute-done | bytes 49184 | tf_op jit(solution)/shard_map/ppermute | solution.py:19
  23.2 1.5 %collective-permute-start.8 = (bf16[16,1536]{1,0:T(8,128)(2,1)S(1)}, bf16[16,1536]{1,0:T(8,128)(2,1)S(1)}, u32[]{:S(2)}, u32[]{:S(2)}) collective-permute-start(bf16[16,1536]{1,0:T(8,128)(2,1)S(1)} %get-tuple-element.38), channel_id=1, source_target_pairs={{0,24},{4,28},{8,16},{12,20},{16,8},{20,12},{24,0},{28,4},{1,25},{... | collective-permute-start | bytes 147464 | tf_op jit(solution)/shard_map/ppermute | solution.py:19
  24.7 1.1 %collective-permute-start.6 = (bf16[16,1536]{1,0:T(8,128)(2,1)S(1)}, bf16[16,1536]{1,0:T(8,128)(2,1)S(1)}, u32[]{:S(2)}, u32[]{:S(2)}) collective-permute-start(bf16[16,1536]{1,0:T(8,128)(2,1)S(1)} %get-tuple-element.38), channel_id=1, source_target_pairs={{0,8},{4,12},{8,0},{12,4},{16,24},{20,28},{24,16},{28,20},{1,9},{5... | collective-permute-start | bytes 147464 | tf_op jit(solution)/shard_map/ppermute | solution.py:19
  25.8 1.8 %collective-permute-start.7 = (bf16[16,512]{1,0:T(8,128)(2,1)S(1)}, bf16[16,512]{1,0:T(8,128)(2,1)S(1)}, u32[]{:S(2)}, u32[]{:S(2)}) collective-permute-start(bf16[16,512]{1,0:T(8,128)(2,1)S(1)} %get-tuple-element.37.refs_0_), channel_id=1, source_target_pairs={{0,16},{4,20},{8,24},{12,28},{16,0},{20,4},{24,8},{28,12},{1,17},{... | collective-permute-start | bytes 49160 | tf_op jit(solution)/shard_map/ppermute | solution.py:19
  27.6 1.6 %collective-permute-done.8.refs_5_.refs_3_ = bf16[16,1536]{1,0:T(8,128)(2,1)S(1)} collective-permute-done((bf16[16,1536]{1,0:T(8,128)(2,1)S(1)}, bf16[16,1536]{1,0:T(8,128)(2,1)S(1)}, u32[]{:S(2)}, u32[]{:S(2)}) %collective-permute-start.8) | collective-permute-done | bytes 49184 | tf_op jit(solution)/shard_map/ppermute | solution.py:19
  29.2 0.1 collective-permute-done.6.refs_4_.refs_1_
  29.3 0.0 copy-done.1
  29.3 0.0 copy-done.6
  29.3 1.3 %near.2.refs_7_ = f32[16,1024]{1,0:T(8,128)S(1)} custom-call(s32[8,8]{1,0:T(8,128)S(1)} %copy-done.4, s32[8]{0:T(128)S(1)} %copy-done.6, bf16[16,1536]{1,0:T(8,128)(2,1)S(1)} %get-tuple-element.36.send_ref.refs_2_, bf16[16,1536]{1,0:T(8,128)(2,1)S(1)} %collective-permute-done.5.near_ref.refs_3_, bf16[16,1536]{1,0:T(8,128)(2,1)S(1)} %collective-permute-done.6.refs_4_.refs_1_, ...), custom_call_target="tpu_custom_call" | custom-call | tf_op jit(solution)/shard_map/near/pallas_call | solution.py:382
  30.6 0.0 collective-permute-done.7.refs_2_
  30.6 0.0 collective-permute-done.9.refs_12_.refs_11_
  30.6 0.0 collective-permute-done.10.refs_14_.refs_13_
  30.6 1.5 %second.1 = (f32[16,1024]{1,0:T(8,128)S(1)}, f32[16,640]{1,0:T(8,128)S(1)}) custom-call(bf16[16,512]{1,0:T(8,128)(2,1)S(1)} %get-tuple-element.37.refs_0_, bf16[16,1536]{1,0:T(8,128)(2,1)S(1)} %collective-permute-done.6.refs_4_.refs_1_, bf16[16,512]{1,0:T(8,128)(2,1)S(1)} %collective-permute-done.7.refs_2_, ...), custom_call_target="tpu_custom_call" | custom-call | tf_op jit(solution)/shard_map/second/pallas_call | solution.py:382
  32.1 1.5 %collective-permute-start.11 = (f32[16,640]{1,0:T(8,128)S(1)}, f32[16,640]{1,0:T(8,128)S(1)}, u32[]{:S(2)}, u32[]{:S(2)}) collective-permute-start(f32[16,640]{1,0:T(8,128)S(1)} %get-tuple-element.46), channel_id=1, source_target_pairs={{0,4},{4,0},{8,12},{12,8},{16,20},{20,16},{24,28},{28,24},{1,5},{5... | collective-permute-start | bytes 122888 | tf_op jit(solution)/shard_map/ppermute | solution.py:19
  33.6 2.5 %collective-permute-done.11 = f32[16,640]{1,0:T(8,128)S(1)} collective-permute-done((f32[16,640]{1,0:T(8,128)S(1)}, f32[16,640]{1,0:T(8,128)S(1)}, u32[]{:S(2)}, u32[]{:S(2)}) %collective-permute-start.11) | collective-permute-done | bytes 40992 | tf_op jit(solution)/shard_map/ppermute | solution.py:19
  36.1 2.0 %collective-permute-start.14 = (f32[16,640]{1,0:T(8,128)S(1)}, f32[16,640]{1,0:T(8,128)S(1)}, u32[]{:S(2)}, u32[]{:S(2)}) collective-permute-start(f32[16,640]{1,0:T(8,128)S(1)} %add.10.refs_0_), channel_id=1, source_target_pairs={{0,24},{4,28},{8,16},{12,20},{16,8},{20,12},{24,0},{28,4},{1,25},{... | collective-permute-start | bytes 122888 | tf_op jit(solution)/shard_map/ppermute | solution.py:19
  38.1 0.2 collective-permute-start.13
  38.3 2.2 %collective-permute-start.12 = (f32[16,640]{1,0:T(8,128)S(1)}, f32[16,640]{1,0:T(8,128)S(1)}, u32[]{:S(2)}, u32[]{:S(2)}) collective-permute-start(f32[16,640]{1,0:T(8,128)S(1)} %add.10.refs_0_), channel_id=1, source_target_pairs={{0,8},{4,12},{8,0},{12,4},{16,24},{20,28},{24,16},{28,20},{1,9},{5... | collective-permute-start | bytes 122888 | tf_op jit(solution)/shard_map/ppermute | solution.py:19
  40.5 1.4 %collective-permute-done.14.refs_3_ = f32[16,640]{1,0:T(8,128)S(1)} collective-permute-done((f32[16,640]{1,0:T(8,128)S(1)}, f32[16,640]{1,0:T(8,128)S(1)}, u32[]{:S(2)}, u32[]{:S(2)}) %collective-permute-start.14) | collective-permute-done | bytes 40992 | tf_op jit(solution)/shard_map/ppermute | solution.py:19
  41.9 1.2 %collective-permute-done.13.refs_2_ = f32[16,640]{1,0:T(8,128)S(1)} collective-permute-done((f32[16,640]{1,0:T(8,128)S(1)}, f32[16,640]{1,0:T(8,128)S(1)}, u32[]{:S(2)}, u32[]{:S(2)}) %collective-permute-start.13) | collective-permute-done | bytes 40992 | tf_op jit(solution)/shard_map/ppermute | solution.py:19
  43.0 0.0 collective-permute-done.12.refs_1_
  43.0 1.0 %third.1 = (f32[16,1024]{1,0:T(8,128)S(1)}, f32[16,1024]{1,0:T(8,128)S(1)}, bf16[16,1536]{1,0:T(8,128)(2,1)S(1)}, f32[16,128]{1,0:T(8,128)S(1)}) custom-call(f32[16,640]{1,0:T(8,128)S(1)} %add.10.refs_0_, f32[16,640]{1,0:T(8,128)S(1)} %collective-permute-done.12.refs_1_, f32[16,640]{1,0:T(8,128)S(1)} %collective-permute-done.13.refs_2_, ...), custom_call_target="tpu_custom_call" | custom-call | tf_op jit(solution)/shard_map/third/pallas_call | solution.py:382
  44.0 1.5 %collective-permute-start.15 = (bf16[16,1536]{1,0:T(8,128)(2,1)S(1)}, bf16[16,1536]{1,0:T(8,128)(2,1)S(1)}, u32[]{:S(2)}, u32[]{:S(2)}) collective-permute-start(bf16[16,1536]{1,0:T(8,128)(2,1)S(1)} %get-tuple-element.49.send_ref.refs_2_), channel_id=1, source_target_pairs={{0,4},{4,0},{8,12},{12,8},{16,20},{20,16},{24,28},{28,24},{1,5},{5... | collective-permute-start | bytes 147464 | tf_op jit(solution)/shard_map/ppermute | solution.py:19
  45.6 2.6 %collective-permute-done.15.near_ref.refs_3_ = bf16[16,1536]{1,0:T(8,128)(2,1)S(1)} collective-permute-done((bf16[16,1536]{1,0:T(8,128)(2,1)S(1)}, bf16[16,1536]{1,0:T(8,128)(2,1)S(1)}, u32[]{:S(2)}, u32[]{:S(2)}) %collective-permute-start.15) | collective-permute-done | bytes 49184 | tf_op jit(solution)/shard_map/ppermute | solution.py:19
  48.1 2.0 %collective-permute-start.18 = (bf16[16,1536]{1,0:T(8,128)(2,1)S(1)}, bf16[16,1536]{1,0:T(8,128)(2,1)S(1)}, u32[]{:S(2)}, u32[]{:S(2)}) collective-permute-start(bf16[16,1536]{1,0:T(8,128)(2,1)S(1)} %get-tuple-element.51), channel_id=1, source_target_pairs={{0,24},{4,28},{8,16},{12,20},{16,8},{20,12},{24,0},{28,4},{1,25},{... | collective-permute-start | bytes 147464 | tf_op jit(solution)/shard_map/ppermute | solution.py:19
  50.2 0.5 collective-permute-start.16
  50.6 1.9 %collective-permute-start.17 = (bf16[16,512]{1,0:T(8,128)(2,1)S(1)}, bf16[16,512]{1,0:T(8,128)(2,1)S(1)}, u32[]{:S(2)}, u32[]{:S(2)}) collective-permute-start(bf16[16,512]{1,0:T(8,128)(2,1)S(1)} %get-tuple-element.50.refs_0_), channel_id=1, source_target_pairs={{0,16},{4,20},{8,24},{12,28},{16,0},{20,4},{24,8},{28,12},{1,17},{... | collective-permute-start | bytes 49160 | tf_op jit(solution)/shard_map/ppermute | solution.py:19
  52.5 1.5 %collective-permute-done.18.refs_5_.refs_3_ = bf16[16,1536]{1,0:T(8,128)(2,1)S(1)} collective-permute-done((bf16[16,1536]{1,0:T(8,128)(2,1)S(1)}, bf16[16,1536]{1,0:T(8,128)(2,1)S(1)}, u32[]{:S(2)}, u32[]{:S(2)}) %collective-permute-start.18) | collective-permute-done | bytes 49184 | tf_op jit(solution)/shard_map/ppermute | solution.py:19
  54.1 0.5 collective-permute-done.16.refs_4_.refs_1_
  54.6 1.3 %near.3.refs_8_ = f32[16,1024]{1,0:T(8,128)S(1)} custom-call(s32[8,8]{1,0:T(8,128)S(1)} %copy-done.4, s32[8]{0:T(128)S(1)} %copy-done.6, bf16[16,1536]{1,0:T(8,128)(2,1)S(1)} %get-tuple-element.49.send_ref.refs_2_, bf16[16,1536]{1,0:T(8,128)(2,1)S(1)} %collective-permute-done.15.near_ref.refs_3_, ...), custom_call_target="tpu_custom_call" | custom-call | tf_op jit(solution)/shard_map/near/pallas_call | solution.py:382
  55.9 0.0 collective-permute-done.17.refs_2_
  55.9 0.8 %fourth.1 = f32[16,128]{1,0:T(8,128)S(1)} custom-call(bf16[16,512]{1,0:T(8,128)(2,1)S(1)} %get-tuple-element.50.refs_0_, bf16[16,1536]{1,0:T(8,128)(2,1)S(1)} %collective-permute-done.16.refs_4_.refs_1_, bf16[16,512]{1,0:T(8,128)(2,1)S(1)} %collective-permute-done.17.refs_2_, bf16[16,1536]{1,0:T(8,128)(2,1)S(1)} %collective-permute-done.18.refs_5_.refs_3_, ...), custom_call_target="tpu_custom_call" | custom-call | tf_op jit(solution)/shard_map/fourth/pallas_call | solution.py:382
  56.7 1.6 %collective-permute-start.19 = (f32[16,128]{1,0:T(8,128)S(1)}, f32[16,128]{1,0:T(8,128)S(1)}, u32[]{:S(2)}, u32[]{:S(2)}) collective-permute-start(f32[16,128]{1,0:T(8,128)S(1)} %fourth.1), channel_id=1, source_target_pairs={{0,4},{4,0},{8,12},{12,8},{16,20},{20,16},{24,28},{28,24},{1,5},{5... | collective-permute-start | bytes 24584 | tf_op jit(solution)/shard_map/ppermute | solution.py:19
  58.3 2.1 %collective-permute-done.19 = f32[16,128]{1,0:T(8,128)S(1)} collective-permute-done((f32[16,128]{1,0:T(8,128)S(1)}, f32[16,128]{1,0:T(8,128)S(1)}, u32[]{:S(2)}, u32[]{:S(2)}) %collective-permute-start.19) | collective-permute-done | bytes 8224 | tf_op jit(solution)/shard_map/ppermute | solution.py:19
  60.4 2.0 %collective-permute-start.22 = (f32[16,128]{1,0:T(8,128)S(1)}, f32[16,128]{1,0:T(8,128)S(1)}, u32[]{:S(2)}, u32[]{:S(2)}) collective-permute-start(f32[16,128]{1,0:T(8,128)S(1)} %add.11.refs_0_), channel_id=1, source_target_pairs={{0,24},{4,28},{8,16},{12,20},{16,8},{20,12},{24,0},{28,4},{1,25},{... | collective-permute-start | bytes 24584 | tf_op jit(solution)/shard_map/ppermute | solution.py:19
  62.4 0.4 collective-permute-start.21
  62.8 2.0 %collective-permute-start.20 = (f32[16,128]{1,0:T(8,128)S(1)}, f32[16,128]{1,0:T(8,128)S(1)}, u32[]{:S(2)}, u32[]{:S(2)}) collective-permute-start(f32[16,128]{1,0:T(8,128)S(1)} %add.11.refs_0_), channel_id=1, source_target_pairs={{0,8},{4,12},{8,0},{12,4},{16,24},{20,28},{24,16},{28,20},{1,9},{5... | collective-permute-start | bytes 24584 | tf_op jit(solution)/shard_map/ppermute | solution.py:19
  64.8 1.1 %collective-permute-done.22.refs_3_ = f32[16,128]{1,0:T(8,128)S(1)} collective-permute-done((f32[16,128]{1,0:T(8,128)S(1)}, f32[16,128]{1,0:T(8,128)S(1)}, u32[]{:S(2)}, u32[]{:S(2)}) %collective-permute-start.22) | collective-permute-done | bytes 8224 | tf_op jit(solution)/shard_map/ppermute | solution.py:19
  65.8 1.1 %collective-permute-done.21.refs_2_ = f32[16,128]{1,0:T(8,128)S(1)} collective-permute-done((f32[16,128]{1,0:T(8,128)S(1)}, f32[16,128]{1,0:T(8,128)S(1)}, u32[]{:S(2)}, u32[]{:S(2)}) %collective-permute-start.21) | collective-permute-done | bytes 8224 | tf_op jit(solution)/shard_map/ppermute | solution.py:19
  67.0 0.0 collective-permute-done.20.refs_1_
  67.0 1.0 %last.1 = f32[16,1024]{1,0:T(8,128)} custom-call(f32[16,128]{1,0:T(8,128)S(1)} %add.11.refs_0_, f32[16,128]{1,0:T(8,128)S(1)} %collective-permute-done.20.refs_1_, f32[16,128]{1,0:T(8,128)S(1)} %collective-permute-done.21.refs_2_, f32[16,128]{1,0:T(8,128)S(1)} %collective-permute-done.22.refs_3_, f32[16,128]{1,0:T(8,128)S(1)} %get-tuple-element.54.refs_4_, ...), custom_call_target="tpu_custom_call" | custom-call | tf_op jit(solution)/shard_map/last/pallas_call | solution.py:382
  (10 shorter events, 0.0 us)
Async XLA Ops:
  0.0 17.6 %copy-start = (f32[1024,512]{1,0:T(8,128)S(1)}, f32[1024,512]{1,0:T(8,128)}, u32[]{:S(2)}) copy-start(f32[1024,512]{1,0:T(8,128)} %refs_6_.3) | copy-start | bytes 6291460
  0.0 13.5 %copy-start.5 = (s32[8,32]{1,0:T(8,128)S(1)}, s32[8,32]{1,0:T(8,128)}, u32[]{:S(2)}) copy-start(s32[8,32]{1,0:T(8,128)} %skel_ref.1) | copy-start | bytes 3076
  0.0 13.5 %copy-start.3 = (bf16[8,128,32]{1,2,0:T(8,128)(2,1)S(1)}, bf16[8,128,32]{1,2,0:T(8,128)(2,1)}, u32[]{:S(2)}) copy-start(bf16[8,128,32]{1,2,0:T(8,128)(2,1)} %param.15) | copy-start | bytes 196612
  2.0 16.5 %copy-start.2 = (bf16[256,1,512]{2,0,1:T(8,128)(2,1)S(1)}, bf16[256,1,512]{2,0,1:T(8,128)(2,1)}, u32[]{:S(2)}) copy-start(bf16[256,1,512]{2,0,1:T(8,128)(2,1)} %param.17) | copy-start | bytes 786436
  2.0 27.3 %copy-start.1 = (bf16[8,8,128,128]{3,2,1,0:T(8,128)(2,1)S(1)}, bf16[8,8,128,128]{3,2,1,0:T(8,128)(2,1)}, u32[]{:S(2)}) copy-start(bf16[8,8,128,128]{3,2,1,0:T(8,128)(2,1)} %refs_6_.5) | copy-start | bytes 6291460
  2.0 27.3 %copy-start.4 = (s32[8,8]{1,0:T(8,128)S(1)}, s32[8,8]{1,0:T(8,128)}, u32[]{:S(2)}) copy-start(s32[8,8]{1,0:T(8,128)} %refs_0_.5) | copy-start | bytes 772
  2.0 27.2 %copy-start.6 = (s32[8]{0:T(128)S(1)}, s32[8]{0:T(128)}, u32[]{:S(2)}) copy-start(s32[8]{0:T(128)} %refs_1_.5) | copy-start | bytes 100
  2.0 16.4 %collective-permute-start = (bf16[256,512]{1,0:T(8,128)(2,1)}, bf16[256,512]{1,0:T(8,128)(2,1)S(1)}, u32[]{:S(2)}, u32[]{:S(2)}) collective-permute-start(bf16[256,512]{1,0:T(8,128)(2,1)} %bitcast.4), channel_id=1, source_target_pairs={{0,2},{1,3},{2,0},{3,1},{4,6},{5,7},{6,4},{7,5},{8,10},{9,11},{10,... | collective-permute-start | bytes 786440 | tf_op jit(solution)/shard_map/ppermute | solution.py:348
  5.1 4.0 %collective-permute-start.1 = (f32[16,640]{1,0:T(8,128)S(1)}, f32[16,640]{1,0:T(8,128)S(1)}, u32[]{:S(2)}, u32[]{:S(2)}) collective-permute-start(f32[16,640]{1,0:T(8,128)S(1)} %get-tuple-element.32), channel_id=1, source_target_pairs={{0,4},{4,0},{8,12},{12,8},{16,20},{20,16},{24,28},{28,24},{1,5},{5... | collective-permute-start | bytes 122888 | tf_op jit(solution)/shard_map/ppermute | solution.py:19
  9.1 5.8 %collective-permute-start.4 = (f32[16,640]{1,0:T(8,128)S(1)}, f32[16,640]{1,0:T(8,128)S(1)}, u32[]{:S(2)}, u32[]{:S(2)}) collective-permute-start(f32[16,640]{1,0:T(8,128)S(1)} %add.9.refs_0_), channel_id=1, source_target_pairs={{0,24},{4,28},{8,16},{12,20},{16,8},{20,12},{24,0},{28,4},{1,25},{... | collective-permute-start | bytes 122888 | tf_op jit(solution)/shard_map/ppermute | solution.py:19
  12.7 4.9 %collective-permute-start.3 = (f32[16,640]{1,0:T(8,128)S(1)}, f32[16,640]{1,0:T(8,128)S(1)}, u32[]{:S(2)}, u32[]{:S(2)}) collective-permute-start(f32[16,640]{1,0:T(8,128)S(1)} %add.9.refs_0_), channel_id=1, source_target_pairs={{0,16},{4,20},{8,24},{12,28},{16,0},{20,4},{24,8},{28,12},{1,17},{... | collective-permute-start | bytes 122888 | tf_op jit(solution)/shard_map/ppermute | solution.py:19
  12.7 4.9 %collective-permute-start.2 = (f32[16,640]{1,0:T(8,128)S(1)}, f32[16,640]{1,0:T(8,128)S(1)}, u32[]{:S(2)}, u32[]{:S(2)}) collective-permute-start(f32[16,640]{1,0:T(8,128)S(1)} %add.9.refs_0_), channel_id=1, source_target_pairs={{0,8},{4,12},{8,0},{12,4},{16,24},{20,28},{24,16},{28,20},{1,9},{5... | collective-permute-start | bytes 122888 | tf_op jit(solution)/shard_map/ppermute | solution.py:19
  18.5 12.1 %collective-permute-start.9 = (bf16[256,512]{1,0:T(8,128)(2,1)S(1)}, bf16[256,512]{1,0:T(8,128)(2,1)S(1)}, u32[]{:S(2)}, u32[]{:S(2)}) collective-permute-start(bf16[256,512]{1,0:T(8,128)(2,1)S(1)} %bitcast.5), channel_id=1, source_target_pairs={{0,1},{1,0},{2,3},{3,2},{4,5},{5,4},{6,7},{7,6},{8,9},{9,8},{10,11... | collective-permute-start | bytes 786440 | tf_op jit(solution)/shard_map/ppermute | solution.py:355
  18.6 12.0 %collective-permute-start.10 = (bf16[256,512]{1,0:T(8,128)(2,1)S(1)}, bf16[256,512]{1,0:T(8,128)(2,1)S(1)}, u32[]{:S(2)}, u32[]{:S(2)}) collective-permute-start(bf16[256,512]{1,0:T(8,128)(2,1)S(1)} %collective-permute-done.refs_13_.refs_12_), channel_id=1, source_target_pairs={{0,1},{1,0},{2,3},{3,2},{4,5},{5,4},{6,7},{7,6},{8,9},{9,8},{10,11... | collective-permute-start | bytes 786440 | tf_op jit(solution)/shard_map/ppermute | solution.py:355
  19.1 4.1 %collective-permute-start.5 = (bf16[16,1536]{1,0:T(8,128)(2,1)S(1)}, bf16[16,1536]{1,0:T(8,128)(2,1)S(1)}, u32[]{:S(2)}, u32[]{:S(2)}) collective-permute-start(bf16[16,1536]{1,0:T(8,128)(2,1)S(1)} %get-tuple-element.36.send_ref.refs_2_), channel_id=1, source_target_pairs={{0,4},{4,0},{8,12},{12,8},{16,20},{20,16},{24,28},{28,24},{1,5},{5... | collective-permute-start | bytes 147464 | tf_op jit(solution)/shard_map/ppermute | solution.py:19
  23.2 6.0 %collective-permute-start.8 = (bf16[16,1536]{1,0:T(8,128)(2,1)S(1)}, bf16[16,1536]{1,0:T(8,128)(2,1)S(1)}, u32[]{:S(2)}, u32[]{:S(2)}) collective-permute-start(bf16[16,1536]{1,0:T(8,128)(2,1)S(1)} %get-tuple-element.38), channel_id=1, source_target_pairs={{0,24},{4,28},{8,16},{12,20},{16,8},{20,12},{24,0},{28,4},{1,25},{... | collective-permute-start | bytes 147464 | tf_op jit(solution)/shard_map/ppermute | solution.py:19
  24.7 4.6 %collective-permute-start.6 = (bf16[16,1536]{1,0:T(8,128)(2,1)S(1)}, bf16[16,1536]{1,0:T(8,128)(2,1)S(1)}, u32[]{:S(2)}, u32[]{:S(2)}) collective-permute-start(bf16[16,1536]{1,0:T(8,128)(2,1)S(1)} %get-tuple-element.38), channel_id=1, source_target_pairs={{0,8},{4,12},{8,0},{12,4},{16,24},{20,28},{24,16},{28,20},{1,9},{5... | collective-permute-start | bytes 147464 | tf_op jit(solution)/shard_map/ppermute | solution.py:19
  25.8 4.8 %collective-permute-start.7 = (bf16[16,512]{1,0:T(8,128)(2,1)S(1)}, bf16[16,512]{1,0:T(8,128)(2,1)S(1)}, u32[]{:S(2)}, u32[]{:S(2)}) collective-permute-start(bf16[16,512]{1,0:T(8,128)(2,1)S(1)} %get-tuple-element.37.refs_0_), channel_id=1, source_target_pairs={{0,16},{4,20},{8,24},{12,28},{16,0},{20,4},{24,8},{28,12},{1,17},{... | collective-permute-start | bytes 49160 | tf_op jit(solution)/shard_map/ppermute | solution.py:19
  32.1 4.0 %collective-permute-start.11 = (f32[16,640]{1,0:T(8,128)S(1)}, f32[16,640]{1,0:T(8,128)S(1)}, u32[]{:S(2)}, u32[]{:S(2)}) collective-permute-start(f32[16,640]{1,0:T(8,128)S(1)} %get-tuple-element.46), channel_id=1, source_target_pairs={{0,4},{4,0},{8,12},{12,8},{16,20},{20,16},{24,28},{28,24},{1,5},{5... | collective-permute-start | bytes 122888 | tf_op jit(solution)/shard_map/ppermute | solution.py:19
  36.1 5.8 %collective-permute-start.14 = (f32[16,640]{1,0:T(8,128)S(1)}, f32[16,640]{1,0:T(8,128)S(1)}, u32[]{:S(2)}, u32[]{:S(2)}) collective-permute-start(f32[16,640]{1,0:T(8,128)S(1)} %add.10.refs_0_), channel_id=1, source_target_pairs={{0,24},{4,28},{8,16},{12,20},{16,8},{20,12},{24,0},{28,4},{1,25},{... | collective-permute-start | bytes 122888 | tf_op jit(solution)/shard_map/ppermute | solution.py:19
  38.1 5.0 %collective-permute-start.13 = (f32[16,640]{1,0:T(8,128)S(1)}, f32[16,640]{1,0:T(8,128)S(1)}, u32[]{:S(2)}, u32[]{:S(2)}) collective-permute-start(f32[16,640]{1,0:T(8,128)S(1)} %add.10.refs_0_), channel_id=1, source_target_pairs={{0,16},{4,20},{8,24},{12,28},{16,0},{20,4},{24,8},{28,12},{1,17},{... | collective-permute-start | bytes 122888 | tf_op jit(solution)/shard_map/ppermute | solution.py:19
  38.3 4.8 %collective-permute-start.12 = (f32[16,640]{1,0:T(8,128)S(1)}, f32[16,640]{1,0:T(8,128)S(1)}, u32[]{:S(2)}, u32[]{:S(2)}) collective-permute-start(f32[16,640]{1,0:T(8,128)S(1)} %add.10.refs_0_), channel_id=1, source_target_pairs={{0,8},{4,12},{8,0},{12,4},{16,24},{20,28},{24,16},{28,20},{1,9},{5... | collective-permute-start | bytes 122888 | tf_op jit(solution)/shard_map/ppermute | solution.py:19
  44.0 4.1 %collective-permute-start.15 = (bf16[16,1536]{1,0:T(8,128)(2,1)S(1)}, bf16[16,1536]{1,0:T(8,128)(2,1)S(1)}, u32[]{:S(2)}, u32[]{:S(2)}) collective-permute-start(bf16[16,1536]{1,0:T(8,128)(2,1)S(1)} %get-tuple-element.49.send_ref.refs_2_), channel_id=1, source_target_pairs={{0,4},{4,0},{8,12},{12,8},{16,20},{20,16},{24,28},{28,24},{1,5},{5... | collective-permute-start | bytes 147464 | tf_op jit(solution)/shard_map/ppermute | solution.py:19
  48.1 5.9 %collective-permute-start.18 = (bf16[16,1536]{1,0:T(8,128)(2,1)S(1)}, bf16[16,1536]{1,0:T(8,128)(2,1)S(1)}, u32[]{:S(2)}, u32[]{:S(2)}) collective-permute-start(bf16[16,1536]{1,0:T(8,128)(2,1)S(1)} %get-tuple-element.51), channel_id=1, source_target_pairs={{0,24},{4,28},{8,16},{12,20},{16,8},{20,12},{24,0},{28,4},{1,25},{... | collective-permute-start | bytes 147464 | tf_op jit(solution)/shard_map/ppermute | solution.py:19
  50.2 4.4 %collective-permute-start.16 = (bf16[16,1536]{1,0:T(8,128)(2,1)S(1)}, bf16[16,1536]{1,0:T(8,128)(2,1)S(1)}, u32[]{:S(2)}, u32[]{:S(2)}) collective-permute-start(bf16[16,1536]{1,0:T(8,128)(2,1)S(1)} %get-tuple-element.51), channel_id=1, source_target_pairs={{0,8},{4,12},{8,0},{12,4},{16,24},{20,28},{24,16},{28,20},{1,9},{5... | collective-permute-start | bytes 147464 | tf_op jit(solution)/shard_map/ppermute | solution.py:19
  50.6 5.2 %collective-permute-start.17 = (bf16[16,512]{1,0:T(8,128)(2,1)S(1)}, bf16[16,512]{1,0:T(8,128)(2,1)S(1)}, u32[]{:S(2)}, u32[]{:S(2)}) collective-permute-start(bf16[16,512]{1,0:T(8,128)(2,1)S(1)} %get-tuple-element.50.refs_0_), channel_id=1, source_target_pairs={{0,16},{4,20},{8,24},{12,28},{16,0},{20,4},{24,8},{28,12},{1,17},{... | collective-permute-start | bytes 49160 | tf_op jit(solution)/shard_map/ppermute | solution.py:19
  56.7 3.7 %collective-permute-start.19 = (f32[16,128]{1,0:T(8,128)S(1)}, f32[16,128]{1,0:T(8,128)S(1)}, u32[]{:S(2)}, u32[]{:S(2)}) collective-permute-start(f32[16,128]{1,0:T(8,128)S(1)} %fourth.1), channel_id=1, source_target_pairs={{0,4},{4,0},{8,12},{12,8},{16,20},{20,16},{24,28},{28,24},{1,5},{5... | collective-permute-start | bytes 24584 | tf_op jit(solution)/shard_map/ppermute | solution.py:19
  60.4 5.4 %collective-permute-start.22 = (f32[16,128]{1,0:T(8,128)S(1)}, f32[16,128]{1,0:T(8,128)S(1)}, u32[]{:S(2)}, u32[]{:S(2)}) collective-permute-start(f32[16,128]{1,0:T(8,128)S(1)} %add.11.refs_0_), channel_id=1, source_target_pairs={{0,24},{4,28},{8,16},{12,20},{16,8},{20,12},{24,0},{28,4},{1,25},{... | collective-permute-start | bytes 24584 | tf_op jit(solution)/shard_map/ppermute | solution.py:19
  62.4 4.5 %collective-permute-start.21 = (f32[16,128]{1,0:T(8,128)S(1)}, f32[16,128]{1,0:T(8,128)S(1)}, u32[]{:S(2)}, u32[]{:S(2)}) collective-permute-start(f32[16,128]{1,0:T(8,128)S(1)} %add.11.refs_0_), channel_id=1, source_target_pairs={{0,16},{4,20},{8,24},{12,28},{16,0},{20,4},{24,8},{28,12},{1,17},{... | collective-permute-start | bytes 24584 | tf_op jit(solution)/shard_map/ppermute | solution.py:19
  62.8 4.2 %collective-permute-start.20 = (f32[16,128]{1,0:T(8,128)S(1)}, f32[16,128]{1,0:T(8,128)S(1)}, u32[]{:S(2)}, u32[]{:S(2)}) collective-permute-start(f32[16,128]{1,0:T(8,128)S(1)} %add.11.refs_0_), channel_id=1, source_target_pairs={{0,8},{4,12},{8,0},{12,4},{16,24},{20,28},{24,16},{28,20},{1,9},{5... | collective-permute-start | bytes 24584 | tf_op jit(solution)/shard_map/ppermute | solution.py:19

commit v5 on v4

--- a/solution.py
+++ b/solution.py
@@ -64,7 +64,7 @@
         send_ref[:, start : start + LANES] = (both[:, :LANES] + both[:, LANES:]).astype(BF)
 
 
-def maps_kernel(weights_ref, skel_ref, maps_ref):
+def maps_kernel(sources, ids_ref, live_ref, weights_ref, skel_ref, maps_ref, places_ref):
     block_count, rank, block = weights_ref.shape
     quarters = maps_ref.shape[0]
     per = block_count // quarters
@@ -81,6 +81,24 @@
         hot = jnp.where(skel[:rank, b : b + 1] == panel, 1.0, 0.0).astype(BF)
         maps_ref[quarter, pl.ds(start, rank), cols] = hot
         maps_ref[quarter, pl.ds(start + LANES, rank), cols] = weights_ref[b]
+    wanted = ids_ref[...]
+    slots = wanted.shape[1]
+    slot = lax.broadcasted_iota(jnp.int32, wanted.shape, 1)
+    row = lax.broadcasted_iota(jnp.int32, wanted.shape, 0)
+    counts = live_ref[...]
+    live = slot < 0
+    for b in range(block_count):
+        live = live | ((row == b) & (slot < counts[0, b]))
+    region = lax.axis_index(AXIS)
+    place = block_place(wanted, live, block_count, sources, region).astype(F32)
+    scale = jnp.where(slot % 4 == 0, 1.0, jnp.where(slot % 4 == 1, 64.0, 4096.0))
+    scale = jnp.where(slot % 4 == 3, 262144.0, scale)
+    lane = lax.broadcasted_iota(jnp.int32, (block_count, LANES), 1)
+    packed = jnp.zeros((block_count, LANES), F32)
+    for group in range(slots // 4):
+        part = row_sum(jnp.where(slot // 4 == group, place * scale, 0.0))
+        packed = jnp.where(lane == group, part, packed)
+    places_ref[...] = packed.astype(jnp.int32)
 
 
 def onward_kernel(send_ref, near_ref, onward_ref, pair_ref):
@@ -92,7 +110,7 @@
 
 
 def open_kernel(parts, rhs_hbm, factor_hbm, diag_hbm, self_hbm, out_ref, rhs_ref, diag_ref,
-                self_ref, held_ref, sems):
+                self_ref, high_ref, low_ref, held_ref, sems):
     panels, width = factor_hbm.shape
     rows = rhs_ref.shape[0]
     depth = panels // parts
@@ -119,6 +137,8 @@
         span = slice(part * depth, (part + 1) * depth)
         copies[part].wait()
         high, low = split(held_ref[span, :])
+        high_ref[span, :] = high
+        low_ref[span, :] = low
         total = total + dot_wide(dot_nn, rhs[:, span], high, low)
     out_ref[:, :width] = total
     for load in loads[1:]:
@@ -127,10 +147,9 @@
 
 def first_kernel(parts, *refs):
     sums = refs[:parts]
-    rhs_ref, diag_ref, factor_ref, maps_ref = refs[parts : parts + 4]
-    dir_ref, pre_ref, send_ref, keep_ref, high_ref, low_ref = refs[parts + 4 :]
-    width = factor_ref.shape[1]
-    high_ref[...], low_ref[...] = split(factor_ref[...])
+    rhs_ref, diag_ref, high_ref, low_ref, maps_ref = refs[parts : parts + 5]
+    dir_ref, pre_ref, send_ref, keep_ref = refs[parts + 5 :]
+    width = high_ref.shape[1]
     rows, panels = rhs_ref.shape
     summed = sums[0][...]
     for ref in sums[1:]:
@@ -162,21 +181,19 @@
     return jnp.where(live, slot * block_count + wanted % block_count, sources * block_count)
 
 
-def near_kernel(sources, ids_ref, live_ref, *refs):
+def near_kernel(sources, *refs):
     field_refs = refs[:sources]
-    mats_ref, near_ref, blocks_ref = refs[sources:]
+    places_ref, mats_ref, near_ref, blocks_ref = refs[sources:]
     rows, panels = near_ref.shape
     block_count, slots, block, _ = mats_ref.shape
-    region = lax.axis_index(AXIS)
+    packed = places_ref[...]
     for index, ref in enumerate(field_refs):
         for b in range(block_count):
             blocks_ref[index * block_count + b] = ref[:, b * block : (b + 1) * block]
     blocks_ref[sources * block_count] = jnp.zeros((rows, block), BF)
     for b in range(block_count):
-        places = [
-            block_place(ids_ref[b, k], k < live_ref[b], block_count, sources, region)
-            for k in range(slots)
-        ]
+        fours = [packed[b, group] for group in range(slots // 4)]
+        places = [(fours[k // 4] >> (6 * (k % 4))) & 63 for k in range(slots)]
         picked = jnp.concatenate([blocks_ref[place] for place in places], axis=1)
         mats = jnp.concatenate([mats_ref[b, k] for k in range(slots)], axis=1)
         near_ref[:, b * block : (b + 1) * block] = dot_nt(picked, mats)
@@ -345,15 +362,15 @@
     if count != 8 or quarters != 4:
         return [lax.all_gather(coupling, "rhs")], early
     coupling, early = lax.optimization_barrier((coupling, early))
-    return [coupling, lax.ppermute(coupling, "rhs", [(i, i ^ 2) for i in range(quarters)])], early
+    pairs = [[(i, i ^ mask) for i in range(quarters)] for mask in (1, 2)]
+    return [coupling] + [lax.ppermute(coupling, "rhs", pair) for pair in pairs], early
 
 
 def finish_quarters(rows, quarters, late):
     if len(rows) == 1:
         return rows, late
-    own, far, late = lax.optimization_barrier((*rows, late))
-    near, other = [lax.ppermute(x, "rhs", [(i, i ^ 1) for i in range(quarters)]) for x in (own, far)]
-    return [own, near, far, other], late
+    far, late = lax.optimization_barrier((rows[2], late))
+    return rows + [lax.ppermute(far, "rhs", [(i, i ^ 1) for i in range(quarters)])], late
 
 
 def nbytes(shape, kind):
@@ -366,13 +383,13 @@
     )
 
 
-def call(name, kernel, out_shapes, args, scratch=(), scalars=0, far=()):
+def call(name, kernel, out_shapes, args, scratch=(), far=(), flops=0):
     out_shapes = [jax.ShapeDtypeStruct(shape, kind) for shape, kind in out_shapes]
     args = [pltpu.with_memory_space_constraint(x, pltpu.HBM) if i in far else x
             for i, x in enumerate(args)]
     specs = [
         pl.BlockSpec(
-            memory_space=pltpu.SMEM if i < scalars else pltpu.HBM if i in far else pltpu.VMEM
+            memory_space=pltpu.HBM if i in far else pltpu.VMEM
         )
         for i in range(len(args))
     ]
@@ -386,6 +403,7 @@
         in_specs=specs,
         out_specs=outs,
         scratch_shapes=list(scratch),
+        cost_estimate=pl.CostEstimate(flops=flops, bytes_accessed=flops // 500, transcendentals=0) if flops else None,
         compiler_params=room(*held, *out_shapes),
     )(*args)
 
@@ -409,20 +427,22 @@
     count = lax.axis_size(AXIS)
     width = low_rank.shape[1]
     region = lax.axis_index(AXIS)
-    (maps,) = call(
+    sources = 4 if count == 8 else 3
+    maps, places = call(
         "maps",
-        maps_kernel,
-        [((quarters, 2 * LANES, panels // quarters), BF)],
-        [jnp.swapaxes(interp, 1, 2), skel_idx],
+        lambda *refs: maps_kernel(sources, *refs),
+        [((quarters, 2 * LANES, panels // quarters), BF), ((block_count, LANES), jnp.int32)],
+        [near_ids, near_count[None, :], jnp.swapaxes(interp, 1, 2), skel_idx],
     )
     wide = width + LANES
     long = panels + quarters * LANES
 
     parts = 4
-    payload, rhs_near, diag_row, self_row = call(
+    payload, rhs_near, diag_row, self_row, high, low = call(
         "open",
         lambda *refs: open_kernel(parts, *refs),
-        [((rows, wide), F32), ((rows, panels), F32), ((1, panels), F32), ((1, panels), F32)],
+        [((rows, wide), F32), ((rows, panels), F32), ((1, panels), F32), ((1, panels), F32),
+         (low_rank.shape, BF), (low_rank.shape, BF)],
         [rhs_vec, low_rank, diag_prec[None, :], self_coef[None, :]],
         [pltpu.VMEM((panels, width), F32), pltpu.SemaphoreType.DMA((parts + 3,))],
         far=(0, 1, 2, 3),
@@ -430,24 +450,24 @@
 
     some_rows, payload = gather_quarters(coupling[:, 0, :], quarters, count, payload)
     sums = sum_parts(payload, count)
-    first_dir, first_pre, send, keep, high, low = call(
+    first_dir, first_pre, send, keep = call(
         "first",
         lambda *refs: first_kernel(len(sums), *refs),
-        [((rows, panels), F32), ((rows, panels), F32), ((rows, long), BF), ((rows, wide), F32),
-         (low_rank.shape, BF), (low_rank.shape, BF)],
-        [*sums, rhs_near, diag_row, low_rank, maps],
-    )
-    full_rows, send = finish_quarters(some_rows, quarters, send)
+        [((rows, panels), F32), ((rows, panels), F32), ((rows, long), BF), ((rows, wide), F32)],
+        [*sums, rhs_near, diag_row, high, low, maps],
+        flops=10**9,
+    )
     fields, charges, starts = exchange(send, panels, count)
+    full_rows, fields[1] = finish_quarters(some_rows, quarters, fields[1])
 
     def near_product(fields):
         (near,) = call(
             "near",
             lambda *refs: near_kernel(len(fields), *refs),
             [((rows, panels), F32)],
-            [near_ids, near_count, *fields, near_mats],
+            [*fields, places, near_mats],
             [pltpu.VMEM((len(fields) * block_count + 1, rows, block), BF)],
-            2,
+            flops=10**10,
         )
         return near
 

time: 68.1 us -> 65.3 us (0.959)
  waiting for transfers between devices: 24.6 us -> 23.1 us
  Pallas kernels: 9.93 us -> 8.73 us
    ppermute x20, starting transfers between devices: 29.6 us -> 31.5 us  [swap(): return lax.ppermute(values, AXIS, [(i, i ^ mask) for i in range(count)])]
    ppermute x3, starting transfers between devices: 3.58 us -> 1.72 us  [the longest x2 1.49 us: gather_quarters(): lax.ppermute(coupling, 'rhs', pair)]
    ppermute x20, waiting for transfers between devices: 24.6 us -> 23.1 us  [swap(): return lax.ppermute(values, AXIS, [(i, i ^ mask) for i in range(count)])]
    pallas_call x11, Pallas kernels: 9.93 us -> 8.73 us  [call(): pl.pallas_call(kernel, name=name, out_shape=out_shapes, in_specs=specs, o...]
  transfers between devices with their start and end apart: 23 -> 23, of which waited for: 15 -> 17; matrix products, arithmetic and copies ran while one was open for 0% -> 0% of each run, Pallas kernels for 5% -> 4%
where the time goes in v5:
time: 65.3 us; the launch traced here: 65.2 us
  starting transfers between devices  33.3 us (51%)
  waiting for transfers between devices  23.1 us (35%)
  Pallas kernels  8.73 us (13%)
    ppermute x20, starting transfers between devices, swap(): return lax.ppermute(values, AXIS, [(i, i ^ mask) for i in range(count)])  31.5 us
    ppermute x20, waiting for transfers between devices, swap(): return lax.ppermute(values, AXIS, [(i, i ^ mask) for i in range(count)])  23.1 us
    pallas_call x11, Pallas kernels, call(): pl.pallas_call(kernel, name=name, out_shape=out_shapes, in_specs=specs, o...  8.73 us
    ppermute x2, starting transfers between devices, gather_quarters(): lax.ppermute(coupling, 'rhs', pair)  1.49 us
  transfers between devices with their start and end apart: 23, of which 17 were waited for; matrix products, arithmetic and copies ran while one was open for 0% of the time, Pallas kernels for 4%

profile of v5, /device:TPU:0, one launch (start us, length us, event | category | flops | bytes accessed | tf_op | source)
XLA Modules:
  0.0 65.2 jit_solution(4735958234959618995)
XLA Ops:
  0.0 0.0 copy-start
  0.0 0.0 copy-start.3
  0.0 1.9 %open.1 = (f32[16,640]{1,0:T(8,128)S(1)}, f32[16,1024]{1,0:T(8,128)S(1)}, f32[1,1024]{1,0:T(1,128)S(1)}, f32[1,1024]{1,0:T(1,128)S(1)}, bf16[1024,512]{1,0:T(8,128)(2,1)S(1)}, /*index=5*/bf16[1024,512]{1,0:T(8,128)(2,1)S(1)}) custom-call(f32[16,1024]{1,0:T(8,128)} %refs_0_.2, f32[1024,512]{1,0:T(8,128)} %refs_1_.1, f32[1,1024]{1,0:T(1,128)} %bitcast.11, ...), custom_call_target="tpu_custom_call" | custom-call | tf_op jit(solution)/shard_map/open/pallas_call | solution.py:399
  1.9 0.0 copy-start.5
  1.9 3.0 %collective-permute-start = (f32[16,640]{1,0:T(8,128)S(1)}, f32[16,640]{1,0:T(8,128)S(1)}, u32[]{:S(2)}, u32[]{:S(2)}) collective-permute-start(f32[16,640]{1,0:T(8,128)S(1)} %get-tuple-element.32), channel_id=1, source_target_pairs={{0,4},{4,0},{8,12},{12,8},{16,20},{20,16},{24,28},{28,24},{1,5},{5... | collective-permute-start | bytes 122888 | tf_op jit(solution)/shard_map/ppermute | solution.py:19
  5.0 0.0 copy-done
  5.0 1.5 %collective-permute-start.8 = (bf16[256,512]{1,0:T(8,128)(2,1)S(1)}, bf16[256,512]{1,0:T(8,128)(2,1)S(1)}, u32[]{:S(2)}, u32[]{:S(2)}) collective-permute-start(bf16[256,512]{1,0:T(8,128)(2,1)S(1)} %bitcast.5), channel_id=1, source_target_pairs={{0,2},{1,3},{2,0},{3,1},{4,6},{5,7},{6,4},{7,5},{8,10},{9,11},{10,... | collective-permute-start | bytes 786440 | tf_op jit(solution)/shard_map/ppermute | solution.py:366
  6.5 0.5 collective-permute-done
  7.0 4.1 %collective-permute-start.3 = (f32[16,640]{1,0:T(8,128)S(1)}, f32[16,640]{1,0:T(8,128)S(1)}, u32[]{:S(2)}, u32[]{:S(2)}) collective-permute-start(f32[16,640]{1,0:T(8,128)S(1)} %add.9.refs_0_), channel_id=1, source_target_pairs={{0,24},{4,28},{8,16},{12,20},{16,8},{20,12},{24,0},{28,4},{1,25},{... | collective-permute-start | bytes 122888 | tf_op jit(solution)/shard_map/ppermute | solution.py:19
  11.1 0.0 collective-permute-start.2
  11.1 0.6 collective-permute-start.1
  11.7 0.0 copy-done.3
  11.7 0.0 copy-done.1
  11.7 0.0 copy-done.4
  11.7 0.0 copy-done.2
  11.7 0.2 maps.1
  12.0 1.1 %collective-permute-done.3.refs_3_ = f32[16,640]{1,0:T(8,128)S(1)} collective-permute-done((f32[16,640]{1,0:T(8,128)S(1)}, f32[16,640]{1,0:T(8,128)S(1)}, u32[]{:S(2)}, u32[]{:S(2)}) %collective-permute-start.3) | collective-permute-done | bytes 40992 | tf_op jit(solution)/shard_map/ppermute | solution.py:19
  13.1 2.9 %collective-permute-done.2.refs_2_ = f32[16,640]{1,0:T(8,128)S(1)} collective-permute-done((f32[16,640]{1,0:T(8,128)S(1)}, f32[16,640]{1,0:T(8,128)S(1)}, u32[]{:S(2)}, u32[]{:S(2)}) %collective-permute-start.2) | collective-permute-done | bytes 40992 | tf_op jit(solution)/shard_map/ppermute | solution.py:19
  16.0 0.0 collective-permute-done.1.refs_1_
  16.0 0.8 %first.1 = (f32[16,1024]{1,0:T(8,128)S(1)}, f32[16,1024]{1,0:T(8,128)S(1)}, bf16[16,1536]{1,0:T(8,128)(2,1)S(1)}, f32[16,640]{1,0:T(8,128)S(1)}) custom-call(f32[16,640]{1,0:T(8,128)S(1)} %add.9.refs_0_, f32[16,640]{1,0:T(8,128)S(1)} %collective-permute-done.1.refs_1_, f32[16,640]{1,0:T(8,128)S(1)} %collective-permute-done.2.refs_2_, ...), custom_call_target="tpu_custom_call" | custom-call | flops 1000000000 | bytes 2000000 | tf_op jit(solution)/shard_map/first/pallas_call | solution.py:399
  16.8 1.5 %collective-permute-start.4 = (bf16[16,1536]{1,0:T(8,128)(2,1)S(1)}, bf16[16,1536]{1,0:T(8,128)(2,1)S(1)}, u32[]{:S(2)}, u32[]{:S(2)}) collective-permute-start(bf16[16,1536]{1,0:T(8,128)(2,1)S(1)} %get-tuple-element.38.send_ref.refs_0_), channel_id=1, source_target_pairs={{0,4},{4,0},{8,12},{12,8},{16,20},{20,16},{24,28},{28,24},{1,5},{5... | collective-permute-start | bytes 147464 | tf_op jit(solution)/shard_map/ppermute | solution.py:19
  18.4 2.6 %collective-permute-done.4.near_ref.refs_1_ = bf16[16,1536]{1,0:T(8,128)(2,1)S(1)} collective-permute-done((bf16[16,1536]{1,0:T(8,128)(2,1)S(1)}, bf16[16,1536]{1,0:T(8,128)(2,1)S(1)}, u32[]{:S(2)}, u32[]{:S(2)}) %collective-permute-start.4) | collective-permute-done | bytes 49184 | tf_op jit(solution)/shard_map/ppermute | solution.py:19
  20.9 1.5 %collective-permute-start.7 = (bf16[16,1536]{1,0:T(8,128)(2,1)S(1)}, bf16[16,1536]{1,0:T(8,128)(2,1)S(1)}, u32[]{:S(2)}, u32[]{:S(2)}) collective-permute-start(bf16[16,1536]{1,0:T(8,128)(2,1)S(1)} %get-tuple-element.40), channel_id=1, source_target_pairs={{0,24},{4,28},{8,16},{12,20},{16,8},{20,12},{24,0},{28,4},{1,25},{... | collective-permute-start | bytes 147464 | tf_op jit(solution)/shard_map/ppermute | solution.py:19
  22.4 1.1 %collective-permute-start.5 = (bf16[16,1536]{1,0:T(8,128)(2,1)S(1)}, bf16[16,1536]{1,0:T(8,128)(2,1)S(1)}, u32[]{:S(2)}, u32[]{:S(2)}) collective-permute-start(bf16[16,1536]{1,0:T(8,128)(2,1)S(1)} %get-tuple-element.40), channel_id=1, source_target_pairs={{0,8},{4,12},{8,0},{12,4},{16,24},{20,28},{24,16},{28,20},{1,9},{5... | collective-permute-start | bytes 147464 | tf_op jit(solution)/shard_map/ppermute | solution.py:19
  23.5 0.0 collective-permute-start.9
  23.5 1.8 %collective-permute-start.6 = (bf16[16,512]{1,0:T(8,128)(2,1)S(1)}, bf16[16,512]{1,0:T(8,128)(2,1)S(1)}, u32[]{:S(2)}, u32[]{:S(2)}) collective-permute-start(bf16[16,512]{1,0:T(8,128)(2,1)S(1)} %get-tuple-element.39.refs_0_), channel_id=1, source_target_pairs={{0,16},{4,20},{8,24},{12,28},{16,0},{20,4},{24,8},{28,12},{1,17},{... | collective-permute-start | bytes 49160 | tf_op jit(solution)/shard_map/ppermute | solution.py:19
  25.3 0.0 collective-permute-done.8.refs_13_.refs_12_
  25.3 0.2 collective-permute-start.10
  25.6 1.4 %collective-permute-done.7.refs_3_ = bf16[16,1536]{1,0:T(8,128)(2,1)S(1)} collective-permute-done((bf16[16,1536]{1,0:T(8,128)(2,1)S(1)}, bf16[16,1536]{1,0:T(8,128)(2,1)S(1)}, u32[]{:S(2)}, u32[]{:S(2)}) %collective-permute-start.7) | collective-permute-done | bytes 49184 | tf_op jit(solution)/shard_map/ppermute | solution.py:19
  26.9 0.1 collective-permute-done.5.refs_2_.refs_1_
  27.0 0.0 copy-done.5
  27.0 0.7 %near.2.refs_7_ = f32[16,1024]{1,0:T(8,128)S(1)} custom-call(bf16[16,1536]{1,0:T(8,128)(2,1)S(1)} %get-tuple-element.38.send_ref.refs_0_, bf16[16,1536]{1,0:T(8,128)(2,1)S(1)} %collective-permute-done.4.near_ref.refs_1_, bf16[16,1536]{1,0:T(8,128)(2,1)S(1)} %collective-permute-done.5.refs_2_.refs_1_, bf16[16,1536]{1,0:T(8,128)(2,1)S(1)} %collective-permute-done.7.refs_3_, ...), custom_call_target="tpu_custom_call" | custom-call | flops 10000000000 | bytes 20000000 | tf_op jit(solution)/shard_map/near/pallas_call | solution.py:399
  27.8 0.4 collective-permute-done.6.refs_2_
  28.2 0.0 collective-permute-done.9.refs_12_.refs_11_
  28.2 0.0 collective-permute-done.10.refs_14_.refs_13_
  28.2 1.4 %second.1 = (f32[16,1024]{1,0:T(8,128)S(1)}, f32[16,640]{1,0:T(8,128)S(1)}) custom-call(bf16[16,512]{1,0:T(8,128)(2,1)S(1)} %get-tuple-element.39.refs_0_, bf16[16,1536]{1,0:T(8,128)(2,1)S(1)} %collective-permute-done.5.refs_2_.refs_1_, bf16[16,512]{1,0:T(8,128)(2,1)S(1)} %collective-permute-done.6.refs_2_, ...), custom_call_target="tpu_custom_call" | custom-call | tf_op jit(solution)/shard_map/second/pallas_call | solution.py:399
  29.7 1.5 %collective-permute-start.11 = (f32[16,640]{1,0:T(8,128)S(1)}, f32[16,640]{1,0:T(8,128)S(1)}, u32[]{:S(2)}, u32[]{:S(2)}) collective-permute-start(f32[16,640]{1,0:T(8,128)S(1)} %get-tuple-element.48), channel_id=1, source_target_pairs={{0,4},{4,0},{8,12},{12,8},{16,20},{20,16},{24,28},{28,24},{1,5},{5... | collective-permute-start | bytes 122888 | tf_op jit(solution)/shard_map/ppermute | solution.py:19
  31.2 2.5 %collective-permute-done.11 = f32[16,640]{1,0:T(8,128)S(1)} collective-permute-done((f32[16,640]{1,0:T(8,128)S(1)}, f32[16,640]{1,0:T(8,128)S(1)}, u32[]{:S(2)}, u32[]{:S(2)}) %collective-permute-start.11) | collective-permute-done | bytes 40992 | tf_op jit(solution)/shard_map/ppermute | solution.py:19
  33.7 1.7 %collective-permute-start.14 = (f32[16,640]{1,0:T(8,128)S(1)}, f32[16,640]{1,0:T(8,128)S(1)}, u32[]{:S(2)}, u32[]{:S(2)}) collective-permute-start(f32[16,640]{1,0:T(8,128)S(1)} %add.10.refs_0_), channel_id=1, source_target_pairs={{0,24},{4,28},{8,16},{12,20},{16,8},{20,12},{24,0},{28,4},{1,25},{... | collective-permute-start | bytes 122888 | tf_op jit(solution)/shard_map/ppermute | solution.py:19
  35.4 0.7 collective-permute-start.13
  36.0 2.1 %collective-permute-start.12 = (f32[16,640]{1,0:T(8,128)S(1)}, f32[16,640]{1,0:T(8,128)S(1)}, u32[]{:S(2)}, u32[]{:S(2)}) collective-permute-start(f32[16,640]{1,0:T(8,128)S(1)} %add.10.refs_0_), channel_id=1, source_target_pairs={{0,8},{4,12},{8,0},{12,4},{16,24},{20,28},{24,16},{28,20},{1,9},{5... | collective-permute-start | bytes 122888 | tf_op jit(solution)/shard_map/ppermute | solution.py:19
  38.1 1.4 %collective-permute-done.14.refs_3_ = f32[16,640]{1,0:T(8,128)S(1)} collective-permute-done((f32[16,640]{1,0:T(8,128)S(1)}, f32[16,640]{1,0:T(8,128)S(1)}, u32[]{:S(2)}, u32[]{:S(2)}) %collective-permute-start.14) | collective-permute-done | bytes 40992 | tf_op jit(solution)/shard_map/ppermute | solution.py:19
  39.5 1.2 %collective-permute-done.13.refs_2_ = f32[16,640]{1,0:T(8,128)S(1)} collective-permute-done((f32[16,640]{1,0:T(8,128)S(1)}, f32[16,640]{1,0:T(8,128)S(1)}, u32[]{:S(2)}, u32[]{:S(2)}) %collective-permute-start.13) | collective-permute-done | bytes 40992 | tf_op jit(solution)/shard_map/ppermute | solution.py:19
  40.7 0.0 collective-permute-done.12.refs_1_
  40.7 1.0 %third.1 = (f32[16,1024]{1,0:T(8,128)S(1)}, f32[16,1024]{1,0:T(8,128)S(1)}, bf16[16,1536]{1,0:T(8,128)(2,1)S(1)}, f32[16,128]{1,0:T(8,128)S(1)}) custom-call(f32[16,640]{1,0:T(8,128)S(1)} %add.10.refs_0_, f32[16,640]{1,0:T(8,128)S(1)} %collective-permute-done.12.refs_1_, f32[16,640]{1,0:T(8,128)S(1)} %collective-permute-done.13.refs_2_, ...), custom_call_target="tpu_custom_call" | custom-call | tf_op jit(solution)/shard_map/third/pallas_call | solution.py:399
  41.7 1.5 %collective-permute-start.15 = (bf16[16,1536]{1,0:T(8,128)(2,1)S(1)}, bf16[16,1536]{1,0:T(8,128)(2,1)S(1)}, u32[]{:S(2)}, u32[]{:S(2)}) collective-permute-start(bf16[16,1536]{1,0:T(8,128)(2,1)S(1)} %get-tuple-element.51.send_ref.refs_0_), channel_id=1, source_target_pairs={{0,4},{4,0},{8,12},{12,8},{16,20},{20,16},{24,28},{28,24},{1,5},{5... | collective-permute-start | bytes 147464 | tf_op jit(solution)/shard_map/ppermute | solution.py:19
  43.2 2.6 %collective-permute-done.15.near_ref.refs_1_ = bf16[16,1536]{1,0:T(8,128)(2,1)S(1)} collective-permute-done((bf16[16,1536]{1,0:T(8,128)(2,1)S(1)}, bf16[16,1536]{1,0:T(8,128)(2,1)S(1)}, u32[]{:S(2)}, u32[]{:S(2)}) %collective-permute-start.15) | collective-permute-done | bytes 49184 | tf_op jit(solution)/shard_map/ppermute | solution.py:19
  45.8 2.1 %collective-permute-start.18 = (bf16[16,1536]{1,0:T(8,128)(2,1)S(1)}, bf16[16,1536]{1,0:T(8,128)(2,1)S(1)}, u32[]{:S(2)}, u32[]{:S(2)}) collective-permute-start(bf16[16,1536]{1,0:T(8,128)(2,1)S(1)} %get-tuple-element.53), channel_id=1, source_target_pairs={{0,24},{4,28},{8,16},{12,20},{16,8},{20,12},{24,0},{28,4},{1,25},{... | collective-permute-start | bytes 147464 | tf_op jit(solution)/shard_map/ppermute | solution.py:19
  47.9 0.0 collective-permute-start.16
  47.9 2.2 %collective-permute-start.17 = (bf16[16,512]{1,0:T(8,128)(2,1)S(1)}, bf16[16,512]{1,0:T(8,128)(2,1)S(1)}, u32[]{:S(2)}, u32[]{:S(2)}) collective-permute-start(bf16[16,512]{1,0:T(8,128)(2,1)S(1)} %get-tuple-element.52.refs_0_), channel_id=1, source_target_pairs={{0,16},{4,20},{8,24},{12,28},{16,0},{20,4},{24,8},{28,12},{1,17},{... | collective-permute-start | bytes 49160 | tf_op jit(solution)/shard_map/ppermute | solution.py:19
  50.2 1.5 %collective-permute-done.18.refs_3_ = bf16[16,1536]{1,0:T(8,128)(2,1)S(1)} collective-permute-done((bf16[16,1536]{1,0:T(8,128)(2,1)S(1)}, bf16[16,1536]{1,0:T(8,128)(2,1)S(1)}, u32[]{:S(2)}, u32[]{:S(2)}) %collective-permute-start.18) | collective-permute-done | bytes 49184 | tf_op jit(solution)/shard_map/ppermute | solution.py:19
  51.7 0.5 collective-permute-done.16.refs_2_.refs_1_
  52.2 0.7 %near.3.refs_8_ = f32[16,1024]{1,0:T(8,128)S(1)} custom-call(bf16[16,1536]{1,0:T(8,128)(2,1)S(1)} %get-tuple-element.51.send_ref.refs_0_, bf16[16,1536]{1,0:T(8,128)(2,1)S(1)} %collective-permute-done.15.near_ref.refs_1_, bf16[16,1536]{1,0:T(8,128)(2,1)S(1)} %collective-permute-done.16.refs_2_.refs_1_, bf16[16,1536]{1,0:T(8,128)(2,1)S(1)} %collective-permute-done.18.refs_3_, ...), custom_call_target="tpu_custom_call" | custom-call | flops 10000000000 | bytes 20000000 | tf_op jit(solution)/shard_map/near/pallas_call | solution.py:399
  53.0 0.0 collective-permute-done.17.refs_2_
  53.0 0.9 %fourth.1 = f32[16,128]{1,0:T(8,128)S(1)} custom-call(bf16[16,512]{1,0:T(8,128)(2,1)S(1)} %get-tuple-element.52.refs_0_, bf16[16,1536]{1,0:T(8,128)(2,1)S(1)} %collective-permute-done.16.refs_2_.refs_1_, bf16[16,512]{1,0:T(8,128)(2,1)S(1)} %collective-permute-done.17.refs_2_, bf16[16,1536]{1,0:T(8,128)(2,1)S(1)} %collective-permute-done.18.refs_3_, ...), custom_call_target="tpu_custom_call" | custom-call | tf_op jit(solution)/shard_map/fourth/pallas_call | solution.py:399
  53.8 1.6 %collective-permute-start.19 = (f32[16,128]{1,0:T(8,128)S(1)}, f32[16,128]{1,0:T(8,128)S(1)}, u32[]{:S(2)}, u32[]{:S(2)}) collective-permute-start(f32[16,128]{1,0:T(8,128)S(1)} %fourth.1), channel_id=1, source_target_pairs={{0,4},{4,0},{8,12},{12,8},{16,20},{20,16},{24,28},{28,24},{1,5},{5... | collective-permute-start | bytes 24584 | tf_op jit(solution)/shard_map/ppermute | solution.py:19
  55.4 2.1 %collective-permute-done.19 = f32[16,128]{1,0:T(8,128)S(1)} collective-permute-done((f32[16,128]{1,0:T(8,128)S(1)}, f32[16,128]{1,0:T(8,128)S(1)}, u32[]{:S(2)}, u32[]{:S(2)}) %collective-permute-start.19) | collective-permute-done | bytes 8224 | tf_op jit(solution)/shard_map/ppermute | solution.py:19
  57.5 2.0 %collective-permute-start.22 = (f32[16,128]{1,0:T(8,128)S(1)}, f32[16,128]{1,0:T(8,128)S(1)}, u32[]{:S(2)}, u32[]{:S(2)}) collective-permute-start(f32[16,128]{1,0:T(8,128)S(1)} %add.11.refs_0_), channel_id=1, source_target_pairs={{0,24},{4,28},{8,16},{12,20},{16,8},{20,12},{24,0},{28,4},{1,25},{... | collective-permute-start | bytes 24584 | tf_op jit(solution)/shard_map/ppermute | solution.py:19
  59.6 1.0 %collective-permute-start.21 = (f32[16,128]{1,0:T(8,128)S(1)}, f32[16,128]{1,0:T(8,128)S(1)}, u32[]{:S(2)}, u32[]{:S(2)}) collective-permute-start(f32[16,128]{1,0:T(8,128)S(1)} %add.11.refs_0_), channel_id=1, source_target_pairs={{0,16},{4,20},{8,24},{12,28},{16,0},{20,4},{24,8},{28,12},{1,17},{... | collective-permute-start | bytes 24584 | tf_op jit(solution)/shard_map/ppermute | solution.py:19
  60.6 1.3 %collective-permute-start.20 = (f32[16,128]{1,0:T(8,128)S(1)}, f32[16,128]{1,0:T(8,128)S(1)}, u32[]{:S(2)}, u32[]{:S(2)}) collective-permute-start(f32[16,128]{1,0:T(8,128)S(1)} %add.11.refs_0_), channel_id=1, source_target_pairs={{0,8},{4,12},{8,0},{12,4},{16,24},{20,28},{24,16},{28,20},{1,9},{5... | collective-permute-start | bytes 24584 | tf_op jit(solution)/shard_map/ppermute | solution.py:19
  61.9 1.1 %collective-permute-done.22.refs_3_ = f32[16,128]{1,0:T(8,128)S(1)} collective-permute-done((f32[16,128]{1,0:T(8,128)S(1)}, f32[16,128]{1,0:T(8,128)S(1)}, u32[]{:S(2)}, u32[]{:S(2)}) %collective-permute-start.22) | collective-permute-done | bytes 8224 | tf_op jit(solution)/shard_map/ppermute | solution.py:19
  63.0 1.1 %collective-permute-done.21.refs_2_ = f32[16,128]{1,0:T(8,128)S(1)} collective-permute-done((f32[16,128]{1,0:T(8,128)S(1)}, f32[16,128]{1,0:T(8,128)S(1)}, u32[]{:S(2)}, u32[]{:S(2)}) %collective-permute-start.21) | collective-permute-done | bytes 8224 | tf_op jit(solution)/shard_map/ppermute | solution.py:19
  64.1 0.1 collective-permute-done.20.refs_1_
  64.2 1.0 %last.1 = f32[16,1024]{1,0:T(8,128)} custom-call(f32[16,128]{1,0:T(8,128)S(1)} %add.11.refs_0_, f32[16,128]{1,0:T(8,128)S(1)} %collective-permute-done.20.refs_1_, f32[16,128]{1,0:T(8,128)S(1)} %collective-permute-done.21.refs_2_, f32[16,128]{1,0:T(8,128)S(1)} %collective-permute-done.22.refs_3_, f32[16,128]{1,0:T(8,128)S(1)} %get-tuple-element.56.refs_4_, ...), custom_call_target="tpu_custom_call" | custom-call | tf_op jit(solution)/shard_map/last/pallas_call | solution.py:399
  (8 shorter events, 0.0 us)
Async XLA Ops:
  0.0 5.0 %copy-start = (bf16[256,1,512]{2,0,1:T(8,128)(2,1)S(1)}, bf16[256,1,512]{2,0,1:T(8,128)(2,1)}, u32[]{:S(2)}) copy-start(bf16[256,1,512]{2,0,1:T(8,128)(2,1)} %param.17) | copy-start | bytes 786436
  0.0 11.7 %copy-start.3 = (s32[8,32]{1,0:T(8,128)S(1)}, s32[8,32]{1,0:T(8,128)}, u32[]{:S(2)}) copy-start(s32[8,32]{1,0:T(8,128)} %refs_3_.1) | copy-start | bytes 3076
  0.0 11.7 %copy-start.1 = (bf16[8,128,32]{1,2,0:T(8,128)(2,1)S(1)}, bf16[8,128,32]{1,2,0:T(8,128)(2,1)}, u32[]{:S(2)}) copy-start(bf16[8,128,32]{1,2,0:T(8,128)(2,1)} %param.15) | copy-start | bytes 196612
  0.0 11.7 %copy-start.4 = (s32[8]{0:T(128)S(1)}, s32[8]{0:T(128)}, u32[]{:S(2)}) copy-start(s32[8]{0:T(128)} %param.14) | copy-start | bytes 100
  0.0 11.7 %copy-start.2 = (s32[8,8]{1,0:T(8,128)S(1)}, s32[8,8]{1,0:T(8,128)}, u32[]{:S(2)}) copy-start(s32[8,8]{1,0:T(8,128)} %refs_0_.3) | copy-start | bytes 772
  1.9 25.1 %copy-start.5 = (bf16[8,8,128,128]{3,2,1,0:T(8,128)(2,1)S(1)}, bf16[8,8,128,128]{3,2,1,0:T(8,128)(2,1)}, u32[]{:S(2)}) copy-start(bf16[8,8,128,128]{3,2,1,0:T(8,128)(2,1)} %refs_5_.3) | copy-start | bytes 6291460
  1.9 5.0 %collective-permute-start = (f32[16,640]{1,0:T(8,128)S(1)}, f32[16,640]{1,0:T(8,128)S(1)}, u32[]{:S(2)}, u32[]{:S(2)}) collective-permute-start(f32[16,640]{1,0:T(8,128)S(1)} %get-tuple-element.32), channel_id=1, source_target_pairs={{0,4},{4,0},{8,12},{12,8},{16,20},{20,16},{24,28},{28,24},{1,5},{5... | collective-permute-start | bytes 122888 | tf_op jit(solution)/shard_map/ppermute | solution.py:19
  5.0 20.3 %collective-permute-start.8 = (bf16[256,512]{1,0:T(8,128)(2,1)S(1)}, bf16[256,512]{1,0:T(8,128)(2,1)S(1)}, u32[]{:S(2)}, u32[]{:S(2)}) collective-permute-start(bf16[256,512]{1,0:T(8,128)(2,1)S(1)} %bitcast.5), channel_id=1, source_target_pairs={{0,2},{1,3},{2,0},{3,1},{4,6},{5,7},{6,4},{7,5},{8,10},{9,11},{10,... | collective-permute-start | bytes 786440 | tf_op jit(solution)/shard_map/ppermute | solution.py:366
  7.0 6.1 %collective-permute-start.3 = (f32[16,640]{1,0:T(8,128)S(1)}, f32[16,640]{1,0:T(8,128)S(1)}, u32[]{:S(2)}, u32[]{:S(2)}) collective-permute-start(f32[16,640]{1,0:T(8,128)S(1)} %add.9.refs_0_), channel_id=1, source_target_pairs={{0,24},{4,28},{8,16},{12,20},{16,8},{20,12},{24,0},{28,4},{1,25},{... | collective-permute-start | bytes 122888 | tf_op jit(solution)/shard_map/ppermute | solution.py:19
  11.1 4.9 %collective-permute-start.2 = (f32[16,640]{1,0:T(8,128)S(1)}, f32[16,640]{1,0:T(8,128)S(1)}, u32[]{:S(2)}, u32[]{:S(2)}) collective-permute-start(f32[16,640]{1,0:T(8,128)S(1)} %add.9.refs_0_), channel_id=1, source_target_pairs={{0,16},{4,20},{8,24},{12,28},{16,0},{20,4},{24,8},{28,12},{1,17},{... | collective-permute-start | bytes 122888 | tf_op jit(solution)/shard_map/ppermute | solution.py:19
  11.1 4.9 %collective-permute-start.1 = (f32[16,640]{1,0:T(8,128)S(1)}, f32[16,640]{1,0:T(8,128)S(1)}, u32[]{:S(2)}, u32[]{:S(2)}) collective-permute-start(f32[16,640]{1,0:T(8,128)S(1)} %add.9.refs_0_), channel_id=1, source_target_pairs={{0,8},{4,12},{8,0},{12,4},{16,24},{20,28},{24,16},{28,20},{1,9},{5... | collective-permute-start | bytes 122888 | tf_op jit(solution)/shard_map/ppermute | solution.py:19
  16.8 4.1 %collective-permute-start.4 = (bf16[16,1536]{1,0:T(8,128)(2,1)S(1)}, bf16[16,1536]{1,0:T(8,128)(2,1)S(1)}, u32[]{:S(2)}, u32[]{:S(2)}) collective-permute-start(bf16[16,1536]{1,0:T(8,128)(2,1)S(1)} %get-tuple-element.38.send_ref.refs_0_), channel_id=1, source_target_pairs={{0,4},{4,0},{8,12},{12,8},{16,20},{20,16},{24,28},{28,24},{1,5},{5... | collective-permute-start | bytes 147464 | tf_op jit(solution)/shard_map/ppermute | solution.py:19
  20.9 6.0 %collective-permute-start.7 = (bf16[16,1536]{1,0:T(8,128)(2,1)S(1)}, bf16[16,1536]{1,0:T(8,128)(2,1)S(1)}, u32[]{:S(2)}, u32[]{:S(2)}) collective-permute-start(bf16[16,1536]{1,0:T(8,128)(2,1)S(1)} %get-tuple-element.40), channel_id=1, source_target_pairs={{0,24},{4,28},{8,16},{12,20},{16,8},{20,12},{24,0},{28,4},{1,25},{... | collective-permute-start | bytes 147464 | tf_op jit(solution)/shard_map/ppermute | solution.py:19
  22.4 4.6 %collective-permute-start.5 = (bf16[16,1536]{1,0:T(8,128)(2,1)S(1)}, bf16[16,1536]{1,0:T(8,128)(2,1)S(1)}, u32[]{:S(2)}, u32[]{:S(2)}) collective-permute-start(bf16[16,1536]{1,0:T(8,128)(2,1)S(1)} %get-tuple-element.40), channel_id=1, source_target_pairs={{0,8},{4,12},{8,0},{12,4},{16,24},{20,28},{24,16},{28,20},{1,9},{5... | collective-permute-start | bytes 147464 | tf_op jit(solution)/shard_map/ppermute | solution.py:19
  23.5 4.7 %collective-permute-start.9 = (bf16[256,512]{1,0:T(8,128)(2,1)S(1)}, bf16[256,512]{1,0:T(8,128)(2,1)S(1)}, u32[]{:S(2)}, u32[]{:S(2)}) collective-permute-start(bf16[256,512]{1,0:T(8,128)(2,1)S(1)} %bitcast.6), channel_id=1, source_target_pairs={{0,1},{1,0},{2,3},{3,2},{4,5},{5,4},{6,7},{7,6},{8,9},{9,8},{10,11... | collective-permute-start | bytes 786440 | tf_op jit(solution)/shard_map/ppermute | solution.py:366
  23.5 4.7 %collective-permute-start.6 = (bf16[16,512]{1,0:T(8,128)(2,1)S(1)}, bf16[16,512]{1,0:T(8,128)(2,1)S(1)}, u32[]{:S(2)}, u32[]{:S(2)}) collective-permute-start(bf16[16,512]{1,0:T(8,128)(2,1)S(1)} %get-tuple-element.39.refs_0_), channel_id=1, source_target_pairs={{0,16},{4,20},{8,24},{12,28},{16,0},{20,4},{24,8},{28,12},{1,17},{... | collective-permute-start | bytes 49160 | tf_op jit(solution)/shard_map/ppermute | solution.py:19
  25.3 2.9 %collective-permute-start.10 = (bf16[256,512]{1,0:T(8,128)(2,1)S(1)}, bf16[256,512]{1,0:T(8,128)(2,1)S(1)}, u32[]{:S(2)}, u32[]{:S(2)}) collective-permute-start(bf16[256,512]{1,0:T(8,128)(2,1)S(1)} %collective-permute-done.8.refs_13_.refs_12_), channel_id=1, source_target_pairs={{0,1},{1,0},{2,3},{3,2},{4,5},{5,4},{6,7},{7,6},{8,9},{9,8},{10,11... | collective-permute-start | bytes 786440 | tf_op jit(solution)/shard_map/ppermute | solution.py:373
  29.7 4.0 %collective-permute-start.11 = (f32[16,640]{1,0:T(8,128)S(1)}, f32[16,640]{1,0:T(8,128)S(1)}, u32[]{:S(2)}, u32[]{:S(2)}) collective-permute-start(f32[16,640]{1,0:T(8,128)S(1)} %get-tuple-element.48), channel_id=1, source_target_pairs={{0,4},{4,0},{8,12},{12,8},{16,20},{20,16},{24,28},{28,24},{1,5},{5... | collective-permute-start | bytes 122888 | tf_op jit(solution)/shard_map/ppermute | solution.py:19
  33.7 5.8 %collective-permute-start.14 = (f32[16,640]{1,0:T(8,128)S(1)}, f32[16,640]{1,0:T(8,128)S(1)}, u32[]{:S(2)}, u32[]{:S(2)}) collective-permute-start(f32[16,640]{1,0:T(8,128)S(1)} %add.10.refs_0_), channel_id=1, source_target_pairs={{0,24},{4,28},{8,16},{12,20},{16,8},{20,12},{24,0},{28,4},{1,25},{... | collective-permute-start | bytes 122888 | tf_op jit(solution)/shard_map/ppermute | solution.py:19
  35.4 5.3 %collective-permute-start.13 = (f32[16,640]{1,0:T(8,128)S(1)}, f32[16,640]{1,0:T(8,128)S(1)}, u32[]{:S(2)}, u32[]{:S(2)}) collective-permute-start(f32[16,640]{1,0:T(8,128)S(1)} %add.10.refs_0_), channel_id=1, source_target_pairs={{0,16},{4,20},{8,24},{12,28},{16,0},{20,4},{24,8},{28,12},{1,17},{... | collective-permute-start | bytes 122888 | tf_op jit(solution)/shard_map/ppermute | solution.py:19
  36.0 4.7 %collective-permute-start.12 = (f32[16,640]{1,0:T(8,128)S(1)}, f32[16,640]{1,0:T(8,128)S(1)}, u32[]{:S(2)}, u32[]{:S(2)}) collective-permute-start(f32[16,640]{1,0:T(8,128)S(1)} %add.10.refs_0_), channel_id=1, source_target_pairs={{0,8},{4,12},{8,0},{12,4},{16,24},{20,28},{24,16},{28,20},{1,9},{5... | collective-permute-start | bytes 122888 | tf_op jit(solution)/shard_map/ppermute | solution.py:19
  41.7 4.1 %collective-permute-start.15 = (bf16[16,1536]{1,0:T(8,128)(2,1)S(1)}, bf16[16,1536]{1,0:T(8,128)(2,1)S(1)}, u32[]{:S(2)}, u32[]{:S(2)}) collective-permute-start(bf16[16,1536]{1,0:T(8,128)(2,1)S(1)} %get-tuple-element.51.send_ref.refs_0_), channel_id=1, source_target_pairs={{0,4},{4,0},{8,12},{12,8},{16,20},{20,16},{24,28},{28,24},{1,5},{5... | collective-permute-start | bytes 147464 | tf_op jit(solution)/shard_map/ppermute | solution.py:19
  45.8 5.9 %collective-permute-start.18 = (bf16[16,1536]{1,0:T(8,128)(2,1)S(1)}, bf16[16,1536]{1,0:T(8,128)(2,1)S(1)}, u32[]{:S(2)}, u32[]{:S(2)}) collective-permute-start(bf16[16,1536]{1,0:T(8,128)(2,1)S(1)} %get-tuple-element.53), channel_id=1, source_target_pairs={{0,24},{4,28},{8,16},{12,20},{16,8},{20,12},{24,0},{28,4},{1,25},{... | collective-permute-start | bytes 147464 | tf_op jit(solution)/shard_map/ppermute | solution.py:19
  47.9 4.3 %collective-permute-start.16 = (bf16[16,1536]{1,0:T(8,128)(2,1)S(1)}, bf16[16,1536]{1,0:T(8,128)(2,1)S(1)}, u32[]{:S(2)}, u32[]{:S(2)}) collective-permute-start(bf16[16,1536]{1,0:T(8,128)(2,1)S(1)} %get-tuple-element.53), channel_id=1, source_target_pairs={{0,8},{4,12},{8,0},{12,4},{16,24},{20,28},{24,16},{28,20},{1,9},{5... | collective-permute-start | bytes 147464 | tf_op jit(solution)/shard_map/ppermute | solution.py:19
  47.9 5.0 %collective-permute-start.17 = (bf16[16,512]{1,0:T(8,128)(2,1)S(1)}, bf16[16,512]{1,0:T(8,128)(2,1)S(1)}, u32[]{:S(2)}, u32[]{:S(2)}) collective-permute-start(bf16[16,512]{1,0:T(8,128)(2,1)S(1)} %get-tuple-element.52.refs_0_), channel_id=1, source_target_pairs={{0,16},{4,20},{8,24},{12,28},{16,0},{20,4},{24,8},{28,12},{1,17},{... | collective-permute-start | bytes 49160 | tf_op jit(solution)/shard_map/ppermute | solution.py:19
  53.8 3.7 %collective-permute-start.19 = (f32[16,128]{1,0:T(8,128)S(1)}, f32[16,128]{1,0:T(8,128)S(1)}, u32[]{:S(2)}, u32[]{:S(2)}) collective-permute-start(f32[16,128]{1,0:T(8,128)S(1)} %fourth.1), channel_id=1, source_target_pairs={{0,4},{4,0},{8,12},{12,8},{16,20},{20,16},{24,28},{28,24},{1,5},{5... | collective-permute-start | bytes 24584 | tf_op jit(solution)/shard_map/ppermute | solution.py:19
  57.5 5.4 %collective-permute-start.22 = (f32[16,128]{1,0:T(8,128)S(1)}, f32[16,128]{1,0:T(8,128)S(1)}, u32[]{:S(2)}, u32[]{:S(2)}) collective-permute-start(f32[16,128]{1,0:T(8,128)S(1)} %add.11.refs_0_), channel_id=1, source_target_pairs={{0,24},{4,28},{8,16},{12,20},{16,8},{20,12},{24,0},{28,4},{1,25},{... | collective-permute-start | bytes 24584 | tf_op jit(solution)/shard_map/ppermute | solution.py:19
  59.6 4.5 %collective-permute-start.21 = (f32[16,128]{1,0:T(8,128)S(1)}, f32[16,128]{1,0:T(8,128)S(1)}, u32[]{:S(2)}, u32[]{:S(2)}) collective-permute-start(f32[16,128]{1,0:T(8,128)S(1)} %add.11.refs_0_), channel_id=1, source_target_pairs={{0,16},{4,20},{8,24},{12,28},{16,0},{20,4},{24,8},{28,12},{1,17},{... | collective-permute-start | bytes 24584 | tf_op jit(solution)/shard_map/ppermute | solution.py:19
  60.6 3.7 %collective-permute-start.20 = (f32[16,128]{1,0:T(8,128)S(1)}, f32[16,128]{1,0:T(8,128)S(1)}, u32[]{:S(2)}, u32[]{:S(2)}) collective-permute-start(f32[16,128]{1,0:T(8,128)S(1)} %add.11.refs_0_), channel_id=1, source_target_pairs={{0,8},{4,12},{8,0},{12,4},{16,24},{20,28},{24,16},{28,20},{1,9},{5... | collective-permute-start | bytes 24584 | tf_op jit(solution)/shard_map/ppermute | solution.py:19

commit v6 on v5

--- a/solution.py
+++ b/solution.py
@@ -64,15 +64,11 @@
         send_ref[:, start : start + LANES] = (both[:, :LANES] + both[:, LANES:]).astype(BF)
 
 
-def maps_kernel(sources, ids_ref, live_ref, weights_ref, skel_ref, maps_ref, places_ref):
-    block_count, rank, block = weights_ref.shape
+def build_maps(maps_ref, odd_start, skel, weights, block_count, rank, block):
     quarters = maps_ref.shape[0]
     per = block_count // quarters
-    odd_start = pl.multiple_of((lax.axis_index(AXIS) % 2) * HALF, HALF)
+    odd_start = pl.multiple_of(odd_start, HALF)
     maps_ref[...] = jnp.zeros(maps_ref.shape, BF)
-    skel = jnp.concatenate(
-        [skel_ref[...].astype(F32), jnp.zeros((block_count, LANES - rank), F32)], axis=1
-    ).T
     panel = lax.broadcasted_iota(jnp.int32, (rank, block), 1).astype(F32)
     for b in range(block_count):
         quarter, index = divmod(b, per)
@@ -80,7 +76,16 @@
         cols = slice(index * block, (index + 1) * block)
         hot = jnp.where(skel[:rank, b : b + 1] == panel, 1.0, 0.0).astype(BF)
         maps_ref[quarter, pl.ds(start, rank), cols] = hot
-        maps_ref[quarter, pl.ds(start + LANES, rank), cols] = weights_ref[b]
+        maps_ref[quarter, pl.ds(start + LANES, rank), cols] = weights(b)
+
+
+def maps_kernel(sources, ids_ref, live_ref, weights_ref, skel_ref, maps_ref, places_ref):
+    block_count, rank, block = weights_ref.shape
+    skel = jnp.concatenate(
+        [skel_ref[...].astype(F32), jnp.zeros((block_count, LANES - rank), F32)], axis=1
+    ).T
+    odd_start = (lax.axis_index(AXIS) % 2) * HALF
+    build_maps(maps_ref, odd_start, skel, lambda b: weights_ref[b], block_count, rank, block)
     wanted = ids_ref[...]
     slots = wanted.shape[1]
     slot = lax.broadcasted_iota(jnp.int32, wanted.shape, 1)
@@ -101,6 +106,35 @@
     places_ref[...] = packed.astype(jnp.int32)
 
 
+def other_maps(base, rank, block, packs, maps_ref):
+    chunks = packs[0][1].shape[1] // block
+    per = maps_ref.shape[2] // block
+    tall = per * rank // chunks
+    odd_start = pl.multiple_of((1 - lax.axis_index(AXIS) % 2) * HALF, HALF)
+    panel = lax.broadcasted_iota(jnp.int32, (rank, block), 1).astype(F32)
+    for mask, ref in packs:
+        quarter = lax.axis_index("rhs") ^ mask
+        skel = ref[base + tall : base + tall + 16, :LANES].astype(F32)
+        skel = jnp.concatenate([skel, jnp.zeros((LANES - 16, LANES), F32)], axis=0).T
+        weights = jnp.concatenate(
+            [ref[base : base + tall, j * block : (j + 1) * block] for j in range(chunks)], axis=0
+        )
+        for index in range(per):
+            start = odd_start + index * rank
+            cols = slice(index * block, (index + 1) * block)
+            hot = jnp.where(skel[:rank, index : index + 1] == panel, 1.0, 0.0).astype(BF)
+            maps_ref[quarter, pl.ds(start, rank), cols] = hot
+            maps_ref[quarter, pl.ds(start + LANES, rank), cols] = weights[
+                index * rank : (index + 1) * rank
+            ]
+
+
+def other_maps_kernel(base, rank, block, *refs):
+    *pack_refs, maps_ref = refs
+    maps_ref[...] = jnp.zeros(maps_ref.shape, BF)
+    other_maps(base, rank, block, list(enumerate(pack_refs)), maps_ref)
+
+
 def onward_kernel(send_ref, near_ref, onward_ref, pair_ref):
     panels = near_ref.shape[1] - pair_ref.shape[1]
     pair = send_ref[:, panels:] + near_ref[:, panels:]
@@ -109,16 +143,44 @@
     pair_ref[...] = pair
 
 
-def open_kernel(parts, rhs_hbm, factor_hbm, diag_hbm, self_hbm, out_ref, rhs_ref, diag_ref,
-                self_ref, high_ref, low_ref, held_ref, sems):
+def neighbour_field(panels, scaled, proj, part_refs, onward_ref):
+    rows = proj.shape[0]
+    both = jnp.concatenate(split(proj), axis=0)
+    size = panels // len(part_refs)
+    for mask, ref in enumerate(part_refs):
+        part = dot_nt(both, ref[:size, :])
+        start = pl.multiple_of((lax.axis_index("rhs") ^ mask) * size, size)
+        field = scaled(start, size) - (part[:rows] + part[rows:])
+        onward_ref[:, pl.ds(start, size)] = field.astype(BF)
+
+
+def pair_charges(field_low, maps_ref, other_maps_ref, onward_ref, pair_ref):
+    panels = field_low.shape[1]
+    quarters, _, width = maps_ref.shape
+    for quarter in range(quarters):
+        cols = slice(quarter * width, (quarter + 1) * width)
+        both = dot_nt(field_low[:, cols], maps_ref[quarter])
+        both = both + dot_nt(onward_ref[:, cols], other_maps_ref[quarter])
+        charge = (both[:, :LANES] + both[:, LANES:]).astype(BF)
+        pair_ref[:, quarter * LANES : (quarter + 1) * LANES] = charge
+        onward_ref[:, panels + quarter * LANES : panels + (quarter + 1) * LANES] = charge
+
+
+def open_kernel(parts, paired, rhs_hbm, factor_hbm, diag_hbm, self_hbm, *refs):
+    if paired:
+        weights_hbm, skel_hbm, out_ref, rhs_ref, diag_ref, self_ref, high_ref, low_ref = refs[:8]
+        pack_ref, held_ref, weights_ref, skel_ref, sems = refs[8:]
+    else:
+        out_ref, rhs_ref, diag_ref, self_ref, high_ref, low_ref, held_ref, sems = refs
     panels, width = factor_hbm.shape
     rows = rhs_ref.shape[0]
     depth = panels // parts
+    pairs = [(rhs_hbm, rhs_ref), (diag_hbm, diag_ref), (self_hbm, self_ref)]
+    if paired:
+        pairs += [(weights_hbm, weights_ref), (skel_hbm, skel_ref)]
     loads = [
         pltpu.make_async_copy(source, target, sems.at[parts + index])
-        for index, (source, target) in enumerate(
-            [(rhs_hbm, rhs_ref), (diag_hbm, diag_ref), (self_hbm, self_ref)]
-        )
+        for index, (source, target) in enumerate(pairs)
     ]
     for load in loads:
         load.start()
@@ -129,9 +191,39 @@
             pltpu.make_async_copy(factor_hbm.at[span], held_ref.at[span], sems.at[part])
         )
         copies[-1].start()
-    loads[0].wait()
+    for load in loads:
+        load.wait()
     rhs = rhs_ref[...]
     out_ref[:, width:] = put_scalars([row_sum(rhs * rhs)], rows)
+    if paired:
+        block_count, rank, block = weights_ref.shape
+        quarters = lax.axis_size("rhs")
+        quarter = lax.axis_index("rhs")
+        size = panels // quarters
+        per = block_count // quarters
+        chunks = width // block
+        tall = per * rank // chunks
+        for index in range(per):
+            values = weights_ref[quarter * per + index]
+            for part in range(rank // tall):
+                chunk = index * (rank // tall) + part
+                pack_ref[size : size + tall, chunk * block : (chunk + 1) * block] = values[
+                    part * tall : (part + 1) * tall
+                ]
+        skel = skel_ref[...].astype(F32)
+        skel = jnp.concatenate([skel, jnp.zeros((block_count, width - rank), F32)], axis=1)
+        row = lax.broadcasted_iota(jnp.int32, skel.shape, 0)
+        picked = [
+            jnp.sum(jnp.where(row == quarter * per + index, skel, 0.0), axis=0, keepdims=True)
+            for index in range(per)
+        ]
+        picked.append(jnp.zeros((16 - per, width), F32))
+        pack_ref[size + tall : size + tall + 16, :] = jnp.concatenate(picked, axis=0).astype(BF)
+        start = size + tall + 16
+        for part in split(diag_ref[...] * rhs):
+            for first in range(0, panels, width):
+                pack_ref[start : start + rows, :] = part[:, first : first + width]
+                start += rows
     total = jnp.zeros((rows, width), F32)
     for part in range(parts):
         span = slice(part * depth, (part + 1) * depth)
@@ -141,14 +233,14 @@
         low_ref[span, :] = low
         total = total + dot_wide(dot_nn, rhs[:, span], high, low)
     out_ref[:, :width] = total
-    for load in loads[1:]:
-        load.wait()
+    if paired:
+        pack_ref[:size, :] = high_ref[pl.ds(pl.multiple_of(quarter * size, size), size), :]
 
 
 def first_kernel(parts, *refs):
     sums = refs[:parts]
     rhs_ref, diag_ref, high_ref, low_ref, maps_ref = refs[parts : parts + 5]
-    dir_ref, pre_ref, send_ref, keep_ref = refs[parts + 5 :]
+    dir_ref, pre_ref, keep_ref, send_ref = refs[parts + 5 :]
     width = high_ref.shape[1]
     rows, panels = rhs_ref.shape
     summed = sums[0][...]
@@ -239,8 +331,9 @@
 def second_kernel(charge_starts, *refs):
     parts = len(charge_starts)
     charge_refs = list(zip(refs[:parts], charge_starts))
-    dir_ref, pre_ref, self_ref, near_ref, maps_ref, high_ref, low_ref = refs[parts : parts + 7]
-    *coupling_refs, res_ref, out_ref, charges_ref = refs[parts + 7 :]
+    dir_ref, pre_ref, self_ref, diag_ref = refs[parts : parts + 4]
+    near_ref, maps_ref, high_ref, low_ref = refs[parts + 4 : parts + 8]
+    *coupling_refs, res_ref, scaled_ref, out_ref, charges_ref = refs[parts + 8 :]
     width = high_ref.shape[1]
     rows = pre_ref.shape[0]
     for cols, values in apply_matrix(
@@ -250,12 +343,15 @@
     res = res_ref[...]
     out_ref[:, :width] = dot_wide(dot_nn, res, high_ref[...], low_ref[...])
     out_ref[:, width:] = put_scalars([row_sum(res * dir_ref[...]), row_sum(res * res)], rows)
-
-
-def third_kernel(parts, *refs):
+    scaled_ref[...] = diag_ref[...] * res
+
+
+def third_kernel(parts, rank, block, *refs):
+    if rank:
+        *refs, other_maps_ref = refs
     sums = refs[:parts]
     res_ref, dir_ref, keep_ref, diag_ref, high_ref, low_ref, maps_ref = refs[parts : parts + 7]
-    next_ref, pre_ref, send_ref, scalars_ref = refs[parts + 7 :]
+    *extra, next_ref, pre_ref, scalars_ref, send_ref = refs[parts + 7 :]
     width = high_ref.shape[1]
     rows, panels = res_ref.shape
     summed = sums[0][...]
@@ -270,10 +366,37 @@
     proj = (summed[:, :width] - diag_one * keep_ref[:, :width]) / below_one
     pre = diag_ref[...] * second_dir - dot_wide(dot_nt, proj, high_ref[...], low_ref[...])
     field_low = pre.astype(BF)
+    pre_ref[...] = pre
+    if extra:
+        got_ref, *part_refs, some_maps_ref, onward_ref, pair_ref = extra
+        other_maps_ref[...] = some_maps_ref[...]
+        last = len(part_refs) - 1
+        other_maps(panels // (last + 1), rank, block, [(last, part_refs[last])], other_maps_ref)
+        ratio = diag_one / start_len
+        count = panels // width
+        base = part_refs[0].shape[0] - 2 * count * rows
+        before = []
+        for index in range(count):
+            high_rows = pl.ds(base + index * rows, rows)
+            low_rows = pl.ds(base + (index + count) * rows, rows)
+            before.append(
+                part_refs[0][high_rows, :].astype(F32) + part_refs[0][low_rows, :].astype(F32)
+            )
+        scaled_ref = next_ref
+        scaled_ref[...] = (
+            got_ref[...] - ratio * jnp.concatenate(before, axis=1)
+        ) / below_one
+
+        def scaled(start, size):
+            return scaled_ref[:, pl.ds(start, size)]
+
+        neighbour_field(panels, scaled, proj, part_refs, onward_ref)
+        send_ref[...] = field_low
+        pair_charges(field_low, maps_ref, other_maps_ref, onward_ref, pair_ref)
+    else:
+        send_ref[:, :panels] = field_low
+        charge_rows(field_low, maps_ref, send_ref)
     next_ref[...] = second_dir
-    pre_ref[...] = pre
-    send_ref[:, :panels] = field_low
-    charge_rows(field_low, maps_ref, send_ref)
     cross = diag_one * (1.0 - first_sq) / below_one
     second_sq = below_sq / (below_one * below_one)
     scalars_ref[...] = put_scalars(
@@ -338,24 +461,29 @@
     return [pair, swap(pair, 2, count), swap(pair, 4, count), swap(pair, 6, count)]
 
 
-def exchange(send, panels, count):
-    if count != 8:
-        field, charges = send[:, :panels], send[:, panels:]
-        ends = count - 1
-        lower = lax.ppermute(field, AXIS, [(i, i + 1) for i in range(ends)])
-        upper = lax.ppermute(field, AXIS, [(i + 1, i) for i in range(ends)])
-        every = lax.all_gather(charges, AXIS)
-        every = every.reshape((count // 2, 2) + charges.shape)
-        return [lower, send, upper], [every[:, 0] + every[:, 1]], [0]
-    near = swap(send, 1, count)
-    rows, long = send.shape
-    onward, pair = call(
-        "onward", onward_kernel, [((rows, long), BF), ((rows, long - panels), BF)], [send, near]
-    )
+def exchange_z(field, onward, pair, panels, count):
     two = swap(onward, 2, count)
     four = swap(pair, 4, count)
     six = swap(onward, 6, count)
-    return [send, near, two, six], [pair, two, four, six], [0, panels, 0, panels]
+    return [field, onward, two, six], [pair, two, four, six], [0, panels, 0, panels]
+
+
+def exchange(send, panels, count):
+    if count == 8:
+        near = swap(send, 1, count)
+        rows, long = send.shape
+        onward, pair = call(
+            "onward", onward_kernel, [((rows, long), BF), ((rows, long - panels), BF)], [send, near]
+        )
+        fields, charges, starts = exchange_z(send, onward, pair, panels, count)
+        return [send, near] + fields[2:], charges, starts
+    field, charges = send[:, :panels], send[:, panels:]
+    ends = count - 1
+    lower = lax.ppermute(field, AXIS, [(i, i + 1) for i in range(ends)])
+    upper = lax.ppermute(field, AXIS, [(i + 1, i) for i in range(ends)])
+    every = lax.all_gather(charges, AXIS)
+    every = every.reshape((count // 2, 2) + charges.shape)
+    return [lower, send, upper], [every[:, 0] + every[:, 1]], [0]
 
 
 def gather_quarters(coupling, quarters, count, early):
@@ -422,43 +550,55 @@
 ):
     rows, panels = rhs_vec.shape
     block_count, slots, block, _ = near_mats.shape
-    skeletons = coupling.shape[0]
+    rank = interp.shape[2]
     quarters = lax.axis_size("rhs")
     count = lax.axis_size(AXIS)
     width = low_rank.shape[1]
-    region = lax.axis_index(AXIS)
     sources = 4 if count == 8 else 3
+    weights = jnp.swapaxes(interp, 1, 2)
     maps, places = call(
         "maps",
         lambda *refs: maps_kernel(sources, *refs),
         [((quarters, 2 * LANES, panels // quarters), BF), ((block_count, LANES), jnp.int32)],
-        [near_ids, near_count[None, :], jnp.swapaxes(interp, 1, 2), skel_idx],
+        [near_ids, near_count[None, :], weights, skel_idx],
     )
     wide = width + LANES
     long = panels + quarters * LANES
-
+    paired = count == 8 and quarters == 4
     parts = 4
-    payload, rhs_near, diag_row, self_row, high, low = call(
+    args = [rhs_vec, low_rank, diag_prec[None, :], self_coef[None, :]]
+    outs = [((rows, wide), F32), ((rows, panels), F32), ((1, panels), F32),
+            ((1, panels), F32), (low_rank.shape, BF), (low_rank.shape, BF)]
+    scratch = [pltpu.VMEM((panels, width), F32)]
+    if paired:
+        args += [weights, skel_idx]
+        tall = block_count // quarters * rank * block // width
+        packed = panels // quarters + tall + 16 + 2 * rows * panels // width
+        outs += [((packed, width), BF)]
+        scratch += [pltpu.VMEM(weights.shape, BF), pltpu.VMEM(skel_idx.shape, jnp.int32)]
+    payload, rhs_near, diag_row, self_row, high, low, *packs = call(
         "open",
-        lambda *refs: open_kernel(parts, *refs),
-        [((rows, wide), F32), ((rows, panels), F32), ((1, panels), F32), ((1, panels), F32),
-         (low_rank.shape, BF), (low_rank.shape, BF)],
-        [rhs_vec, low_rank, diag_prec[None, :], self_coef[None, :]],
-        [pltpu.VMEM((panels, width), F32), pltpu.SemaphoreType.DMA((parts + 3,))],
-        far=(0, 1, 2, 3),
-    )
-
+        lambda *refs: open_kernel(parts, paired, *refs),
+        outs,
+        args,
+        scratch + [pltpu.SemaphoreType.DMA((parts + 5,))],
+        far=range(len(args)),
+    )
     some_rows, payload = gather_quarters(coupling[:, 0, :], quarters, count, payload)
     sums = sum_parts(payload, count)
-    first_dir, first_pre, send, keep = call(
+    if paired:
+        mine = swap(packs[0], 1, count)
+    first_dir, first_pre, keep, send = call(
         "first",
         lambda *refs: first_kernel(len(sums), *refs),
-        [((rows, panels), F32), ((rows, panels), F32), ((rows, long), BF), ((rows, wide), F32)],
+        [((rows, panels), F32), ((rows, panels), F32), ((rows, wide), F32), ((rows, long), BF)],
         [*sums, rhs_near, diag_row, high, low, maps],
-        flops=10**9,
+        flops=2*10**9,
     )
     fields, charges, starts = exchange(send, panels, count)
     full_rows, fields[1] = finish_quarters(some_rows, quarters, fields[1])
+    if paired:
+        mine, fields[1] = gather_quarters(mine, quarters, count, fields[1])
 
     def near_product(fields):
         (near,) = call(
@@ -473,21 +613,42 @@
 
     near = near_product(fields)
     scratch = [pltpu.VMEM((quarters, count // 2, rows, LANES), BF)]
-    residue, payload = call(
+    residue, scaled, payload = call(
         "second",
         lambda *refs: second_kernel(starts, *refs),
-        [((rows, panels), F32), ((rows, wide), F32)],
-        [*charges, first_dir, first_pre, self_row, near, maps, high, low, *full_rows],
+        [((rows, panels), F32), ((rows, panels), F32), ((rows, wide), F32)],
+        [*charges, first_dir, first_pre, self_row, diag_row, near, maps, high, low, *full_rows],
         scratch,
+        flops=10**10,
     )
     sums = sum_parts(payload, count)
-    second_dir, second_pre, send, scalars = call(
+    outs = [((rows, panels), F32), ((rows, panels), F32), ((rows, LANES), F32)]
+    extra = []
+    if paired:
+        again = swap(scaled, 1, count)
+        mine, sums[0] = finish_quarters(mine, quarters, sums[0])
+        (some_maps,) = call(
+            "other_maps",
+            lambda *refs: other_maps_kernel(panels // quarters, rank, block, *refs),
+            [(maps.shape, BF)],
+            mine[:-1],
+            flops=10**10,
+        )
+        extra = [again, *mine, some_maps]
+        outs = [((rows, long), BF), ((rows, long - panels), BF), *outs, ((rows, panels), BF)]
+    else:
+        outs += [((rows, long), BF)]
+    *onward, second_dir, second_pre, scalars, send = call(
         "third",
-        lambda *refs: third_kernel(len(sums), *refs),
-        [((rows, panels), F32), ((rows, panels), F32), ((rows, long), BF), ((rows, LANES), F32)],
-        [*sums, residue, first_dir, keep, diag_row, high, low, maps],
-    )
-    fields, charges, starts = exchange(send, panels, count)
+        lambda *refs: third_kernel(len(sums), paired * rank, block, *refs),
+        outs,
+        [*sums, residue, first_dir, keep, diag_row, high, low, maps, *extra],
+        [pltpu.VMEM(maps.shape, BF)] if paired else [],
+    )
+    if paired:
+        fields, charges, starts = exchange_z(send, *onward, panels, count)
+    else:
+        fields, charges, starts = exchange(send, panels, count)
     near = near_product(fields)
     (tail,) = call(
         "fourth",

time: 65.3 us -> 63.5 us (0.972)
  waiting for transfers between devices: 23.1 us -> 19.8 us
  Pallas kernels: 8.73 us -> 9.46 us
  starting transfers between devices: 33.3 us -> 34 us
    ppermute x20 -> x21, waiting for transfers between devices: 23.1 us -> 19.3 us  [swap(): return lax.ppermute(values, AXIS, [(i, i ^ mask) for i in range(count)])]
    ppermute x2 -> x4, starting transfers between devices: 1.49 us -> 3.14 us  [gather_quarters(): lax.ppermute(coupling, 'rhs', pair)]
    ppermute x20 -> x21, starting transfers between devices: 31.5 us -> 30.6 us  [swap(): return lax.ppermute(values, AXIS, [(i, i ^ mask) for i in range(count)])]
    pallas_call x11, Pallas kernels: 8.73 us -> 9.46 us  [call(): pl.pallas_call(kernel, name=name, out_shape=out_shapes, in_specs=specs, o...]
  transfers between devices with their start and end apart: 23 -> 27, of which waited for: 17 -> 14; matrix products, arithmetic and copies ran while one was open for 0% -> 0% of each run, Pallas kernels for 4% -> 7%
where the time goes in v6:
time: 63.5 us; the launch traced here: 63.4 us
  starting transfers between devices  34 us (54%)
  waiting for transfers between devices  19.8 us (31%)
  Pallas kernels  9.46 us (15%)
    ppermute x21, starting transfers between devices, swap(): return lax.ppermute(values, AXIS, [(i, i ^ mask) for i in range(count)])  30.6 us
    ppermute x21, waiting for transfers between devices, swap(): return lax.ppermute(values, AXIS, [(i, i ^ mask) for i in range(count)])  19.3 us
    pallas_call x11, Pallas kernels, call(): pl.pallas_call(kernel, name=name, out_shape=out_shapes, in_specs=specs, o...  9.46 us
    ppermute x4, starting transfers between devices, gather_quarters(): lax.ppermute(coupling, 'rhs', pair)  3.14 us
  transfers between devices with their start and end apart: 27, of which 14 were waited for; matrix products, arithmetic and copies ran while one was open for 0% of the time, Pallas kernels for 7%

profile of v6, /device:TPU:0, one launch (start us, length us, event | category | flops | bytes accessed | tf_op | source)
XLA Modules:
  0.0 63.4 jit_solution(6487431803487339945)
XLA Ops:
  0.0 2.0 %open.1 = (f32[16,640]{1,0:T(8,128)S(1)}, f32[16,1024]{1,0:T(8,128)S(1)}, f32[1,1024]{1,0:T(1,128)S(1)}, f32[1,1024]{1,0:T(1,128)S(1)}, bf16[1024,512]{1,0:T(8,1...) custom-call(f32[16,1024]{1,0:T(8,128)} %refs_0_.2, f32[1024,512]{1,0:T(8,128)} %refs_1_.1, ...), custom_call_target="tpu_custom_call" | custom-call | tf_op jit(solution)/shard_map/open/pallas_call | solution.py:527
  2.0 3.1 %collective-permute-start.2 = (f32[16,640]{1,0:T(8,128)S(1)}, f32[16,640]{1,0:T(8,128)S(1)}, u32[]{:S(2)}, u32[]{:S(2)}) collective-permute-start(f32[16,640]{1,0:T(8,128)S(1)} %get-tuple-element.40), channel_id=1, source_target_pairs={{0,4},{4,0},{8,12},{12,8},{16,20},{20,16},{24,28},{28,24},{1,5},{5... | collective-permute-start | bytes 122888 | tf_op jit(solution)/shard_map/ppermute | solution.py:19
  5.1 0.1 collective-permute-start
  5.2 1.9 %collective-permute-done.2 = f32[16,640]{1,0:T(8,128)S(1)} collective-permute-done((f32[16,640]{1,0:T(8,128)S(1)}, f32[16,640]{1,0:T(8,128)S(1)}, u32[]{:S(2)}, u32[]{:S(2)}) %collective-permute-start.2) | collective-permute-done | bytes 40992 | tf_op jit(solution)/shard_map/ppermute | solution.py:19
  7.1 4.4 %collective-permute-start.5 = (f32[16,640]{1,0:T(8,128)S(1)}, f32[16,640]{1,0:T(8,128)S(1)}, u32[]{:S(2)}, u32[]{:S(2)}) collective-permute-start(f32[16,640]{1,0:T(8,128)S(1)} %add.9.refs_0_), channel_id=1, source_target_pairs={{0,24},{4,28},{8,16},{12,20},{16,8},{20,12},{24,0},{28,4},{1,25},{... | collective-permute-start | bytes 122888 | tf_op jit(solution)/shard_map/ppermute | solution.py:19
  11.5 0.0 collective-permute-start.4
  11.5 0.6 %collective-permute-start.3 = (f32[16,640]{1,0:T(8,128)S(1)}, f32[16,640]{1,0:T(8,128)S(1)}, u32[]{:S(2)}, u32[]{:S(2)}) collective-permute-start(f32[16,640]{1,0:T(8,128)S(1)} %add.9.refs_0_), channel_id=1, source_target_pairs={{0,8},{4,12},{8,0},{12,4},{16,24},{20,28},{24,16},{28,20},{1,9},{5... | collective-permute-start | bytes 122888 | tf_op jit(solution)/shard_map/ppermute | solution.py:19
  12.2 1.6 %collective-permute-start.1 = (bf16[256,512]{1,0:T(8,128)(2,1)S(1)}, bf16[256,512]{1,0:T(8,128)(2,1)S(1)}, u32[]{:S(2)}, u32[]{:S(2)}) collective-permute-start(bf16[256,512]{1,0:T(8,128)(2,1)S(1)} %bitcast.5), channel_id=1, source_target_pairs={{0,2},{1,3},{2,0},{3,1},{4,6},{5,7},{6,4},{7,5},{8,10},{9,11},{10,... | collective-permute-start | bytes 786440 | tf_op jit(solution)/shard_map/ppermute | solution.py:494
  13.8 0.2 maps.1
  14.1 0.0 collective-permute-done.5.refs_3_
  14.1 2.4 %collective-permute-done.4.refs_2_ = f32[16,640]{1,0:T(8,128)S(1)} collective-permute-done((f32[16,640]{1,0:T(8,128)S(1)}, f32[16,640]{1,0:T(8,128)S(1)}, u32[]{:S(2)}, u32[]{:S(2)}) %collective-permute-start.4) | collective-permute-done | bytes 40992 | tf_op jit(solution)/shard_map/ppermute | solution.py:19
  16.4 0.0 collective-permute-done.3.refs_1_
  16.4 0.8 %first.1 = (f32[16,1024]{1,0:T(8,128)S(1)}, f32[16,1024]{1,0:T(8,128)S(1)}, f32[16,640]{1,0:T(8,128)S(1)}, bf16[16,1536]{1,0:T(8,128)(2,1)S(1)}) custom-call(f32[16,640]{1,0:T(8,128)S(1)} %add.9.refs_0_, f32[16,640]{1,0:T(8,128)S(1)} %collective-permute-done.3.refs_1_, f32[16,640]{1,0:T(8,128)S(1)} %collective-permute-done.4.refs_2_, ...), custom_call_target="tpu_custom_call" | custom-call | flops 2000000000 | bytes 4000000 | tf_op jit(solution)/shard_map/first/pallas_call | solution.py:527
  17.3 1.7 %collective-permute-start.6 = (bf16[16,1536]{1,0:T(8,128)(2,1)S(1)}, bf16[16,1536]{1,0:T(8,128)(2,1)S(1)}, u32[]{:S(2)}, u32[]{:S(2)}) collective-permute-start(bf16[16,1536]{1,0:T(8,128)(2,1)S(1)} %get-tuple-element.46.send_ref.refs_0_), channel_id=1, source_target_pairs={{0,4},{4,0},{8,12},{12,8},{16,20},{20,16},{24,28},{28,24},{1,5},{5... | collective-permute-start | bytes 147464 | tf_op jit(solution)/shard_map/ppermute | solution.py:19
  18.9 2.5 %collective-permute-done.6.near_ref.refs_1_ = bf16[16,1536]{1,0:T(8,128)(2,1)S(1)} collective-permute-done((bf16[16,1536]{1,0:T(8,128)(2,1)S(1)}, bf16[16,1536]{1,0:T(8,128)(2,1)S(1)}, u32[]{:S(2)}, u32[]{:S(2)}) %collective-permute-start.6) | collective-permute-done | bytes 49184 | tf_op jit(solution)/shard_map/ppermute | solution.py:19
  21.4 1.5 %collective-permute-start.10 = (bf16[16,1536]{1,0:T(8,128)(2,1)S(1)}, bf16[16,1536]{1,0:T(8,128)(2,1)S(1)}, u32[]{:S(2)}, u32[]{:S(2)}) collective-permute-start(bf16[16,1536]{1,0:T(8,128)(2,1)S(1)} %get-tuple-element.50), channel_id=1, source_target_pairs={{0,24},{4,28},{8,16},{12,20},{16,8},{20,12},{24,0},{28,4},{1,25},{... | collective-permute-start | bytes 147464 | tf_op jit(solution)/shard_map/ppermute | solution.py:19
  22.8 1.1 %collective-permute-start.8 = (bf16[16,1536]{1,0:T(8,128)(2,1)S(1)}, bf16[16,1536]{1,0:T(8,128)(2,1)S(1)}, u32[]{:S(2)}, u32[]{:S(2)}) collective-permute-start(bf16[16,1536]{1,0:T(8,128)(2,1)S(1)} %get-tuple-element.50), channel_id=1, source_target_pairs={{0,8},{4,12},{8,0},{12,4},{16,24},{20,28},{24,16},{28,20},{1,9},{5... | collective-permute-start | bytes 147464 | tf_op jit(solution)/shard_map/ppermute | solution.py:19
  24.0 0.0 collective-permute-start.11
  24.0 0.0 collective-permute-done.1.refs_14_.refs_12_
  24.0 1.8 %collective-permute-start.9 = (bf16[16,512]{1,0:T(8,128)(2,1)S(1)}, bf16[16,512]{1,0:T(8,128)(2,1)S(1)}, u32[]{:S(2)}, u32[]{:S(2)}) collective-permute-start(bf16[16,512]{1,0:T(8,128)(2,1)S(1)} %get-tuple-element.49.refs_0_), channel_id=1, source_target_pairs={{0,16},{4,20},{8,24},{12,28},{16,0},{20,4},{24,8},{28,12},{1,17},{... | collective-permute-start | bytes 49160 | tf_op jit(solution)/shard_map/ppermute | solution.py:19
  25.8 0.0 collective-permute-done.refs_0_.refs_12_
  25.8 0.2 collective-permute-start.12
  26.0 1.4 %collective-permute-done.10.refs_3_ = bf16[16,1536]{1,0:T(8,128)(2,1)S(1)} collective-permute-done((bf16[16,1536]{1,0:T(8,128)(2,1)S(1)}, bf16[16,1536]{1,0:T(8,128)(2,1)S(1)}, u32[]{:S(2)}, u32[]{:S(2)}) %collective-permute-start.10) | collective-permute-done | bytes 49184 | tf_op jit(solution)/shard_map/ppermute | solution.py:19
  27.4 0.0 collective-permute-start.18
  27.4 0.1 collective-permute-done.8.refs_2_.refs_1_
  27.5 1.5 %collective-permute-start.7 = (bf16[352,512]{1,0:T(8,128)(2,1)S(1)}, bf16[352,512]{1,0:T(8,128)(2,1)S(1)}, u32[]{:S(2)}, u32[]{:S(2)}) collective-permute-start(bf16[352,512]{1,0:T(8,128)(2,1)S(1)} %collective-permute-done.refs_0_.refs_12_), channel_id=1, source_target_pairs={{0,2},{1,3},{2,0},{3,1},{4,6},{5,7},{6,4},{7,5},{8,10},{9,11},{10,... | collective-permute-start | bytes 1081352 | tf_op jit(solution)/shard_map/ppermute | solution.py:494
  29.0 0.7 %near.2.refs_8_ = f32[16,1024]{1,0:T(8,128)S(1)} custom-call(bf16[16,1536]{1,0:T(8,128)(2,1)S(1)} %get-tuple-element.46.send_ref.refs_0_, bf16[16,1536]{1,0:T(8,128)(2,1)S(1)} %collective-permute-done.6.near_ref.refs_1_, bf16[16,1536]{1,0:T(8,128)(2,1)S(1)} %collective-permute-done.8.refs_2_.refs_1_, bf16[16,1536]{1,0:T(8,128)(2,1)S(1)} %collective-permute-done.10.refs_3_, ...), custom_call_target="tpu_custom_call" | custom-call | flops 10000000000 | bytes 20000000 | tf_op jit(solution)/shard_map/near/pallas_call | solution.py:527
  29.7 0.0 collective-permute-done.9.refs_2_
  29.7 0.0 collective-permute-done.11.refs_13_.refs_11_
  29.7 0.0 collective-permute-done.12.refs_15_.refs_13_
  29.7 1.4 %second.1 = (f32[16,1024]{1,0:T(8,128)S(1)}, f32[16,1024]{1,0:T(8,128)S(1)}, f32[16,640]{1,0:T(8,128)S(1)}) custom-call(bf16[16,512]{1,0:T(8,128)(2,1)S(1)} %get-tuple-element.49.refs_0_, bf16[16,1536]{1,0:T(8,128)(2,1)S(1)} %collective-permute-done.8.refs_2_.refs_1_, bf16[16,512]{1,0:T(8,128)(2,1)S(1)} %collective-permute-done.9.refs_2_, ...), custom_call_target="tpu_custom_call" | custom-call | flops 10000000000 | bytes 20000000 | tf_op jit(solution)/shard_map/second/pallas_call | solution.py:527
  31.2 1.7 %collective-permute-start.13 = (f32[16,640]{1,0:T(8,128)S(1)}, f32[16,640]{1,0:T(8,128)S(1)}, u32[]{:S(2)}, u32[]{:S(2)}) collective-permute-start(f32[16,640]{1,0:T(8,128)S(1)} %get-tuple-element.57), channel_id=1, source_target_pairs={{0,4},{4,0},{8,12},{12,8},{16,20},{20,16},{24,28},{28,24},{1,5},{5... | collective-permute-start | bytes 122888 | tf_op jit(solution)/shard_map/ppermute | solution.py:19
  32.9 0.4 collective-permute-start.17
  33.2 2.0 %collective-permute-done.13 = f32[16,640]{1,0:T(8,128)S(1)} collective-permute-done((f32[16,640]{1,0:T(8,128)S(1)}, f32[16,640]{1,0:T(8,128)S(1)}, u32[]{:S(2)}, u32[]{:S(2)}) %collective-permute-start.13) | collective-permute-done | bytes 40992 | tf_op jit(solution)/shard_map/ppermute | solution.py:19
  35.2 2.5 %collective-permute-start.16 = (f32[16,640]{1,0:T(8,128)S(1)}, f32[16,640]{1,0:T(8,128)S(1)}, u32[]{:S(2)}, u32[]{:S(2)}) collective-permute-start(f32[16,640]{1,0:T(8,128)S(1)} %add.10.refs_0_), channel_id=1, source_target_pairs={{0,24},{4,28},{8,16},{12,20},{16,8},{20,12},{24,0},{28,4},{1,25},{... | collective-permute-start | bytes 122888 | tf_op jit(solution)/shard_map/ppermute | solution.py:19
  37.7 0.0 collective-permute-start.15
  37.7 0.5 collective-permute-done.7.refs_2_.refs_14_
  38.2 1.4 %collective-permute-start.14 = (f32[16,640]{1,0:T(8,128)S(1)}, f32[16,640]{1,0:T(8,128)S(1)}, u32[]{:S(2)}, u32[]{:S(2)}) collective-permute-start(f32[16,640]{1,0:T(8,128)S(1)} %add.10.refs_0_), channel_id=1, source_target_pairs={{0,8},{4,12},{8,0},{12,4},{16,24},{20,28},{24,16},{28,20},{1,9},{5... | collective-permute-start | bytes 122888 | tf_op jit(solution)/shard_map/ppermute | solution.py:19
  39.6 0.0 collective-permute-done.18.refs_1_.refs_13_
  39.6 0.0 collective-permute-start.19
  39.6 0.2 other_maps.1.refs_16_
  39.8 0.0 collective-permute-done.17.refs_11_
  39.8 1.5 %collective-permute-done.16.refs_3_ = f32[16,640]{1,0:T(8,128)S(1)} collective-permute-done((f32[16,640]{1,0:T(8,128)S(1)}, f32[16,640]{1,0:T(8,128)S(1)}, u32[]{:S(2)}, u32[]{:S(2)}) %collective-permute-start.16) | collective-permute-done | bytes 40992 | tf_op jit(solution)/shard_map/ppermute | solution.py:19
  41.3 1.4 %collective-permute-done.15.refs_2_ = f32[16,640]{1,0:T(8,128)S(1)} collective-permute-done((f32[16,640]{1,0:T(8,128)S(1)}, f32[16,640]{1,0:T(8,128)S(1)}, u32[]{:S(2)}, u32[]{:S(2)}) %collective-permute-start.15) | collective-permute-done | bytes 40992 | tf_op jit(solution)/shard_map/ppermute | solution.py:19
  42.7 0.0 collective-permute-done.14.refs_1_
  42.7 0.0 collective-permute-done.19.refs_15_
  42.7 1.5 %third.1 = (bf16[16,1536]{1,0:T(8,128)(2,1)S(1)}, bf16[16,512]{1,0:T(8,128)(2,1)S(1)}, f32[16,1024]{1,0:T(8,128)S(1)}, f32[16,1024]{1,0:T(8,128)S(1)}, f32[16,12...) custom-call(f32[16,640]{1,0:T(8,128)S(1)} %add.10.refs_0_, f32[16,640]{1,0:T(8,128)S(1)} %collective-permute-done.14.refs_1_, ...), custom_call_target="tpu_custom_call" | custom-call | tf_op jit(solution)/shard_map/third/pallas_call | solution.py:527
  44.1 1.9 %collective-permute-start.22 = (bf16[16,1536]{1,0:T(8,128)(2,1)S(1)}, bf16[16,1536]{1,0:T(8,128)(2,1)S(1)}, u32[]{:S(2)}, u32[]{:S(2)}) collective-permute-start(bf16[16,1536]{1,0:T(8,128)(2,1)S(1)} %get-tuple-element.64.refs_1_), channel_id=1, source_target_pairs={{0,24},{4,28},{8,16},{12,20},{16,8},{20,12},{24,0},{28,4},{1,25},{... | collective-permute-start | bytes 147464 | tf_op jit(solution)/shard_map/ppermute | solution.py:19
  46.0 0.7 %collective-permute-start.20 = (bf16[16,1536]{1,0:T(8,128)(2,1)S(1)}, bf16[16,1536]{1,0:T(8,128)(2,1)S(1)}, u32[]{:S(2)}, u32[]{:S(2)}) collective-permute-start(bf16[16,1536]{1,0:T(8,128)(2,1)S(1)} %get-tuple-element.64.refs_1_), channel_id=1, source_target_pairs={{0,8},{4,12},{8,0},{12,4},{16,24},{20,28},{24,16},{28,20},{1,9},{5... | collective-permute-start | bytes 147464 | tf_op jit(solution)/shard_map/ppermute | solution.py:19
  46.7 1.8 %collective-permute-start.21 = (bf16[16,512]{1,0:T(8,128)(2,1)S(1)}, bf16[16,512]{1,0:T(8,128)(2,1)S(1)}, u32[]{:S(2)}, u32[]{:S(2)}) collective-permute-start(bf16[16,512]{1,0:T(8,128)(2,1)S(1)} %get-tuple-element.63.refs_0_), channel_id=1, source_target_pairs={{0,16},{4,20},{8,24},{12,28},{16,0},{20,4},{24,8},{28,12},{1,17},{... | collective-permute-start | bytes 49160 | tf_op jit(solution)/shard_map/ppermute | solution.py:19
  48.5 1.7 %collective-permute-done.22.refs_3_ = bf16[16,1536]{1,0:T(8,128)(2,1)S(1)} collective-permute-done((bf16[16,1536]{1,0:T(8,128)(2,1)S(1)}, bf16[16,1536]{1,0:T(8,128)(2,1)S(1)}, u32[]{:S(2)}, u32[]{:S(2)}) %collective-permute-start.22) | collective-permute-done | bytes 49184 | tf_op jit(solution)/shard_map/ppermute | solution.py:19
  50.2 0.4 collective-permute-done.20.refs_2_.refs_1_
  50.6 0.7 %near.3.refs_8_ = f32[16,1024]{1,0:T(8,128)S(1)} custom-call(bf16[16,1024]{1,0:T(8,128)(2,1)S(1)} %get-tuple-element.67.refs_0_, bf16[16,1536]{1,0:T(8,128)(2,1)S(1)} %get-tuple-element.64.refs_1_, bf16[16,1536]{1,0:T(8,128)(2,1)S(1)} %collective-permute-done.20.refs_2_.refs_1_, bf16[16,1536]{1,0:T(8,128)(2,1)S(1)} %collective-permute-done.22.refs_3_, ...), custom_call_target="tpu_custom_call" | custom-call | flops 10000000000 | bytes 20000000 | tf_op jit(solution)/shard_map/near/pallas_call | solution.py:527
  51.3 0.0 collective-permute-done.21.refs_2_
  51.3 0.8 %fourth.1 = f32[16,128]{1,0:T(8,128)S(1)} custom-call(bf16[16,512]{1,0:T(8,128)(2,1)S(1)} %get-tuple-element.63.refs_0_, bf16[16,1536]{1,0:T(8,128)(2,1)S(1)} %collective-permute-done.20.refs_2_.refs_1_, bf16[16,512]{1,0:T(8,128)(2,1)S(1)} %collective-permute-done.21.refs_2_, bf16[16,1536]{1,0:T(8,128)(2,1)S(1)} %collective-permute-done.22.refs_3_, ...), custom_call_target="tpu_custom_call" | custom-call | tf_op jit(solution)/shard_map/fourth/pallas_call | solution.py:527
  52.2 1.6 %collective-permute-start.23 = (f32[16,128]{1,0:T(8,128)S(1)}, f32[16,128]{1,0:T(8,128)S(1)}, u32[]{:S(2)}, u32[]{:S(2)}) collective-permute-start(f32[16,128]{1,0:T(8,128)S(1)} %fourth.1), channel_id=1, source_target_pairs={{0,4},{4,0},{8,12},{12,8},{16,20},{20,16},{24,28},{28,24},{1,5},{5... | collective-permute-start | bytes 24584 | tf_op jit(solution)/shard_map/ppermute | solution.py:19
  53.8 2.1 %collective-permute-done.23 = f32[16,128]{1,0:T(8,128)S(1)} collective-permute-done((f32[16,128]{1,0:T(8,128)S(1)}, f32[16,128]{1,0:T(8,128)S(1)}, u32[]{:S(2)}, u32[]{:S(2)}) %collective-permute-start.23) | collective-permute-done | bytes 8224 | tf_op jit(solution)/shard_map/ppermute | solution.py:19
  55.9 1.9 %collective-permute-start.26 = (f32[16,128]{1,0:T(8,128)S(1)}, f32[16,128]{1,0:T(8,128)S(1)}, u32[]{:S(2)}, u32[]{:S(2)}) collective-permute-start(f32[16,128]{1,0:T(8,128)S(1)} %add.11.refs_0_), channel_id=1, source_target_pairs={{0,24},{4,28},{8,16},{12,20},{16,8},{20,12},{24,0},{28,4},{1,25},{... | collective-permute-start | bytes 24584 | tf_op jit(solution)/shard_map/ppermute | solution.py:19
  57.8 0.9 %collective-permute-start.25 = (f32[16,128]{1,0:T(8,128)S(1)}, f32[16,128]{1,0:T(8,128)S(1)}, u32[]{:S(2)}, u32[]{:S(2)}) collective-permute-start(f32[16,128]{1,0:T(8,128)S(1)} %add.11.refs_0_), channel_id=1, source_target_pairs={{0,16},{4,20},{8,24},{12,28},{16,0},{20,4},{24,8},{28,12},{1,17},{... | collective-permute-start | bytes 24584 | tf_op jit(solution)/shard_map/ppermute | solution.py:19
  58.7 1.6 %collective-permute-start.24 = (f32[16,128]{1,0:T(8,128)S(1)}, f32[16,128]{1,0:T(8,128)S(1)}, u32[]{:S(2)}, u32[]{:S(2)}) collective-permute-start(f32[16,128]{1,0:T(8,128)S(1)} %add.11.refs_0_), channel_id=1, source_target_pairs={{0,8},{4,12},{8,0},{12,4},{16,24},{20,28},{24,16},{28,20},{1,9},{5... | collective-permute-start | bytes 24584 | tf_op jit(solution)/shard_map/ppermute | solution.py:19
  60.3 1.1 %collective-permute-done.26.refs_3_ = f32[16,128]{1,0:T(8,128)S(1)} collective-permute-done((f32[16,128]{1,0:T(8,128)S(1)}, f32[16,128]{1,0:T(8,128)S(1)}, u32[]{:S(2)}, u32[]{:S(2)}) %collective-permute-start.26) | collective-permute-done | bytes 8224 | tf_op jit(solution)/shard_map/ppermute | solution.py:19
  61.3 1.1 %collective-permute-done.25.refs_2_ = f32[16,128]{1,0:T(8,128)S(1)} collective-permute-done((f32[16,128]{1,0:T(8,128)S(1)}, f32[16,128]{1,0:T(8,128)S(1)}, u32[]{:S(2)}, u32[]{:S(2)}) %collective-permute-start.25) | collective-permute-done | bytes 8224 | tf_op jit(solution)/shard_map/ppermute | solution.py:19
  62.4 0.0 collective-permute-done.24.refs_1_
  62.4 1.0 %last.1 = f32[16,1024]{1,0:T(8,128)} custom-call(f32[16,128]{1,0:T(8,128)S(1)} %add.11.refs_0_, f32[16,128]{1,0:T(8,128)S(1)} %collective-permute-done.24.refs_1_, f32[16,128]{1,0:T(8,128)S(1)} %collective-permute-done.25.refs_2_, f32[16,128]{1,0:T(8,128)S(1)} %collective-permute-done.26.refs_3_, f32[16,128]{1,0:T(8,128)S(1)} %get-tuple-element.68.refs_4_, ...), custom_call_target="tpu_custom_call" | custom-call | tf_op jit(solution)/shard_map/last/pallas_call | solution.py:527
  (16 shorter events, 0.0 us)
Async XLA Ops:
  0.0 13.8 %copy-start.2 = (s32[8,32]{1,0:T(8,128)S(1)}, s32[8,32]{1,0:T(8,128)}, u32[]{:S(2)}) copy-start(s32[8,32]{1,0:T(8,128)} %refs_3_.1) | copy-start | bytes 3076
  0.0 13.8 %copy-start.1 = (bf16[8,128,32]{1,2,0:T(8,128)(2,1)S(1)}, bf16[8,128,32]{1,2,0:T(8,128)(2,1)}, u32[]{:S(2)}) copy-start(bf16[8,128,32]{1,2,0:T(8,128)(2,1)} %param.15) | copy-start | bytes 196612
  0.0 12.2 %copy-start = (bf16[256,1,512]{2,0,1:T(8,128)(2,1)S(1)}, bf16[256,1,512]{2,0,1:T(8,128)(2,1)}, u32[]{:S(2)}) copy-start(bf16[256,1,512]{2,0,1:T(8,128)(2,1)} %param.17) | copy-start | bytes 786436
  0.0 13.8 %copy-start.4 = (s32[8]{0:T(128)S(1)}, s32[8]{0:T(128)}, u32[]{:S(2)}) copy-start(s32[8]{0:T(128)} %param.14) | copy-start | bytes 100
  0.0 13.8 %copy-start.3 = (s32[8,8]{1,0:T(8,128)S(1)}, s32[8,8]{1,0:T(8,128)}, u32[]{:S(2)}) copy-start(s32[8,8]{1,0:T(8,128)} %refs_0_.3) | copy-start | bytes 772
  2.0 5.0 %collective-permute-start.2 = (f32[16,640]{1,0:T(8,128)S(1)}, f32[16,640]{1,0:T(8,128)S(1)}, u32[]{:S(2)}, u32[]{:S(2)}) collective-permute-start(f32[16,640]{1,0:T(8,128)S(1)} %get-tuple-element.40), channel_id=1, source_target_pairs={{0,4},{4,0},{8,12},{12,8},{16,20},{20,16},{24,28},{28,24},{1,5},{5... | collective-permute-start | bytes 122888 | tf_op jit(solution)/shard_map/ppermute | solution.py:19
  5.1 20.7 %collective-permute-start = (bf16[352,512]{1,0:T(8,128)(2,1)S(1)}, bf16[352,512]{1,0:T(8,128)(2,1)S(1)}, u32[]{:S(2)}, u32[]{:S(2)}) collective-permute-start(bf16[352,512]{1,0:T(8,128)(2,1)S(1)} %get-tuple-element.37), channel_id=1, source_target_pairs={{0,4},{4,0},{8,12},{12,8},{16,20},{20,16},{24,28},{28,24},{1,5},{5... | collective-permute-start | bytes 1081352 | tf_op jit(solution)/shard_map/ppermute | solution.py:19
  7.1 7.0 %collective-permute-start.5 = (f32[16,640]{1,0:T(8,128)S(1)}, f32[16,640]{1,0:T(8,128)S(1)}, u32[]{:S(2)}, u32[]{:S(2)}) collective-permute-start(f32[16,640]{1,0:T(8,128)S(1)} %add.9.refs_0_), channel_id=1, source_target_pairs={{0,24},{4,28},{8,16},{12,20},{16,8},{20,12},{24,0},{28,4},{1,25},{... | collective-permute-start | bytes 122888 | tf_op jit(solution)/shard_map/ppermute | solution.py:19
  11.5 4.9 %collective-permute-start.4 = (f32[16,640]{1,0:T(8,128)S(1)}, f32[16,640]{1,0:T(8,128)S(1)}, u32[]{:S(2)}, u32[]{:S(2)}) collective-permute-start(f32[16,640]{1,0:T(8,128)S(1)} %add.9.refs_0_), channel_id=1, source_target_pairs={{0,16},{4,20},{8,24},{12,28},{16,0},{20,4},{24,8},{28,12},{1,17},{... | collective-permute-start | bytes 122888 | tf_op jit(solution)/shard_map/ppermute | solution.py:19
  11.5 4.9 %collective-permute-start.3 = (f32[16,640]{1,0:T(8,128)S(1)}, f32[16,640]{1,0:T(8,128)S(1)}, u32[]{:S(2)}, u32[]{:S(2)}) collective-permute-start(f32[16,640]{1,0:T(8,128)S(1)} %add.9.refs_0_), channel_id=1, source_target_pairs={{0,8},{4,12},{8,0},{12,4},{16,24},{20,28},{24,16},{28,20},{1,9},{5... | collective-permute-start | bytes 122888 | tf_op jit(solution)/shard_map/ppermute | solution.py:19
  12.2 11.8 %collective-permute-start.1 = (bf16[256,512]{1,0:T(8,128)(2,1)S(1)}, bf16[256,512]{1,0:T(8,128)(2,1)S(1)}, u32[]{:S(2)}, u32[]{:S(2)}) collective-permute-start(bf16[256,512]{1,0:T(8,128)(2,1)S(1)} %bitcast.5), channel_id=1, source_target_pairs={{0,2},{1,3},{2,0},{3,1},{4,6},{5,7},{6,4},{7,5},{8,10},{9,11},{10,... | collective-permute-start | bytes 786440 | tf_op jit(solution)/shard_map/ppermute | solution.py:494
  16.4 12.5 %copy-start.5 = (bf16[8,8,128,128]{3,2,1,0:T(8,128)(2,1)S(1)}, bf16[8,8,128,128]{3,2,1,0:T(8,128)(2,1)}, u32[]{:S(2)}) copy-start(bf16[8,8,128,128]{3,2,1,0:T(8,128)(2,1)} %refs_5_.5) | copy-start | bytes 6291460
  17.3 4.1 %collective-permute-start.6 = (bf16[16,1536]{1,0:T(8,128)(2,1)S(1)}, bf16[16,1536]{1,0:T(8,128)(2,1)S(1)}, u32[]{:S(2)}, u32[]{:S(2)}) collective-permute-start(bf16[16,1536]{1,0:T(8,128)(2,1)S(1)} %get-tuple-element.46.send_ref.refs_0_), channel_id=1, source_target_pairs={{0,4},{4,0},{8,12},{12,8},{16,20},{20,16},{24,28},{28,24},{1,5},{5... | collective-permute-start | bytes 147464 | tf_op jit(solution)/shard_map/ppermute | solution.py:19
  21.4 6.0 %collective-permute-start.10 = (bf16[16,1536]{1,0:T(8,128)(2,1)S(1)}, bf16[16,1536]{1,0:T(8,128)(2,1)S(1)}, u32[]{:S(2)}, u32[]{:S(2)}) collective-permute-start(bf16[16,1536]{1,0:T(8,128)(2,1)S(1)} %get-tuple-element.50), channel_id=1, source_target_pairs={{0,24},{4,28},{8,16},{12,20},{16,8},{20,12},{24,0},{28,4},{1,25},{... | collective-permute-start | bytes 147464 | tf_op jit(solution)/shard_map/ppermute | solution.py:19
  22.8 4.6 %collective-permute-start.8 = (bf16[16,1536]{1,0:T(8,128)(2,1)S(1)}, bf16[16,1536]{1,0:T(8,128)(2,1)S(1)}, u32[]{:S(2)}, u32[]{:S(2)}) collective-permute-start(bf16[16,1536]{1,0:T(8,128)(2,1)S(1)} %get-tuple-element.50), channel_id=1, source_target_pairs={{0,8},{4,12},{8,0},{12,4},{16,24},{20,28},{24,16},{28,20},{1,9},{5... | collective-permute-start | bytes 147464 | tf_op jit(solution)/shard_map/ppermute | solution.py:19
  24.0 5.7 %collective-permute-start.11 = (bf16[256,512]{1,0:T(8,128)(2,1)S(1)}, bf16[256,512]{1,0:T(8,128)(2,1)S(1)}, u32[]{:S(2)}, u32[]{:S(2)}) collective-permute-start(bf16[256,512]{1,0:T(8,128)(2,1)S(1)} %bitcast.6), channel_id=1, source_target_pairs={{0,1},{1,0},{2,3},{3,2},{4,5},{5,4},{6,7},{7,6},{8,9},{9,8},{10,11... | collective-permute-start | bytes 786440 | tf_op jit(solution)/shard_map/ppermute | solution.py:494
  24.0 5.7 %collective-permute-start.9 = (bf16[16,512]{1,0:T(8,128)(2,1)S(1)}, bf16[16,512]{1,0:T(8,128)(2,1)S(1)}, u32[]{:S(2)}, u32[]{:S(2)}) collective-permute-start(bf16[16,512]{1,0:T(8,128)(2,1)S(1)} %get-tuple-element.49.refs_0_), channel_id=1, source_target_pairs={{0,16},{4,20},{8,24},{12,28},{16,0},{20,4},{24,8},{28,12},{1,17},{... | collective-permute-start | bytes 49160 | tf_op jit(solution)/shard_map/ppermute | solution.py:19
  25.8 4.0 %collective-permute-start.12 = (bf16[256,512]{1,0:T(8,128)(2,1)S(1)}, bf16[256,512]{1,0:T(8,128)(2,1)S(1)}, u32[]{:S(2)}, u32[]{:S(2)}) collective-permute-start(bf16[256,512]{1,0:T(8,128)(2,1)S(1)} %collective-permute-done.1.refs_14_.refs_12_), channel_id=1, source_target_pairs={{0,1},{1,0},{2,3},{3,2},{4,5},{5,4},{6,7},{7,6},{8,9},{9,8},{10,11... | collective-permute-start | bytes 786440 | tf_op jit(solution)/shard_map/ppermute | solution.py:501
  27.4 12.2 %collective-permute-start.18 = (bf16[352,512]{1,0:T(8,128)(2,1)S(1)}, bf16[352,512]{1,0:T(8,128)(2,1)S(1)}, u32[]{:S(2)}, u32[]{:S(2)}) collective-permute-start(bf16[352,512]{1,0:T(8,128)(2,1)S(1)} %collective-permute-done.refs_0_.refs_12_), channel_id=1, source_target_pairs={{0,1},{1,0},{2,3},{3,2},{4,5},{5,4},{6,7},{7,6},{8,9},{9,8},{10,11... | collective-permute-start | bytes 1081352 | tf_op jit(solution)/shard_map/ppermute | solution.py:494
  27.5 10.8 %collective-permute-start.7 = (bf16[352,512]{1,0:T(8,128)(2,1)S(1)}, bf16[352,512]{1,0:T(8,128)(2,1)S(1)}, u32[]{:S(2)}, u32[]{:S(2)}) collective-permute-start(bf16[352,512]{1,0:T(8,128)(2,1)S(1)} %collective-permute-done.refs_0_.refs_12_), channel_id=1, source_target_pairs={{0,2},{1,3},{2,0},{3,1},{4,6},{5,7},{6,4},{7,5},{8,10},{9,11},{10,... | collective-permute-start | bytes 1081352 | tf_op jit(solution)/shard_map/ppermute | solution.py:494
  31.2 4.0 %collective-permute-start.13 = (f32[16,640]{1,0:T(8,128)S(1)}, f32[16,640]{1,0:T(8,128)S(1)}, u32[]{:S(2)}, u32[]{:S(2)}) collective-permute-start(f32[16,640]{1,0:T(8,128)S(1)} %get-tuple-element.57), channel_id=1, source_target_pairs={{0,4},{4,0},{8,12},{12,8},{16,20},{20,16},{24,28},{28,24},{1,5},{5... | collective-permute-start | bytes 122888 | tf_op jit(solution)/shard_map/ppermute | solution.py:19
  32.9 6.9 %collective-permute-start.17 = (f32[16,1024]{1,0:T(8,128)S(1)}, f32[16,1024]{1,0:T(8,128)S(1)}, u32[]{:S(2)}, u32[]{:S(2)}) collective-permute-start(f32[16,1024]{1,0:T(8,128)S(1)} %get-tuple-element.61), channel_id=1, source_target_pairs={{0,4},{4,0},{8,12},{12,8},{16,20},{20,16},{24,28},{28,24},{1,5},{5... | collective-permute-start | bytes 196616 | tf_op jit(solution)/shard_map/ppermute | solution.py:19
  35.2 6.1 %collective-permute-start.16 = (f32[16,640]{1,0:T(8,128)S(1)}, f32[16,640]{1,0:T(8,128)S(1)}, u32[]{:S(2)}, u32[]{:S(2)}) collective-permute-start(f32[16,640]{1,0:T(8,128)S(1)} %add.10.refs_0_), channel_id=1, source_target_pairs={{0,24},{4,28},{8,16},{12,20},{16,8},{20,12},{24,0},{28,4},{1,25},{... | collective-permute-start | bytes 122888 | tf_op jit(solution)/shard_map/ppermute | solution.py:19
  37.7 4.9 %collective-permute-start.15 = (f32[16,640]{1,0:T(8,128)S(1)}, f32[16,640]{1,0:T(8,128)S(1)}, u32[]{:S(2)}, u32[]{:S(2)}) collective-permute-start(f32[16,640]{1,0:T(8,128)S(1)} %add.10.refs_0_), channel_id=1, source_target_pairs={{0,16},{4,20},{8,24},{12,28},{16,0},{20,4},{24,8},{28,12},{1,17},{... | collective-permute-start | bytes 122888 | tf_op jit(solution)/shard_map/ppermute | solution.py:19
  38.2 4.4 %collective-permute-start.14 = (f32[16,640]{1,0:T(8,128)S(1)}, f32[16,640]{1,0:T(8,128)S(1)}, u32[]{:S(2)}, u32[]{:S(2)}) collective-permute-start(f32[16,640]{1,0:T(8,128)S(1)} %add.10.refs_0_), channel_id=1, source_target_pairs={{0,8},{4,12},{8,0},{12,4},{16,24},{20,28},{24,16},{28,20},{1,9},{5... | collective-permute-start | bytes 122888 | tf_op jit(solution)/shard_map/ppermute | solution.py:19
  39.6 3.1 %collective-permute-start.19 = (bf16[352,512]{1,0:T(8,128)(2,1)S(1)}, bf16[352,512]{1,0:T(8,128)(2,1)S(1)}, u32[]{:S(2)}, u32[]{:S(2)}) collective-permute-start(bf16[352,512]{1,0:T(8,128)(2,1)S(1)} %collective-permute-done.7.refs_2_.refs_14_), channel_id=1, source_target_pairs={{0,1},{1,0},{2,3},{3,2},{4,5},{5,4},{6,7},{7,6},{8,9},{9,8},{10,11... | collective-permute-start | bytes 1081352 | tf_op jit(solution)/shard_map/ppermute | solution.py:501
  44.1 6.1 %collective-permute-start.22 = (bf16[16,1536]{1,0:T(8,128)(2,1)S(1)}, bf16[16,1536]{1,0:T(8,128)(2,1)S(1)}, u32[]{:S(2)}, u32[]{:S(2)}) collective-permute-start(bf16[16,1536]{1,0:T(8,128)(2,1)S(1)} %get-tuple-element.64.refs_1_), channel_id=1, source_target_pairs={{0,24},{4,28},{8,16},{12,20},{16,8},{20,12},{24,0},{28,4},{1,25},{... | collective-permute-start | bytes 147464 | tf_op jit(solution)/shard_map/ppermute | solution.py:19
  46.0 4.5 %collective-permute-start.20 = (bf16[16,1536]{1,0:T(8,128)(2,1)S(1)}, bf16[16,1536]{1,0:T(8,128)(2,1)S(1)}, u32[]{:S(2)}, u32[]{:S(2)}) collective-permute-start(bf16[16,1536]{1,0:T(8,128)(2,1)S(1)} %get-tuple-element.64.refs_1_), channel_id=1, source_target_pairs={{0,8},{4,12},{8,0},{12,4},{16,24},{20,28},{24,16},{28,20},{1,9},{5... | collective-permute-start | bytes 147464 | tf_op jit(solution)/shard_map/ppermute | solution.py:19
  46.7 4.6 %collective-permute-start.21 = (bf16[16,512]{1,0:T(8,128)(2,1)S(1)}, bf16[16,512]{1,0:T(8,128)(2,1)S(1)}, u32[]{:S(2)}, u32[]{:S(2)}) collective-permute-start(bf16[16,512]{1,0:T(8,128)(2,1)S(1)} %get-tuple-element.63.refs_0_), channel_id=1, source_target_pairs={{0,16},{4,20},{8,24},{12,28},{16,0},{20,4},{24,8},{28,12},{1,17},{... | collective-permute-start | bytes 49160 | tf_op jit(solution)/shard_map/ppermute | solution.py:19
  52.2 3.7 %collective-permute-start.23 = (f32[16,128]{1,0:T(8,128)S(1)}, f32[16,128]{1,0:T(8,128)S(1)}, u32[]{:S(2)}, u32[]{:S(2)}) collective-permute-start(f32[16,128]{1,0:T(8,128)S(1)} %fourth.1), channel_id=1, source_target_pairs={{0,4},{4,0},{8,12},{12,8},{16,20},{20,16},{24,28},{28,24},{1,5},{5... | collective-permute-start | bytes 24584 | tf_op jit(solution)/shard_map/ppermute | solution.py:19
  55.9 5.4 %collective-permute-start.26 = (f32[16,128]{1,0:T(8,128)S(1)}, f32[16,128]{1,0:T(8,128)S(1)}, u32[]{:S(2)}, u32[]{:S(2)}) collective-permute-start(f32[16,128]{1,0:T(8,128)S(1)} %add.11.refs_0_), channel_id=1, source_target_pairs={{0,24},{4,28},{8,16},{12,20},{16,8},{20,12},{24,0},{28,4},{1,25},{... | collective-permute-start | bytes 24584 | tf_op jit(solution)/shard_map/ppermute | solution.py:19
  57.8 4.7 %collective-permute-start.25 = (f32[16,128]{1,0:T(8,128)S(1)}, f32[16,128]{1,0:T(8,128)S(1)}, u32[]{:S(2)}, u32[]{:S(2)}) collective-permute-start(f32[16,128]{1,0:T(8,128)S(1)} %add.11.refs_0_), channel_id=1, source_target_pairs={{0,16},{4,20},{8,24},{12,28},{16,0},{20,4},{24,8},{28,12},{1,17},{... | collective-permute-start | bytes 24584 | tf_op jit(solution)/shard_map/ppermute | solution.py:19
  58.7 3.7 %collective-permute-start.24 = (f32[16,128]{1,0:T(8,128)S(1)}, f32[16,128]{1,0:T(8,128)S(1)}, u32[]{:S(2)}, u32[]{:S(2)}) collective-permute-start(f32[16,128]{1,0:T(8,128)S(1)} %add.11.refs_0_), channel_id=1, source_target_pairs={{0,8},{4,12},{8,0},{12,4},{16,24},{20,28},{24,16},{28,20},{1,9},{5... | collective-permute-start | bytes 24584 | tf_op jit(solution)/shard_map/ppermute | solution.py:19

commit v7 on v6

--- a/solution.py
+++ b/solution.py
@@ -598,7 +598,8 @@
     fields, charges, starts = exchange(send, panels, count)
     full_rows, fields[1] = finish_quarters(some_rows, quarters, fields[1])
     if paired:
-        mine, fields[1] = gather_quarters(mine, quarters, count, fields[1])
+        mine, fields[1] = lax.optimization_barrier((mine, fields[1]))
+        far = lax.ppermute(mine, "rhs", [(i, i ^ 2) for i in range(quarters)])
 
     def near_product(fields):
         (near,) = call(
@@ -621,12 +622,18 @@
         scratch,
         flops=10**10,
     )
+    if paired:
+        mine, payload = lax.optimization_barrier((mine, payload))
     sums = sum_parts(payload, count)
     outs = [((rows, panels), F32), ((rows, panels), F32), ((rows, LANES), F32)]
     extra = []
     if paired:
         again = swap(scaled, 1, count)
-        mine, sums[0] = finish_quarters(mine, quarters, sums[0])
+        far, sums[0] = lax.optimization_barrier((far, sums[0]))
+        near_pack, last_pack = [
+            lax.ppermute(x, "rhs", [(i, i ^ 1) for i in range(quarters)]) for x in (mine, far)
+        ]
+        mine = [mine, near_pack, far, last_pack]
         (some_maps,) = call(
             "other_maps",
             lambda *refs: other_maps_kernel(panels // quarters, rank, block, *refs),

time: 63.5 us -> 62.9 us (level)
  waiting for transfers between devices: 19.8 us -> 18.2 us
  starting transfers between devices: 34 us -> 34.9 us
    ppermute x4 -> x2, starting transfers between devices: 3.14 us -> 1.64 us  [gather_quarters(): lax.ppermute(coupling, 'rhs', pair)]
    ppermute x0 -> x3, starting transfers between devices: none -> 1.5 us  [the longest x1 1.49 us: on_device(): far = lax.ppermute(mine, 'rhs', [(i, i ^ 2) for i in range(quarters)])]
    ppermute x21, waiting for transfers between devices: 19.3 us -> 18.2 us  [swap(): return lax.ppermute(values, AXIS, [(i, i ^ mask) for i in range(count)])]
    ppermute x21, starting transfers between devices: 30.6 us -> 31.5 us  [swap(): return lax.ppermute(values, AXIS, [(i, i ^ mask) for i in range(count)])]
  transfers between devices with their start and end apart: 27 -> 27, of which waited for: 14 -> 12; matrix products, arithmetic and copies ran while one was open for 0% -> 0% of each run, Pallas kernels for 7% -> 7%
where the time goes in v7:
time: 62.9 us; the launch traced here: 62.7 us
  starting transfers between devices  34.9 us (55%)
  waiting for transfers between devices  18.2 us (29%)
  Pallas kernels  9.49 us (15%)
    ppermute x21, starting transfers between devices, swap(): return lax.ppermute(values, AXIS, [(i, i ^ mask) for i in range(count)])  31.5 us
    ppermute x21, waiting for transfers between devices, swap(): return lax.ppermute(values, AXIS, [(i, i ^ mask) for i in range(count)])  18.2 us
    pallas_call x11, Pallas kernels, call(): pl.pallas_call(kernel, name=name, out_shape=out_shapes, in_specs=specs, o...  9.49 us
    ppermute x2, starting transfers between devices, gather_quarters(): lax.ppermute(coupling, 'rhs', pair)  1.64 us
    ppermute x1, starting transfers between devices, on_device(): far = lax.ppermute(mine, 'rhs', [(i, i ^ 2) for i in range(quarters)])  1.49 us
  transfers between devices with their start and end apart: 27, of which 12 were waited for; matrix products, arithmetic and copies ran while one was open for 0% of the time, Pallas kernels for 7%

profile of v7, /device:TPU:0, one launch (start us, length us, event | category | flops | bytes accessed | tf_op | source)
XLA Modules:
  0.0 62.7 jit_solution(7948259868817721056)
XLA Ops:
  0.0 2.0 %open.1 = (f32[16,640]{1,0:T(8,128)S(1)}, f32[16,1024]{1,0:T(8,128)S(1)}, f32[1,1024]{1,0:T(1,128)S(1)}, f32[1,1024]{1,0:T(1,128)S(1)}, bf16[1024,512]{1,0:T(8,1...) custom-call(f32[16,1024]{1,0:T(8,128)} %refs_0_.2, f32[1024,512]{1,0:T(8,128)} %refs_1_.1, ...), custom_call_target="tpu_custom_call" | custom-call | tf_op jit(solution)/shard_map/open/pallas_call | solution.py:527
  2.0 3.1 %collective-permute-start.2 = (f32[16,640]{1,0:T(8,128)S(1)}, f32[16,640]{1,0:T(8,128)S(1)}, u32[]{:S(2)}, u32[]{:S(2)}) collective-permute-start(f32[16,640]{1,0:T(8,128)S(1)} %get-tuple-element.42), channel_id=1, source_target_pairs={{0,4},{4,0},{8,12},{12,8},{16,20},{20,16},{24,28},{28,24},{1,5},{5... | collective-permute-start | bytes 122888 | tf_op jit(solution)/shard_map/ppermute | solution.py:19
  5.1 0.1 collective-permute-start
  5.2 1.9 %collective-permute-done.2 = f32[16,640]{1,0:T(8,128)S(1)} collective-permute-done((f32[16,640]{1,0:T(8,128)S(1)}, f32[16,640]{1,0:T(8,128)S(1)}, u32[]{:S(2)}, u32[]{:S(2)}) %collective-permute-start.2) | collective-permute-done | bytes 40992 | tf_op jit(solution)/shard_map/ppermute | solution.py:19
  7.1 4.4 %collective-permute-start.5 = (f32[16,640]{1,0:T(8,128)S(1)}, f32[16,640]{1,0:T(8,128)S(1)}, u32[]{:S(2)}, u32[]{:S(2)}) collective-permute-start(f32[16,640]{1,0:T(8,128)S(1)} %add.9.refs_0_), channel_id=1, source_target_pairs={{0,24},{4,28},{8,16},{12,20},{16,8},{20,12},{24,0},{28,4},{1,25},{... | collective-permute-start | bytes 122888 | tf_op jit(solution)/shard_map/ppermute | solution.py:19
  11.5 0.0 collective-permute-start.4
  11.5 0.6 %collective-permute-start.3 = (f32[16,640]{1,0:T(8,128)S(1)}, f32[16,640]{1,0:T(8,128)S(1)}, u32[]{:S(2)}, u32[]{:S(2)}) collective-permute-start(f32[16,640]{1,0:T(8,128)S(1)} %add.9.refs_0_), channel_id=1, source_target_pairs={{0,8},{4,12},{8,0},{12,4},{16,24},{20,28},{24,16},{28,20},{1,9},{5... | collective-permute-start | bytes 122888 | tf_op jit(solution)/shard_map/ppermute | solution.py:19
  12.2 1.6 %collective-permute-start.1 = (bf16[256,512]{1,0:T(8,128)(2,1)S(1)}, bf16[256,512]{1,0:T(8,128)(2,1)S(1)}, u32[]{:S(2)}, u32[]{:S(2)}) collective-permute-start(bf16[256,512]{1,0:T(8,128)(2,1)S(1)} %bitcast.5), channel_id=1, source_target_pairs={{0,2},{1,3},{2,0},{3,1},{4,6},{5,7},{6,4},{7,5},{8,10},{9,11},{10,... | collective-permute-start | bytes 786440 | tf_op jit(solution)/shard_map/ppermute | solution.py:494
  13.8 0.2 maps.1
  14.1 0.0 collective-permute-done.5.refs_3_
  14.1 2.4 %collective-permute-done.4.refs_2_ = f32[16,640]{1,0:T(8,128)S(1)} collective-permute-done((f32[16,640]{1,0:T(8,128)S(1)}, f32[16,640]{1,0:T(8,128)S(1)}, u32[]{:S(2)}, u32[]{:S(2)}) %collective-permute-start.4) | collective-permute-done | bytes 40992 | tf_op jit(solution)/shard_map/ppermute | solution.py:19
  16.4 0.0 collective-permute-done.3.refs_1_
  16.4 0.8 %first.1 = (f32[16,1024]{1,0:T(8,128)S(1)}, f32[16,1024]{1,0:T(8,128)S(1)}, f32[16,640]{1,0:T(8,128)S(1)}, bf16[16,1536]{1,0:T(8,128)(2,1)S(1)}) custom-call(f32[16,640]{1,0:T(8,128)S(1)} %add.9.refs_0_, f32[16,640]{1,0:T(8,128)S(1)} %collective-permute-done.3.refs_1_, f32[16,640]{1,0:T(8,128)S(1)} %collective-permute-done.4.refs_2_, ...), custom_call_target="tpu_custom_call" | custom-call | flops 2000000000 | bytes 4000000 | tf_op jit(solution)/shard_map/first/pallas_call | solution.py:527
  17.3 1.7 %collective-permute-start.6 = (bf16[16,1536]{1,0:T(8,128)(2,1)S(1)}, bf16[16,1536]{1,0:T(8,128)(2,1)S(1)}, u32[]{:S(2)}, u32[]{:S(2)}) collective-permute-start(bf16[16,1536]{1,0:T(8,128)(2,1)S(1)} %get-tuple-element.48.send_ref.refs_0_), channel_id=1, source_target_pairs={{0,4},{4,0},{8,12},{12,8},{16,20},{20,16},{24,28},{28,24},{1,5},{5... | collective-permute-start | bytes 147464 | tf_op jit(solution)/shard_map/ppermute | solution.py:19
  18.9 2.5 %collective-permute-done.6.near_ref.refs_1_ = bf16[16,1536]{1,0:T(8,128)(2,1)S(1)} collective-permute-done((bf16[16,1536]{1,0:T(8,128)(2,1)S(1)}, bf16[16,1536]{1,0:T(8,128)(2,1)S(1)}, u32[]{:S(2)}, u32[]{:S(2)}) %collective-permute-start.6) | collective-permute-done | bytes 49184 | tf_op jit(solution)/shard_map/ppermute | solution.py:19
  21.4 1.5 %collective-permute-start.10 = (bf16[16,1536]{1,0:T(8,128)(2,1)S(1)}, bf16[16,1536]{1,0:T(8,128)(2,1)S(1)}, u32[]{:S(2)}, u32[]{:S(2)}) collective-permute-start(bf16[16,1536]{1,0:T(8,128)(2,1)S(1)} %get-tuple-element.52), channel_id=1, source_target_pairs={{0,24},{4,28},{8,16},{12,20},{16,8},{20,12},{24,0},{28,4},{1,25},{... | collective-permute-start | bytes 147464 | tf_op jit(solution)/shard_map/ppermute | solution.py:19
  22.8 1.1 %collective-permute-start.8 = (bf16[16,1536]{1,0:T(8,128)(2,1)S(1)}, bf16[16,1536]{1,0:T(8,128)(2,1)S(1)}, u32[]{:S(2)}, u32[]{:S(2)}) collective-permute-start(bf16[16,1536]{1,0:T(8,128)(2,1)S(1)} %get-tuple-element.52), channel_id=1, source_target_pairs={{0,8},{4,12},{8,0},{12,4},{16,24},{20,28},{24,16},{28,20},{1,9},{5... | collective-permute-start | bytes 147464 | tf_op jit(solution)/shard_map/ppermute | solution.py:19
  24.0 0.0 collective-permute-start.11
  24.0 0.0 collective-permute-done.1.refs_14_.refs_12_
  24.0 1.8 %collective-permute-start.9 = (bf16[16,512]{1,0:T(8,128)(2,1)S(1)}, bf16[16,512]{1,0:T(8,128)(2,1)S(1)}, u32[]{:S(2)}, u32[]{:S(2)}) collective-permute-start(bf16[16,512]{1,0:T(8,128)(2,1)S(1)} %get-tuple-element.51.refs_0_), channel_id=1, source_target_pairs={{0,16},{4,20},{8,24},{12,28},{16,0},{20,4},{24,8},{28,12},{1,17},{... | collective-permute-start | bytes 49160 | tf_op jit(solution)/shard_map/ppermute | solution.py:19
  25.8 0.0 collective-permute-done.refs_0_.refs_12_
  25.8 0.2 collective-permute-start.12
  26.0 1.4 %collective-permute-done.10.refs_3_ = bf16[16,1536]{1,0:T(8,128)(2,1)S(1)} collective-permute-done((bf16[16,1536]{1,0:T(8,128)(2,1)S(1)}, bf16[16,1536]{1,0:T(8,128)(2,1)S(1)}, u32[]{:S(2)}, u32[]{:S(2)}) %collective-permute-start.10) | collective-permute-done | bytes 49184 | tf_op jit(solution)/shard_map/ppermute | solution.py:19
  27.4 1.5 %collective-permute-start.7 = (bf16[352,512]{1,0:T(8,128)(2,1)S(1)}, bf16[352,512]{1,0:T(8,128)(2,1)S(1)}, u32[]{:S(2)}, u32[]{:S(2)}) collective-permute-start(bf16[352,512]{1,0:T(8,128)(2,1)S(1)} %collective-permute-done.refs_0_.refs_12_), channel_id=1, source_target_pairs={{0,2},{1,3},{2,0},{3,1},{4,6},{5,7},{6,4},{7,5},{8,10},{9,11},{10,... | collective-permute-start | bytes 1081352 | tf_op jit(solution)/shard_map/ppermute | solution.py:602
  28.9 0.0 collective-permute-done.8.refs_2_.refs_1_
  28.9 0.7 %near.2.refs_8_ = f32[16,1024]{1,0:T(8,128)S(1)} custom-call(bf16[16,1536]{1,0:T(8,128)(2,1)S(1)} %get-tuple-element.48.send_ref.refs_0_, bf16[16,1536]{1,0:T(8,128)(2,1)S(1)} %collective-permute-done.6.near_ref.refs_1_, bf16[16,1536]{1,0:T(8,128)(2,1)S(1)} %collective-permute-done.8.refs_2_.refs_1_, bf16[16,1536]{1,0:T(8,128)(2,1)S(1)} %collective-permute-done.10.refs_3_, ...), custom_call_target="tpu_custom_call" | custom-call | flops 10000000000 | bytes 20000000 | tf_op jit(solution)/shard_map/near/pallas_call | solution.py:527
  29.6 0.0 collective-permute-done.9.refs_2_
  29.6 0.0 collective-permute-done.11.refs_13_.refs_11_
  29.6 0.0 collective-permute-done.12.refs_15_.refs_13_
  29.7 1.5 %second.1 = (f32[16,1024]{1,0:T(8,128)S(1)}, f32[16,1024]{1,0:T(8,128)S(1)}, f32[16,640]{1,0:T(8,128)S(1)}) custom-call(bf16[16,512]{1,0:T(8,128)(2,1)S(1)} %get-tuple-element.51.refs_0_, bf16[16,1536]{1,0:T(8,128)(2,1)S(1)} %collective-permute-done.8.refs_2_.refs_1_, bf16[16,512]{1,0:T(8,128)(2,1)S(1)} %collective-permute-done.9.refs_2_, ...), custom_call_target="tpu_custom_call" | custom-call | flops 10000000000 | bytes 20000000 | tf_op jit(solution)/shard_map/second/pallas_call | solution.py:527
  31.1 0.0 collective-permute-start.18
  31.1 1.7 %collective-permute-start.13 = (f32[16,640]{1,0:T(8,128)S(1)}, f32[16,640]{1,0:T(8,128)S(1)}, u32[]{:S(2)}, u32[]{:S(2)}) collective-permute-start(f32[16,640]{1,0:T(8,128)S(1)} %get-tuple-element.60), channel_id=1, source_target_pairs={{0,4},{4,0},{8,12},{12,8},{16,20},{20,16},{24,28},{28,24},{1,5},{5... | collective-permute-start | bytes 122888 | tf_op jit(solution)/shard_map/ppermute | solution.py:19
  32.8 0.4 collective-permute-start.17
  33.2 2.0 %collective-permute-done.13 = f32[16,640]{1,0:T(8,128)S(1)} collective-permute-done((f32[16,640]{1,0:T(8,128)S(1)}, f32[16,640]{1,0:T(8,128)S(1)}, u32[]{:S(2)}, u32[]{:S(2)}) %collective-permute-start.13) | collective-permute-done | bytes 40992 | tf_op jit(solution)/shard_map/ppermute | solution.py:19
  35.2 1.5 %collective-permute-start.16 = (f32[16,640]{1,0:T(8,128)S(1)}, f32[16,640]{1,0:T(8,128)S(1)}, u32[]{:S(2)}, u32[]{:S(2)}) collective-permute-start(f32[16,640]{1,0:T(8,128)S(1)} %add.10.refs_0_), channel_id=1, source_target_pairs={{0,24},{4,28},{8,16},{12,20},{16,8},{20,12},{24,0},{28,4},{1,25},{... | collective-permute-start | bytes 122888 | tf_op jit(solution)/shard_map/ppermute | solution.py:19
  36.6 0.0 collective-permute-start.15
  36.6 0.0 collective-permute-done.7.refs_2_.refs_14_
  36.6 2.9 %collective-permute-start.14 = (f32[16,640]{1,0:T(8,128)S(1)}, f32[16,640]{1,0:T(8,128)S(1)}, u32[]{:S(2)}, u32[]{:S(2)}) collective-permute-start(f32[16,640]{1,0:T(8,128)S(1)} %add.10.refs_0_), channel_id=1, source_target_pairs={{0,8},{4,12},{8,0},{12,4},{16,24},{20,28},{24,16},{28,20},{1,9},{5... | collective-permute-start | bytes 122888 | tf_op jit(solution)/shard_map/ppermute | solution.py:19
  39.6 0.0 collective-permute-done.18.refs_1_.refs_13_
  39.6 0.0 collective-permute-start.19
  39.6 0.2 other_maps.1.refs_16_
  39.7 0.0 collective-permute-done.17.refs_11_
  39.7 1.5 %collective-permute-done.16.refs_3_ = f32[16,640]{1,0:T(8,128)S(1)} collective-permute-done((f32[16,640]{1,0:T(8,128)S(1)}, f32[16,640]{1,0:T(8,128)S(1)}, u32[]{:S(2)}, u32[]{:S(2)}) %collective-permute-start.16) | collective-permute-done | bytes 40992 | tf_op jit(solution)/shard_map/ppermute | solution.py:19
  41.3 0.8 %collective-permute-done.15.refs_2_ = f32[16,640]{1,0:T(8,128)S(1)} collective-permute-done((f32[16,640]{1,0:T(8,128)S(1)}, f32[16,640]{1,0:T(8,128)S(1)}, u32[]{:S(2)}, u32[]{:S(2)}) %collective-permute-start.15) | collective-permute-done | bytes 40992 | tf_op jit(solution)/shard_map/ppermute | solution.py:19
  42.1 0.0 collective-permute-done.14.refs_1_
  42.1 0.0 collective-permute-done.19.refs_15_
  42.1 1.5 %third.1 = (bf16[16,1536]{1,0:T(8,128)(2,1)S(1)}, bf16[16,512]{1,0:T(8,128)(2,1)S(1)}, f32[16,1024]{1,0:T(8,128)S(1)}, f32[16,1024]{1,0:T(8,128)S(1)}, f32[16,12...) custom-call(f32[16,640]{1,0:T(8,128)S(1)} %add.10.refs_0_, f32[16,640]{1,0:T(8,128)S(1)} %collective-permute-done.14.refs_1_, ...), custom_call_target="tpu_custom_call" | custom-call | tf_op jit(solution)/shard_map/third/pallas_call | solution.py:527
  43.5 1.8 %collective-permute-start.22 = (bf16[16,1536]{1,0:T(8,128)(2,1)S(1)}, bf16[16,1536]{1,0:T(8,128)(2,1)S(1)}, u32[]{:S(2)}, u32[]{:S(2)}) collective-permute-start(bf16[16,1536]{1,0:T(8,128)(2,1)S(1)} %get-tuple-element.68.refs_1_), channel_id=1, source_target_pairs={{0,24},{4,28},{8,16},{12,20},{16,8},{20,12},{24,0},{28,4},{1,25},{... | collective-permute-start | bytes 147464 | tf_op jit(solution)/shard_map/ppermute | solution.py:19
  45.4 0.2 collective-permute-start.20
  45.6 2.3 %collective-permute-start.21 = (bf16[16,512]{1,0:T(8,128)(2,1)S(1)}, bf16[16,512]{1,0:T(8,128)(2,1)S(1)}, u32[]{:S(2)}, u32[]{:S(2)}) collective-permute-start(bf16[16,512]{1,0:T(8,128)(2,1)S(1)} %get-tuple-element.67.refs_0_), channel_id=1, source_target_pairs={{0,16},{4,20},{8,24},{12,28},{16,0},{20,4},{24,8},{28,12},{1,17},{... | collective-permute-start | bytes 49160 | tf_op jit(solution)/shard_map/ppermute | solution.py:19
  47.9 1.7 %collective-permute-done.22.refs_3_ = bf16[16,1536]{1,0:T(8,128)(2,1)S(1)} collective-permute-done((bf16[16,1536]{1,0:T(8,128)(2,1)S(1)}, bf16[16,1536]{1,0:T(8,128)(2,1)S(1)}, u32[]{:S(2)}, u32[]{:S(2)}) %collective-permute-start.22) | collective-permute-done | bytes 49184 | tf_op jit(solution)/shard_map/ppermute | solution.py:19
  49.6 0.3 collective-permute-done.20.refs_2_.refs_1_
  50.0 0.7 %near.3.refs_8_ = f32[16,1024]{1,0:T(8,128)S(1)} custom-call(bf16[16,1024]{1,0:T(8,128)(2,1)S(1)} %get-tuple-element.71.refs_0_, bf16[16,1536]{1,0:T(8,128)(2,1)S(1)} %get-tuple-element.68.refs_1_, bf16[16,1536]{1,0:T(8,128)(2,1)S(1)} %collective-permute-done.20.refs_2_.refs_1_, bf16[16,1536]{1,0:T(8,128)(2,1)S(1)} %collective-permute-done.22.refs_3_, ...), custom_call_target="tpu_custom_call" | custom-call | flops 10000000000 | bytes 20000000 | tf_op jit(solution)/shard_map/near/pallas_call | solution.py:527
  50.7 0.0 collective-permute-done.21.refs_2_
  50.7 0.9 %fourth.1 = f32[16,128]{1,0:T(8,128)S(1)} custom-call(bf16[16,512]{1,0:T(8,128)(2,1)S(1)} %get-tuple-element.67.refs_0_, bf16[16,1536]{1,0:T(8,128)(2,1)S(1)} %collective-permute-done.20.refs_2_.refs_1_, bf16[16,512]{1,0:T(8,128)(2,1)S(1)} %collective-permute-done.21.refs_2_, bf16[16,1536]{1,0:T(8,128)(2,1)S(1)} %collective-permute-done.22.refs_3_, ...), custom_call_target="tpu_custom_call" | custom-call | tf_op jit(solution)/shard_map/fourth/pallas_call | solution.py:527
  51.6 2.0 %collective-permute-start.23 = (f32[16,128]{1,0:T(8,128)S(1)}, f32[16,128]{1,0:T(8,128)S(1)}, u32[]{:S(2)}, u32[]{:S(2)}) collective-permute-start(f32[16,128]{1,0:T(8,128)S(1)} %fourth.1), channel_id=1, source_target_pairs={{0,4},{4,0},{8,12},{12,8},{16,20},{20,16},{24,28},{28,24},{1,5},{5... | collective-permute-start | bytes 24584 | tf_op jit(solution)/shard_map/ppermute | solution.py:19
  53.6 1.7 %collective-permute-done.23 = f32[16,128]{1,0:T(8,128)S(1)} collective-permute-done((f32[16,128]{1,0:T(8,128)S(1)}, f32[16,128]{1,0:T(8,128)S(1)}, u32[]{:S(2)}, u32[]{:S(2)}) %collective-permute-start.23) | collective-permute-done | bytes 8224 | tf_op jit(solution)/shard_map/ppermute | solution.py:19
  55.3 1.9 %collective-permute-start.26 = (f32[16,128]{1,0:T(8,128)S(1)}, f32[16,128]{1,0:T(8,128)S(1)}, u32[]{:S(2)}, u32[]{:S(2)}) collective-permute-start(f32[16,128]{1,0:T(8,128)S(1)} %add.11.refs_0_), channel_id=1, source_target_pairs={{0,24},{4,28},{8,16},{12,20},{16,8},{20,12},{24,0},{28,4},{1,25},{... | collective-permute-start | bytes 24584 | tf_op jit(solution)/shard_map/ppermute | solution.py:19
  57.1 0.9 %collective-permute-start.25 = (f32[16,128]{1,0:T(8,128)S(1)}, f32[16,128]{1,0:T(8,128)S(1)}, u32[]{:S(2)}, u32[]{:S(2)}) collective-permute-start(f32[16,128]{1,0:T(8,128)S(1)} %add.11.refs_0_), channel_id=1, source_target_pairs={{0,16},{4,20},{8,24},{12,28},{16,0},{20,4},{24,8},{28,12},{1,17},{... | collective-permute-start | bytes 24584 | tf_op jit(solution)/shard_map/ppermute | solution.py:19
  58.0 1.6 %collective-permute-start.24 = (f32[16,128]{1,0:T(8,128)S(1)}, f32[16,128]{1,0:T(8,128)S(1)}, u32[]{:S(2)}, u32[]{:S(2)}) collective-permute-start(f32[16,128]{1,0:T(8,128)S(1)} %add.11.refs_0_), channel_id=1, source_target_pairs={{0,8},{4,12},{8,0},{12,4},{16,24},{20,28},{24,16},{28,20},{1,9},{5... | collective-permute-start | bytes 24584 | tf_op jit(solution)/shard_map/ppermute | solution.py:19
  59.7 1.1 %collective-permute-done.26.refs_3_ = f32[16,128]{1,0:T(8,128)S(1)} collective-permute-done((f32[16,128]{1,0:T(8,128)S(1)}, f32[16,128]{1,0:T(8,128)S(1)}, u32[]{:S(2)}, u32[]{:S(2)}) %collective-permute-start.26) | collective-permute-done | bytes 8224 | tf_op jit(solution)/shard_map/ppermute | solution.py:19
  60.7 1.0 %collective-permute-done.25.refs_2_ = f32[16,128]{1,0:T(8,128)S(1)} collective-permute-done((f32[16,128]{1,0:T(8,128)S(1)}, f32[16,128]{1,0:T(8,128)S(1)}, u32[]{:S(2)}, u32[]{:S(2)}) %collective-permute-start.25) | collective-permute-done | bytes 8224 | tf_op jit(solution)/shard_map/ppermute | solution.py:19
  61.8 0.0 collective-permute-done.24.refs_1_
  61.8 1.0 %last.1 = f32[16,1024]{1,0:T(8,128)} custom-call(f32[16,128]{1,0:T(8,128)S(1)} %add.11.refs_0_, f32[16,128]{1,0:T(8,128)S(1)} %collective-permute-done.24.refs_1_, f32[16,128]{1,0:T(8,128)S(1)} %collective-permute-done.25.refs_2_, f32[16,128]{1,0:T(8,128)S(1)} %collective-permute-done.26.refs_3_, f32[16,128]{1,0:T(8,128)S(1)} %get-tuple-element.72.refs_4_, ...), custom_call_target="tpu_custom_call" | custom-call | tf_op jit(solution)/shard_map/last/pallas_call | solution.py:527
  (16 shorter events, 0.0 us)
Async XLA Ops:
  0.0 13.8 %copy-start.2 = (s32[8,32]{1,0:T(8,128)S(1)}, s32[8,32]{1,0:T(8,128)}, u32[]{:S(2)}) copy-start(s32[8,32]{1,0:T(8,128)} %refs_3_.1) | copy-start | bytes 3076
  0.0 13.8 %copy-start.1 = (bf16[8,128,32]{1,2,0:T(8,128)(2,1)S(1)}, bf16[8,128,32]{1,2,0:T(8,128)(2,1)}, u32[]{:S(2)}) copy-start(bf16[8,128,32]{1,2,0:T(8,128)(2,1)} %param.15) | copy-start | bytes 196612
  0.0 12.2 %copy-start = (bf16[256,1,512]{2,0,1:T(8,128)(2,1)S(1)}, bf16[256,1,512]{2,0,1:T(8,128)(2,1)}, u32[]{:S(2)}) copy-start(bf16[256,1,512]{2,0,1:T(8,128)(2,1)} %param.17) | copy-start | bytes 786436
  0.0 13.8 %copy-start.4 = (s32[8]{0:T(128)S(1)}, s32[8]{0:T(128)}, u32[]{:S(2)}) copy-start(s32[8]{0:T(128)} %param.14) | copy-start | bytes 100
  0.0 13.8 %copy-start.3 = (s32[8,8]{1,0:T(8,128)S(1)}, s32[8,8]{1,0:T(8,128)}, u32[]{:S(2)}) copy-start(s32[8,8]{1,0:T(8,128)} %refs_0_.3) | copy-start | bytes 772
  2.0 5.0 %collective-permute-start.2 = (f32[16,640]{1,0:T(8,128)S(1)}, f32[16,640]{1,0:T(8,128)S(1)}, u32[]{:S(2)}, u32[]{:S(2)}) collective-permute-start(f32[16,640]{1,0:T(8,128)S(1)} %get-tuple-element.42), channel_id=1, source_target_pairs={{0,4},{4,0},{8,12},{12,8},{16,20},{20,16},{24,28},{28,24},{1,5},{5... | collective-permute-start | bytes 122888 | tf_op jit(solution)/shard_map/ppermute | solution.py:19
  5.1 20.7 %collective-permute-start = (bf16[352,512]{1,0:T(8,128)(2,1)S(1)}, bf16[352,512]{1,0:T(8,128)(2,1)S(1)}, u32[]{:S(2)}, u32[]{:S(2)}) collective-permute-start(bf16[352,512]{1,0:T(8,128)(2,1)S(1)} %get-tuple-element.39), channel_id=1, source_target_pairs={{0,4},{4,0},{8,12},{12,8},{16,20},{20,16},{24,28},{28,24},{1,5},{5... | collective-permute-start | bytes 1081352 | tf_op jit(solution)/shard_map/ppermute | solution.py:19
  7.1 7.0 %collective-permute-start.5 = (f32[16,640]{1,0:T(8,128)S(1)}, f32[16,640]{1,0:T(8,128)S(1)}, u32[]{:S(2)}, u32[]{:S(2)}) collective-permute-start(f32[16,640]{1,0:T(8,128)S(1)} %add.9.refs_0_), channel_id=1, source_target_pairs={{0,24},{4,28},{8,16},{12,20},{16,8},{20,12},{24,0},{28,4},{1,25},{... | collective-permute-start | bytes 122888 | tf_op jit(solution)/shard_map/ppermute | solution.py:19
  11.5 4.9 %collective-permute-start.4 = (f32[16,640]{1,0:T(8,128)S(1)}, f32[16,640]{1,0:T(8,128)S(1)}, u32[]{:S(2)}, u32[]{:S(2)}) collective-permute-start(f32[16,640]{1,0:T(8,128)S(1)} %add.9.refs_0_), channel_id=1, source_target_pairs={{0,16},{4,20},{8,24},{12,28},{16,0},{20,4},{24,8},{28,12},{1,17},{... | collective-permute-start | bytes 122888 | tf_op jit(solution)/shard_map/ppermute | solution.py:19
  11.5 4.9 %collective-permute-start.3 = (f32[16,640]{1,0:T(8,128)S(1)}, f32[16,640]{1,0:T(8,128)S(1)}, u32[]{:S(2)}, u32[]{:S(2)}) collective-permute-start(f32[16,640]{1,0:T(8,128)S(1)} %add.9.refs_0_), channel_id=1, source_target_pairs={{0,8},{4,12},{8,0},{12,4},{16,24},{20,28},{24,16},{28,20},{1,9},{5... | collective-permute-start | bytes 122888 | tf_op jit(solution)/shard_map/ppermute | solution.py:19
  12.2 11.8 %collective-permute-start.1 = (bf16[256,512]{1,0:T(8,128)(2,1)S(1)}, bf16[256,512]{1,0:T(8,128)(2,1)S(1)}, u32[]{:S(2)}, u32[]{:S(2)}) collective-permute-start(bf16[256,512]{1,0:T(8,128)(2,1)S(1)} %bitcast.5), channel_id=1, source_target_pairs={{0,2},{1,3},{2,0},{3,1},{4,6},{5,7},{6,4},{7,5},{8,10},{9,11},{10,... | collective-permute-start | bytes 786440 | tf_op jit(solution)/shard_map/ppermute | solution.py:494
  16.4 12.5 %copy-start.5 = (bf16[8,8,128,128]{3,2,1,0:T(8,128)(2,1)S(1)}, bf16[8,8,128,128]{3,2,1,0:T(8,128)(2,1)}, u32[]{:S(2)}) copy-start(bf16[8,8,128,128]{3,2,1,0:T(8,128)(2,1)} %refs_5_.5) | copy-start | bytes 6291460
  17.3 4.1 %collective-permute-start.6 = (bf16[16,1536]{1,0:T(8,128)(2,1)S(1)}, bf16[16,1536]{1,0:T(8,128)(2,1)S(1)}, u32[]{:S(2)}, u32[]{:S(2)}) collective-permute-start(bf16[16,1536]{1,0:T(8,128)(2,1)S(1)} %get-tuple-element.48.send_ref.refs_0_), channel_id=1, source_target_pairs={{0,4},{4,0},{8,12},{12,8},{16,20},{20,16},{24,28},{28,24},{1,5},{5... | collective-permute-start | bytes 147464 | tf_op jit(solution)/shard_map/ppermute | solution.py:19
  21.4 6.0 %collective-permute-start.10 = (bf16[16,1536]{1,0:T(8,128)(2,1)S(1)}, bf16[16,1536]{1,0:T(8,128)(2,1)S(1)}, u32[]{:S(2)}, u32[]{:S(2)}) collective-permute-start(bf16[16,1536]{1,0:T(8,128)(2,1)S(1)} %get-tuple-element.52), channel_id=1, source_target_pairs={{0,24},{4,28},{8,16},{12,20},{16,8},{20,12},{24,0},{28,4},{1,25},{... | collective-permute-start | bytes 147464 | tf_op jit(solution)/shard_map/ppermute | solution.py:19
  22.8 6.0 %collective-permute-start.8 = (bf16[16,1536]{1,0:T(8,128)(2,1)S(1)}, bf16[16,1536]{1,0:T(8,128)(2,1)S(1)}, u32[]{:S(2)}, u32[]{:S(2)}) collective-permute-start(bf16[16,1536]{1,0:T(8,128)(2,1)S(1)} %get-tuple-element.52), channel_id=1, source_target_pairs={{0,8},{4,12},{8,0},{12,4},{16,24},{20,28},{24,16},{28,20},{1,9},{5... | collective-permute-start | bytes 147464 | tf_op jit(solution)/shard_map/ppermute | solution.py:19
  24.0 5.7 %collective-permute-start.11 = (bf16[256,512]{1,0:T(8,128)(2,1)S(1)}, bf16[256,512]{1,0:T(8,128)(2,1)S(1)}, u32[]{:S(2)}, u32[]{:S(2)}) collective-permute-start(bf16[256,512]{1,0:T(8,128)(2,1)S(1)} %bitcast.6), channel_id=1, source_target_pairs={{0,1},{1,0},{2,3},{3,2},{4,5},{5,4},{6,7},{7,6},{8,9},{9,8},{10,11... | collective-permute-start | bytes 786440 | tf_op jit(solution)/shard_map/ppermute | solution.py:494
  24.0 5.7 %collective-permute-start.9 = (bf16[16,512]{1,0:T(8,128)(2,1)S(1)}, bf16[16,512]{1,0:T(8,128)(2,1)S(1)}, u32[]{:S(2)}, u32[]{:S(2)}) collective-permute-start(bf16[16,512]{1,0:T(8,128)(2,1)S(1)} %get-tuple-element.51.refs_0_), channel_id=1, source_target_pairs={{0,16},{4,20},{8,24},{12,28},{16,0},{20,4},{24,8},{28,12},{1,17},{... | collective-permute-start | bytes 49160 | tf_op jit(solution)/shard_map/ppermute | solution.py:19
  25.8 3.9 %collective-permute-start.12 = (bf16[256,512]{1,0:T(8,128)(2,1)S(1)}, bf16[256,512]{1,0:T(8,128)(2,1)S(1)}, u32[]{:S(2)}, u32[]{:S(2)}) collective-permute-start(bf16[256,512]{1,0:T(8,128)(2,1)S(1)} %collective-permute-done.1.refs_14_.refs_12_), channel_id=1, source_target_pairs={{0,1},{1,0},{2,3},{3,2},{4,5},{5,4},{6,7},{7,6},{8,9},{9,8},{10,11... | collective-permute-start | bytes 786440 | tf_op jit(solution)/shard_map/ppermute | solution.py:501
  27.4 9.3 %collective-permute-start.7 = (bf16[352,512]{1,0:T(8,128)(2,1)S(1)}, bf16[352,512]{1,0:T(8,128)(2,1)S(1)}, u32[]{:S(2)}, u32[]{:S(2)}) collective-permute-start(bf16[352,512]{1,0:T(8,128)(2,1)S(1)} %collective-permute-done.refs_0_.refs_12_), channel_id=1, source_target_pairs={{0,2},{1,3},{2,0},{3,1},{4,6},{5,7},{6,4},{7,5},{8,10},{9,11},{10,... | collective-permute-start | bytes 1081352 | tf_op jit(solution)/shard_map/ppermute | solution.py:602
  31.1 8.4 %collective-permute-start.18 = (bf16[352,512]{1,0:T(8,128)(2,1)S(1)}, bf16[352,512]{1,0:T(8,128)(2,1)S(1)}, u32[]{:S(2)}, u32[]{:S(2)}) collective-permute-start(bf16[352,512]{1,0:T(8,128)(2,1)S(1)} %collective-permute-done.refs_0_.refs_12_), channel_id=1, source_target_pairs={{0,1},{1,0},{2,3},{3,2},{4,5},{5,4},{6,7},{7,6},{8,9},{9,8},{10,11... | collective-permute-start | bytes 1081352 | tf_op jit(solution)/shard_map/ppermute | solution.py:634
  31.1 4.0 %collective-permute-start.13 = (f32[16,640]{1,0:T(8,128)S(1)}, f32[16,640]{1,0:T(8,128)S(1)}, u32[]{:S(2)}, u32[]{:S(2)}) collective-permute-start(f32[16,640]{1,0:T(8,128)S(1)} %get-tuple-element.60), channel_id=1, source_target_pairs={{0,4},{4,0},{8,12},{12,8},{16,20},{20,16},{24,28},{28,24},{1,5},{5... | collective-permute-start | bytes 122888 | tf_op jit(solution)/shard_map/ppermute | solution.py:19
  32.8 6.9 %collective-permute-start.17 = (f32[16,1024]{1,0:T(8,128)S(1)}, f32[16,1024]{1,0:T(8,128)S(1)}, u32[]{:S(2)}, u32[]{:S(2)}) collective-permute-start(f32[16,1024]{1,0:T(8,128)S(1)} %get-tuple-element.64), channel_id=1, source_target_pairs={{0,4},{4,0},{8,12},{12,8},{16,20},{20,16},{24,28},{28,24},{1,5},{5... | collective-permute-start | bytes 196616 | tf_op jit(solution)/shard_map/ppermute | solution.py:19
  35.2 6.1 %collective-permute-start.16 = (f32[16,640]{1,0:T(8,128)S(1)}, f32[16,640]{1,0:T(8,128)S(1)}, u32[]{:S(2)}, u32[]{:S(2)}) collective-permute-start(f32[16,640]{1,0:T(8,128)S(1)} %add.10.refs_0_), channel_id=1, source_target_pairs={{0,24},{4,28},{8,16},{12,20},{16,8},{20,12},{24,0},{28,4},{1,25},{... | collective-permute-start | bytes 122888 | tf_op jit(solution)/shard_map/ppermute | solution.py:19
  36.6 5.4 %collective-permute-start.15 = (f32[16,640]{1,0:T(8,128)S(1)}, f32[16,640]{1,0:T(8,128)S(1)}, u32[]{:S(2)}, u32[]{:S(2)}) collective-permute-start(f32[16,640]{1,0:T(8,128)S(1)} %add.10.refs_0_), channel_id=1, source_target_pairs={{0,16},{4,20},{8,24},{12,28},{16,0},{20,4},{24,8},{28,12},{1,17},{... | collective-permute-start | bytes 122888 | tf_op jit(solution)/shard_map/ppermute | solution.py:19
  36.6 5.4 %collective-permute-start.14 = (f32[16,640]{1,0:T(8,128)S(1)}, f32[16,640]{1,0:T(8,128)S(1)}, u32[]{:S(2)}, u32[]{:S(2)}) collective-permute-start(f32[16,640]{1,0:T(8,128)S(1)} %add.10.refs_0_), channel_id=1, source_target_pairs={{0,8},{4,12},{8,0},{12,4},{16,24},{20,28},{24,16},{28,20},{1,9},{5... | collective-permute-start | bytes 122888 | tf_op jit(solution)/shard_map/ppermute | solution.py:19
  39.6 2.5 %collective-permute-start.19 = (bf16[352,512]{1,0:T(8,128)(2,1)S(1)}, bf16[352,512]{1,0:T(8,128)(2,1)S(1)}, u32[]{:S(2)}, u32[]{:S(2)}) collective-permute-start(bf16[352,512]{1,0:T(8,128)(2,1)S(1)} %collective-permute-done.7.refs_2_.refs_14_), channel_id=1, source_target_pairs={{0,1},{1,0},{2,3},{3,2},{4,5},{5,4},{6,7},{7,6},{8,9},{9,8},{10,11... | collective-permute-start | bytes 1081352 | tf_op jit(solution)/shard_map/ppermute | solution.py:634
  43.5 6.1 %collective-permute-start.22 = (bf16[16,1536]{1,0:T(8,128)(2,1)S(1)}, bf16[16,1536]{1,0:T(8,128)(2,1)S(1)}, u32[]{:S(2)}, u32[]{:S(2)}) collective-permute-start(bf16[16,1536]{1,0:T(8,128)(2,1)S(1)} %get-tuple-element.68.refs_1_), channel_id=1, source_target_pairs={{0,24},{4,28},{8,16},{12,20},{16,8},{20,12},{24,0},{28,4},{1,25},{... | collective-permute-start | bytes 147464 | tf_op jit(solution)/shard_map/ppermute | solution.py:19
  45.4 4.6 %collective-permute-start.20 = (bf16[16,1536]{1,0:T(8,128)(2,1)S(1)}, bf16[16,1536]{1,0:T(8,128)(2,1)S(1)}, u32[]{:S(2)}, u32[]{:S(2)}) collective-permute-start(bf16[16,1536]{1,0:T(8,128)(2,1)S(1)} %get-tuple-element.68.refs_1_), channel_id=1, source_target_pairs={{0,8},{4,12},{8,0},{12,4},{16,24},{20,28},{24,16},{28,20},{1,9},{5... | collective-permute-start | bytes 147464 | tf_op jit(solution)/shard_map/ppermute | solution.py:19
  45.6 5.1 %collective-permute-start.21 = (bf16[16,512]{1,0:T(8,128)(2,1)S(1)}, bf16[16,512]{1,0:T(8,128)(2,1)S(1)}, u32[]{:S(2)}, u32[]{:S(2)}) collective-permute-start(bf16[16,512]{1,0:T(8,128)(2,1)S(1)} %get-tuple-element.67.refs_0_), channel_id=1, source_target_pairs={{0,16},{4,20},{8,24},{12,28},{16,0},{20,4},{24,8},{28,12},{1,17},{... | collective-permute-start | bytes 49160 | tf_op jit(solution)/shard_map/ppermute | solution.py:19
  51.6 3.7 %collective-permute-start.23 = (f32[16,128]{1,0:T(8,128)S(1)}, f32[16,128]{1,0:T(8,128)S(1)}, u32[]{:S(2)}, u32[]{:S(2)}) collective-permute-start(f32[16,128]{1,0:T(8,128)S(1)} %fourth.1), channel_id=1, source_target_pairs={{0,4},{4,0},{8,12},{12,8},{16,20},{20,16},{24,28},{28,24},{1,5},{5... | collective-permute-start | bytes 24584 | tf_op jit(solution)/shard_map/ppermute | solution.py:19
  55.3 5.4 %collective-permute-start.26 = (f32[16,128]{1,0:T(8,128)S(1)}, f32[16,128]{1,0:T(8,128)S(1)}, u32[]{:S(2)}, u32[]{:S(2)}) collective-permute-start(f32[16,128]{1,0:T(8,128)S(1)} %add.11.refs_0_), channel_id=1, source_target_pairs={{0,24},{4,28},{8,16},{12,20},{16,8},{20,12},{24,0},{28,4},{1,25},{... | collective-permute-start | bytes 24584 | tf_op jit(solution)/shard_map/ppermute | solution.py:19
  57.1 4.6 %collective-permute-start.25 = (f32[16,128]{1,0:T(8,128)S(1)}, f32[16,128]{1,0:T(8,128)S(1)}, u32[]{:S(2)}, u32[]{:S(2)}) collective-permute-start(f32[16,128]{1,0:T(8,128)S(1)} %add.11.refs_0_), channel_id=1, source_target_pairs={{0,16},{4,20},{8,24},{12,28},{16,0},{20,4},{24,8},{28,12},{1,17},{... | collective-permute-start | bytes 24584 | tf_op jit(solution)/shard_map/ppermute | solution.py:19
  58.0 3.7 %collective-permute-start.24 = (f32[16,128]{1,0:T(8,128)S(1)}, f32[16,128]{1,0:T(8,128)S(1)}, u32[]{:S(2)}, u32[]{:S(2)}) collective-permute-start(f32[16,128]{1,0:T(8,128)S(1)} %add.11.refs_0_), channel_id=1, source_target_pairs={{0,8},{4,12},{8,0},{12,4},{16,24},{20,28},{24,16},{28,20},{1,9},{5... | collective-permute-start | bytes 24584 | tf_op jit(solution)/shard_map/ppermute | solution.py:19

commit v8 on v7

--- a/solution.py
+++ b/solution.py
@@ -237,11 +237,16 @@
         pack_ref[:size, :] = high_ref[pl.ds(pl.multiple_of(quarter * size, size), size), :]
 
 
+def turn_kernel(high_ref, low_ref, high_turned_ref, low_turned_ref):
+    high_turned_ref[...] = high_ref[...].T
+    low_turned_ref[...] = low_ref[...].T
+
+
 def first_kernel(parts, *refs):
     sums = refs[:parts]
     rhs_ref, diag_ref, high_ref, low_ref, maps_ref = refs[parts : parts + 5]
     dir_ref, pre_ref, keep_ref, send_ref = refs[parts + 5 :]
-    width = high_ref.shape[1]
+    width = high_ref.shape[0]
     rows, panels = rhs_ref.shape
     summed = sums[0][...]
     for ref in sums[1:]:
@@ -250,7 +255,7 @@
     start_len = jnp.sqrt(rhs_sq + EPS)
     first_dir = rhs_ref[...] / start_len
     proj = summed[:, :width] / start_len
-    first_pre = diag_ref[...] * first_dir - dot_wide(dot_nt, proj, high_ref[...], low_ref[...])
+    first_pre = diag_ref[...] * first_dir - dot_wide(dot_nn, proj, high_ref[...], low_ref[...])
     field_low = first_pre.astype(BF)
     dir_ref[...] = first_dir
     pre_ref[...] = first_pre
@@ -352,7 +357,7 @@
     sums = refs[:parts]
     res_ref, dir_ref, keep_ref, diag_ref, high_ref, low_ref, maps_ref = refs[parts : parts + 7]
     *extra, next_ref, pre_ref, scalars_ref, send_ref = refs[parts + 7 :]
-    width = high_ref.shape[1]
+    width = high_ref.shape[0]
     rows, panels = res_ref.shape
     summed = sums[0][...]
     for ref in sums[1:]:
@@ -364,7 +369,7 @@
     below_one = jnp.sqrt(below_sq + EPS)
     second_dir = (res_ref[...] - diag_one * dir_ref[...]) / below_one
     proj = (summed[:, :width] - diag_one * keep_ref[:, :width]) / below_one
-    pre = diag_ref[...] * second_dir - dot_wide(dot_nt, proj, high_ref[...], low_ref[...])
+    pre = diag_ref[...] * second_dir - dot_wide(dot_nn, proj, high_ref[...], low_ref[...])
     field_low = pre.astype(BF)
     pre_ref[...] = pre
     if extra:
@@ -454,11 +459,12 @@
     out_ref[...] = step_one * first_ref[...] + step_two * second_ref[...]
 
 
-def sum_parts(values, count):
+def sum_parts(values, count, beside=()):
     if count != 8:
-        return [lax.psum(values, AXIS)]
+        return [lax.psum(values, AXIS)], beside
     pair = values + swap(values, 1, count)
-    return [pair, swap(pair, 2, count), swap(pair, 4, count), swap(pair, 6, count)]
+    pair, *beside = lax.optimization_barrier((pair, *beside))
+    return [pair, swap(pair, 2, count), swap(pair, 4, count), swap(pair, 6, count)], beside
 
 
 def exchange_z(field, onward, pair, panels, count):
@@ -584,15 +590,16 @@
         scratch + [pltpu.SemaphoreType.DMA((parts + 5,))],
         far=range(len(args)),
     )
+    turned = call("turn", turn_kernel, [((width, panels), BF)] * 2, [high, low])
     some_rows, payload = gather_quarters(coupling[:, 0, :], quarters, count, payload)
-    sums = sum_parts(payload, count)
+    sums, turned = sum_parts(payload, count, turned)
     if paired:
         mine = swap(packs[0], 1, count)
     first_dir, first_pre, keep, send = call(
         "first",
         lambda *refs: first_kernel(len(sums), *refs),
         [((rows, panels), F32), ((rows, panels), F32), ((rows, wide), F32), ((rows, long), BF)],
-        [*sums, rhs_near, diag_row, high, low, maps],
+        [*sums, rhs_near, diag_row, *turned, maps],
         flops=2*10**9,
     )
     fields, charges, starts = exchange(send, panels, count)
@@ -624,7 +631,7 @@
     )
     if paired:
         mine, payload = lax.optimization_barrier((mine, payload))
-    sums = sum_parts(payload, count)
+    sums, _ = sum_parts(payload, count)
     outs = [((rows, panels), F32), ((rows, panels), F32), ((rows, LANES), F32)]
     extra = []
     if paired:
@@ -649,7 +656,7 @@
         "third",
         lambda *refs: third_kernel(len(sums), paired * rank, block, *refs),
         outs,
-        [*sums, residue, first_dir, keep, diag_row, high, low, maps, *extra],
+        [*sums, residue, first_dir, keep, diag_row, *turned, maps, *extra],
         [pltpu.VMEM(maps.shape, BF)] if paired else [],
     )
     if paired:
@@ -664,7 +671,7 @@
         [*charges, first_dir, second_dir, second_pre, self_row, near, maps, *full_rows],
         scratch,
     )
-    sums = sum_parts(tail, count)
+    sums, _ = sum_parts(tail, count)
     (result,) = call(
         "last",
         lambda *refs: last_kernel(len(sums), *refs),

time: 62.9 us -> 62.4 us (level)
    ppermute x21, waiting for transfers between devices: 18.2 us -> 17.5 us  [swap(): return lax.ppermute(values, AXIS, [(i, i ^ mask) for i in range(count)])]
    pallas_call x11 -> x12, Pallas kernels: 9.49 us -> 9.69 us  [call(): pl.pallas_call(kernel, name=name, out_shape=out_shapes, in_specs=specs, o...]
where the time goes in v8:
time: 62.4 us; the launch traced here: 62.3 us
  starting transfers between devices  34.9 us (56%)
  waiting for transfers between devices  17.6 us (28%)
  Pallas kernels  9.69 us (16%)
    ppermute x21, starting transfers between devices, swap(): return lax.ppermute(values, AXIS, [(i, i ^ mask) for i in range(count)])  31.5 us
    ppermute x21, waiting for transfers between devices, swap(): return lax.ppermute(values, AXIS, [(i, i ^ mask) for i in range(count)])  17.5 us
    pallas_call x12, Pallas kernels, call(): pl.pallas_call(kernel, name=name, out_shape=out_shapes, in_specs=specs, o...  9.69 us
    ppermute x2, starting transfers between devices, gather_quarters(): lax.ppermute(coupling, 'rhs', pair)  1.64 us
    ppermute x1, starting transfers between devices, on_device(): far = lax.ppermute(mine, 'rhs', [(i, i ^ 2) for i in range(quarters)])  1.49 us
  transfers between devices with their start and end apart: 27, of which 12 were waited for; matrix products, arithmetic and copies ran while one was open for 0% of the time, Pallas kernels for 7%

profile of v8, /device:TPU:0, one launch (start us, length us, event | category | flops | bytes accessed | tf_op | source)
XLA Modules:
  0.0 62.3 jit_solution(8067348876479007822)
XLA Ops:
  0.0 2.0 %open.1 = (f32[16,640]{1,0:T(8,128)S(1)}, f32[16,1024]{1,0:T(8,128)S(1)}, f32[1,1024]{1,0:T(1,128)S(1)}, f32[1,1024]{1,0:T(1,128)S(1)}, bf16[1024,512]{1,0:T(8,1...) custom-call(f32[16,1024]{1,0:T(8,128)} %refs_0_.2, f32[1024,512]{1,0:T(8,128)} %refs_1_.1, ...), custom_call_target="tpu_custom_call" | custom-call | tf_op jit(solution)/shard_map/open/pallas_call | solution.py:533
  2.0 3.0 %collective-permute-start.2 = (f32[16,640]{1,0:T(8,128)S(1)}, f32[16,640]{1,0:T(8,128)S(1)}, u32[]{:S(2)}, u32[]{:S(2)}) collective-permute-start(f32[16,640]{1,0:T(8,128)S(1)} %get-tuple-element.47), channel_id=1, source_target_pairs={{0,4},{4,0},{8,12},{12,8},{16,20},{20,16},{24,28},{28,24},{1,5},{5... | collective-permute-start | bytes 122888 | tf_op jit(solution)/shard_map/ppermute | solution.py:19
  5.1 0.1 collective-permute-start
  5.2 0.6 %turn.1 = (bf16[512,1024]{1,0:T(8,128)(2,1)S(1)}, bf16[512,1024]{1,0:T(8,128)(2,1)S(1)}) custom-call(bf16[1024,512]{1,0:T(8,128)(2,1)S(1)} %get-tuple-element.48.high_ref.refs_10_, bf16[1024,512]{1,0:T(8,128)(2,1)S(1)} %get-tuple-element.49.low_ref.refs_11_), custom_call_target="tpu_custom_call" | custom-call | tf_op jit(solution)/shard_map/turn/pallas_call | solution.py:533
  5.8 1.3 %collective-permute-done.2 = f32[16,640]{1,0:T(8,128)S(1)} collective-permute-done((f32[16,640]{1,0:T(8,128)S(1)}, f32[16,640]{1,0:T(8,128)S(1)}, u32[]{:S(2)}, u32[]{:S(2)}) %collective-permute-start.2) | collective-permute-done | bytes 40992 | tf_op jit(solution)/shard_map/ppermute | solution.py:19
  7.1 4.4 %collective-permute-start.5 = (f32[16,640]{1,0:T(8,128)S(1)}, f32[16,640]{1,0:T(8,128)S(1)}, u32[]{:S(2)}, u32[]{:S(2)}) collective-permute-start(f32[16,640]{1,0:T(8,128)S(1)} %add.9.refs_0_), channel_id=1, source_target_pairs={{0,24},{4,28},{8,16},{12,20},{16,8},{20,12},{24,0},{28,4},{1,25},{... | collective-permute-start | bytes 122888 | tf_op jit(solution)/shard_map/ppermute | solution.py:19
  11.5 0.0 collective-permute-start.4
  11.5 0.6 %collective-permute-start.3 = (f32[16,640]{1,0:T(8,128)S(1)}, f32[16,640]{1,0:T(8,128)S(1)}, u32[]{:S(2)}, u32[]{:S(2)}) collective-permute-start(f32[16,640]{1,0:T(8,128)S(1)} %add.9.refs_0_), channel_id=1, source_target_pairs={{0,8},{4,12},{8,0},{12,4},{16,24},{20,28},{24,16},{28,20},{1,9},{5... | collective-permute-start | bytes 122888 | tf_op jit(solution)/shard_map/ppermute | solution.py:19
  12.1 1.6 %collective-permute-start.1 = (bf16[256,512]{1,0:T(8,128)(2,1)S(1)}, bf16[256,512]{1,0:T(8,128)(2,1)S(1)}, u32[]{:S(2)}, u32[]{:S(2)}) collective-permute-start(bf16[256,512]{1,0:T(8,128)(2,1)S(1)} %bitcast.5), channel_id=1, source_target_pairs={{0,2},{1,3},{2,0},{3,1},{4,6},{5,7},{6,4},{7,5},{8,10},{9,11},{10,... | collective-permute-start | bytes 786440 | tf_op jit(solution)/shard_map/ppermute | solution.py:500
  13.8 0.2 maps.1
  14.0 0.0 collective-permute-done.5.refs_3_
  14.1 2.4 %collective-permute-done.4.refs_2_ = f32[16,640]{1,0:T(8,128)S(1)} collective-permute-done((f32[16,640]{1,0:T(8,128)S(1)}, f32[16,640]{1,0:T(8,128)S(1)}, u32[]{:S(2)}, u32[]{:S(2)}) %collective-permute-start.4) | collective-permute-done | bytes 40992 | tf_op jit(solution)/shard_map/ppermute | solution.py:19
  16.4 0.0 collective-permute-done.3.refs_1_
  16.4 0.6 first.1
  17.0 1.7 %collective-permute-start.6 = (bf16[16,1536]{1,0:T(8,128)(2,1)S(1)}, bf16[16,1536]{1,0:T(8,128)(2,1)S(1)}, u32[]{:S(2)}, u32[]{:S(2)}) collective-permute-start(bf16[16,1536]{1,0:T(8,128)(2,1)S(1)} %get-tuple-element.58.send_ref.refs_0_), channel_id=1, source_target_pairs={{0,4},{4,0},{8,12},{12,8},{16,20},{20,16},{24,28},{28,24},{1,5},{5... | collective-permute-start | bytes 147464 | tf_op jit(solution)/shard_map/ppermute | solution.py:19
  18.7 2.4 %collective-permute-done.6.near_ref.refs_1_ = bf16[16,1536]{1,0:T(8,128)(2,1)S(1)} collective-permute-done((bf16[16,1536]{1,0:T(8,128)(2,1)S(1)}, bf16[16,1536]{1,0:T(8,128)(2,1)S(1)}, u32[]{:S(2)}, u32[]{:S(2)}) %collective-permute-start.6) | collective-permute-done | bytes 49184 | tf_op jit(solution)/shard_map/ppermute | solution.py:19
  21.1 1.5 %collective-permute-start.10 = (bf16[16,1536]{1,0:T(8,128)(2,1)S(1)}, bf16[16,1536]{1,0:T(8,128)(2,1)S(1)}, u32[]{:S(2)}, u32[]{:S(2)}) collective-permute-start(bf16[16,1536]{1,0:T(8,128)(2,1)S(1)} %get-tuple-element.62), channel_id=1, source_target_pairs={{0,24},{4,28},{8,16},{12,20},{16,8},{20,12},{24,0},{28,4},{1,25},{... | collective-permute-start | bytes 147464 | tf_op jit(solution)/shard_map/ppermute | solution.py:19
  22.6 1.1 %collective-permute-start.8 = (bf16[16,1536]{1,0:T(8,128)(2,1)S(1)}, bf16[16,1536]{1,0:T(8,128)(2,1)S(1)}, u32[]{:S(2)}, u32[]{:S(2)}) collective-permute-start(bf16[16,1536]{1,0:T(8,128)(2,1)S(1)} %get-tuple-element.62), channel_id=1, source_target_pairs={{0,8},{4,12},{8,0},{12,4},{16,24},{20,28},{24,16},{28,20},{1,9},{5... | collective-permute-start | bytes 147464 | tf_op jit(solution)/shard_map/ppermute | solution.py:19
  23.7 0.0 collective-permute-start.11
  23.7 0.0 collective-permute-done.1.refs_14_.refs_12_
  23.7 1.8 %collective-permute-start.9 = (bf16[16,512]{1,0:T(8,128)(2,1)S(1)}, bf16[16,512]{1,0:T(8,128)(2,1)S(1)}, u32[]{:S(2)}, u32[]{:S(2)}) collective-permute-start(bf16[16,512]{1,0:T(8,128)(2,1)S(1)} %get-tuple-element.61.refs_0_), channel_id=1, source_target_pairs={{0,16},{4,20},{8,24},{12,28},{16,0},{20,4},{24,8},{28,12},{1,17},{... | collective-permute-start | bytes 49160 | tf_op jit(solution)/shard_map/ppermute | solution.py:19
  25.5 0.0 collective-permute-done.refs_0_.refs_12_
  25.5 0.2 collective-permute-start.12
  25.8 1.4 %collective-permute-done.10.refs_3_ = bf16[16,1536]{1,0:T(8,128)(2,1)S(1)} collective-permute-done((bf16[16,1536]{1,0:T(8,128)(2,1)S(1)}, bf16[16,1536]{1,0:T(8,128)(2,1)S(1)}, u32[]{:S(2)}, u32[]{:S(2)}) %collective-permute-start.10) | collective-permute-done | bytes 49184 | tf_op jit(solution)/shard_map/ppermute | solution.py:19
  27.1 1.5 %collective-permute-start.7 = (bf16[352,512]{1,0:T(8,128)(2,1)S(1)}, bf16[352,512]{1,0:T(8,128)(2,1)S(1)}, u32[]{:S(2)}, u32[]{:S(2)}) collective-permute-start(bf16[352,512]{1,0:T(8,128)(2,1)S(1)} %collective-permute-done.refs_0_.refs_12_), channel_id=1, source_target_pairs={{0,2},{1,3},{2,0},{3,1},{4,6},{5,7},{6,4},{7,5},{8,10},{9,11},{10,... | collective-permute-start | bytes 1081352 | tf_op jit(solution)/shard_map/ppermute | solution.py:609
  28.6 0.0 collective-permute-done.8.refs_2_.refs_1_
  28.6 0.7 %near.2.refs_8_ = f32[16,1024]{1,0:T(8,128)S(1)} custom-call(bf16[16,1536]{1,0:T(8,128)(2,1)S(1)} %get-tuple-element.58.send_ref.refs_0_, bf16[16,1536]{1,0:T(8,128)(2,1)S(1)} %collective-permute-done.6.near_ref.refs_1_, bf16[16,1536]{1,0:T(8,128)(2,1)S(1)} %collective-permute-done.8.refs_2_.refs_1_, bf16[16,1536]{1,0:T(8,128)(2,1)S(1)} %collective-permute-done.10.refs_3_, ...), custom_call_target="tpu_custom_call" | custom-call | flops 10000000000 | bytes 20000000 | tf_op jit(solution)/shard_map/near/pallas_call | solution.py:533
  29.4 0.0 collective-permute-done.9.refs_2_
  29.4 0.0 collective-permute-done.11.refs_13_.refs_11_
  29.4 0.0 collective-permute-done.12.refs_15_.refs_13_
  29.4 1.5 %second.1 = (f32[16,1024]{1,0:T(8,128)S(1)}, f32[16,1024]{1,0:T(8,128)S(1)}, f32[16,640]{1,0:T(8,128)S(1)}) custom-call(bf16[16,512]{1,0:T(8,128)(2,1)S(1)} %get-tuple-element.61.refs_0_, bf16[16,1536]{1,0:T(8,128)(2,1)S(1)} %collective-permute-done.8.refs_2_.refs_1_, bf16[16,512]{1,0:T(8,128)(2,1)S(1)} %collective-permute-done.9.refs_2_, ...), custom_call_target="tpu_custom_call" | custom-call | flops 10000000000 | bytes 20000000 | tf_op jit(solution)/shard_map/second/pallas_call | solution.py:533
  30.9 0.0 collective-permute-start.18
  30.9 1.7 %collective-permute-start.13 = (f32[16,640]{1,0:T(8,128)S(1)}, f32[16,640]{1,0:T(8,128)S(1)}, u32[]{:S(2)}, u32[]{:S(2)}) collective-permute-start(f32[16,640]{1,0:T(8,128)S(1)} %get-tuple-element.70), channel_id=1, source_target_pairs={{0,4},{4,0},{8,12},{12,8},{16,20},{20,16},{24,28},{28,24},{1,5},{5... | collective-permute-start | bytes 122888 | tf_op jit(solution)/shard_map/ppermute | solution.py:19
  32.6 0.4 collective-permute-start.17
  33.0 2.0 %collective-permute-done.13 = f32[16,640]{1,0:T(8,128)S(1)} collective-permute-done((f32[16,640]{1,0:T(8,128)S(1)}, f32[16,640]{1,0:T(8,128)S(1)}, u32[]{:S(2)}, u32[]{:S(2)}) %collective-permute-start.13) | collective-permute-done | bytes 40992 | tf_op jit(solution)/shard_map/ppermute | solution.py:19
  34.9 1.5 %collective-permute-start.16 = (f32[16,640]{1,0:T(8,128)S(1)}, f32[16,640]{1,0:T(8,128)S(1)}, u32[]{:S(2)}, u32[]{:S(2)}) collective-permute-start(f32[16,640]{1,0:T(8,128)S(1)} %add.10.refs_0_), channel_id=1, source_target_pairs={{0,24},{4,28},{8,16},{12,20},{16,8},{20,12},{24,0},{28,4},{1,25},{... | collective-permute-start | bytes 122888 | tf_op jit(solution)/shard_map/ppermute | solution.py:19
  36.4 0.0 collective-permute-start.15
  36.4 0.0 collective-permute-done.7.refs_2_.refs_14_
  36.4 2.9 %collective-permute-start.14 = (f32[16,640]{1,0:T(8,128)S(1)}, f32[16,640]{1,0:T(8,128)S(1)}, u32[]{:S(2)}, u32[]{:S(2)}) collective-permute-start(f32[16,640]{1,0:T(8,128)S(1)} %add.10.refs_0_), channel_id=1, source_target_pairs={{0,8},{4,12},{8,0},{12,4},{16,24},{20,28},{24,16},{28,20},{1,9},{5... | collective-permute-start | bytes 122888 | tf_op jit(solution)/shard_map/ppermute | solution.py:19
  39.3 0.0 collective-permute-done.18.refs_1_.refs_13_
  39.3 0.0 collective-permute-start.19
  39.3 0.2 other_maps.1.refs_16_
  39.5 0.0 collective-permute-done.17.refs_11_
  39.5 1.5 %collective-permute-done.16.refs_3_ = f32[16,640]{1,0:T(8,128)S(1)} collective-permute-done((f32[16,640]{1,0:T(8,128)S(1)}, f32[16,640]{1,0:T(8,128)S(1)}, u32[]{:S(2)}, u32[]{:S(2)}) %collective-permute-start.16) | collective-permute-done | bytes 40992 | tf_op jit(solution)/shard_map/ppermute | solution.py:19
  41.1 0.8 %collective-permute-done.15.refs_2_ = f32[16,640]{1,0:T(8,128)S(1)} collective-permute-done((f32[16,640]{1,0:T(8,128)S(1)}, f32[16,640]{1,0:T(8,128)S(1)}, u32[]{:S(2)}, u32[]{:S(2)}) %collective-permute-start.15) | collective-permute-done | bytes 40992 | tf_op jit(solution)/shard_map/ppermute | solution.py:19
  41.8 0.0 collective-permute-done.14.refs_1_
  41.8 0.0 collective-permute-done.19.refs_15_
  41.8 1.3 %third.1 = (bf16[16,1536]{1,0:T(8,128)(2,1)S(1)}, bf16[16,512]{1,0:T(8,128)(2,1)S(1)}, f32[16,1024]{1,0:T(8,128)S(1)}, f32[16,1024]{1,0:T(8,128)S(1)}, f32[16,12...) custom-call(f32[16,640]{1,0:T(8,128)S(1)} %add.10.refs_0_, f32[16,640]{1,0:T(8,128)S(1)} %collective-permute-done.14.refs_1_, ...), custom_call_target="tpu_custom_call" | custom-call | tf_op jit(solution)/shard_map/third/pallas_call | solution.py:533
  43.1 1.8 %collective-permute-start.22 = (bf16[16,1536]{1,0:T(8,128)(2,1)S(1)}, bf16[16,1536]{1,0:T(8,128)(2,1)S(1)}, u32[]{:S(2)}, u32[]{:S(2)}) collective-permute-start(bf16[16,1536]{1,0:T(8,128)(2,1)S(1)} %get-tuple-element.78.refs_1_), channel_id=1, source_target_pairs={{0,24},{4,28},{8,16},{12,20},{16,8},{20,12},{24,0},{28,4},{1,25},{... | collective-permute-start | bytes 147464 | tf_op jit(solution)/shard_map/ppermute | solution.py:19
  44.9 0.2 collective-permute-start.20
  45.2 2.3 %collective-permute-start.21 = (bf16[16,512]{1,0:T(8,128)(2,1)S(1)}, bf16[16,512]{1,0:T(8,128)(2,1)S(1)}, u32[]{:S(2)}, u32[]{:S(2)}) collective-permute-start(bf16[16,512]{1,0:T(8,128)(2,1)S(1)} %get-tuple-element.77.refs_0_), channel_id=1, source_target_pairs={{0,16},{4,20},{8,24},{12,28},{16,0},{20,4},{24,8},{28,12},{1,17},{... | collective-permute-start | bytes 49160 | tf_op jit(solution)/shard_map/ppermute | solution.py:19
  47.5 1.7 %collective-permute-done.22.refs_3_ = bf16[16,1536]{1,0:T(8,128)(2,1)S(1)} collective-permute-done((bf16[16,1536]{1,0:T(8,128)(2,1)S(1)}, bf16[16,1536]{1,0:T(8,128)(2,1)S(1)}, u32[]{:S(2)}, u32[]{:S(2)}) %collective-permute-start.22) | collective-permute-done | bytes 49184 | tf_op jit(solution)/shard_map/ppermute | solution.py:19
  49.2 0.3 collective-permute-done.20.refs_2_.refs_1_
  49.5 0.7 %near.3.refs_8_ = f32[16,1024]{1,0:T(8,128)S(1)} custom-call(bf16[16,1024]{1,0:T(8,128)(2,1)S(1)} %get-tuple-element.81.refs_0_, bf16[16,1536]{1,0:T(8,128)(2,1)S(1)} %get-tuple-element.78.refs_1_, bf16[16,1536]{1,0:T(8,128)(2,1)S(1)} %collective-permute-done.20.refs_2_.refs_1_, bf16[16,1536]{1,0:T(8,128)(2,1)S(1)} %collective-permute-done.22.refs_3_, ...), custom_call_target="tpu_custom_call" | custom-call | flops 10000000000 | bytes 20000000 | tf_op jit(solution)/shard_map/near/pallas_call | solution.py:533
  50.3 0.0 collective-permute-done.21.refs_2_
  50.3 0.9 %fourth.1 = f32[16,128]{1,0:T(8,128)S(1)} custom-call(bf16[16,512]{1,0:T(8,128)(2,1)S(1)} %get-tuple-element.77.refs_0_, bf16[16,1536]{1,0:T(8,128)(2,1)S(1)} %collective-permute-done.20.refs_2_.refs_1_, bf16[16,512]{1,0:T(8,128)(2,1)S(1)} %collective-permute-done.21.refs_2_, bf16[16,1536]{1,0:T(8,128)(2,1)S(1)} %collective-permute-done.22.refs_3_, ...), custom_call_target="tpu_custom_call" | custom-call | tf_op jit(solution)/shard_map/fourth/pallas_call | solution.py:533
  51.1 2.0 %collective-permute-start.23 = (f32[16,128]{1,0:T(8,128)S(1)}, f32[16,128]{1,0:T(8,128)S(1)}, u32[]{:S(2)}, u32[]{:S(2)}) collective-permute-start(f32[16,128]{1,0:T(8,128)S(1)} %fourth.1), channel_id=1, source_target_pairs={{0,4},{4,0},{8,12},{12,8},{16,20},{20,16},{24,28},{28,24},{1,5},{5... | collective-permute-start | bytes 24584 | tf_op jit(solution)/shard_map/ppermute | solution.py:19
  53.2 1.7 %collective-permute-done.23 = f32[16,128]{1,0:T(8,128)S(1)} collective-permute-done((f32[16,128]{1,0:T(8,128)S(1)}, f32[16,128]{1,0:T(8,128)S(1)}, u32[]{:S(2)}, u32[]{:S(2)}) %collective-permute-start.23) | collective-permute-done | bytes 8224 | tf_op jit(solution)/shard_map/ppermute | solution.py:19
  54.8 1.9 %collective-permute-start.26 = (f32[16,128]{1,0:T(8,128)S(1)}, f32[16,128]{1,0:T(8,128)S(1)}, u32[]{:S(2)}, u32[]{:S(2)}) collective-permute-start(f32[16,128]{1,0:T(8,128)S(1)} %add.11.refs_0_), channel_id=1, source_target_pairs={{0,24},{4,28},{8,16},{12,20},{16,8},{20,12},{24,0},{28,4},{1,25},{... | collective-permute-start | bytes 24584 | tf_op jit(solution)/shard_map/ppermute | solution.py:19
  56.7 0.9 %collective-permute-start.25 = (f32[16,128]{1,0:T(8,128)S(1)}, f32[16,128]{1,0:T(8,128)S(1)}, u32[]{:S(2)}, u32[]{:S(2)}) collective-permute-start(f32[16,128]{1,0:T(8,128)S(1)} %add.11.refs_0_), channel_id=1, source_target_pairs={{0,16},{4,20},{8,24},{12,28},{16,0},{20,4},{24,8},{28,12},{1,17},{... | collective-permute-start | bytes 24584 | tf_op jit(solution)/shard_map/ppermute | solution.py:19
  57.6 1.6 %collective-permute-start.24 = (f32[16,128]{1,0:T(8,128)S(1)}, f32[16,128]{1,0:T(8,128)S(1)}, u32[]{:S(2)}, u32[]{:S(2)}) collective-permute-start(f32[16,128]{1,0:T(8,128)S(1)} %add.11.refs_0_), channel_id=1, source_target_pairs={{0,8},{4,12},{8,0},{12,4},{16,24},{20,28},{24,16},{28,20},{1,9},{5... | collective-permute-start | bytes 24584 | tf_op jit(solution)/shard_map/ppermute | solution.py:19
  59.2 1.1 %collective-permute-done.26.refs_3_ = f32[16,128]{1,0:T(8,128)S(1)} collective-permute-done((f32[16,128]{1,0:T(8,128)S(1)}, f32[16,128]{1,0:T(8,128)S(1)}, u32[]{:S(2)}, u32[]{:S(2)}) %collective-permute-start.26) | collective-permute-done | bytes 8224 | tf_op jit(solution)/shard_map/ppermute | solution.py:19
  60.3 1.0 %collective-permute-done.25.refs_2_ = f32[16,128]{1,0:T(8,128)S(1)} collective-permute-done((f32[16,128]{1,0:T(8,128)S(1)}, f32[16,128]{1,0:T(8,128)S(1)}, u32[]{:S(2)}, u32[]{:S(2)}) %collective-permute-start.25) | collective-permute-done | bytes 8224 | tf_op jit(solution)/shard_map/ppermute | solution.py:19
  61.4 1.0 %last.1 = f32[16,1024]{1,0:T(8,128)} custom-call(f32[16,128]{1,0:T(8,128)S(1)} %add.11.refs_0_, f32[16,128]{1,0:T(8,128)S(1)} %collective-permute-done.24.refs_1_, f32[16,128]{1,0:T(8,128)S(1)} %collective-permute-done.25.refs_2_, f32[16,128]{1,0:T(8,128)S(1)} %collective-permute-done.26.refs_3_, f32[16,128]{1,0:T(8,128)S(1)} %get-tuple-element.82.refs_4_, ...), custom_call_target="tpu_custom_call" | custom-call | tf_op jit(solution)/shard_map/last/pallas_call | solution.py:533
  (17 shorter events, 0.0 us)
Async XLA Ops:
  0.0 12.1 %copy-start = (bf16[256,1,512]{2,0,1:T(8,128)(2,1)S(1)}, bf16[256,1,512]{2,0,1:T(8,128)(2,1)}, u32[]{:S(2)}) copy-start(bf16[256,1,512]{2,0,1:T(8,128)(2,1)} %param.17) | copy-start | bytes 786436
  0.0 13.8 %copy-start.1 = (bf16[8,128,32]{1,2,0:T(8,128)(2,1)S(1)}, bf16[8,128,32]{1,2,0:T(8,128)(2,1)}, u32[]{:S(2)}) copy-start(bf16[8,128,32]{1,2,0:T(8,128)(2,1)} %param.15) | copy-start | bytes 196612
  0.0 13.8 %copy-start.2 = (s32[8,32]{1,0:T(8,128)S(1)}, s32[8,32]{1,0:T(8,128)}, u32[]{:S(2)}) copy-start(s32[8,32]{1,0:T(8,128)} %refs_3_.1) | copy-start | bytes 3076
  0.0 13.8 %copy-start.3 = (s32[8,8]{1,0:T(8,128)S(1)}, s32[8,8]{1,0:T(8,128)}, u32[]{:S(2)}) copy-start(s32[8,8]{1,0:T(8,128)} %refs_0_.3) | copy-start | bytes 772
  0.0 13.8 %copy-start.4 = (s32[8]{0:T(128)S(1)}, s32[8]{0:T(128)}, u32[]{:S(2)}) copy-start(s32[8]{0:T(128)} %param.14) | copy-start | bytes 100
  2.0 5.0 %collective-permute-start.2 = (f32[16,640]{1,0:T(8,128)S(1)}, f32[16,640]{1,0:T(8,128)S(1)}, u32[]{:S(2)}, u32[]{:S(2)}) collective-permute-start(f32[16,640]{1,0:T(8,128)S(1)} %get-tuple-element.47), channel_id=1, source_target_pairs={{0,4},{4,0},{8,12},{12,8},{16,20},{20,16},{24,28},{28,24},{1,5},{5... | collective-permute-start | bytes 122888 | tf_op jit(solution)/shard_map/ppermute | solution.py:19
  5.1 20.5 %collective-permute-start = (bf16[352,512]{1,0:T(8,128)(2,1)S(1)}, bf16[352,512]{1,0:T(8,128)(2,1)S(1)}, u32[]{:S(2)}, u32[]{:S(2)}) collective-permute-start(bf16[352,512]{1,0:T(8,128)(2,1)S(1)} %get-tuple-element.44), channel_id=1, source_target_pairs={{0,4},{4,0},{8,12},{12,8},{16,20},{20,16},{24,28},{28,24},{1,5},{5... | collective-permute-start | bytes 1081352 | tf_op jit(solution)/shard_map/ppermute | solution.py:19
  7.1 7.0 %collective-permute-start.5 = (f32[16,640]{1,0:T(8,128)S(1)}, f32[16,640]{1,0:T(8,128)S(1)}, u32[]{:S(2)}, u32[]{:S(2)}) collective-permute-start(f32[16,640]{1,0:T(8,128)S(1)} %add.9.refs_0_), channel_id=1, source_target_pairs={{0,24},{4,28},{8,16},{12,20},{16,8},{20,12},{24,0},{28,4},{1,25},{... | collective-permute-start | bytes 122888 | tf_op jit(solution)/shard_map/ppermute | solution.py:19
  11.5 4.9 %collective-permute-start.4 = (f32[16,640]{1,0:T(8,128)S(1)}, f32[16,640]{1,0:T(8,128)S(1)}, u32[]{:S(2)}, u32[]{:S(2)}) collective-permute-start(f32[16,640]{1,0:T(8,128)S(1)} %add.9.refs_0_), channel_id=1, source_target_pairs={{0,16},{4,20},{8,24},{12,28},{16,0},{20,4},{24,8},{28,12},{1,17},{... | collective-permute-start | bytes 122888 | tf_op jit(solution)/shard_map/ppermute | solution.py:19
  11.5 4.9 %collective-permute-start.3 = (f32[16,640]{1,0:T(8,128)S(1)}, f32[16,640]{1,0:T(8,128)S(1)}, u32[]{:S(2)}, u32[]{:S(2)}) collective-permute-start(f32[16,640]{1,0:T(8,128)S(1)} %add.9.refs_0_), channel_id=1, source_target_pairs={{0,8},{4,12},{8,0},{12,4},{16,24},{20,28},{24,16},{28,20},{1,9},{5... | collective-permute-start | bytes 122888 | tf_op jit(solution)/shard_map/ppermute | solution.py:19
  12.1 11.6 %collective-permute-start.1 = (bf16[256,512]{1,0:T(8,128)(2,1)S(1)}, bf16[256,512]{1,0:T(8,128)(2,1)S(1)}, u32[]{:S(2)}, u32[]{:S(2)}) collective-permute-start(bf16[256,512]{1,0:T(8,128)(2,1)S(1)} %bitcast.5), channel_id=1, source_target_pairs={{0,2},{1,3},{2,0},{3,1},{4,6},{5,7},{6,4},{7,5},{8,10},{9,11},{10,... | collective-permute-start | bytes 786440 | tf_op jit(solution)/shard_map/ppermute | solution.py:500
  16.4 12.2 %copy-start.5 = (bf16[8,8,128,128]{3,2,1,0:T(8,128)(2,1)S(1)}, bf16[8,8,128,128]{3,2,1,0:T(8,128)(2,1)}, u32[]{:S(2)}) copy-start(bf16[8,8,128,128]{3,2,1,0:T(8,128)(2,1)} %refs_5_.5) | copy-start | bytes 6291460
  17.0 4.1 %collective-permute-start.6 = (bf16[16,1536]{1,0:T(8,128)(2,1)S(1)}, bf16[16,1536]{1,0:T(8,128)(2,1)S(1)}, u32[]{:S(2)}, u32[]{:S(2)}) collective-permute-start(bf16[16,1536]{1,0:T(8,128)(2,1)S(1)} %get-tuple-element.58.send_ref.refs_0_), channel_id=1, source_target_pairs={{0,4},{4,0},{8,12},{12,8},{16,20},{20,16},{24,28},{28,24},{1,5},{5... | collective-permute-start | bytes 147464 | tf_op jit(solution)/shard_map/ppermute | solution.py:19
  21.1 6.0 %collective-permute-start.10 = (bf16[16,1536]{1,0:T(8,128)(2,1)S(1)}, bf16[16,1536]{1,0:T(8,128)(2,1)S(1)}, u32[]{:S(2)}, u32[]{:S(2)}) collective-permute-start(bf16[16,1536]{1,0:T(8,128)(2,1)S(1)} %get-tuple-element.62), channel_id=1, source_target_pairs={{0,24},{4,28},{8,16},{12,20},{16,8},{20,12},{24,0},{28,4},{1,25},{... | collective-permute-start | bytes 147464 | tf_op jit(solution)/shard_map/ppermute | solution.py:19
  22.6 6.0 %collective-permute-start.8 = (bf16[16,1536]{1,0:T(8,128)(2,1)S(1)}, bf16[16,1536]{1,0:T(8,128)(2,1)S(1)}, u32[]{:S(2)}, u32[]{:S(2)}) collective-permute-start(bf16[16,1536]{1,0:T(8,128)(2,1)S(1)} %get-tuple-element.62), channel_id=1, source_target_pairs={{0,8},{4,12},{8,0},{12,4},{16,24},{20,28},{24,16},{28,20},{1,9},{5... | collective-permute-start | bytes 147464 | tf_op jit(solution)/shard_map/ppermute | solution.py:19
  23.7 5.7 %collective-permute-start.11 = (bf16[256,512]{1,0:T(8,128)(2,1)S(1)}, bf16[256,512]{1,0:T(8,128)(2,1)S(1)}, u32[]{:S(2)}, u32[]{:S(2)}) collective-permute-start(bf16[256,512]{1,0:T(8,128)(2,1)S(1)} %bitcast.6), channel_id=1, source_target_pairs={{0,1},{1,0},{2,3},{3,2},{4,5},{5,4},{6,7},{7,6},{8,9},{9,8},{10,11... | collective-permute-start | bytes 786440 | tf_op jit(solution)/shard_map/ppermute | solution.py:500
  23.7 5.6 %collective-permute-start.9 = (bf16[16,512]{1,0:T(8,128)(2,1)S(1)}, bf16[16,512]{1,0:T(8,128)(2,1)S(1)}, u32[]{:S(2)}, u32[]{:S(2)}) collective-permute-start(bf16[16,512]{1,0:T(8,128)(2,1)S(1)} %get-tuple-element.61.refs_0_), channel_id=1, source_target_pairs={{0,16},{4,20},{8,24},{12,28},{16,0},{20,4},{24,8},{28,12},{1,17},{... | collective-permute-start | bytes 49160 | tf_op jit(solution)/shard_map/ppermute | solution.py:19
  25.5 3.9 %collective-permute-start.12 = (bf16[256,512]{1,0:T(8,128)(2,1)S(1)}, bf16[256,512]{1,0:T(8,128)(2,1)S(1)}, u32[]{:S(2)}, u32[]{:S(2)}) collective-permute-start(bf16[256,512]{1,0:T(8,128)(2,1)S(1)} %collective-permute-done.1.refs_14_.refs_12_), channel_id=1, source_target_pairs={{0,1},{1,0},{2,3},{3,2},{4,5},{5,4},{6,7},{7,6},{8,9},{9,8},{10,11... | collective-permute-start | bytes 786440 | tf_op jit(solution)/shard_map/ppermute | solution.py:507
  27.1 9.3 %collective-permute-start.7 = (bf16[352,512]{1,0:T(8,128)(2,1)S(1)}, bf16[352,512]{1,0:T(8,128)(2,1)S(1)}, u32[]{:S(2)}, u32[]{:S(2)}) collective-permute-start(bf16[352,512]{1,0:T(8,128)(2,1)S(1)} %collective-permute-done.refs_0_.refs_12_), channel_id=1, source_target_pairs={{0,2},{1,3},{2,0},{3,1},{4,6},{5,7},{6,4},{7,5},{8,10},{9,11},{10,... | collective-permute-start | bytes 1081352 | tf_op jit(solution)/shard_map/ppermute | solution.py:609
  30.9 8.4 %collective-permute-start.18 = (bf16[352,512]{1,0:T(8,128)(2,1)S(1)}, bf16[352,512]{1,0:T(8,128)(2,1)S(1)}, u32[]{:S(2)}, u32[]{:S(2)}) collective-permute-start(bf16[352,512]{1,0:T(8,128)(2,1)S(1)} %collective-permute-done.refs_0_.refs_12_), channel_id=1, source_target_pairs={{0,1},{1,0},{2,3},{3,2},{4,5},{5,4},{6,7},{7,6},{8,9},{9,8},{10,11... | collective-permute-start | bytes 1081352 | tf_op jit(solution)/shard_map/ppermute | solution.py:641
  30.9 4.0 %collective-permute-start.13 = (f32[16,640]{1,0:T(8,128)S(1)}, f32[16,640]{1,0:T(8,128)S(1)}, u32[]{:S(2)}, u32[]{:S(2)}) collective-permute-start(f32[16,640]{1,0:T(8,128)S(1)} %get-tuple-element.70), channel_id=1, source_target_pairs={{0,4},{4,0},{8,12},{12,8},{16,20},{20,16},{24,28},{28,24},{1,5},{5... | collective-permute-start | bytes 122888 | tf_op jit(solution)/shard_map/ppermute | solution.py:19
  32.6 6.9 %collective-permute-start.17 = (f32[16,1024]{1,0:T(8,128)S(1)}, f32[16,1024]{1,0:T(8,128)S(1)}, u32[]{:S(2)}, u32[]{:S(2)}) collective-permute-start(f32[16,1024]{1,0:T(8,128)S(1)} %get-tuple-element.74), channel_id=1, source_target_pairs={{0,4},{4,0},{8,12},{12,8},{16,20},{20,16},{24,28},{28,24},{1,5},{5... | collective-permute-start | bytes 196616 | tf_op jit(solution)/shard_map/ppermute | solution.py:19
  34.9 6.1 %collective-permute-start.16 = (f32[16,640]{1,0:T(8,128)S(1)}, f32[16,640]{1,0:T(8,128)S(1)}, u32[]{:S(2)}, u32[]{:S(2)}) collective-permute-start(f32[16,640]{1,0:T(8,128)S(1)} %add.10.refs_0_), channel_id=1, source_target_pairs={{0,24},{4,28},{8,16},{12,20},{16,8},{20,12},{24,0},{28,4},{1,25},{... | collective-permute-start | bytes 122888 | tf_op jit(solution)/shard_map/ppermute | solution.py:19
  36.4 5.4 %collective-permute-start.15 = (f32[16,640]{1,0:T(8,128)S(1)}, f32[16,640]{1,0:T(8,128)S(1)}, u32[]{:S(2)}, u32[]{:S(2)}) collective-permute-start(f32[16,640]{1,0:T(8,128)S(1)} %add.10.refs_0_), channel_id=1, source_target_pairs={{0,16},{4,20},{8,24},{12,28},{16,0},{20,4},{24,8},{28,12},{1,17},{... | collective-permute-start | bytes 122888 | tf_op jit(solution)/shard_map/ppermute | solution.py:19
  36.4 5.4 %collective-permute-start.14 = (f32[16,640]{1,0:T(8,128)S(1)}, f32[16,640]{1,0:T(8,128)S(1)}, u32[]{:S(2)}, u32[]{:S(2)}) collective-permute-start(f32[16,640]{1,0:T(8,128)S(1)} %add.10.refs_0_), channel_id=1, source_target_pairs={{0,8},{4,12},{8,0},{12,4},{16,24},{20,28},{24,16},{28,20},{1,9},{5... | collective-permute-start | bytes 122888 | tf_op jit(solution)/shard_map/ppermute | solution.py:19
  39.3 2.5 %collective-permute-start.19 = (bf16[352,512]{1,0:T(8,128)(2,1)S(1)}, bf16[352,512]{1,0:T(8,128)(2,1)S(1)}, u32[]{:S(2)}, u32[]{:S(2)}) collective-permute-start(bf16[352,512]{1,0:T(8,128)(2,1)S(1)} %collective-permute-done.7.refs_2_.refs_14_), channel_id=1, source_target_pairs={{0,1},{1,0},{2,3},{3,2},{4,5},{5,4},{6,7},{7,6},{8,9},{9,8},{10,11... | collective-permute-start | bytes 1081352 | tf_op jit(solution)/shard_map/ppermute | solution.py:641
  43.1 6.1 %collective-permute-start.22 = (bf16[16,1536]{1,0:T(8,128)(2,1)S(1)}, bf16[16,1536]{1,0:T(8,128)(2,1)S(1)}, u32[]{:S(2)}, u32[]{:S(2)}) collective-permute-start(bf16[16,1536]{1,0:T(8,128)(2,1)S(1)} %get-tuple-element.78.refs_1_), channel_id=1, source_target_pairs={{0,24},{4,28},{8,16},{12,20},{16,8},{20,12},{24,0},{28,4},{1,25},{... | collective-permute-start | bytes 147464 | tf_op jit(solution)/shard_map/ppermute | solution.py:19
  44.9 4.6 %collective-permute-start.20 = (bf16[16,1536]{1,0:T(8,128)(2,1)S(1)}, bf16[16,1536]{1,0:T(8,128)(2,1)S(1)}, u32[]{:S(2)}, u32[]{:S(2)}) collective-permute-start(bf16[16,1536]{1,0:T(8,128)(2,1)S(1)} %get-tuple-element.78.refs_1_), channel_id=1, source_target_pairs={{0,8},{4,12},{8,0},{12,4},{16,24},{20,28},{24,16},{28,20},{1,9},{5... | collective-permute-start | bytes 147464 | tf_op jit(solution)/shard_map/ppermute | solution.py:19
  45.2 5.1 %collective-permute-start.21 = (bf16[16,512]{1,0:T(8,128)(2,1)S(1)}, bf16[16,512]{1,0:T(8,128)(2,1)S(1)}, u32[]{:S(2)}, u32[]{:S(2)}) collective-permute-start(bf16[16,512]{1,0:T(8,128)(2,1)S(1)} %get-tuple-element.77.refs_0_), channel_id=1, source_target_pairs={{0,16},{4,20},{8,24},{12,28},{16,0},{20,4},{24,8},{28,12},{1,17},{... | collective-permute-start | bytes 49160 | tf_op jit(solution)/shard_map/ppermute | solution.py:19
  51.1 3.7 %collective-permute-start.23 = (f32[16,128]{1,0:T(8,128)S(1)}, f32[16,128]{1,0:T(8,128)S(1)}, u32[]{:S(2)}, u32[]{:S(2)}) collective-permute-start(f32[16,128]{1,0:T(8,128)S(1)} %fourth.1), channel_id=1, source_target_pairs={{0,4},{4,0},{8,12},{12,8},{16,20},{20,16},{24,28},{28,24},{1,5},{5... | collective-permute-start | bytes 24584 | tf_op jit(solution)/shard_map/ppermute | solution.py:19
  54.8 5.4 %collective-permute-start.26 = (f32[16,128]{1,0:T(8,128)S(1)}, f32[16,128]{1,0:T(8,128)S(1)}, u32[]{:S(2)}, u32[]{:S(2)}) collective-permute-start(f32[16,128]{1,0:T(8,128)S(1)} %add.11.refs_0_), channel_id=1, source_target_pairs={{0,24},{4,28},{8,16},{12,20},{16,8},{20,12},{24,0},{28,4},{1,25},{... | collective-permute-start | bytes 24584 | tf_op jit(solution)/shard_map/ppermute | solution.py:19
  56.7 4.6 %collective-permute-start.25 = (f32[16,128]{1,0:T(8,128)S(1)}, f32[16,128]{1,0:T(8,128)S(1)}, u32[]{:S(2)}, u32[]{:S(2)}) collective-permute-start(f32[16,128]{1,0:T(8,128)S(1)} %add.11.refs_0_), channel_id=1, source_target_pairs={{0,16},{4,20},{8,24},{12,28},{16,0},{20,4},{24,8},{28,12},{1,17},{... | collective-permute-start | bytes 24584 | tf_op jit(solution)/shard_map/ppermute | solution.py:19
  57.6 3.7 %collective-permute-start.24 = (f32[16,128]{1,0:T(8,128)S(1)}, f32[16,128]{1,0:T(8,128)S(1)}, u32[]{:S(2)}, u32[]{:S(2)}) collective-permute-start(f32[16,128]{1,0:T(8,128)S(1)} %add.11.refs_0_), channel_id=1, source_target_pairs={{0,8},{4,12},{8,0},{12,4},{16,24},{20,28},{24,16},{28,20},{1,9},{5... | collective-permute-start | bytes 24584 | tf_op jit(solution)/shard_map/ppermute | solution.py:19

commit v9 on v8

--- a/solution.py
+++ b/solution.py
@@ -130,7 +130,9 @@
 
 
 def other_maps_kernel(base, rank, block, *refs):
-    *pack_refs, maps_ref = refs
+    *pack_refs, maps_ref, turned_ref = refs
+    for place, ref in enumerate(pack_refs):
+        turned_ref[place] = ref[:base, :].T
     maps_ref[...] = jnp.zeros(maps_ref.shape, BF)
     other_maps(base, rank, block, list(enumerate(pack_refs)), maps_ref)
 
@@ -143,12 +145,15 @@
     pair_ref[...] = pair
 
 
-def neighbour_field(panels, scaled, proj, part_refs, onward_ref):
+def neighbour_field(panels, scaled, proj, turned_ref, part_refs, onward_ref):
     rows = proj.shape[0]
     both = jnp.concatenate(split(proj), axis=0)
     size = panels // len(part_refs)
     for mask, ref in enumerate(part_refs):
-        part = dot_nt(both, ref[:size, :])
+        if mask < turned_ref.shape[0]:
+            part = dot_nn(both, turned_ref[mask])
+        else:
+            part = dot_nt(both, ref[:size, :])
         start = pl.multiple_of((lax.axis_index("rhs") ^ mask) * size, size)
         field = scaled(start, size) - (part[:rows] + part[rows:])
         onward_ref[:, pl.ds(start, size)] = field.astype(BF)
@@ -373,7 +378,7 @@
     field_low = pre.astype(BF)
     pre_ref[...] = pre
     if extra:
-        got_ref, *part_refs, some_maps_ref, onward_ref, pair_ref = extra
+        got_ref, *part_refs, some_maps_ref, turned_ref, onward_ref, pair_ref = extra
         other_maps_ref[...] = some_maps_ref[...]
         last = len(part_refs) - 1
         other_maps(panels // (last + 1), rank, block, [(last, part_refs[last])], other_maps_ref)
@@ -395,7 +400,7 @@
         def scaled(start, size):
             return scaled_ref[:, pl.ds(start, size)]
 
-        neighbour_field(panels, scaled, proj, part_refs, onward_ref)
+        neighbour_field(panels, scaled, proj, turned_ref, part_refs, onward_ref)
         send_ref[...] = field_low
         pair_charges(field_low, maps_ref, other_maps_ref, onward_ref, pair_ref)
     else:
@@ -641,14 +646,14 @@
             lax.ppermute(x, "rhs", [(i, i ^ 1) for i in range(quarters)]) for x in (mine, far)
         ]
         mine = [mine, near_pack, far, last_pack]
-        (some_maps,) = call(
+        extra = call(
             "other_maps",
             lambda *refs: other_maps_kernel(panels // quarters, rank, block, *refs),
-            [(maps.shape, BF)],
+            [(maps.shape, BF), ((quarters - 1, width, panels // quarters), BF)],
             mine[:-1],
             flops=10**10,
         )
-        extra = [again, *mine, some_maps]
+        extra = [again, *mine, *extra]
         outs = [((rows, long), BF), ((rows, long - panels), BF), *outs, ((rows, panels), BF)]
     else:
         outs += [((rows, long), BF)]

time: 62.4 us -> 62.3 us (level)
  transfers between devices with their start and end apart: 27 -> 27, of which waited for: 12 -> 12; matrix products, arithmetic and copies ran while one was open for 0% -> 0% of each run, Pallas kernels for 7% -> 8%
where the time goes in v9:
time: 62.3 us; the launch traced here: 62.2 us
  starting transfers between devices  34.9 us (56%)
  waiting for transfers between devices  17.4 us (28%)
  Pallas kernels  9.78 us (16%)
    ppermute x21, starting transfers between devices, swap(): return lax.ppermute(values, AXIS, [(i, i ^ mask) for i in range(count)])  31.5 us
    ppermute x21, waiting for transfers between devices, swap(): return lax.ppermute(values, AXIS, [(i, i ^ mask) for i in range(count)])  17.3 us
    pallas_call x12, Pallas kernels, call(): pl.pallas_call(kernel, name=name, out_shape=out_shapes, in_specs=specs, o...  9.78 us
    ppermute x2, starting transfers between devices, gather_quarters(): lax.ppermute(coupling, 'rhs', pair)  1.64 us
    ppermute x1, starting transfers between devices, on_device(): far = lax.ppermute(mine, 'rhs', [(i, i ^ 2) for i in range(quarters)])  1.49 us
  transfers between devices with their start and end apart: 27, of which 12 were waited for; matrix products, arithmetic and copies ran while one was open for 0% of the time, Pallas kernels for 8%

profile of v9, /device:TPU:0, one launch (start us, length us, event | category | flops | bytes accessed | tf_op | source)
XLA Modules:
  0.0 62.2 jit_solution(12372808513311639586)
XLA Ops:
  0.0 2.0 %open.1 = (f32[16,640]{1,0:T(8,128)S(1)}, f32[16,1024]{1,0:T(8,128)S(1)}, f32[1,1024]{1,0:T(1,128)S(1)}, f32[1,1024]{1,0:T(1,128)S(1)}, bf16[1024,512]{1,0:T(8,1...) custom-call(f32[16,1024]{1,0:T(8,128)} %refs_0_.2, f32[1024,512]{1,0:T(8,128)} %refs_1_.1, ...), custom_call_target="tpu_custom_call" | custom-call | tf_op jit(solution)/shard_map/open/pallas_call | solution.py:538
  2.0 3.0 %collective-permute-start.2 = (f32[16,640]{1,0:T(8,128)S(1)}, f32[16,640]{1,0:T(8,128)S(1)}, u32[]{:S(2)}, u32[]{:S(2)}) collective-permute-start(f32[16,640]{1,0:T(8,128)S(1)} %get-tuple-element.49), channel_id=1, source_target_pairs={{0,4},{4,0},{8,12},{12,8},{16,20},{20,16},{24,28},{28,24},{1,5},{5... | collective-permute-start | bytes 122888 | tf_op jit(solution)/shard_map/ppermute | solution.py:19
  5.1 0.1 collective-permute-start
  5.2 0.6 %turn.1 = (bf16[512,1024]{1,0:T(8,128)(2,1)S(1)}, bf16[512,1024]{1,0:T(8,128)(2,1)S(1)}) custom-call(bf16[1024,512]{1,0:T(8,128)(2,1)S(1)} %get-tuple-element.50.high_ref.refs_10_, bf16[1024,512]{1,0:T(8,128)(2,1)S(1)} %get-tuple-element.51.low_ref.refs_11_), custom_call_target="tpu_custom_call" | custom-call | tf_op jit(solution)/shard_map/turn/pallas_call | solution.py:538
  5.8 1.3 %collective-permute-done.2 = f32[16,640]{1,0:T(8,128)S(1)} collective-permute-done((f32[16,640]{1,0:T(8,128)S(1)}, f32[16,640]{1,0:T(8,128)S(1)}, u32[]{:S(2)}, u32[]{:S(2)}) %collective-permute-start.2) | collective-permute-done | bytes 40992 | tf_op jit(solution)/shard_map/ppermute | solution.py:19
  7.1 4.4 %collective-permute-start.5 = (f32[16,640]{1,0:T(8,128)S(1)}, f32[16,640]{1,0:T(8,128)S(1)}, u32[]{:S(2)}, u32[]{:S(2)}) collective-permute-start(f32[16,640]{1,0:T(8,128)S(1)} %add.9.refs_0_), channel_id=1, source_target_pairs={{0,24},{4,28},{8,16},{12,20},{16,8},{20,12},{24,0},{28,4},{1,25},{... | collective-permute-start | bytes 122888 | tf_op jit(solution)/shard_map/ppermute | solution.py:19
  11.5 0.0 collective-permute-start.4
  11.5 0.6 %collective-permute-start.3 = (f32[16,640]{1,0:T(8,128)S(1)}, f32[16,640]{1,0:T(8,128)S(1)}, u32[]{:S(2)}, u32[]{:S(2)}) collective-permute-start(f32[16,640]{1,0:T(8,128)S(1)} %add.9.refs_0_), channel_id=1, source_target_pairs={{0,8},{4,12},{8,0},{12,4},{16,24},{20,28},{24,16},{28,20},{1,9},{5... | collective-permute-start | bytes 122888 | tf_op jit(solution)/shard_map/ppermute | solution.py:19
  12.1 1.6 %collective-permute-start.1 = (bf16[256,512]{1,0:T(8,128)(2,1)S(1)}, bf16[256,512]{1,0:T(8,128)(2,1)S(1)}, u32[]{:S(2)}, u32[]{:S(2)}) collective-permute-start(bf16[256,512]{1,0:T(8,128)(2,1)S(1)} %bitcast.5), channel_id=1, source_target_pairs={{0,2},{1,3},{2,0},{3,1},{4,6},{5,7},{6,4},{7,5},{8,10},{9,11},{10,... | collective-permute-start | bytes 786440 | tf_op jit(solution)/shard_map/ppermute | solution.py:505
  13.8 0.2 maps.1
  14.0 0.0 collective-permute-done.5.refs_3_
  14.1 2.4 %collective-permute-done.4.refs_2_ = f32[16,640]{1,0:T(8,128)S(1)} collective-permute-done((f32[16,640]{1,0:T(8,128)S(1)}, f32[16,640]{1,0:T(8,128)S(1)}, u32[]{:S(2)}, u32[]{:S(2)}) %collective-permute-start.4) | collective-permute-done | bytes 40992 | tf_op jit(solution)/shard_map/ppermute | solution.py:19
  16.4 0.0 collective-permute-done.3.refs_1_
  16.4 0.6 first.1
  17.0 1.7 %collective-permute-start.6 = (bf16[16,1536]{1,0:T(8,128)(2,1)S(1)}, bf16[16,1536]{1,0:T(8,128)(2,1)S(1)}, u32[]{:S(2)}, u32[]{:S(2)}) collective-permute-start(bf16[16,1536]{1,0:T(8,128)(2,1)S(1)} %get-tuple-element.60.send_ref.refs_0_), channel_id=1, source_target_pairs={{0,4},{4,0},{8,12},{12,8},{16,20},{20,16},{24,28},{28,24},{1,5},{5... | collective-permute-start | bytes 147464 | tf_op jit(solution)/shard_map/ppermute | solution.py:19
  18.7 2.4 %collective-permute-done.6.near_ref.refs_1_ = bf16[16,1536]{1,0:T(8,128)(2,1)S(1)} collective-permute-done((bf16[16,1536]{1,0:T(8,128)(2,1)S(1)}, bf16[16,1536]{1,0:T(8,128)(2,1)S(1)}, u32[]{:S(2)}, u32[]{:S(2)}) %collective-permute-start.6) | collective-permute-done | bytes 49184 | tf_op jit(solution)/shard_map/ppermute | solution.py:19
  21.1 1.5 %collective-permute-start.10 = (bf16[16,1536]{1,0:T(8,128)(2,1)S(1)}, bf16[16,1536]{1,0:T(8,128)(2,1)S(1)}, u32[]{:S(2)}, u32[]{:S(2)}) collective-permute-start(bf16[16,1536]{1,0:T(8,128)(2,1)S(1)} %get-tuple-element.64), channel_id=1, source_target_pairs={{0,24},{4,28},{8,16},{12,20},{16,8},{20,12},{24,0},{28,4},{1,25},{... | collective-permute-start | bytes 147464 | tf_op jit(solution)/shard_map/ppermute | solution.py:19
  22.6 1.1 %collective-permute-start.8 = (bf16[16,1536]{1,0:T(8,128)(2,1)S(1)}, bf16[16,1536]{1,0:T(8,128)(2,1)S(1)}, u32[]{:S(2)}, u32[]{:S(2)}) collective-permute-start(bf16[16,1536]{1,0:T(8,128)(2,1)S(1)} %get-tuple-element.64), channel_id=1, source_target_pairs={{0,8},{4,12},{8,0},{12,4},{16,24},{20,28},{24,16},{28,20},{1,9},{5... | collective-permute-start | bytes 147464 | tf_op jit(solution)/shard_map/ppermute | solution.py:19
  23.7 0.0 collective-permute-start.11
  23.7 0.0 collective-permute-done.1.refs_14_.refs_12_
  23.7 1.8 %collective-permute-start.9 = (bf16[16,512]{1,0:T(8,128)(2,1)S(1)}, bf16[16,512]{1,0:T(8,128)(2,1)S(1)}, u32[]{:S(2)}, u32[]{:S(2)}) collective-permute-start(bf16[16,512]{1,0:T(8,128)(2,1)S(1)} %get-tuple-element.63.refs_0_), channel_id=1, source_target_pairs={{0,16},{4,20},{8,24},{12,28},{16,0},{20,4},{24,8},{28,12},{1,17},{... | collective-permute-start | bytes 49160 | tf_op jit(solution)/shard_map/ppermute | solution.py:19
  25.5 0.0 collective-permute-done.refs_0_.refs_12_
  25.5 0.2 collective-permute-start.12
  25.8 1.4 %collective-permute-done.10.refs_3_ = bf16[16,1536]{1,0:T(8,128)(2,1)S(1)} collective-permute-done((bf16[16,1536]{1,0:T(8,128)(2,1)S(1)}, bf16[16,1536]{1,0:T(8,128)(2,1)S(1)}, u32[]{:S(2)}, u32[]{:S(2)}) %collective-permute-start.10) | collective-permute-done | bytes 49184 | tf_op jit(solution)/shard_map/ppermute | solution.py:19
  27.1 1.5 %collective-permute-start.7 = (bf16[352,512]{1,0:T(8,128)(2,1)S(1)}, bf16[352,512]{1,0:T(8,128)(2,1)S(1)}, u32[]{:S(2)}, u32[]{:S(2)}) collective-permute-start(bf16[352,512]{1,0:T(8,128)(2,1)S(1)} %collective-permute-done.refs_0_.refs_12_), channel_id=1, source_target_pairs={{0,2},{1,3},{2,0},{3,1},{4,6},{5,7},{6,4},{7,5},{8,10},{9,11},{10,... | collective-permute-start | bytes 1081352 | tf_op jit(solution)/shard_map/ppermute | solution.py:614
  28.6 0.0 collective-permute-done.8.refs_2_.refs_1_
  28.6 0.7 %near.2.refs_8_ = f32[16,1024]{1,0:T(8,128)S(1)} custom-call(bf16[16,1536]{1,0:T(8,128)(2,1)S(1)} %get-tuple-element.60.send_ref.refs_0_, bf16[16,1536]{1,0:T(8,128)(2,1)S(1)} %collective-permute-done.6.near_ref.refs_1_, bf16[16,1536]{1,0:T(8,128)(2,1)S(1)} %collective-permute-done.8.refs_2_.refs_1_, bf16[16,1536]{1,0:T(8,128)(2,1)S(1)} %collective-permute-done.10.refs_3_, ...), custom_call_target="tpu_custom_call" | custom-call | flops 10000000000 | bytes 20000000 | tf_op jit(solution)/shard_map/near/pallas_call | solution.py:538
  29.4 0.0 collective-permute-done.9.refs_2_
  29.4 0.0 collective-permute-done.11.refs_13_.refs_11_
  29.4 0.0 collective-permute-done.12.refs_15_.refs_13_
  29.4 1.5 %second.1 = (f32[16,1024]{1,0:T(8,128)S(1)}, f32[16,1024]{1,0:T(8,128)S(1)}, f32[16,640]{1,0:T(8,128)S(1)}) custom-call(bf16[16,512]{1,0:T(8,128)(2,1)S(1)} %get-tuple-element.63.refs_0_, bf16[16,1536]{1,0:T(8,128)(2,1)S(1)} %collective-permute-done.8.refs_2_.refs_1_, bf16[16,512]{1,0:T(8,128)(2,1)S(1)} %collective-permute-done.9.refs_2_, ...), custom_call_target="tpu_custom_call" | custom-call | flops 10000000000 | bytes 20000000 | tf_op jit(solution)/shard_map/second/pallas_call | solution.py:538
  30.9 0.0 collective-permute-start.18
  30.9 1.7 %collective-permute-start.13 = (f32[16,640]{1,0:T(8,128)S(1)}, f32[16,640]{1,0:T(8,128)S(1)}, u32[]{:S(2)}, u32[]{:S(2)}) collective-permute-start(f32[16,640]{1,0:T(8,128)S(1)} %get-tuple-element.72), channel_id=1, source_target_pairs={{0,4},{4,0},{8,12},{12,8},{16,20},{20,16},{24,28},{28,24},{1,5},{5... | collective-permute-start | bytes 122888 | tf_op jit(solution)/shard_map/ppermute | solution.py:19
  32.6 0.4 collective-permute-start.17
  33.0 2.0 %collective-permute-done.13 = f32[16,640]{1,0:T(8,128)S(1)} collective-permute-done((f32[16,640]{1,0:T(8,128)S(1)}, f32[16,640]{1,0:T(8,128)S(1)}, u32[]{:S(2)}, u32[]{:S(2)}) %collective-permute-start.13) | collective-permute-done | bytes 40992 | tf_op jit(solution)/shard_map/ppermute | solution.py:19
  34.9 1.5 %collective-permute-start.16 = (f32[16,640]{1,0:T(8,128)S(1)}, f32[16,640]{1,0:T(8,128)S(1)}, u32[]{:S(2)}, u32[]{:S(2)}) collective-permute-start(f32[16,640]{1,0:T(8,128)S(1)} %add.10.refs_0_), channel_id=1, source_target_pairs={{0,24},{4,28},{8,16},{12,20},{16,8},{20,12},{24,0},{28,4},{1,25},{... | collective-permute-start | bytes 122888 | tf_op jit(solution)/shard_map/ppermute | solution.py:19
  36.4 0.0 collective-permute-start.15
  36.4 0.0 collective-permute-done.7.refs_2_.refs_14_
  36.4 2.9 %collective-permute-start.14 = (f32[16,640]{1,0:T(8,128)S(1)}, f32[16,640]{1,0:T(8,128)S(1)}, u32[]{:S(2)}, u32[]{:S(2)}) collective-permute-start(f32[16,640]{1,0:T(8,128)S(1)} %add.10.refs_0_), channel_id=1, source_target_pairs={{0,8},{4,12},{8,0},{12,4},{16,24},{20,28},{24,16},{28,20},{1,9},{5... | collective-permute-start | bytes 122888 | tf_op jit(solution)/shard_map/ppermute | solution.py:19
  39.3 0.0 collective-permute-done.18.refs_1_.refs_13_
  39.3 0.0 collective-permute-start.19
  39.3 0.4 other_maps.1
  39.7 0.0 collective-permute-done.17.refs_11_
  39.7 1.4 %collective-permute-done.16.refs_3_ = f32[16,640]{1,0:T(8,128)S(1)} collective-permute-done((f32[16,640]{1,0:T(8,128)S(1)}, f32[16,640]{1,0:T(8,128)S(1)}, u32[]{:S(2)}, u32[]{:S(2)}) %collective-permute-start.16) | collective-permute-done | bytes 40992 | tf_op jit(solution)/shard_map/ppermute | solution.py:19
  41.1 0.8 %collective-permute-done.15.refs_2_ = f32[16,640]{1,0:T(8,128)S(1)} collective-permute-done((f32[16,640]{1,0:T(8,128)S(1)}, f32[16,640]{1,0:T(8,128)S(1)}, u32[]{:S(2)}, u32[]{:S(2)}) %collective-permute-start.15) | collective-permute-done | bytes 40992 | tf_op jit(solution)/shard_map/ppermute | solution.py:19
  41.8 0.0 collective-permute-done.14.refs_1_
  41.8 0.0 collective-permute-done.19.refs_15_
  41.8 1.1 %third.1 = (bf16[16,1536]{1,0:T(8,128)(2,1)S(1)}, bf16[16,512]{1,0:T(8,128)(2,1)S(1)}, f32[16,1024]{1,0:T(8,128)S(1)}, f32[16,1024]{1,0:T(8,128)S(1)}, f32[16,12...) custom-call(f32[16,640]{1,0:T(8,128)S(1)} %add.10.refs_0_, f32[16,640]{1,0:T(8,128)S(1)} %collective-permute-done.14.refs_1_, ...), custom_call_target="tpu_custom_call" | custom-call | tf_op jit(solution)/shard_map/third/pallas_call | solution.py:538
  43.0 1.8 %collective-permute-start.22 = (bf16[16,1536]{1,0:T(8,128)(2,1)S(1)}, bf16[16,1536]{1,0:T(8,128)(2,1)S(1)}, u32[]{:S(2)}, u32[]{:S(2)}) collective-permute-start(bf16[16,1536]{1,0:T(8,128)(2,1)S(1)} %get-tuple-element.82.refs_1_), channel_id=1, source_target_pairs={{0,24},{4,28},{8,16},{12,20},{16,8},{20,12},{24,0},{28,4},{1,25},{... | collective-permute-start | bytes 147464 | tf_op jit(solution)/shard_map/ppermute | solution.py:19
  44.8 0.2 collective-permute-start.20
  45.0 2.3 %collective-permute-start.21 = (bf16[16,512]{1,0:T(8,128)(2,1)S(1)}, bf16[16,512]{1,0:T(8,128)(2,1)S(1)}, u32[]{:S(2)}, u32[]{:S(2)}) collective-permute-start(bf16[16,512]{1,0:T(8,128)(2,1)S(1)} %get-tuple-element.81.refs_0_), channel_id=1, source_target_pairs={{0,16},{4,20},{8,24},{12,28},{16,0},{20,4},{24,8},{28,12},{1,17},{... | collective-permute-start | bytes 49160 | tf_op jit(solution)/shard_map/ppermute | solution.py:19
  47.4 1.7 %collective-permute-done.22.refs_3_ = bf16[16,1536]{1,0:T(8,128)(2,1)S(1)} collective-permute-done((bf16[16,1536]{1,0:T(8,128)(2,1)S(1)}, bf16[16,1536]{1,0:T(8,128)(2,1)S(1)}, u32[]{:S(2)}, u32[]{:S(2)}) %collective-permute-start.22) | collective-permute-done | bytes 49184 | tf_op jit(solution)/shard_map/ppermute | solution.py:19
  49.1 0.3 collective-permute-done.20.refs_2_.refs_1_
  49.4 0.7 %near.3.refs_8_ = f32[16,1024]{1,0:T(8,128)S(1)} custom-call(bf16[16,1024]{1,0:T(8,128)(2,1)S(1)} %get-tuple-element.85.refs_0_, bf16[16,1536]{1,0:T(8,128)(2,1)S(1)} %get-tuple-element.82.refs_1_, bf16[16,1536]{1,0:T(8,128)(2,1)S(1)} %collective-permute-done.20.refs_2_.refs_1_, bf16[16,1536]{1,0:T(8,128)(2,1)S(1)} %collective-permute-done.22.refs_3_, ...), custom_call_target="tpu_custom_call" | custom-call | flops 10000000000 | bytes 20000000 | tf_op jit(solution)/shard_map/near/pallas_call | solution.py:538
  50.2 0.0 collective-permute-done.21.refs_2_
  50.2 0.9 %fourth.1 = f32[16,128]{1,0:T(8,128)S(1)} custom-call(bf16[16,512]{1,0:T(8,128)(2,1)S(1)} %get-tuple-element.81.refs_0_, bf16[16,1536]{1,0:T(8,128)(2,1)S(1)} %collective-permute-done.20.refs_2_.refs_1_, bf16[16,512]{1,0:T(8,128)(2,1)S(1)} %collective-permute-done.21.refs_2_, bf16[16,1536]{1,0:T(8,128)(2,1)S(1)} %collective-permute-done.22.refs_3_, ...), custom_call_target="tpu_custom_call" | custom-call | tf_op jit(solution)/shard_map/fourth/pallas_call | solution.py:538
  51.0 2.0 %collective-permute-start.23 = (f32[16,128]{1,0:T(8,128)S(1)}, f32[16,128]{1,0:T(8,128)S(1)}, u32[]{:S(2)}, u32[]{:S(2)}) collective-permute-start(f32[16,128]{1,0:T(8,128)S(1)} %fourth.1), channel_id=1, source_target_pairs={{0,4},{4,0},{8,12},{12,8},{16,20},{20,16},{24,28},{28,24},{1,5},{5... | collective-permute-start | bytes 24584 | tf_op jit(solution)/shard_map/ppermute | solution.py:19
  53.1 1.7 %collective-permute-done.23 = f32[16,128]{1,0:T(8,128)S(1)} collective-permute-done((f32[16,128]{1,0:T(8,128)S(1)}, f32[16,128]{1,0:T(8,128)S(1)}, u32[]{:S(2)}, u32[]{:S(2)}) %collective-permute-start.23) | collective-permute-done | bytes 8224 | tf_op jit(solution)/shard_map/ppermute | solution.py:19
  54.7 1.9 %collective-permute-start.26 = (f32[16,128]{1,0:T(8,128)S(1)}, f32[16,128]{1,0:T(8,128)S(1)}, u32[]{:S(2)}, u32[]{:S(2)}) collective-permute-start(f32[16,128]{1,0:T(8,128)S(1)} %add.11.refs_0_), channel_id=1, source_target_pairs={{0,24},{4,28},{8,16},{12,20},{16,8},{20,12},{24,0},{28,4},{1,25},{... | collective-permute-start | bytes 24584 | tf_op jit(solution)/shard_map/ppermute | solution.py:19
  56.6 0.9 %collective-permute-start.25 = (f32[16,128]{1,0:T(8,128)S(1)}, f32[16,128]{1,0:T(8,128)S(1)}, u32[]{:S(2)}, u32[]{:S(2)}) collective-permute-start(f32[16,128]{1,0:T(8,128)S(1)} %add.11.refs_0_), channel_id=1, source_target_pairs={{0,16},{4,20},{8,24},{12,28},{16,0},{20,4},{24,8},{28,12},{1,17},{... | collective-permute-start | bytes 24584 | tf_op jit(solution)/shard_map/ppermute | solution.py:19
  57.5 1.6 %collective-permute-start.24 = (f32[16,128]{1,0:T(8,128)S(1)}, f32[16,128]{1,0:T(8,128)S(1)}, u32[]{:S(2)}, u32[]{:S(2)}) collective-permute-start(f32[16,128]{1,0:T(8,128)S(1)} %add.11.refs_0_), channel_id=1, source_target_pairs={{0,8},{4,12},{8,0},{12,4},{16,24},{20,28},{24,16},{28,20},{1,9},{5... | collective-permute-start | bytes 24584 | tf_op jit(solution)/shard_map/ppermute | solution.py:19
  59.1 1.1 %collective-permute-done.26.refs_3_ = f32[16,128]{1,0:T(8,128)S(1)} collective-permute-done((f32[16,128]{1,0:T(8,128)S(1)}, f32[16,128]{1,0:T(8,128)S(1)}, u32[]{:S(2)}, u32[]{:S(2)}) %collective-permute-start.26) | collective-permute-done | bytes 8224 | tf_op jit(solution)/shard_map/ppermute | solution.py:19
  60.2 1.0 %collective-permute-done.25.refs_2_ = f32[16,128]{1,0:T(8,128)S(1)} collective-permute-done((f32[16,128]{1,0:T(8,128)S(1)}, f32[16,128]{1,0:T(8,128)S(1)}, u32[]{:S(2)}, u32[]{:S(2)}) %collective-permute-start.25) | collective-permute-done | bytes 8224 | tf_op jit(solution)/shard_map/ppermute | solution.py:19
  61.2 1.0 %last.1 = f32[16,1024]{1,0:T(8,128)} custom-call(f32[16,128]{1,0:T(8,128)S(1)} %add.11.refs_0_, f32[16,128]{1,0:T(8,128)S(1)} %collective-permute-done.24.refs_1_, f32[16,128]{1,0:T(8,128)S(1)} %collective-permute-done.25.refs_2_, f32[16,128]{1,0:T(8,128)S(1)} %collective-permute-done.26.refs_3_, f32[16,128]{1,0:T(8,128)S(1)} %get-tuple-element.86.refs_4_, ...), custom_call_target="tpu_custom_call" | custom-call | tf_op jit(solution)/shard_map/last/pallas_call | solution.py:538
  (17 shorter events, 0.0 us)
Async XLA Ops:
  0.0 12.1 %copy-start = (bf16[256,1,512]{2,0,1:T(8,128)(2,1)S(1)}, bf16[256,1,512]{2,0,1:T(8,128)(2,1)}, u32[]{:S(2)}) copy-start(bf16[256,1,512]{2,0,1:T(8,128)(2,1)} %param.17) | copy-start | bytes 786436
  0.0 13.8 %copy-start.1 = (bf16[8,128,32]{1,2,0:T(8,128)(2,1)S(1)}, bf16[8,128,32]{1,2,0:T(8,128)(2,1)}, u32[]{:S(2)}) copy-start(bf16[8,128,32]{1,2,0:T(8,128)(2,1)} %param.15) | copy-start | bytes 196612
  0.0 13.8 %copy-start.2 = (s32[8,32]{1,0:T(8,128)S(1)}, s32[8,32]{1,0:T(8,128)}, u32[]{:S(2)}) copy-start(s32[8,32]{1,0:T(8,128)} %refs_3_.1) | copy-start | bytes 3076
  0.0 13.8 %copy-start.3 = (s32[8,8]{1,0:T(8,128)S(1)}, s32[8,8]{1,0:T(8,128)}, u32[]{:S(2)}) copy-start(s32[8,8]{1,0:T(8,128)} %refs_0_.3) | copy-start | bytes 772
  0.0 13.8 %copy-start.4 = (s32[8]{0:T(128)S(1)}, s32[8]{0:T(128)}, u32[]{:S(2)}) copy-start(s32[8]{0:T(128)} %param.14) | copy-start | bytes 100
  2.0 5.0 %collective-permute-start.2 = (f32[16,640]{1,0:T(8,128)S(1)}, f32[16,640]{1,0:T(8,128)S(1)}, u32[]{:S(2)}, u32[]{:S(2)}) collective-permute-start(f32[16,640]{1,0:T(8,128)S(1)} %get-tuple-element.49), channel_id=1, source_target_pairs={{0,4},{4,0},{8,12},{12,8},{16,20},{20,16},{24,28},{28,24},{1,5},{5... | collective-permute-start | bytes 122888 | tf_op jit(solution)/shard_map/ppermute | solution.py:19
  5.1 20.5 %collective-permute-start = (bf16[352,512]{1,0:T(8,128)(2,1)S(1)}, bf16[352,512]{1,0:T(8,128)(2,1)S(1)}, u32[]{:S(2)}, u32[]{:S(2)}) collective-permute-start(bf16[352,512]{1,0:T(8,128)(2,1)S(1)} %get-tuple-element.46), channel_id=1, source_target_pairs={{0,4},{4,0},{8,12},{12,8},{16,20},{20,16},{24,28},{28,24},{1,5},{5... | collective-permute-start | bytes 1081352 | tf_op jit(solution)/shard_map/ppermute | solution.py:19
  7.1 7.0 %collective-permute-start.5 = (f32[16,640]{1,0:T(8,128)S(1)}, f32[16,640]{1,0:T(8,128)S(1)}, u32[]{:S(2)}, u32[]{:S(2)}) collective-permute-start(f32[16,640]{1,0:T(8,128)S(1)} %add.9.refs_0_), channel_id=1, source_target_pairs={{0,24},{4,28},{8,16},{12,20},{16,8},{20,12},{24,0},{28,4},{1,25},{... | collective-permute-start | bytes 122888 | tf_op jit(solution)/shard_map/ppermute | solution.py:19
  11.5 4.9 %collective-permute-start.4 = (f32[16,640]{1,0:T(8,128)S(1)}, f32[16,640]{1,0:T(8,128)S(1)}, u32[]{:S(2)}, u32[]{:S(2)}) collective-permute-start(f32[16,640]{1,0:T(8,128)S(1)} %add.9.refs_0_), channel_id=1, source_target_pairs={{0,16},{4,20},{8,24},{12,28},{16,0},{20,4},{24,8},{28,12},{1,17},{... | collective-permute-start | bytes 122888 | tf_op jit(solution)/shard_map/ppermute | solution.py:19
  11.5 4.9 %collective-permute-start.3 = (f32[16,640]{1,0:T(8,128)S(1)}, f32[16,640]{1,0:T(8,128)S(1)}, u32[]{:S(2)}, u32[]{:S(2)}) collective-permute-start(f32[16,640]{1,0:T(8,128)S(1)} %add.9.refs_0_), channel_id=1, source_target_pairs={{0,8},{4,12},{8,0},{12,4},{16,24},{20,28},{24,16},{28,20},{1,9},{5... | collective-permute-start | bytes 122888 | tf_op jit(solution)/shard_map/ppermute | solution.py:19
  12.1 11.6 %collective-permute-start.1 = (bf16[256,512]{1,0:T(8,128)(2,1)S(1)}, bf16[256,512]{1,0:T(8,128)(2,1)S(1)}, u32[]{:S(2)}, u32[]{:S(2)}) collective-permute-start(bf16[256,512]{1,0:T(8,128)(2,1)S(1)} %bitcast.5), channel_id=1, source_target_pairs={{0,2},{1,3},{2,0},{3,1},{4,6},{5,7},{6,4},{7,5},{8,10},{9,11},{10,... | collective-permute-start | bytes 786440 | tf_op jit(solution)/shard_map/ppermute | solution.py:505
  16.4 12.2 %copy-start.5 = (bf16[8,8,128,128]{3,2,1,0:T(8,128)(2,1)S(1)}, bf16[8,8,128,128]{3,2,1,0:T(8,128)(2,1)}, u32[]{:S(2)}) copy-start(bf16[8,8,128,128]{3,2,1,0:T(8,128)(2,1)} %refs_5_.5) | copy-start | bytes 6291460
  17.0 4.1 %collective-permute-start.6 = (bf16[16,1536]{1,0:T(8,128)(2,1)S(1)}, bf16[16,1536]{1,0:T(8,128)(2,1)S(1)}, u32[]{:S(2)}, u32[]{:S(2)}) collective-permute-start(bf16[16,1536]{1,0:T(8,128)(2,1)S(1)} %get-tuple-element.60.send_ref.refs_0_), channel_id=1, source_target_pairs={{0,4},{4,0},{8,12},{12,8},{16,20},{20,16},{24,28},{28,24},{1,5},{5... | collective-permute-start | bytes 147464 | tf_op jit(solution)/shard_map/ppermute | solution.py:19
  21.1 6.0 %collective-permute-start.10 = (bf16[16,1536]{1,0:T(8,128)(2,1)S(1)}, bf16[16,1536]{1,0:T(8,128)(2,1)S(1)}, u32[]{:S(2)}, u32[]{:S(2)}) collective-permute-start(bf16[16,1536]{1,0:T(8,128)(2,1)S(1)} %get-tuple-element.64), channel_id=1, source_target_pairs={{0,24},{4,28},{8,16},{12,20},{16,8},{20,12},{24,0},{28,4},{1,25},{... | collective-permute-start | bytes 147464 | tf_op jit(solution)/shard_map/ppermute | solution.py:19
  22.6 6.0 %collective-permute-start.8 = (bf16[16,1536]{1,0:T(8,128)(2,1)S(1)}, bf16[16,1536]{1,0:T(8,128)(2,1)S(1)}, u32[]{:S(2)}, u32[]{:S(2)}) collective-permute-start(bf16[16,1536]{1,0:T(8,128)(2,1)S(1)} %get-tuple-element.64), channel_id=1, source_target_pairs={{0,8},{4,12},{8,0},{12,4},{16,24},{20,28},{24,16},{28,20},{1,9},{5... | collective-permute-start | bytes 147464 | tf_op jit(solution)/shard_map/ppermute | solution.py:19
  23.7 5.7 %collective-permute-start.11 = (bf16[256,512]{1,0:T(8,128)(2,1)S(1)}, bf16[256,512]{1,0:T(8,128)(2,1)S(1)}, u32[]{:S(2)}, u32[]{:S(2)}) collective-permute-start(bf16[256,512]{1,0:T(8,128)(2,1)S(1)} %bitcast.6), channel_id=1, source_target_pairs={{0,1},{1,0},{2,3},{3,2},{4,5},{5,4},{6,7},{7,6},{8,9},{9,8},{10,11... | collective-permute-start | bytes 786440 | tf_op jit(solution)/shard_map/ppermute | solution.py:505
  23.7 5.7 %collective-permute-start.9 = (bf16[16,512]{1,0:T(8,128)(2,1)S(1)}, bf16[16,512]{1,0:T(8,128)(2,1)S(1)}, u32[]{:S(2)}, u32[]{:S(2)}) collective-permute-start(bf16[16,512]{1,0:T(8,128)(2,1)S(1)} %get-tuple-element.63.refs_0_), channel_id=1, source_target_pairs={{0,16},{4,20},{8,24},{12,28},{16,0},{20,4},{24,8},{28,12},{1,17},{... | collective-permute-start | bytes 49160 | tf_op jit(solution)/shard_map/ppermute | solution.py:19
  25.5 3.9 %collective-permute-start.12 = (bf16[256,512]{1,0:T(8,128)(2,1)S(1)}, bf16[256,512]{1,0:T(8,128)(2,1)S(1)}, u32[]{:S(2)}, u32[]{:S(2)}) collective-permute-start(bf16[256,512]{1,0:T(8,128)(2,1)S(1)} %collective-permute-done.1.refs_14_.refs_12_), channel_id=1, source_target_pairs={{0,1},{1,0},{2,3},{3,2},{4,5},{5,4},{6,7},{7,6},{8,9},{9,8},{10,11... | collective-permute-start | bytes 786440 | tf_op jit(solution)/shard_map/ppermute | solution.py:512
  27.1 9.3 %collective-permute-start.7 = (bf16[352,512]{1,0:T(8,128)(2,1)S(1)}, bf16[352,512]{1,0:T(8,128)(2,1)S(1)}, u32[]{:S(2)}, u32[]{:S(2)}) collective-permute-start(bf16[352,512]{1,0:T(8,128)(2,1)S(1)} %collective-permute-done.refs_0_.refs_12_), channel_id=1, source_target_pairs={{0,2},{1,3},{2,0},{3,1},{4,6},{5,7},{6,4},{7,5},{8,10},{9,11},{10,... | collective-permute-start | bytes 1081352 | tf_op jit(solution)/shard_map/ppermute | solution.py:614
  30.9 8.4 %collective-permute-start.18 = (bf16[352,512]{1,0:T(8,128)(2,1)S(1)}, bf16[352,512]{1,0:T(8,128)(2,1)S(1)}, u32[]{:S(2)}, u32[]{:S(2)}) collective-permute-start(bf16[352,512]{1,0:T(8,128)(2,1)S(1)} %collective-permute-done.refs_0_.refs_12_), channel_id=1, source_target_pairs={{0,1},{1,0},{2,3},{3,2},{4,5},{5,4},{6,7},{7,6},{8,9},{9,8},{10,11... | collective-permute-start | bytes 1081352 | tf_op jit(solution)/shard_map/ppermute | solution.py:646
  30.9 4.0 %collective-permute-start.13 = (f32[16,640]{1,0:T(8,128)S(1)}, f32[16,640]{1,0:T(8,128)S(1)}, u32[]{:S(2)}, u32[]{:S(2)}) collective-permute-start(f32[16,640]{1,0:T(8,128)S(1)} %get-tuple-element.72), channel_id=1, source_target_pairs={{0,4},{4,0},{8,12},{12,8},{16,20},{20,16},{24,28},{28,24},{1,5},{5... | collective-permute-start | bytes 122888 | tf_op jit(solution)/shard_map/ppermute | solution.py:19
  32.6 7.1 %collective-permute-start.17 = (f32[16,1024]{1,0:T(8,128)S(1)}, f32[16,1024]{1,0:T(8,128)S(1)}, u32[]{:S(2)}, u32[]{:S(2)}) collective-permute-start(f32[16,1024]{1,0:T(8,128)S(1)} %get-tuple-element.76), channel_id=1, source_target_pairs={{0,4},{4,0},{8,12},{12,8},{16,20},{20,16},{24,28},{28,24},{1,5},{5... | collective-permute-start | bytes 196616 | tf_op jit(solution)/shard_map/ppermute | solution.py:19
  34.9 6.1 %collective-permute-start.16 = (f32[16,640]{1,0:T(8,128)S(1)}, f32[16,640]{1,0:T(8,128)S(1)}, u32[]{:S(2)}, u32[]{:S(2)}) collective-permute-start(f32[16,640]{1,0:T(8,128)S(1)} %add.10.refs_0_), channel_id=1, source_target_pairs={{0,24},{4,28},{8,16},{12,20},{16,8},{20,12},{24,0},{28,4},{1,25},{... | collective-permute-start | bytes 122888 | tf_op jit(solution)/shard_map/ppermute | solution.py:19
  36.4 5.4 %collective-permute-start.15 = (f32[16,640]{1,0:T(8,128)S(1)}, f32[16,640]{1,0:T(8,128)S(1)}, u32[]{:S(2)}, u32[]{:S(2)}) collective-permute-start(f32[16,640]{1,0:T(8,128)S(1)} %add.10.refs_0_), channel_id=1, source_target_pairs={{0,16},{4,20},{8,24},{12,28},{16,0},{20,4},{24,8},{28,12},{1,17},{... | collective-permute-start | bytes 122888 | tf_op jit(solution)/shard_map/ppermute | solution.py:19
  36.4 5.4 %collective-permute-start.14 = (f32[16,640]{1,0:T(8,128)S(1)}, f32[16,640]{1,0:T(8,128)S(1)}, u32[]{:S(2)}, u32[]{:S(2)}) collective-permute-start(f32[16,640]{1,0:T(8,128)S(1)} %add.10.refs_0_), channel_id=1, source_target_pairs={{0,8},{4,12},{8,0},{12,4},{16,24},{20,28},{24,16},{28,20},{1,9},{5... | collective-permute-start | bytes 122888 | tf_op jit(solution)/shard_map/ppermute | solution.py:19
  39.3 2.5 %collective-permute-start.19 = (bf16[352,512]{1,0:T(8,128)(2,1)S(1)}, bf16[352,512]{1,0:T(8,128)(2,1)S(1)}, u32[]{:S(2)}, u32[]{:S(2)}) collective-permute-start(bf16[352,512]{1,0:T(8,128)(2,1)S(1)} %collective-permute-done.7.refs_2_.refs_14_), channel_id=1, source_target_pairs={{0,1},{1,0},{2,3},{3,2},{4,5},{5,4},{6,7},{7,6},{8,9},{9,8},{10,11... | collective-permute-start | bytes 1081352 | tf_op jit(solution)/shard_map/ppermute | solution.py:646
  43.0 6.1 %collective-permute-start.22 = (bf16[16,1536]{1,0:T(8,128)(2,1)S(1)}, bf16[16,1536]{1,0:T(8,128)(2,1)S(1)}, u32[]{:S(2)}, u32[]{:S(2)}) collective-permute-start(bf16[16,1536]{1,0:T(8,128)(2,1)S(1)} %get-tuple-element.82.refs_1_), channel_id=1, source_target_pairs={{0,24},{4,28},{8,16},{12,20},{16,8},{20,12},{24,0},{28,4},{1,25},{... | collective-permute-start | bytes 147464 | tf_op jit(solution)/shard_map/ppermute | solution.py:19
  44.8 4.6 %collective-permute-start.20 = (bf16[16,1536]{1,0:T(8,128)(2,1)S(1)}, bf16[16,1536]{1,0:T(8,128)(2,1)S(1)}, u32[]{:S(2)}, u32[]{:S(2)}) collective-permute-start(bf16[16,1536]{1,0:T(8,128)(2,1)S(1)} %get-tuple-element.82.refs_1_), channel_id=1, source_target_pairs={{0,8},{4,12},{8,0},{12,4},{16,24},{20,28},{24,16},{28,20},{1,9},{5... | collective-permute-start | bytes 147464 | tf_op jit(solution)/shard_map/ppermute | solution.py:19
  45.0 5.1 %collective-permute-start.21 = (bf16[16,512]{1,0:T(8,128)(2,1)S(1)}, bf16[16,512]{1,0:T(8,128)(2,1)S(1)}, u32[]{:S(2)}, u32[]{:S(2)}) collective-permute-start(bf16[16,512]{1,0:T(8,128)(2,1)S(1)} %get-tuple-element.81.refs_0_), channel_id=1, source_target_pairs={{0,16},{4,20},{8,24},{12,28},{16,0},{20,4},{24,8},{28,12},{1,17},{... | collective-permute-start | bytes 49160 | tf_op jit(solution)/shard_map/ppermute | solution.py:19
  51.0 3.7 %collective-permute-start.23 = (f32[16,128]{1,0:T(8,128)S(1)}, f32[16,128]{1,0:T(8,128)S(1)}, u32[]{:S(2)}, u32[]{:S(2)}) collective-permute-start(f32[16,128]{1,0:T(8,128)S(1)} %fourth.1), channel_id=1, source_target_pairs={{0,4},{4,0},{8,12},{12,8},{16,20},{20,16},{24,28},{28,24},{1,5},{5... | collective-permute-start | bytes 24584 | tf_op jit(solution)/shard_map/ppermute | solution.py:19
  54.7 5.4 %collective-permute-start.26 = (f32[16,128]{1,0:T(8,128)S(1)}, f32[16,128]{1,0:T(8,128)S(1)}, u32[]{:S(2)}, u32[]{:S(2)}) collective-permute-start(f32[16,128]{1,0:T(8,128)S(1)} %add.11.refs_0_), channel_id=1, source_target_pairs={{0,24},{4,28},{8,16},{12,20},{16,8},{20,12},{24,0},{28,4},{1,25},{... | collective-permute-start | bytes 24584 | tf_op jit(solution)/shard_map/ppermute | solution.py:19
  56.6 4.6 %collective-permute-start.25 = (f32[16,128]{1,0:T(8,128)S(1)}, f32[16,128]{1,0:T(8,128)S(1)}, u32[]{:S(2)}, u32[]{:S(2)}) collective-permute-start(f32[16,128]{1,0:T(8,128)S(1)} %add.11.refs_0_), channel_id=1, source_target_pairs={{0,16},{4,20},{8,24},{12,28},{16,0},{20,4},{24,8},{28,12},{1,17},{... | collective-permute-start | bytes 24584 | tf_op jit(solution)/shard_map/ppermute | solution.py:19
  57.5 3.7 %collective-permute-start.24 = (f32[16,128]{1,0:T(8,128)S(1)}, f32[16,128]{1,0:T(8,128)S(1)}, u32[]{:S(2)}, u32[]{:S(2)}) collective-permute-start(f32[16,128]{1,0:T(8,128)S(1)} %add.11.refs_0_), channel_id=1, source_target_pairs={{0,8},{4,12},{8,0},{12,4},{16,24},{20,28},{24,16},{28,20},{1,9},{5... | collective-permute-start | bytes 24584 | tf_op jit(solution)/shard_map/ppermute | solution.py:19

commit v10 on v9

--- a/solution.py
+++ b/solution.py
@@ -247,6 +247,13 @@
     low_turned_ref[...] = low_ref[...].T
 
 
+def turn_blocks_kernel(mats_ref, turned_ref):
+    block_count, slots, block, _ = mats_ref.shape
+    for b in range(block_count):
+        for k in range(slots):
+            turned_ref[b, k * block : (k + 1) * block, :] = mats_ref[b, k].T
+
+
 def first_kernel(parts, *refs):
     sums = refs[:parts]
     rhs_ref, diag_ref, high_ref, low_ref, maps_ref = refs[parts : parts + 5]
@@ -287,7 +294,8 @@
     field_refs = refs[:sources]
     places_ref, mats_ref, near_ref, blocks_ref = refs[sources:]
     rows, panels = near_ref.shape
-    block_count, slots, block, _ = mats_ref.shape
+    block_count, deep, block = mats_ref.shape
+    slots = deep // block
     packed = places_ref[...]
     for index, ref in enumerate(field_refs):
         for b in range(block_count):
@@ -297,8 +305,7 @@
         fours = [packed[b, group] for group in range(slots // 4)]
         places = [(fours[k // 4] >> (6 * (k % 4))) & 63 for k in range(slots)]
         picked = jnp.concatenate([blocks_ref[place] for place in places], axis=1)
-        mats = jnp.concatenate([mats_ref[b, k] for k in range(slots)], axis=1)
-        near_ref[:, b * block : (b + 1) * block] = dot_nt(picked, mats)
+        near_ref[:, b * block : (b + 1) * block] = dot_nn(picked, mats_ref[b])
 
 
 def apply_matrix(field_ref, self_ref, near_ref, charge_refs, coupling_refs, maps_ref, charges_ref):
@@ -595,9 +602,15 @@
         scratch + [pltpu.SemaphoreType.DMA((parts + 5,))],
         far=range(len(args)),
     )
+    (blocks,) = call(
+        "turn_blocks",
+        turn_blocks_kernel,
+        [((block_count, slots * block, block), BF)],
+        [near_mats],
+    )
     turned = call("turn", turn_kernel, [((width, panels), BF)] * 2, [high, low])
     some_rows, payload = gather_quarters(coupling[:, 0, :], quarters, count, payload)
-    sums, turned = sum_parts(payload, count, turned)
+    sums, (*turned, blocks) = sum_parts(payload, count, [*turned, blocks])
     if paired:
         mine = swap(packs[0], 1, count)
     first_dir, first_pre, keep, send = call(
@@ -618,7 +631,7 @@
             "near",
             lambda *refs: near_kernel(len(fields), *refs),
             [((rows, panels), F32)],
-            [*fields, places, near_mats],
+            [*fields, places, blocks],
             [pltpu.VMEM((len(fields) * block_count + 1, rows, block), BF)],
             flops=10**10,
         )

time: 62.3 us -> 62.2 us (level)
    pallas_call x12 -> x13, Pallas kernels: 9.78 us -> 9.89 us  [call(): pl.pallas_call(kernel, name=name, out_shape=out_shapes, in_specs=specs, o...]
  transfers between devices with their start and end apart: 27 -> 27, of which waited for: 12 -> 13; matrix products, arithmetic and copies ran while one was open for 0% -> 0% of each run, Pallas kernels for 8% -> 8%
where the time goes in v10:
time: 62.2 us; the launch traced here: 62 us
  starting transfers between devices  34.8 us (56%)
  waiting for transfers between devices  17.2 us (28%)
  Pallas kernels  9.89 us (16%)
    ppermute x21, starting transfers between devices, swap(): return lax.ppermute(values, AXIS, [(i, i ^ mask) for i in range(count)])  31.4 us
    ppermute x21, waiting for transfers between devices, swap(): return lax.ppermute(values, AXIS, [(i, i ^ mask) for i in range(count)])  17 us
    pallas_call x13, Pallas kernels, call(): pl.pallas_call(kernel, name=name, out_shape=out_shapes, in_specs=specs, o...  9.89 us
    ppermute x2, starting transfers between devices, gather_quarters(): lax.ppermute(coupling, 'rhs', pair)  1.64 us
    ppermute x1, starting transfers between devices, on_device(): far = lax.ppermute(mine, 'rhs', [(i, i ^ 2) for i in range(quarters)])  1.49 us
  transfers between devices with their start and end apart: 27, of which 13 were waited for; matrix products, arithmetic and copies ran while one was open for 0% of the time, Pallas kernels for 8%

profile of v10, /device:TPU:0, one launch (start us, length us, event | category | flops | bytes accessed | tf_op | source)
XLA Modules:
  0.0 62.0 jit_solution(2242833630611819754)
XLA Ops:
  0.0 2.1 %open.1 = (f32[16,640]{1,0:T(8,128)S(1)}, f32[16,1024]{1,0:T(8,128)S(1)}, f32[1,1024]{1,0:T(1,128)S(1)}, f32[1,1024]{1,0:T(1,128)S(1)}, bf16[1024,512]{1,0:T(8,1...) custom-call(f32[16,1024]{1,0:T(8,128)} %refs_0_.2, f32[1024,512]{1,0:T(8,128)} %refs_1_.1, ...), custom_call_target="tpu_custom_call" | custom-call | tf_op jit(solution)/shard_map/open/pallas_call | solution.py:545
  2.1 3.0 %collective-permute-start.2 = (f32[16,640]{1,0:T(8,128)S(1)}, f32[16,640]{1,0:T(8,128)S(1)}, u32[]{:S(2)}, u32[]{:S(2)}) collective-permute-start(f32[16,640]{1,0:T(8,128)S(1)} %get-tuple-element.50), channel_id=1, source_target_pairs={{0,4},{4,0},{8,12},{12,8},{16,20},{20,16},{24,28},{28,24},{1,5},{5... | collective-permute-start | bytes 122888 | tf_op jit(solution)/shard_map/ppermute | solution.py:19
  5.2 0.1 collective-permute-start
  5.2 0.6 turn_blocks.1.refs_5_
  5.8 0.0 copy-start.1
  5.9 0.0 copy-start.2
  5.9 0.0 copy-start.3
  5.9 0.0 copy-start.4
  5.9 0.0 copy-start.5
  5.9 0.6 %turn.1 = (bf16[512,1024]{1,0:T(8,128)(2,1)S(1)}, bf16[512,1024]{1,0:T(8,128)(2,1)S(1)}) custom-call(bf16[1024,512]{1,0:T(8,128)(2,1)S(1)} %get-tuple-element.51.high_ref.refs_10_, bf16[1024,512]{1,0:T(8,128)(2,1)S(1)} %get-tuple-element.52.low_ref.refs_11_), custom_call_target="tpu_custom_call" | custom-call | tf_op jit(solution)/shard_map/turn/pallas_call | solution.py:545
  6.5 0.6 collective-permute-done.2
  7.2 4.4 %collective-permute-start.5 = (f32[16,640]{1,0:T(8,128)S(1)}, f32[16,640]{1,0:T(8,128)S(1)}, u32[]{:S(2)}, u32[]{:S(2)}) collective-permute-start(f32[16,640]{1,0:T(8,128)S(1)} %add.9.refs_0_), channel_id=1, source_target_pairs={{0,24},{4,28},{8,16},{12,20},{16,8},{20,12},{24,0},{28,4},{1,25},{... | collective-permute-start | bytes 122888 | tf_op jit(solution)/shard_map/ppermute | solution.py:19
  11.6 0.6 %collective-permute-start.3 = (f32[16,640]{1,0:T(8,128)S(1)}, f32[16,640]{1,0:T(8,128)S(1)}, u32[]{:S(2)}, u32[]{:S(2)}) collective-permute-start(f32[16,640]{1,0:T(8,128)S(1)} %add.9.refs_0_), channel_id=1, source_target_pairs={{0,8},{4,12},{8,0},{12,4},{16,24},{20,28},{24,16},{28,20},{1,9},{5... | collective-permute-start | bytes 122888 | tf_op jit(solution)/shard_map/ppermute | solution.py:19
  12.2 1.6 %collective-permute-start.1 = (bf16[256,512]{1,0:T(8,128)(2,1)S(1)}, bf16[256,512]{1,0:T(8,128)(2,1)S(1)}, u32[]{:S(2)}, u32[]{:S(2)}) collective-permute-start(bf16[256,512]{1,0:T(8,128)(2,1)S(1)} %bitcast.5), channel_id=1, source_target_pairs={{0,2},{1,3},{2,0},{3,1},{4,6},{5,7},{6,4},{7,5},{8,10},{9,11},{10,... | collective-permute-start | bytes 786440 | tf_op jit(solution)/shard_map/ppermute | solution.py:512
  13.9 0.2 maps.1
  14.1 2.4 %collective-permute-done.4.refs_2_ = f32[16,640]{1,0:T(8,128)S(1)} collective-permute-done((f32[16,640]{1,0:T(8,128)S(1)}, f32[16,640]{1,0:T(8,128)S(1)}, u32[]{:S(2)}, u32[]{:S(2)}) %collective-permute-start.4) | collective-permute-done | bytes 40992 | tf_op jit(solution)/shard_map/ppermute | solution.py:19
  16.5 0.6 first.1
  17.1 1.7 %collective-permute-start.6 = (bf16[16,1536]{1,0:T(8,128)(2,1)S(1)}, bf16[16,1536]{1,0:T(8,128)(2,1)S(1)}, u32[]{:S(2)}, u32[]{:S(2)}) collective-permute-start(bf16[16,1536]{1,0:T(8,128)(2,1)S(1)} %get-tuple-element.61.send_ref.refs_0_), channel_id=1, source_target_pairs={{0,4},{4,0},{8,12},{12,8},{16,20},{20,16},{24,28},{28,24},{1,5},{5... | collective-permute-start | bytes 147464 | tf_op jit(solution)/shard_map/ppermute | solution.py:19
  18.8 2.5 %collective-permute-done.6.near_ref.refs_1_ = bf16[16,1536]{1,0:T(8,128)(2,1)S(1)} collective-permute-done((bf16[16,1536]{1,0:T(8,128)(2,1)S(1)}, bf16[16,1536]{1,0:T(8,128)(2,1)S(1)}, u32[]{:S(2)}, u32[]{:S(2)}) %collective-permute-start.6) | collective-permute-done | bytes 49184 | tf_op jit(solution)/shard_map/ppermute | solution.py:19
  21.2 1.5 %collective-permute-start.10 = (bf16[16,1536]{1,0:T(8,128)(2,1)S(1)}, bf16[16,1536]{1,0:T(8,128)(2,1)S(1)}, u32[]{:S(2)}, u32[]{:S(2)}) collective-permute-start(bf16[16,1536]{1,0:T(8,128)(2,1)S(1)} %get-tuple-element.65), channel_id=1, source_target_pairs={{0,24},{4,28},{8,16},{12,20},{16,8},{20,12},{24,0},{28,4},{1,25},{... | collective-permute-start | bytes 147464 | tf_op jit(solution)/shard_map/ppermute | solution.py:19
  22.7 1.1 %collective-permute-start.8 = (bf16[16,1536]{1,0:T(8,128)(2,1)S(1)}, bf16[16,1536]{1,0:T(8,128)(2,1)S(1)}, u32[]{:S(2)}, u32[]{:S(2)}) collective-permute-start(bf16[16,1536]{1,0:T(8,128)(2,1)S(1)} %get-tuple-element.65), channel_id=1, source_target_pairs={{0,8},{4,12},{8,0},{12,4},{16,24},{20,28},{24,16},{28,20},{1,9},{5... | collective-permute-start | bytes 147464 | tf_op jit(solution)/shard_map/ppermute | solution.py:19
  23.8 0.0 collective-permute-start.11
  23.8 0.0 collective-permute-done.1.refs_14_.refs_12_
  23.8 1.8 %collective-permute-start.9 = (bf16[16,512]{1,0:T(8,128)(2,1)S(1)}, bf16[16,512]{1,0:T(8,128)(2,1)S(1)}, u32[]{:S(2)}, u32[]{:S(2)}) collective-permute-start(bf16[16,512]{1,0:T(8,128)(2,1)S(1)} %get-tuple-element.64.refs_0_), channel_id=1, source_target_pairs={{0,16},{4,20},{8,24},{12,28},{16,0},{20,4},{24,8},{28,12},{1,17},{... | collective-permute-start | bytes 49160 | tf_op jit(solution)/shard_map/ppermute | solution.py:19
  25.6 0.0 collective-permute-done.refs_0_.refs_12_
  25.6 0.2 collective-permute-start.12
  25.9 1.4 %collective-permute-done.10.refs_3_ = bf16[16,1536]{1,0:T(8,128)(2,1)S(1)} collective-permute-done((bf16[16,1536]{1,0:T(8,128)(2,1)S(1)}, bf16[16,1536]{1,0:T(8,128)(2,1)S(1)}, u32[]{:S(2)}, u32[]{:S(2)}) %collective-permute-start.10) | collective-permute-done | bytes 49184 | tf_op jit(solution)/shard_map/ppermute | solution.py:19
  27.2 1.5 %collective-permute-start.7 = (bf16[352,512]{1,0:T(8,128)(2,1)S(1)}, bf16[352,512]{1,0:T(8,128)(2,1)S(1)}, u32[]{:S(2)}, u32[]{:S(2)}) collective-permute-start(bf16[352,512]{1,0:T(8,128)(2,1)S(1)} %collective-permute-done.refs_0_.refs_12_), channel_id=1, source_target_pairs={{0,2},{1,3},{2,0},{3,1},{4,6},{5,7},{6,4},{7,5},{8,10},{9,11},{10,... | collective-permute-start | bytes 1081352 | tf_op jit(solution)/shard_map/ppermute | solution.py:627
  28.7 0.0 collective-permute-done.8.refs_2_.refs_1_
  28.7 0.5 near.2.refs_8_
  29.2 0.0 collective-permute-done.9.refs_2_
  29.2 0.0 collective-permute-done.11.refs_13_.refs_11_
  29.2 0.0 collective-permute-done.12.refs_15_.refs_13_
  29.2 1.5 %second.1 = (f32[16,1024]{1,0:T(8,128)S(1)}, f32[16,1024]{1,0:T(8,128)S(1)}, f32[16,640]{1,0:T(8,128)S(1)}) custom-call(bf16[16,512]{1,0:T(8,128)(2,1)S(1)} %get-tuple-element.64.refs_0_, bf16[16,1536]{1,0:T(8,128)(2,1)S(1)} %collective-permute-done.8.refs_2_.refs_1_, bf16[16,512]{1,0:T(8,128)(2,1)S(1)} %collective-permute-done.9.refs_2_, ...), custom_call_target="tpu_custom_call" | custom-call | flops 10000000000 | bytes 20000000 | tf_op jit(solution)/shard_map/second/pallas_call | solution.py:545
  30.7 1.7 %collective-permute-start.13 = (f32[16,640]{1,0:T(8,128)S(1)}, f32[16,640]{1,0:T(8,128)S(1)}, u32[]{:S(2)}, u32[]{:S(2)}) collective-permute-start(f32[16,640]{1,0:T(8,128)S(1)} %get-tuple-element.74), channel_id=1, source_target_pairs={{0,4},{4,0},{8,12},{12,8},{16,20},{20,16},{24,28},{28,24},{1,5},{5... | collective-permute-start | bytes 122888 | tf_op jit(solution)/shard_map/ppermute | solution.py:19
  32.4 0.4 collective-permute-start.17
  32.7 2.0 %collective-permute-done.13 = f32[16,640]{1,0:T(8,128)S(1)} collective-permute-done((f32[16,640]{1,0:T(8,128)S(1)}, f32[16,640]{1,0:T(8,128)S(1)}, u32[]{:S(2)}, u32[]{:S(2)}) %collective-permute-start.13) | collective-permute-done | bytes 40992 | tf_op jit(solution)/shard_map/ppermute | solution.py:19
  34.7 1.5 %collective-permute-start.16 = (f32[16,640]{1,0:T(8,128)S(1)}, f32[16,640]{1,0:T(8,128)S(1)}, u32[]{:S(2)}, u32[]{:S(2)}) collective-permute-start(f32[16,640]{1,0:T(8,128)S(1)} %add.10.refs_0_), channel_id=1, source_target_pairs={{0,24},{4,28},{8,16},{12,20},{16,8},{20,12},{24,0},{28,4},{1,25},{... | collective-permute-start | bytes 122888 | tf_op jit(solution)/shard_map/ppermute | solution.py:19
  36.2 0.2 collective-permute-start.15
  36.3 0.1 collective-permute-done.7.refs_2_.refs_14_
  36.5 2.7 %collective-permute-start.14 = (f32[16,640]{1,0:T(8,128)S(1)}, f32[16,640]{1,0:T(8,128)S(1)}, u32[]{:S(2)}, u32[]{:S(2)}) collective-permute-start(f32[16,640]{1,0:T(8,128)S(1)} %add.10.refs_0_), channel_id=1, source_target_pairs={{0,8},{4,12},{8,0},{12,4},{16,24},{20,28},{24,16},{28,20},{1,9},{5... | collective-permute-start | bytes 122888 | tf_op jit(solution)/shard_map/ppermute | solution.py:19
  39.1 0.0 collective-permute-done.18.refs_1_.refs_13_
  39.1 0.4 other_maps.1
  39.5 0.0 collective-permute-done.17.refs_11_
  39.5 1.3 %collective-permute-done.16.refs_3_ = f32[16,640]{1,0:T(8,128)S(1)} collective-permute-done((f32[16,640]{1,0:T(8,128)S(1)}, f32[16,640]{1,0:T(8,128)S(1)}, u32[]{:S(2)}, u32[]{:S(2)}) %collective-permute-start.16) | collective-permute-done | bytes 40992 | tf_op jit(solution)/shard_map/ppermute | solution.py:19
  40.9 0.8 %collective-permute-done.15.refs_2_ = f32[16,640]{1,0:T(8,128)S(1)} collective-permute-done((f32[16,640]{1,0:T(8,128)S(1)}, f32[16,640]{1,0:T(8,128)S(1)}, u32[]{:S(2)}, u32[]{:S(2)}) %collective-permute-start.15) | collective-permute-done | bytes 40992 | tf_op jit(solution)/shard_map/ppermute | solution.py:19
  41.6 0.0 collective-permute-done.14.refs_1_
  41.6 0.0 collective-permute-done.19.refs_15_
  41.6 1.1 %third.1 = (bf16[16,1536]{1,0:T(8,128)(2,1)S(1)}, bf16[16,512]{1,0:T(8,128)(2,1)S(1)}, f32[16,1024]{1,0:T(8,128)S(1)}, f32[16,1024]{1,0:T(8,128)S(1)}, f32[16,12...) custom-call(f32[16,640]{1,0:T(8,128)S(1)} %add.10.refs_0_, f32[16,640]{1,0:T(8,128)S(1)} %collective-permute-done.14.refs_1_, ...), custom_call_target="tpu_custom_call" | custom-call | tf_op jit(solution)/shard_map/third/pallas_call | solution.py:545
  42.8 1.9 %collective-permute-start.22 = (bf16[16,1536]{1,0:T(8,128)(2,1)S(1)}, bf16[16,1536]{1,0:T(8,128)(2,1)S(1)}, u32[]{:S(2)}, u32[]{:S(2)}) collective-permute-start(bf16[16,1536]{1,0:T(8,128)(2,1)S(1)} %get-tuple-element.84.refs_1_), channel_id=1, source_target_pairs={{0,24},{4,28},{8,16},{12,20},{16,8},{20,12},{24,0},{28,4},{1,25},{... | collective-permute-start | bytes 147464 | tf_op jit(solution)/shard_map/ppermute | solution.py:19
  44.7 0.2 collective-permute-start.20
  44.8 2.3 %collective-permute-start.21 = (bf16[16,512]{1,0:T(8,128)(2,1)S(1)}, bf16[16,512]{1,0:T(8,128)(2,1)S(1)}, u32[]{:S(2)}, u32[]{:S(2)}) collective-permute-start(bf16[16,512]{1,0:T(8,128)(2,1)S(1)} %get-tuple-element.83.refs_0_), channel_id=1, source_target_pairs={{0,16},{4,20},{8,24},{12,28},{16,0},{20,4},{24,8},{28,12},{1,17},{... | collective-permute-start | bytes 49160 | tf_op jit(solution)/shard_map/ppermute | solution.py:19
  47.2 1.7 %collective-permute-done.22.refs_3_ = bf16[16,1536]{1,0:T(8,128)(2,1)S(1)} collective-permute-done((bf16[16,1536]{1,0:T(8,128)(2,1)S(1)}, bf16[16,1536]{1,0:T(8,128)(2,1)S(1)}, u32[]{:S(2)}, u32[]{:S(2)}) %collective-permute-start.22) | collective-permute-done | bytes 49184 | tf_op jit(solution)/shard_map/ppermute | solution.py:19
  48.9 0.3 collective-permute-done.20.refs_2_.refs_1_
  49.2 0.5 near.3.refs_8_
  49.7 0.8 %fourth.1 = f32[16,128]{1,0:T(8,128)S(1)} custom-call(bf16[16,512]{1,0:T(8,128)(2,1)S(1)} %get-tuple-element.83.refs_0_, bf16[16,1536]{1,0:T(8,128)(2,1)S(1)} %collective-permute-done.20.refs_2_.refs_1_, bf16[16,512]{1,0:T(8,128)(2,1)S(1)} %collective-permute-done.21.refs_2_, bf16[16,1536]{1,0:T(8,128)(2,1)S(1)} %collective-permute-done.22.refs_3_, ...), custom_call_target="tpu_custom_call" | custom-call | tf_op jit(solution)/shard_map/fourth/pallas_call | solution.py:545
  50.5 2.0 %collective-permute-start.23 = (f32[16,128]{1,0:T(8,128)S(1)}, f32[16,128]{1,0:T(8,128)S(1)}, u32[]{:S(2)}, u32[]{:S(2)}) collective-permute-start(f32[16,128]{1,0:T(8,128)S(1)} %fourth.1), channel_id=1, source_target_pairs={{0,4},{4,0},{8,12},{12,8},{16,20},{20,16},{24,28},{28,24},{1,5},{5... | collective-permute-start | bytes 24584 | tf_op jit(solution)/shard_map/ppermute | solution.py:19
  52.5 1.7 %collective-permute-done.23 = f32[16,128]{1,0:T(8,128)S(1)} collective-permute-done((f32[16,128]{1,0:T(8,128)S(1)}, f32[16,128]{1,0:T(8,128)S(1)}, u32[]{:S(2)}, u32[]{:S(2)}) %collective-permute-start.23) | collective-permute-done | bytes 8224 | tf_op jit(solution)/shard_map/ppermute | solution.py:19
  54.2 2.2 %collective-permute-start.26 = (f32[16,128]{1,0:T(8,128)S(1)}, f32[16,128]{1,0:T(8,128)S(1)}, u32[]{:S(2)}, u32[]{:S(2)}) collective-permute-start(f32[16,128]{1,0:T(8,128)S(1)} %add.11.refs_0_), channel_id=1, source_target_pairs={{0,24},{4,28},{8,16},{12,20},{16,8},{20,12},{24,0},{28,4},{1,25},{... | collective-permute-start | bytes 24584 | tf_op jit(solution)/shard_map/ppermute | solution.py:19
  56.4 1.0 %collective-permute-start.25 = (f32[16,128]{1,0:T(8,128)S(1)}, f32[16,128]{1,0:T(8,128)S(1)}, u32[]{:S(2)}, u32[]{:S(2)}) collective-permute-start(f32[16,128]{1,0:T(8,128)S(1)} %add.11.refs_0_), channel_id=1, source_target_pairs={{0,16},{4,20},{8,24},{12,28},{16,0},{20,4},{24,8},{28,12},{1,17},{... | collective-permute-start | bytes 24584 | tf_op jit(solution)/shard_map/ppermute | solution.py:19
  57.3 1.3 %collective-permute-start.24 = (f32[16,128]{1,0:T(8,128)S(1)}, f32[16,128]{1,0:T(8,128)S(1)}, u32[]{:S(2)}, u32[]{:S(2)}) collective-permute-start(f32[16,128]{1,0:T(8,128)S(1)} %add.11.refs_0_), channel_id=1, source_target_pairs={{0,8},{4,12},{8,0},{12,4},{16,24},{20,28},{24,16},{28,20},{1,9},{5... | collective-permute-start | bytes 24584 | tf_op jit(solution)/shard_map/ppermute | solution.py:19
  58.6 1.1 %collective-permute-done.26.refs_3_ = f32[16,128]{1,0:T(8,128)S(1)} collective-permute-done((f32[16,128]{1,0:T(8,128)S(1)}, f32[16,128]{1,0:T(8,128)S(1)}, u32[]{:S(2)}, u32[]{:S(2)}) %collective-permute-start.26) | collective-permute-done | bytes 8224 | tf_op jit(solution)/shard_map/ppermute | solution.py:19
  59.7 1.4 %collective-permute-done.25.refs_2_ = f32[16,128]{1,0:T(8,128)S(1)} collective-permute-done((f32[16,128]{1,0:T(8,128)S(1)}, f32[16,128]{1,0:T(8,128)S(1)}, u32[]{:S(2)}, u32[]{:S(2)}) %collective-permute-start.25) | collective-permute-done | bytes 8224 | tf_op jit(solution)/shard_map/ppermute | solution.py:19
  61.1 1.0 %last.1 = f32[16,1024]{1,0:T(8,128)} custom-call(f32[16,128]{1,0:T(8,128)S(1)} %add.11.refs_0_, f32[16,128]{1,0:T(8,128)S(1)} %collective-permute-done.24.refs_1_, f32[16,128]{1,0:T(8,128)S(1)} %collective-permute-done.25.refs_2_, f32[16,128]{1,0:T(8,128)S(1)} %collective-permute-done.26.refs_3_, f32[16,128]{1,0:T(8,128)S(1)} %get-tuple-element.88.refs_4_, ...), custom_call_target="tpu_custom_call" | custom-call | tf_op jit(solution)/shard_map/last/pallas_call | solution.py:545
  (18 shorter events, 0.1 us)
Async XLA Ops:
  0.0 5.2 %copy-start = (bf16[8,8,128,128]{3,2,1,0:T(8,128)(2,1)S(1)}, bf16[8,8,128,128]{3,2,1,0:T(8,128)(2,1)}, u32[]{:S(2)}) copy-start(bf16[8,8,128,128]{3,2,1,0:T(8,128)(2,1)} %mats_ref.1) | copy-start | bytes 6291460
  2.1 5.0 %collective-permute-start.2 = (f32[16,640]{1,0:T(8,128)S(1)}, f32[16,640]{1,0:T(8,128)S(1)}, u32[]{:S(2)}, u32[]{:S(2)}) collective-permute-start(f32[16,640]{1,0:T(8,128)S(1)} %get-tuple-element.50), channel_id=1, source_target_pairs={{0,4},{4,0},{8,12},{12,8},{16,20},{20,16},{24,28},{28,24},{1,5},{5... | collective-permute-start | bytes 122888 | tf_op jit(solution)/shard_map/ppermute | solution.py:19
  5.2 20.5 %collective-permute-start = (bf16[352,512]{1,0:T(8,128)(2,1)S(1)}, bf16[352,512]{1,0:T(8,128)(2,1)S(1)}, u32[]{:S(2)}, u32[]{:S(2)}) collective-permute-start(bf16[352,512]{1,0:T(8,128)(2,1)S(1)} %get-tuple-element.47), channel_id=1, source_target_pairs={{0,4},{4,0},{8,12},{12,8},{16,20},{20,16},{24,28},{28,24},{1,5},{5... | collective-permute-start | bytes 1081352 | tf_op jit(solution)/shard_map/ppermute | solution.py:19
  5.8 6.4 %copy-start.1 = (bf16[256,1,512]{2,0,1:T(8,128)(2,1)S(1)}, bf16[256,1,512]{2,0,1:T(8,128)(2,1)}, u32[]{:S(2)}) copy-start(bf16[256,1,512]{2,0,1:T(8,128)(2,1)} %param.17) | copy-start | bytes 786436
  5.9 8.0 %copy-start.2 = (bf16[8,128,32]{1,2,0:T(8,128)(2,1)S(1)}, bf16[8,128,32]{1,2,0:T(8,128)(2,1)}, u32[]{:S(2)}) copy-start(bf16[8,128,32]{1,2,0:T(8,128)(2,1)} %param.15) | copy-start | bytes 196612
  5.9 8.0 %copy-start.3 = (s32[8,32]{1,0:T(8,128)S(1)}, s32[8,32]{1,0:T(8,128)}, u32[]{:S(2)}) copy-start(s32[8,32]{1,0:T(8,128)} %refs_3_.1) | copy-start | bytes 3076
  5.9 8.0 %copy-start.4 = (s32[8,8]{1,0:T(8,128)S(1)}, s32[8,8]{1,0:T(8,128)}, u32[]{:S(2)}) copy-start(s32[8,8]{1,0:T(8,128)} %refs_0_.3) | copy-start | bytes 772
  5.9 8.0 %copy-start.5 = (s32[8]{0:T(128)S(1)}, s32[8]{0:T(128)}, u32[]{:S(2)}) copy-start(s32[8]{0:T(128)} %param.14) | copy-start | bytes 100
  7.2 7.0 %collective-permute-start.5 = (f32[16,640]{1,0:T(8,128)S(1)}, f32[16,640]{1,0:T(8,128)S(1)}, u32[]{:S(2)}, u32[]{:S(2)}) collective-permute-start(f32[16,640]{1,0:T(8,128)S(1)} %add.9.refs_0_), channel_id=1, source_target_pairs={{0,24},{4,28},{8,16},{12,20},{16,8},{20,12},{24,0},{28,4},{1,25},{... | collective-permute-start | bytes 122888 | tf_op jit(solution)/shard_map/ppermute | solution.py:19
  11.6 4.9 %collective-permute-start.4 = (f32[16,640]{1,0:T(8,128)S(1)}, f32[16,640]{1,0:T(8,128)S(1)}, u32[]{:S(2)}, u32[]{:S(2)}) collective-permute-start(f32[16,640]{1,0:T(8,128)S(1)} %add.9.refs_0_), channel_id=1, source_target_pairs={{0,16},{4,20},{8,24},{12,28},{16,0},{20,4},{24,8},{28,12},{1,17},{... | collective-permute-start | bytes 122888 | tf_op jit(solution)/shard_map/ppermute | solution.py:19
  11.6 4.9 %collective-permute-start.3 = (f32[16,640]{1,0:T(8,128)S(1)}, f32[16,640]{1,0:T(8,128)S(1)}, u32[]{:S(2)}, u32[]{:S(2)}) collective-permute-start(f32[16,640]{1,0:T(8,128)S(1)} %add.9.refs_0_), channel_id=1, source_target_pairs={{0,8},{4,12},{8,0},{12,4},{16,24},{20,28},{24,16},{28,20},{1,9},{5... | collective-permute-start | bytes 122888 | tf_op jit(solution)/shard_map/ppermute | solution.py:19
  12.2 11.6 %collective-permute-start.1 = (bf16[256,512]{1,0:T(8,128)(2,1)S(1)}, bf16[256,512]{1,0:T(8,128)(2,1)S(1)}, u32[]{:S(2)}, u32[]{:S(2)}) collective-permute-start(bf16[256,512]{1,0:T(8,128)(2,1)S(1)} %bitcast.5), channel_id=1, source_target_pairs={{0,2},{1,3},{2,0},{3,1},{4,6},{5,7},{6,4},{7,5},{8,10},{9,11},{10,... | collective-permute-start | bytes 786440 | tf_op jit(solution)/shard_map/ppermute | solution.py:512
  17.1 4.1 %collective-permute-start.6 = (bf16[16,1536]{1,0:T(8,128)(2,1)S(1)}, bf16[16,1536]{1,0:T(8,128)(2,1)S(1)}, u32[]{:S(2)}, u32[]{:S(2)}) collective-permute-start(bf16[16,1536]{1,0:T(8,128)(2,1)S(1)} %get-tuple-element.61.send_ref.refs_0_), channel_id=1, source_target_pairs={{0,4},{4,0},{8,12},{12,8},{16,20},{20,16},{24,28},{28,24},{1,5},{5... | collective-permute-start | bytes 147464 | tf_op jit(solution)/shard_map/ppermute | solution.py:19
  21.2 6.0 %collective-permute-start.10 = (bf16[16,1536]{1,0:T(8,128)(2,1)S(1)}, bf16[16,1536]{1,0:T(8,128)(2,1)S(1)}, u32[]{:S(2)}, u32[]{:S(2)}) collective-permute-start(bf16[16,1536]{1,0:T(8,128)(2,1)S(1)} %get-tuple-element.65), channel_id=1, source_target_pairs={{0,24},{4,28},{8,16},{12,20},{16,8},{20,12},{24,0},{28,4},{1,25},{... | collective-permute-start | bytes 147464 | tf_op jit(solution)/shard_map/ppermute | solution.py:19
  22.7 6.0 %collective-permute-start.8 = (bf16[16,1536]{1,0:T(8,128)(2,1)S(1)}, bf16[16,1536]{1,0:T(8,128)(2,1)S(1)}, u32[]{:S(2)}, u32[]{:S(2)}) collective-permute-start(bf16[16,1536]{1,0:T(8,128)(2,1)S(1)} %get-tuple-element.65), channel_id=1, source_target_pairs={{0,8},{4,12},{8,0},{12,4},{16,24},{20,28},{24,16},{28,20},{1,9},{5... | collective-permute-start | bytes 147464 | tf_op jit(solution)/shard_map/ppermute | solution.py:19
  23.8 5.4 %collective-permute-start.11 = (bf16[256,512]{1,0:T(8,128)(2,1)S(1)}, bf16[256,512]{1,0:T(8,128)(2,1)S(1)}, u32[]{:S(2)}, u32[]{:S(2)}) collective-permute-start(bf16[256,512]{1,0:T(8,128)(2,1)S(1)} %bitcast.6), channel_id=1, source_target_pairs={{0,1},{1,0},{2,3},{3,2},{4,5},{5,4},{6,7},{7,6},{8,9},{9,8},{10,11... | collective-permute-start | bytes 786440 | tf_op jit(solution)/shard_map/ppermute | solution.py:512
  23.8 5.4 %collective-permute-start.9 = (bf16[16,512]{1,0:T(8,128)(2,1)S(1)}, bf16[16,512]{1,0:T(8,128)(2,1)S(1)}, u32[]{:S(2)}, u32[]{:S(2)}) collective-permute-start(bf16[16,512]{1,0:T(8,128)(2,1)S(1)} %get-tuple-element.64.refs_0_), channel_id=1, source_target_pairs={{0,16},{4,20},{8,24},{12,28},{16,0},{20,4},{24,8},{28,12},{1,17},{... | collective-permute-start | bytes 49160 | tf_op jit(solution)/shard_map/ppermute | solution.py:19
  25.6 3.6 %collective-permute-start.12 = (bf16[256,512]{1,0:T(8,128)(2,1)S(1)}, bf16[256,512]{1,0:T(8,128)(2,1)S(1)}, u32[]{:S(2)}, u32[]{:S(2)}) collective-permute-start(bf16[256,512]{1,0:T(8,128)(2,1)S(1)} %collective-permute-done.1.refs_14_.refs_12_), channel_id=1, source_target_pairs={{0,1},{1,0},{2,3},{3,2},{4,5},{5,4},{6,7},{7,6},{8,9},{9,8},{10,11... | collective-permute-start | bytes 786440 | tf_op jit(solution)/shard_map/ppermute | solution.py:519
  27.2 9.2 %collective-permute-start.7 = (bf16[352,512]{1,0:T(8,128)(2,1)S(1)}, bf16[352,512]{1,0:T(8,128)(2,1)S(1)}, u32[]{:S(2)}, u32[]{:S(2)}) collective-permute-start(bf16[352,512]{1,0:T(8,128)(2,1)S(1)} %collective-permute-done.refs_0_.refs_12_), channel_id=1, source_target_pairs={{0,2},{1,3},{2,0},{3,1},{4,6},{5,7},{6,4},{7,5},{8,10},{9,11},{10,... | collective-permute-start | bytes 1081352 | tf_op jit(solution)/shard_map/ppermute | solution.py:627
  30.7 8.4 %collective-permute-start.18 = (bf16[352,512]{1,0:T(8,128)(2,1)S(1)}, bf16[352,512]{1,0:T(8,128)(2,1)S(1)}, u32[]{:S(2)}, u32[]{:S(2)}) collective-permute-start(bf16[352,512]{1,0:T(8,128)(2,1)S(1)} %collective-permute-done.refs_0_.refs_12_), channel_id=1, source_target_pairs={{0,1},{1,0},{2,3},{3,2},{4,5},{5,4},{6,7},{7,6},{8,9},{9,8},{10,11... | collective-permute-start | bytes 1081352 | tf_op jit(solution)/shard_map/ppermute | solution.py:659
  30.7 4.0 %collective-permute-start.13 = (f32[16,640]{1,0:T(8,128)S(1)}, f32[16,640]{1,0:T(8,128)S(1)}, u32[]{:S(2)}, u32[]{:S(2)}) collective-permute-start(f32[16,640]{1,0:T(8,128)S(1)} %get-tuple-element.74), channel_id=1, source_target_pairs={{0,4},{4,0},{8,12},{12,8},{16,20},{20,16},{24,28},{28,24},{1,5},{5... | collective-permute-start | bytes 122888 | tf_op jit(solution)/shard_map/ppermute | solution.py:19
  32.4 7.1 %collective-permute-start.17 = (f32[16,1024]{1,0:T(8,128)S(1)}, f32[16,1024]{1,0:T(8,128)S(1)}, u32[]{:S(2)}, u32[]{:S(2)}) collective-permute-start(f32[16,1024]{1,0:T(8,128)S(1)} %get-tuple-element.78), channel_id=1, source_target_pairs={{0,4},{4,0},{8,12},{12,8},{16,20},{20,16},{24,28},{28,24},{1,5},{5... | collective-permute-start | bytes 196616 | tf_op jit(solution)/shard_map/ppermute | solution.py:19
  34.7 6.1 %collective-permute-start.16 = (f32[16,640]{1,0:T(8,128)S(1)}, f32[16,640]{1,0:T(8,128)S(1)}, u32[]{:S(2)}, u32[]{:S(2)}) collective-permute-start(f32[16,640]{1,0:T(8,128)S(1)} %add.10.refs_0_), channel_id=1, source_target_pairs={{0,24},{4,28},{8,16},{12,20},{16,8},{20,12},{24,0},{28,4},{1,25},{... | collective-permute-start | bytes 122888 | tf_op jit(solution)/shard_map/ppermute | solution.py:19
  36.2 5.4 %collective-permute-start.15 = (f32[16,640]{1,0:T(8,128)S(1)}, f32[16,640]{1,0:T(8,128)S(1)}, u32[]{:S(2)}, u32[]{:S(2)}) collective-permute-start(f32[16,640]{1,0:T(8,128)S(1)} %add.10.refs_0_), channel_id=1, source_target_pairs={{0,16},{4,20},{8,24},{12,28},{16,0},{20,4},{24,8},{28,12},{1,17},{... | collective-permute-start | bytes 122888 | tf_op jit(solution)/shard_map/ppermute | solution.py:19
  36.5 5.2 %collective-permute-start.14 = (f32[16,640]{1,0:T(8,128)S(1)}, f32[16,640]{1,0:T(8,128)S(1)}, u32[]{:S(2)}, u32[]{:S(2)}) collective-permute-start(f32[16,640]{1,0:T(8,128)S(1)} %add.10.refs_0_), channel_id=1, source_target_pairs={{0,8},{4,12},{8,0},{12,4},{16,24},{20,28},{24,16},{28,20},{1,9},{5... | collective-permute-start | bytes 122888 | tf_op jit(solution)/shard_map/ppermute | solution.py:19
  39.1 2.5 %collective-permute-start.19 = (bf16[352,512]{1,0:T(8,128)(2,1)S(1)}, bf16[352,512]{1,0:T(8,128)(2,1)S(1)}, u32[]{:S(2)}, u32[]{:S(2)}) collective-permute-start(bf16[352,512]{1,0:T(8,128)(2,1)S(1)} %collective-permute-done.7.refs_2_.refs_14_), channel_id=1, source_target_pairs={{0,1},{1,0},{2,3},{3,2},{4,5},{5,4},{6,7},{7,6},{8,9},{9,8},{10,11... | collective-permute-start | bytes 1081352 | tf_op jit(solution)/shard_map/ppermute | solution.py:659
  42.8 6.1 %collective-permute-start.22 = (bf16[16,1536]{1,0:T(8,128)(2,1)S(1)}, bf16[16,1536]{1,0:T(8,128)(2,1)S(1)}, u32[]{:S(2)}, u32[]{:S(2)}) collective-permute-start(bf16[16,1536]{1,0:T(8,128)(2,1)S(1)} %get-tuple-element.84.refs_1_), channel_id=1, source_target_pairs={{0,24},{4,28},{8,16},{12,20},{16,8},{20,12},{24,0},{28,4},{1,25},{... | collective-permute-start | bytes 147464 | tf_op jit(solution)/shard_map/ppermute | solution.py:19
  44.7 4.5 %collective-permute-start.20 = (bf16[16,1536]{1,0:T(8,128)(2,1)S(1)}, bf16[16,1536]{1,0:T(8,128)(2,1)S(1)}, u32[]{:S(2)}, u32[]{:S(2)}) collective-permute-start(bf16[16,1536]{1,0:T(8,128)(2,1)S(1)} %get-tuple-element.84.refs_1_), channel_id=1, source_target_pairs={{0,8},{4,12},{8,0},{12,4},{16,24},{20,28},{24,16},{28,20},{1,9},{5... | collective-permute-start | bytes 147464 | tf_op jit(solution)/shard_map/ppermute | solution.py:19
  44.8 4.8 %collective-permute-start.21 = (bf16[16,512]{1,0:T(8,128)(2,1)S(1)}, bf16[16,512]{1,0:T(8,128)(2,1)S(1)}, u32[]{:S(2)}, u32[]{:S(2)}) collective-permute-start(bf16[16,512]{1,0:T(8,128)(2,1)S(1)} %get-tuple-element.83.refs_0_), channel_id=1, source_target_pairs={{0,16},{4,20},{8,24},{12,28},{16,0},{20,4},{24,8},{28,12},{1,17},{... | collective-permute-start | bytes 49160 | tf_op jit(solution)/shard_map/ppermute | solution.py:19
  50.5 3.7 %collective-permute-start.23 = (f32[16,128]{1,0:T(8,128)S(1)}, f32[16,128]{1,0:T(8,128)S(1)}, u32[]{:S(2)}, u32[]{:S(2)}) collective-permute-start(f32[16,128]{1,0:T(8,128)S(1)} %fourth.1), channel_id=1, source_target_pairs={{0,4},{4,0},{8,12},{12,8},{16,20},{20,16},{24,28},{28,24},{1,5},{5... | collective-permute-start | bytes 24584 | tf_op jit(solution)/shard_map/ppermute | solution.py:19
  54.2 5.4 %collective-permute-start.26 = (f32[16,128]{1,0:T(8,128)S(1)}, f32[16,128]{1,0:T(8,128)S(1)}, u32[]{:S(2)}, u32[]{:S(2)}) collective-permute-start(f32[16,128]{1,0:T(8,128)S(1)} %add.11.refs_0_), channel_id=1, source_target_pairs={{0,24},{4,28},{8,16},{12,20},{16,8},{20,12},{24,0},{28,4},{1,25},{... | collective-permute-start | bytes 24584 | tf_op jit(solution)/shard_map/ppermute | solution.py:19
  56.4 4.7 %collective-permute-start.25 = (f32[16,128]{1,0:T(8,128)S(1)}, f32[16,128]{1,0:T(8,128)S(1)}, u32[]{:S(2)}, u32[]{:S(2)}) collective-permute-start(f32[16,128]{1,0:T(8,128)S(1)} %add.11.refs_0_), channel_id=1, source_target_pairs={{0,16},{4,20},{8,24},{12,28},{16,0},{20,4},{24,8},{28,12},{1,17},{... | collective-permute-start | bytes 24584 | tf_op jit(solution)/shard_map/ppermute | solution.py:19
  57.3 3.7 %collective-permute-start.24 = (f32[16,128]{1,0:T(8,128)S(1)}, f32[16,128]{1,0:T(8,128)S(1)}, u32[]{:S(2)}, u32[]{:S(2)}) collective-permute-start(f32[16,128]{1,0:T(8,128)S(1)} %add.11.refs_0_), channel_id=1, source_target_pairs={{0,8},{4,12},{8,0},{12,4},{16,24},{20,28},{24,16},{28,20},{1,9},{5... | collective-permute-start | bytes 24584 | tf_op jit(solution)/shard_map/ppermute | solution.py:19
